TPU v7x, 32 devices: a whole 2x2x4 slice. The times are simulated.
32 devices in a mesh: groups: 2 (over y), brick: 8 (over z, x), batch: 2 (over core).
Axes of the slice: x: 2, y: 2, z: 4, core: 2. Of those that a mesh axis runs over, the one named last changes fastest.
Arguments:
- features: bfloat16 [4, 2048, 128], P(('groups', 'batch'), 'brick'), parts along dimension 0, may hold values from -6 to 6
- cotangent: bfloat16 [4, 2048, 128], P(('groups', 'batch'), 'brick'), parts along dimension 0, may hold values from -6 to 6
- neighbours: int32 [27, 4096], P(None, ('groups', 'brick')), parts along dimension 1, may hold values from -1 to 2047, as said below
- timesteps: int32 [4], P(('groups', 'batch')), parts along dimension 0, may hold values from 0 to 999
- condition: bfloat16 [4, 128], P(('groups', 'batch')), parts along dimension 0, may hold values from -6 to 6
- w_time: bfloat16 [128, 128], replicated, may hold values from -0.5 to 0.5
- w_conv: bfloat16 [27, 128, 128], replicated, may hold values from -0.109375 to 0.109375
Outputs:
- conv_out: bfloat16 [4, 2048, 128], P(('groups', 'batch'), 'brick'), parts along dimension 0
- feature_grad: bfloat16 [4, 2048, 128], P(('groups', 'batch'), 'brick'), parts along dimension 0
- weight_grad: float32 [54, 128, 128], P('groups'), parts along dimension 0
There are 2 independent parts, one for each index of `groups`. A program takes and returns all parts, laid end to end along the dimension named above; an argument that names none is the same for every part. Nothing has to cross between parts.
Inputs may be any that keep to these rules, and one draw needn't show every extreme that they name: `neighbours`: entry k, b is the voxel at offset (k // 9 - 1, k // 3 % 3 - 1, k % 3 - 1) from voxel b, or -1 if it is not occupied; entry 13 is b itself; c stands at offset k of b exactly when b stands at offset 26 - k of c. The ground is a grid of device tiles of 4 x 4 columns, 2 ** ((log2 8 + 1) // 2) tiles along the first dimension and 2 ** (log2 8 // 2) along the second, device i holding tile (i // tiles along the second, i % tiles along the second) and voxels i * 256 to (i + 1) * 256 - 1; within a device, voxel ((u * 4) + v) * 16 + l is layer l of column (u, v) of its tile. Neighbours differ by at most one column along each ground dimension.
All inputs are finite; a program needn't handle non-finite values.
Results may differ from a plain program's by a relative error of at most 0.0052.
Values may be sent and summed in bfloat16 or wider, within the bound.
No kernel may reach another device: no remote copies, remote signals or barrier semaphores. Data moves between devices by JAX's collectives and lax.ppermute only.
A program may use at most 64 MiB of HBM per device.

v0:
```python
import jax
import jax.numpy as jnp
from jax import lax
from jax.sharding import PartitionSpec as P

LAYERS = 16
TILE = 4


def passed_along(block, axis, distance):
    devices = range(lax.axis_size(axis))
    route = [(i - distance, i) for i in devices if i - distance in devices]
    return lax.ppermute(block, axis, route)


def shifted(timesteps, condition, w_time):
    half = condition.shape[1] // 2
    freq = jnp.exp(-jnp.log(10000.0) * jnp.arange(half, dtype=jnp.float32) / half)
    angle = timesteps.astype(jnp.float32)[:, None] * freq[None, :]
    temb = jnp.concatenate([jnp.sin(angle), jnp.cos(angle)], axis=1).astype(jnp.bfloat16)
    return jnp.dot(temb, w_time, preferred_element_type=jnp.float32) + condition.astype(jnp.float32)


def slab_rows(block, side_recv, front_recv, width):
    widened = jnp.concatenate([side_recv[0], block, side_recv[1]], axis=1)
    slab = jnp.concatenate([front_recv[0][None], widened, front_recv[1][None]], axis=0)
    flat = slab.reshape(-1, width)
    return jnp.concatenate([flat, jnp.zeros((1, width), jnp.bfloat16)], axis=0)


def shards(features, cotangent, neighbours, timesteps, condition, w_time, w_conv):
    rows_here = features.shape[1]
    width = features.shape[2]
    peers = lax.axis_size("brick")
    bits = peers.bit_length() - 1
    tiles_y = 2 ** (bits // 2)
    here = lax.axis_index("brick")
    tile_x = here // tiles_y
    tile_y = here % tiles_y
    side = TILE
    layers = LAYERS
    wide = side + 2
    valid = neighbours >= 0
    safe = jnp.where(valid, neighbours, 0)
    owner = safe // rows_here
    inside = safe % rows_here
    column = inside // layers
    layer = inside % layers
    local_x = (owner // tiles_y - tile_x) * side + column // side + 1
    local_y = (owner % tiles_y - tile_y) * side + column % side + 1
    sentinel = wide * wide * layers
    ext_index = jnp.where(valid, (local_x * wide + local_y) * layers + layer, sentinel).T
    shift = shifted(timesteps, condition, w_time)
    z_val = features[0].astype(jnp.float32) + shift[0][None, :]
    act = jax.nn.silu(z_val).astype(jnp.bfloat16)
    cot = cotangent[0]
    act_block = act.reshape(side, side, layers, width)
    cot_block = cot.reshape(side, side, layers, width)
    w_forward = w_conv.reshape(27 * width, width)
    w_backward = jnp.transpose(w_conv[::-1], (0, 2, 1)).reshape(27 * width, width)
    side_moves = ((1, side - 1), (-1, 0))
    front_moves = ((tiles_y, side - 1), (-tiles_y, 0))
    act_list = []
    for by, edge in side_moves:
        act_list.append(passed_along(act_block[:, edge], "brick", by))
    act_side = (act_list[0][:, None], act_list[1][:, None])
    act_wide = jnp.concatenate([act_side[0], act_block, act_side[1]], axis=1)
    act_fronts = []
    for by, edge in front_moves:
        act_fronts.append(passed_along(act_wide[edge], "brick", by))
    act_front = (act_fronts[0], act_fronts[1])
    act_ext = slab_rows(act_block, act_side, act_front, width)
    gathered = act_ext[ext_index].reshape(rows_here, 27 * width)
    conv_out = jnp.dot(gathered, w_forward, preferred_element_type=jnp.float32).astype(jnp.bfloat16)
    partial_grad = lax.dot_general(
        gathered, cot, (((0,), (0,)), ((), ())), preferred_element_type=jnp.float32
    )
    weight_grad = lax.psum(partial_grad.reshape(27, width, width), ("brick", "batch"))
    cot_list = []
    for by, edge in side_moves:
        cot_list.append(passed_along(cot_block[:, edge], "brick", by))
    cot_side = (cot_list[0][:, None], cot_list[1][:, None])
    cot_wide = jnp.concatenate([cot_side[0], cot_block, cot_side[1]], axis=1)
    cot_fronts = []
    for by, edge in front_moves:
        cot_fronts.append(passed_along(cot_wide[edge], "brick", by))
    cot_front = (cot_fronts[0], cot_fronts[1])
    cot_ext = slab_rows(cot_block, cot_side, cot_front, width)
    cot_gathered = cot_ext[ext_index].reshape(rows_here, 27 * width)
    back = jnp.dot(cot_gathered, w_backward, preferred_element_type=jnp.float32)
    sig = jax.nn.sigmoid(z_val)
    feature_grad = (back * sig * (1.0 + z_val * (1.0 - sig))).astype(jnp.bfloat16)
    return (conv_out[None], feature_grad[None], weight_grad)


def solution(mesh):
    in_specs = (
        P(("groups", "batch"), "brick", None),
        P(("groups", "batch"), "brick", None),
        P(None, ("groups", "brick")),
        P(("groups", "batch")),
        P(("groups", "batch"), None),
        P(),
        P(),
    )
    out_specs = (
        P(("groups", "batch"), "brick", None),
        P(("groups", "batch"), "brick", None),
        P("groups", None, None),
    )
    return jax.shard_map(shards, mesh=mesh, in_specs=in_specs, out_specs=out_specs, check_vma=False)
```

profile of v0, /device:TPU:0, one launch (start us, length us, event | category | flops | bytes accessed | tf_op | source)
XLA Modules:
  0.0 159.2 jit_solution(205310506975385260)
XLA Ops:
  7.2 0.0 copy-start
  7.2 0.0 all-reduce.4.cloned.1.call-start
  7.9 0.1 cosine_convert_fusion
  7.9 0.0 copy-done
  7.9 0.8 fusion.28
  8.8 0.9 multiply_convert_fusion
  9.7 1.3 collective-permute-start.1
  11.0 5.5 %collective-permute-start = (bf16[4,16,128]{2,1,0:T(8,128)(2,1)S(1)}, bf16[4,16,128]{2,1,0:T(8,128)(2,1)S(1)}, u32[]{:S(2)}, u32[]{:S(2)}) collective-permute-start(bf16[4,16,128]{2,1,0:T(8,128)(2,1)S(1)} %get-tuple-element.9), channel_id=1, source_target_pairs={{0,2},{2,4},{4,6},{6,8},{8,10},{10,12},{12,14},{1,3},{3,5},{5,7},{... | collective-permute-start | bytes 49160 | tf_op jit(solution)/shard_map/ppermute | solution.py:13
  16.5 0.9 compare_select_fusion
  17.4 0.1 copy.20
  17.5 0.2 reshape.57
  17.7 0.0 collective-permute-done.1
  17.7 0.2 collective-permute-done
  17.9 1.3 collective-permute-start.3
  19.2 7.2 %collective-permute-start.2 = (bf16[6,16,128]{2,1,0:T(8,128)(2,1)S(1)}, bf16[6,16,128]{2,1,0:T(8,128)(2,1)S(1)}, u32[]{:S(2)}, u32[]{:S(2)}) collective-permute-start(bf16[6,16,128]{2,1,0:T(8,128)(2,1)S(1)} %get-tuple-element.5), channel_id=1, source_target_pairs={{0,4},{2,6},{4,8},{6,10},{8,12},{10,14},{1,5},{3,7},{5,9},{7,11},{... | collective-permute-start | bytes 73736 | tf_op jit(solution)/shard_map/ppermute | solution.py:13
  26.4 0.0 collective-permute-done.3
  26.4 1.5 collective-permute-done.2
  27.9 13.0 %gather_fusion = bf16[6912,128]{1,0:T(8,128)(2,1)S(1)} fusion(bf16[577,128]{1,0:T(8,128)(2,1)S(1)} %concatenate.30, s32[7168]{0:T(1024)S(1)} %pad_clamp_fusion), kind=kCustom, calls=%fused_computation | custom fusion | bytes 3566592 | tf_op jit(solution)/shard_map/gather | solution.py:73
  41.0 2.9 %reshape.52 = bf16[256,3456]{1,0:T(8,128)(2,1)} reshape(bf16[6912,128]{1,0:T(8,128)(2,1)S(1)} %gather_fusion) | data formatting | bytes 3538944 | tf_op jit(solution)/shard_map/reshape | solution.py:73
  43.9 0.0 copy-start.4
  43.9 3.9 %copy.26 = bf16[3456,256]{1,0:T(8,128)(2,1)} copy(bf16[3456,256]{0,1:T(8,128)(2,1)} %bitcast.85) | data formatting | bytes 3538944 | tf_op jit(solution)/shard_map/dot_general | solution.py:75
  47.8 0.0 copy-done.4
  47.8 3.3 %fusion.30 = f32[27,128,128]{2,1,0:T(8,128)} fusion(bf16[27,128,256]{2,1,0:T(8,128)(2,1)} %bitcast.84, bf16[1,256,128]{2,1,0:T(8,128)(2,1)S(1)} %copy-done.4), kind=kOutput, calls=%fused_computation.22 | convolution fusion | flops 226492416 | bytes 3604480 | tf_op jit(solution)/shard_map/dot_general | solution.py:75
  51.1 0.0 copy-start.2
  51.1 0.0 all-reduce.4.cloned.1.call-update
  51.1 1.4 collective-permute-start.5
  52.6 4.5 %collective-permute-start.4 = (bf16[4,16,128]{2,1,0:T(8,128)(2,1)S(1)}, bf16[4,16,128]{2,1,0:T(8,128)(2,1)S(1)}, u32[]{:S(2)}, u32[]{:S(2)}) collective-permute-start(bf16[4,16,128]{2,1,0:T(8,128)(2,1)S(1)} %get-tuple-element.7), channel_id=1, source_target_pairs={{0,2},{2,4},{4,6},{6,8},{8,10},{10,12},{12,14},{1,3},{3,5},{5,7},{... | collective-permute-start | bytes 49160 | tf_op jit(solution)/shard_map/ppermute | solution.py:13
  57.1 0.0 collective-permute-done.5
  57.1 1.4 collective-permute-done.4
  58.5 1.3 collective-permute-start.7
  59.8 6.1 %collective-permute-start.6 = (bf16[6,16,128]{2,1,0:T(8,128)(2,1)S(1)}, bf16[6,16,128]{2,1,0:T(8,128)(2,1)S(1)}, u32[]{:S(2)}, u32[]{:S(2)}) collective-permute-start(bf16[6,16,128]{2,1,0:T(8,128)(2,1)S(1)} %get-tuple-element.3), channel_id=1, source_target_pairs={{0,4},{2,6},{4,8},{6,10},{8,12},{10,14},{1,5},{3,7},{5,9},{7,11},{... | collective-permute-start | bytes 73736 | tf_op jit(solution)/shard_map/ppermute | solution.py:13
  66.0 0.0 copy-done.2
  66.0 1.0 rev.3
  67.0 1.6 %reshape.56 = bf16[256,27,128]{2,1,0:T(8,128)(2,1)} reshape(bf16[6912,128]{1,0:T(8,128)(2,1)S(1)} %gather_fusion) | data formatting | bytes 3538944 | tf_op jit(solution)/shard_map/gather | solution.py:73
  68.6 0.0 collective-permute-done.7
  68.6 0.0 collective-permute-done.6
  68.7 13.0 %gather_fusion.1 = bf16[6912,128]{1,0:T(8,128)(2,1)S(1)} fusion(bf16[577,128]{1,0:T(8,128)(2,1)S(1)} %concatenate.33, s32[7168]{0:T(1024)S(1)} %pad_clamp_fusion), kind=kCustom, calls=%fused_computation.1 | custom fusion | bytes 3566592 | tf_op jit(solution)/shard_map/gather | solution.py:89
  81.7 1.6 %reshape.64 = bf16[256,27,128]{2,1,0:T(8,128)(2,1)} reshape(bf16[6912,128]{1,0:T(8,128)(2,1)S(1)} %gather_fusion.1) | data formatting | bytes 3538944 | tf_op jit(solution)/shard_map/gather | solution.py:89
  83.4 0.0 copy-start.1
  83.4 0.0 copy-start.3
  83.4 0.0 copy-start.5
  83.4 3.1 %fusion.22 = bf16[1,256,128]{2,1,0:T(8,128)(2,1)} fusion(bf16[27,128,128]{2,1,0:T(8,128)(2,1)S(1)} %copy-done.2, bf16[256,27,128]{2,1,0:T(8,128)(2,1)} %reshape.56), kind=kOutput, calls=%fused_computation.12 | convolution fusion | flops 226525184 | bytes 2719744 | tf_op jit(solution)/shard_map/dot_general | solution.py:74
  86.5 0.0 copy-done.1
  86.5 0.0 copy-done.3
  86.5 0.0 copy-done.5
  86.5 1.3 fusion.25
  87.8 61.7 %all-reduce.4.cloned.1.call-done = f32[27,128,128]{2,1,0:T(8,128)} async-done(((f32[27,128,128]{2,1,0:T(8,128)}), f32[27,128,128]{2,1,0:T(8,128)}) %all-reduce.4.cloned.1.call-update) | async-done | bytes 1769488 | tf_op jit(solution)/shard_map/psum | solution.py:78
  149.5 2.9 %copy.53 = f32[27,128,128]{2,1,0:T(8,128)} copy(f32[27,128,128]{2,1,0:T(8,128)} %all-reduce.4.cloned.1.call-done) | data formatting | bytes 3538944
  (9 shorter events, 0.1 us)
Async XLA Ops:
  7.2 0.8 copy-start
  7.2 142.3 %all-reduce.4.cloned.1.call-start = ((), (), s32[]{:S(2)}) async-start(), calls=%async_computation | async-start | bytes 3538944 | tf_op jit(solution)/shard_map/psum | solution.py:78
  9.7 8.0 %collective-permute-start.1 = (bf16[4,16,128]{2,1,0:T(8,128)(2,1)S(1)}, bf16[4,16,128]{2,1,0:T(8,128)(2,1)S(1)}, u32[]{:S(2)}, u32[]{:S(2)}) collective-permute-start(bf16[4,16,128]{2,1,0:T(8,128)(2,1)S(1)} %get-tuple-element.10), channel_id=1, source_target_pairs={{2,0},{4,2},{6,4},{8,6},{10,8},{12,10},{14,12},{3,1},{5,3},{7,5},{... | collective-permute-start | bytes 49160 | tf_op jit(solution)/shard_map/ppermute | solution.py:13
  11.0 6.9 %collective-permute-start = (bf16[4,16,128]{2,1,0:T(8,128)(2,1)S(1)}, bf16[4,16,128]{2,1,0:T(8,128)(2,1)S(1)}, u32[]{:S(2)}, u32[]{:S(2)}) collective-permute-start(bf16[4,16,128]{2,1,0:T(8,128)(2,1)S(1)} %get-tuple-element.9), channel_id=1, source_target_pairs={{0,2},{2,4},{4,6},{6,8},{8,10},{10,12},{12,14},{1,3},{3,5},{5,7},{... | collective-permute-start | bytes 49160 | tf_op jit(solution)/shard_map/ppermute | solution.py:13
  17.9 8.5 %collective-permute-start.3 = (bf16[6,16,128]{2,1,0:T(8,128)(2,1)S(1)}, bf16[6,16,128]{2,1,0:T(8,128)(2,1)S(1)}, u32[]{:S(2)}, u32[]{:S(2)}) collective-permute-start(bf16[6,16,128]{2,1,0:T(8,128)(2,1)S(1)} %get-tuple-element.6), channel_id=1, source_target_pairs={{4,0},{6,2},{8,4},{10,6},{12,8},{14,10},{5,1},{7,3},{9,5},{11,7},{... | collective-permute-start | bytes 73736 | tf_op jit(solution)/shard_map/ppermute | solution.py:13
  19.2 8.7 %collective-permute-start.2 = (bf16[6,16,128]{2,1,0:T(8,128)(2,1)S(1)}, bf16[6,16,128]{2,1,0:T(8,128)(2,1)S(1)}, u32[]{:S(2)}, u32[]{:S(2)}) collective-permute-start(bf16[6,16,128]{2,1,0:T(8,128)(2,1)S(1)} %get-tuple-element.5), channel_id=1, source_target_pairs={{0,4},{2,6},{4,8},{6,10},{8,12},{10,14},{1,5},{3,7},{5,9},{7,11},{... | collective-permute-start | bytes 73736 | tf_op jit(solution)/shard_map/ppermute | solution.py:13
  43.9 3.9 %copy-start.4 = (bf16[1,256,128]{2,1,0:T(8,128)(2,1)S(1)}, bf16[1,256,128]{2,1,0:T(8,128)(2,1)}, u32[]{:S(2)}) copy-start(bf16[1,256,128]{2,1,0:T(8,128)(2,1)} %param.8) | copy-start | bytes 196612
  51.1 14.9 %copy-start.2 = (bf16[27,128,128]{2,1,0:T(8,128)(2,1)S(1)}, bf16[27,128,128]{2,1,0:T(8,128)(2,1)}, u32[]{:S(2)}) copy-start(bf16[27,128,128]{2,1,0:T(8,128)(2,1)} %param.13) | copy-start | bytes 2654212
  51.1 6.0 %collective-permute-start.5 = (bf16[4,16,128]{2,1,0:T(8,128)(2,1)S(1)}, bf16[4,16,128]{2,1,0:T(8,128)(2,1)S(1)}, u32[]{:S(2)}, u32[]{:S(2)}) collective-permute-start(bf16[4,16,128]{2,1,0:T(8,128)(2,1)S(1)} %get-tuple-element.8), channel_id=1, source_target_pairs={{2,0},{4,2},{6,4},{8,6},{10,8},{12,10},{14,12},{3,1},{5,3},{7,5},{... | collective-permute-start | bytes 49160 | tf_op jit(solution)/shard_map/ppermute | solution.py:13
  52.6 6.0 %collective-permute-start.4 = (bf16[4,16,128]{2,1,0:T(8,128)(2,1)S(1)}, bf16[4,16,128]{2,1,0:T(8,128)(2,1)S(1)}, u32[]{:S(2)}, u32[]{:S(2)}) collective-permute-start(bf16[4,16,128]{2,1,0:T(8,128)(2,1)S(1)} %get-tuple-element.7), channel_id=1, source_target_pairs={{0,2},{2,4},{4,6},{6,8},{8,10},{10,12},{12,14},{1,3},{3,5},{5,7},{... | collective-permute-start | bytes 49160 | tf_op jit(solution)/shard_map/ppermute | solution.py:13
  58.5 10.1 %collective-permute-start.7 = (bf16[6,16,128]{2,1,0:T(8,128)(2,1)S(1)}, bf16[6,16,128]{2,1,0:T(8,128)(2,1)S(1)}, u32[]{:S(2)}, u32[]{:S(2)}) collective-permute-start(bf16[6,16,128]{2,1,0:T(8,128)(2,1)S(1)} %get-tuple-element.4), channel_id=1, source_target_pairs={{4,0},{6,2},{8,4},{10,6},{12,8},{14,10},{5,1},{7,3},{9,5},{11,7},{... | collective-permute-start | bytes 73736 | tf_op jit(solution)/shard_map/ppermute | solution.py:13
  59.8 8.8 %collective-permute-start.6 = (bf16[6,16,128]{2,1,0:T(8,128)(2,1)S(1)}, bf16[6,16,128]{2,1,0:T(8,128)(2,1)S(1)}, u32[]{:S(2)}, u32[]{:S(2)}) collective-permute-start(bf16[6,16,128]{2,1,0:T(8,128)(2,1)S(1)} %get-tuple-element.3), channel_id=1, source_target_pairs={{0,4},{2,6},{4,8},{6,10},{8,12},{10,14},{1,5},{3,7},{5,9},{7,11},{... | collective-permute-start | bytes 73736 | tf_op jit(solution)/shard_map/ppermute | solution.py:13
  83.4 3.1 %copy-start.1 = (bf16[256,27,128]{2,1,0:T(8,128)(2,1)S(1)}, bf16[256,27,128]{2,1,0:T(8,128)(2,1)}, u32[]{:S(2)}) copy-start(bf16[256,27,128]{2,1,0:T(8,128)(2,1)} %reshape.64) | copy-start | bytes 5308420
  83.4 3.1 %copy-start.3 = (bf16[27,128,128]{2,1,0:T(8,128)(2,1)S(1)}, bf16[27,128,128]{2,1,0:T(8,128)(2,1)}, u32[]{:S(2)}) copy-start(bf16[27,128,128]{2,1,0:T(8,128)(2,1)} %rev.3) | copy-start | bytes 2654212
  83.4 3.1 %copy-start.5 = (bf16[1,256,128]{2,1,0:T(8,128)(2,1)S(1)}, bf16[1,256,128]{2,1,0:T(8,128)(2,1)}, u32[]{:S(2)}) copy-start(bf16[1,256,128]{2,1,0:T(8,128)(2,1)} %param.7) | copy-start | bytes 196612
Sparse Core Ops, SparseCore 0:
  51.2 98.2 all-reduce.3
where the time goes:
time: 160 us; the launch traced here: 159 us
  waiting for transfers between devices  64.8 us (40%)
  local copies, waits for them, and re-layouts  40.4 us (25%)
  starting transfers between devices  28.7 us (18%)
  between operations  14.9 us (9%)
  matrix products  8.61 us (5%)
  other arithmetic  1.92 us (1%)
    psum x1, waiting for transfers between devices, shards(): lax.psum(partial_grad.reshape(27, width, width), ('brick', 'batch'))  61.7 us
    ppermute x8, starting transfers between devices, passed_along(): return lax.ppermute(block, axis, route)  28.6 us
    gather x2, local copies, waits for them, and re-layouts, shards(): cot_gathered = cot_ext[ext_index].reshape(rows_here, 27 * width)  14.7 us
    gather x2, local copies, waits for them, and re-layouts, shards(): gathered = act_ext[ext_index].reshape(rows_here, 27 * width)  14.7 us
    dot_general x1, local copies, waits for them, and re-layouts, shards(): lax.dot_general(gathered, cot, (((0,), (0,)), ((), ())), preferred_elemen...  3.91 us
    dot_general x1, matrix products, shards(): lax.dot_general(gathered, cot, (((0,), (0,)), ((), ())), preferred_elemen...  3.31 us
  transfers between devices with their start and end apart: 9, of which 4 were waited for; matrix products, arithmetic and copies ran while one was open for 14% of the time, Pallas kernels for 0%

commit v1 on v0

--- a/solution.py
+++ b/solution.py
@@ -75,7 +75,15 @@
     partial_grad = lax.dot_general(
         gathered, cot, (((0,), (0,)), ((), ())), preferred_element_type=jnp.float32
     )
-    weight_grad = lax.psum(partial_grad.reshape(27, width, width), ("brick", "batch"))
+    both = ("brick", "batch")
+    parts = peers * lax.axis_size("batch")
+    rows = 27 * width
+    extra = -rows % (8 * parts)
+    pieces = jnp.pad(partial_grad.astype(jnp.bfloat16), ((0, extra), (0, 0))).reshape(parts, -1, width)
+    arrived = lax.all_to_all(pieces, both, 0, 0)
+    summed = arrived.astype(jnp.float32).sum(0).astype(jnp.bfloat16)
+    whole = lax.all_gather(summed, both, axis=0, tiled=True)
+    weight_grad = whole[:rows].astype(jnp.float32).reshape(27, width, width)
     cot_list = []
     for by, edge in side_moves:
         cot_list.append(passed_along(cot_block[:, edge], "brick", by))

time: 160 us -> 121 us (0.76)
  waiting for transfers between devices: 64.8 us -> 3.69 us
  blocking collectives: 0 us -> 26.1 us
  starting transfers between devices: 28.7 us -> 42.4 us
  between operations: 14.9 us -> 1.51 us
  local copies, waits for them, and re-layouts: 40.4 us -> 34.8 us
    psum x1 -> x0, waiting for transfers between devices: 61.7 us -> none  [shards(): lax.psum(partial_grad.reshape(27, width, width), ('brick', 'batch'))]
    all_gather x0 -> x1, blocking collectives: none -> 26.1 us  [shards(): whole = lax.all_gather(summed, both, axis=0, tiled=True)]
    ppermute x8, starting transfers between devices: 28.6 us -> 36.3 us  [passed_along(): return lax.ppermute(block, axis, route)]
    all_to_all x0 -> x1, starting transfers between devices: none -> 6.14 us  [shards(): arrived = lax.all_to_all(pieces, both, 0, 0)]
    dot_general x1 -> x0, local copies, waits for them, and re-layouts: 3.91 us -> none  [shards(): lax.dot_general(gathered, cot, (((0,), (0,)), ((), ())), preferred_elemen...]
    unnamed x13 -> x10, local copies, waits for them, and re-layouts: 2.9 us -> 0.08 us
  transfers between devices with their start and end apart: 9 -> 9, of which waited for: 4 -> 3; matrix products, arithmetic and copies ran while one was open for 14% -> 20% of each run, Pallas kernels for 0% -> 0%
where the time goes in v1:
time: 121 us
  starting transfers between devices  42.4 us (35%)
  local copies, waits for them, and re-layouts  34.8 us (29%)
  blocking collectives  26.1 us (22%)
  matrix products  8.58 us (7%)
  waiting for transfers between devices  3.69 us (3%)
  other arithmetic  3.46 us (3%)
  between operations  1.51 us (1%)
    ppermute x8, starting transfers between devices, passed_along(): return lax.ppermute(block, axis, route)  36.3 us
    all_gather x1, blocking collectives, shards(): whole = lax.all_gather(summed, both, axis=0, tiled=True)  26.1 us
    gather x2, local copies, waits for them, and re-layouts, shards(): gathered = act_ext[ext_index].reshape(rows_here, 27 * width)  14.7 us
    gather x2, local copies, waits for them, and re-layouts, shards(): cot_gathered = cot_ext[ext_index].reshape(rows_here, 27 * width)  14.7 us
    all_to_all x1, starting transfers between devices, shards(): arrived = lax.all_to_all(pieces, both, 0, 0)  6.14 us
    ppermute x8, waiting for transfers between devices, passed_along(): return lax.ppermute(block, axis, route)  3.68 us
    dot_general x1, matrix products, shards(): jnp.dot(gathered, w_forward, preferred_element_type=jnp.float32)  3.35 us
    dot_general x1, matrix products, shards(): lax.dot_general(gathered, cot, (((0,), (0,)), ((), ())), preferred_elemen...  3.07 us
  transfers between devices with their start and end apart: 9, of which 3 were waited for; matrix products, arithmetic and copies ran while one was open for 20% of the time, Pallas kernels for 0%

profile of v1, /device:TPU:0, one launch (start us, length us, event | category | flops | bytes accessed | tf_op | source)
XLA Modules:
  0.0 120.5 jit_solution(653244935613179622)
XLA Ops:
  0.6 0.0 copy-start
  1.3 0.1 cosine_convert_fusion
  1.4 0.1 copy-done
  1.4 0.8 fusion.28
  2.2 0.9 multiply_convert_fusion
  3.2 1.3 %collective-permute-start.1 = (bf16[4,16,128]{2,1,0:T(8,128)(2,1)S(1)}, bf16[4,16,128]{2,1,0:T(8,128)(2,1)S(1)}, u32[]{:S(2)}, u32[]{:S(2)}) collective-permute-start(bf16[4,16,128]{2,1,0:T(8,128)(2,1)S(1)} %get-tuple-element.10), channel_id=1, source_target_pairs={{2,0},{4,2},{6,4},{8,6},{10,8},{12,10},{14,12},{3,1},{5,3},{7,5},{... | collective-permute-start | bytes 49160 | tf_op jit(solution)/shard_map/ppermute | solution.py:13
  4.5 5.5 %collective-permute-start = (bf16[4,16,128]{2,1,0:T(8,128)(2,1)S(1)}, bf16[4,16,128]{2,1,0:T(8,128)(2,1)S(1)}, u32[]{:S(2)}, u32[]{:S(2)}) collective-permute-start(bf16[4,16,128]{2,1,0:T(8,128)(2,1)S(1)} %get-tuple-element.9), channel_id=1, source_target_pairs={{0,2},{2,4},{4,6},{6,8},{8,10},{10,12},{12,14},{1,3},{3,5},{5,7},{... | collective-permute-start | bytes 49160 | tf_op jit(solution)/shard_map/ppermute | solution.py:13
  10.0 0.9 compare_select_fusion
  10.9 0.1 copy.19
  11.0 0.2 reshape.69
  11.2 0.0 collective-permute-done.1
  11.2 0.2 collective-permute-done
  11.4 1.3 %collective-permute-start.3 = (bf16[6,16,128]{2,1,0:T(8,128)(2,1)S(1)}, bf16[6,16,128]{2,1,0:T(8,128)(2,1)S(1)}, u32[]{:S(2)}, u32[]{:S(2)}) collective-permute-start(bf16[6,16,128]{2,1,0:T(8,128)(2,1)S(1)} %get-tuple-element.6), channel_id=1, source_target_pairs={{4,0},{6,2},{8,4},{10,6},{12,8},{14,10},{5,1},{7,3},{9,5},{11,7},{... | collective-permute-start | bytes 73736 | tf_op jit(solution)/shard_map/ppermute | solution.py:13
  12.7 7.2 %collective-permute-start.2 = (bf16[6,16,128]{2,1,0:T(8,128)(2,1)S(1)}, bf16[6,16,128]{2,1,0:T(8,128)(2,1)S(1)}, u32[]{:S(2)}, u32[]{:S(2)}) collective-permute-start(bf16[6,16,128]{2,1,0:T(8,128)(2,1)S(1)} %get-tuple-element.5), channel_id=1, source_target_pairs={{0,4},{2,6},{4,8},{6,10},{8,12},{10,14},{1,5},{3,7},{5,9},{7,11},{... | collective-permute-start | bytes 73736 | tf_op jit(solution)/shard_map/ppermute | solution.py:13
  19.9 0.0 collective-permute-done.3
  19.9 1.5 %collective-permute-done.2 = bf16[6,16,128]{2,1,0:T(8,128)(2,1)S(1)} collective-permute-done((bf16[6,16,128]{2,1,0:T(8,128)(2,1)S(1)}, bf16[6,16,128]{2,1,0:T(8,128)(2,1)S(1)}, u32[]{:S(2)}, u32[]{:S(2)}) %collective-permute-start.2) | collective-permute-done | bytes 24608 | tf_op jit(solution)/shard_map/ppermute | solution.py:13
  21.4 13.0 %gather_fusion = bf16[6912,128]{1,0:T(8,128)(2,1)S(1)} fusion(bf16[577,128]{1,0:T(8,128)(2,1)S(1)} %concatenate.30, s32[7168]{0:T(1024)S(1)} %pad_clamp_fusion), kind=kCustom, calls=%fused_computation | custom fusion | bytes 3566592 | tf_op jit(solution)/shard_map/gather | solution.py:73
  34.5 0.0 copy-start.3
  34.5 2.9 %reshape.59 = bf16[256,3456]{1,0:T(8,128)(2,1)} reshape(bf16[6912,128]{1,0:T(8,128)(2,1)S(1)} %gather_fusion) | data formatting | bytes 3538944 | tf_op jit(solution)/shard_map/reshape | solution.py:73
  37.3 0.0 copy-done.3
  37.3 3.1 %convolution_convert_fusion = bf16[3456,128]{1,0:T(8,128)(2,1)} fusion(bf16[256,3456]{1,0:T(8,128)(2,1)} %reshape.59, bf16[1,256,128]{2,1,0:T(8,128)(2,1)S(1)} %copy-done.3), kind=kOutput, calls=%fused_computation.2 | convolution fusion | flops 226934784 | bytes 2719744 | tf_op jit(solution)/shard_map/dot_general | solution.py:75
  40.4 6.1 %all-to-all-start = ((bf16[16,216,128]{2,1,0:T(8,128)(2,1)}), bf16[16,216,128]{2,1,0:T(8,128)(2,1)S(1)}, u32[]{:S(2)}, u32[]{:S(2)}) async-start(bf16[16,216,128]{2,1,0:T(8,128)(2,1)} %bitcast.84), calls=%async_computation | async-start | bytes 1769472 | tf_op jit(solution)/shard_map/all_to_all | solution.py:83
  46.6 1.3 %collective-permute-start.5 = (bf16[4,16,128]{2,1,0:T(8,128)(2,1)S(1)}, bf16[4,16,128]{2,1,0:T(8,128)(2,1)S(1)}, u32[]{:S(2)}, u32[]{:S(2)}) collective-permute-start(bf16[4,16,128]{2,1,0:T(8,128)(2,1)S(1)} %get-tuple-element.8), channel_id=1, source_target_pairs={{2,0},{4,2},{6,4},{8,6},{10,8},{12,10},{14,12},{3,1},{5,3},{7,5},{... | collective-permute-start | bytes 49160 | tf_op jit(solution)/shard_map/ppermute | solution.py:13
  47.9 4.5 %collective-permute-start.4 = (bf16[4,16,128]{2,1,0:T(8,128)(2,1)S(1)}, bf16[4,16,128]{2,1,0:T(8,128)(2,1)S(1)}, u32[]{:S(2)}, u32[]{:S(2)}) collective-permute-start(bf16[4,16,128]{2,1,0:T(8,128)(2,1)S(1)} %get-tuple-element.7), channel_id=1, source_target_pairs={{0,2},{2,4},{4,6},{6,8},{8,10},{10,12},{12,14},{1,3},{3,5},{5,7},{... | collective-permute-start | bytes 49160 | tf_op jit(solution)/shard_map/ppermute | solution.py:13
  52.4 2.0 %collective-permute-done.5 = bf16[4,16,128]{2,1,0:T(8,128)(2,1)S(1)} collective-permute-done((bf16[4,16,128]{2,1,0:T(8,128)(2,1)S(1)}, bf16[4,16,128]{2,1,0:T(8,128)(2,1)S(1)}, u32[]{:S(2)}, u32[]{:S(2)}) %collective-permute-start.5) | collective-permute-done | bytes 16416 | tf_op jit(solution)/shard_map/ppermute | solution.py:13
  54.5 0.0 collective-permute-done.4
  54.5 1.3 %collective-permute-start.7 = (bf16[6,16,128]{2,1,0:T(8,128)(2,1)S(1)}, bf16[6,16,128]{2,1,0:T(8,128)(2,1)S(1)}, u32[]{:S(2)}, u32[]{:S(2)}) collective-permute-start(bf16[6,16,128]{2,1,0:T(8,128)(2,1)S(1)} %get-tuple-element.4), channel_id=1, source_target_pairs={{4,0},{6,2},{8,4},{10,6},{12,8},{14,10},{5,1},{7,3},{9,5},{11,7},{... | collective-permute-start | bytes 73736 | tf_op jit(solution)/shard_map/ppermute | solution.py:13
  55.8 13.9 %collective-permute-start.6 = (bf16[6,16,128]{2,1,0:T(8,128)(2,1)S(1)}, bf16[6,16,128]{2,1,0:T(8,128)(2,1)S(1)}, u32[]{:S(2)}, u32[]{:S(2)}) collective-permute-start(bf16[6,16,128]{2,1,0:T(8,128)(2,1)S(1)} %get-tuple-element.3), channel_id=1, source_target_pairs={{0,4},{2,6},{4,8},{6,10},{8,12},{10,14},{1,5},{3,7},{5,9},{7,11},{... | collective-permute-start | bytes 73736 | tf_op jit(solution)/shard_map/ppermute | solution.py:13
  69.7 2.2 %rev.3 = bf16[27,128,128]{2,1,0:T(8,128)(2,1)} reverse(bf16[27,128,128]{2,1,0:T(8,128)(2,1)} %param.13), dimensions={0} | reverse | bytes 1769472 | tf_op jit(solution)/shard_map/rev | solution.py:60
  71.8 1.6 %reshape.68 = bf16[256,27,128]{2,1,0:T(8,128)(2,1)} reshape(bf16[6912,128]{1,0:T(8,128)(2,1)S(1)} %gather_fusion) | data formatting | bytes 3538944 | tf_op jit(solution)/shard_map/gather | solution.py:73
  73.5 0.0 collective-permute-done.7
  73.5 0.0 collective-permute-done.6
  73.5 13.0 %gather_fusion.1 = bf16[6912,128]{1,0:T(8,128)(2,1)S(1)} fusion(bf16[577,128]{1,0:T(8,128)(2,1)S(1)} %concatenate.33, s32[7168]{0:T(1024)S(1)} %pad_clamp_fusion), kind=kCustom, calls=%fused_computation.1 | custom fusion | bytes 3566592 | tf_op jit(solution)/shard_map/gather | solution.py:97
  86.6 1.6 %reshape.76 = bf16[256,27,128]{2,1,0:T(8,128)(2,1)} reshape(bf16[6912,128]{1,0:T(8,128)(2,1)S(1)} %gather_fusion.1) | data formatting | bytes 3538944 | tf_op jit(solution)/shard_map/gather | solution.py:97
  88.2 0.0 copy-start.1
  88.2 0.0 copy-start.2
  88.2 0.0 copy-start.4
  88.2 3.3 %fusion.22 = bf16[1,256,128]{2,1,0:T(8,128)(2,1)} fusion(bf16[27,128,128]{2,1,0:T(8,128)(2,1)} %param.13, bf16[256,27,128]{2,1,0:T(8,128)(2,1)} %reshape.68), kind=kOutput, calls=%fused_computation.13 | convolution fusion | flops 226525184 | bytes 2719744 | tf_op jit(solution)/shard_map/dot_general | solution.py:74
  91.6 0.0 copy-done.1
  91.6 0.0 copy-done.2
  91.6 0.0 copy-done.4
  91.6 1.3 %fusion.25 = bf16[1,256,128]{2,1,0:T(8,128)(2,1)} fusion(bf16[256,27,128]{2,1,0:T(8,128)(2,1)S(1)} %copy-done.1, bf16[27,128,128]{2,1,0:T(8,128)(2,1)S(1)} %copy-done.2, f32[128]{0:T(128)S(1)} %fusion.28, bf16[1,256,128]{2,1,0:T(8,128)(2,1)S(1)} %copy-done.4), kind=kOutput, calls=%fused_computation.14 | convolution fusion | flops 226852864 | bytes 2785792 | tf_op jit(solution)/shard_map/dot_general | solution.py:98
  92.9 0.0 all-to-all-done
  92.9 0.1 reduce_sum.12
  93.0 26.1 %all_gather.3 = bf16[3456,128]{1,0:T(8,128)(2,1)S(1)} all-gather(bf16[216,128]{1,0:T(8,128)(2,1)S(1)} %reduce_sum.12), channel_id=1, replica_groups=mesh['groups'=2,'brick'=8,'batch'=2] {'brick','batch'}, dimensions={0}, use_global_device_ids=true | all-gather | bytes 940032 | tf_op jit(solution)/shard_map/all_gather | solution.py:85
  119.1 1.4 %convert.12 = f32[27,128,128]{2,1,0:T(8,128)} convert(bf16[27,128,128]{2,1,0:T(8,128)(2,1)S(1)} %bitcast.85) | non-fusion elementwise | flops 442368 | bytes 2654208 | tf_op jit(solution)/shard_map/reshape | solution.py:86
  (9 shorter events, 0.1 us)
Async XLA Ops:
  0.6 0.8 copy-start
  3.2 8.0 %collective-permute-start.1 = (bf16[4,16,128]{2,1,0:T(8,128)(2,1)S(1)}, bf16[4,16,128]{2,1,0:T(8,128)(2,1)S(1)}, u32[]{:S(2)}, u32[]{:S(2)}) collective-permute-start(bf16[4,16,128]{2,1,0:T(8,128)(2,1)S(1)} %get-tuple-element.10), channel_id=1, source_target_pairs={{2,0},{4,2},{6,4},{8,6},{10,8},{12,10},{14,12},{3,1},{5,3},{7,5},{... | collective-permute-start | bytes 49160 | tf_op jit(solution)/shard_map/ppermute | solution.py:13
  4.5 6.9 %collective-permute-start = (bf16[4,16,128]{2,1,0:T(8,128)(2,1)S(1)}, bf16[4,16,128]{2,1,0:T(8,128)(2,1)S(1)}, u32[]{:S(2)}, u32[]{:S(2)}) collective-permute-start(bf16[4,16,128]{2,1,0:T(8,128)(2,1)S(1)} %get-tuple-element.9), channel_id=1, source_target_pairs={{0,2},{2,4},{4,6},{6,8},{8,10},{10,12},{12,14},{1,3},{3,5},{5,7},{... | collective-permute-start | bytes 49160 | tf_op jit(solution)/shard_map/ppermute | solution.py:13
  11.4 8.5 %collective-permute-start.3 = (bf16[6,16,128]{2,1,0:T(8,128)(2,1)S(1)}, bf16[6,16,128]{2,1,0:T(8,128)(2,1)S(1)}, u32[]{:S(2)}, u32[]{:S(2)}) collective-permute-start(bf16[6,16,128]{2,1,0:T(8,128)(2,1)S(1)} %get-tuple-element.6), channel_id=1, source_target_pairs={{4,0},{6,2},{8,4},{10,6},{12,8},{14,10},{5,1},{7,3},{9,5},{11,7},{... | collective-permute-start | bytes 73736 | tf_op jit(solution)/shard_map/ppermute | solution.py:13
  12.7 8.7 %collective-permute-start.2 = (bf16[6,16,128]{2,1,0:T(8,128)(2,1)S(1)}, bf16[6,16,128]{2,1,0:T(8,128)(2,1)S(1)}, u32[]{:S(2)}, u32[]{:S(2)}) collective-permute-start(bf16[6,16,128]{2,1,0:T(8,128)(2,1)S(1)} %get-tuple-element.5), channel_id=1, source_target_pairs={{0,4},{2,6},{4,8},{6,10},{8,12},{10,14},{1,5},{3,7},{5,9},{7,11},{... | collective-permute-start | bytes 73736 | tf_op jit(solution)/shard_map/ppermute | solution.py:13
  34.5 2.9 %copy-start.3 = (bf16[1,256,128]{2,1,0:T(8,128)(2,1)S(1)}, bf16[1,256,128]{2,1,0:T(8,128)(2,1)}, u32[]{:S(2)}) copy-start(bf16[1,256,128]{2,1,0:T(8,128)(2,1)} %param.8) | copy-start | bytes 196612
  40.4 52.5 %all-to-all-start = ((bf16[16,216,128]{2,1,0:T(8,128)(2,1)}), bf16[16,216,128]{2,1,0:T(8,128)(2,1)S(1)}, u32[]{:S(2)}, u32[]{:S(2)}) async-start(bf16[16,216,128]{2,1,0:T(8,128)(2,1)} %bitcast.84), calls=%async_computation | async-start | bytes 1769472 | tf_op jit(solution)/shard_map/all_to_all | solution.py:83
  46.6 7.9 %collective-permute-start.5 = (bf16[4,16,128]{2,1,0:T(8,128)(2,1)S(1)}, bf16[4,16,128]{2,1,0:T(8,128)(2,1)S(1)}, u32[]{:S(2)}, u32[]{:S(2)}) collective-permute-start(bf16[4,16,128]{2,1,0:T(8,128)(2,1)S(1)} %get-tuple-element.8), channel_id=1, source_target_pairs={{2,0},{4,2},{6,4},{8,6},{10,8},{12,10},{14,12},{3,1},{5,3},{7,5},{... | collective-permute-start | bytes 49160 | tf_op jit(solution)/shard_map/ppermute | solution.py:13
  47.9 6.6 %collective-permute-start.4 = (bf16[4,16,128]{2,1,0:T(8,128)(2,1)S(1)}, bf16[4,16,128]{2,1,0:T(8,128)(2,1)S(1)}, u32[]{:S(2)}, u32[]{:S(2)}) collective-permute-start(bf16[4,16,128]{2,1,0:T(8,128)(2,1)S(1)} %get-tuple-element.7), channel_id=1, source_target_pairs={{0,2},{2,4},{4,6},{6,8},{8,10},{10,12},{12,14},{1,3},{3,5},{5,7},{... | collective-permute-start | bytes 49160 | tf_op jit(solution)/shard_map/ppermute | solution.py:13
  54.5 19.0 %collective-permute-start.7 = (bf16[6,16,128]{2,1,0:T(8,128)(2,1)S(1)}, bf16[6,16,128]{2,1,0:T(8,128)(2,1)S(1)}, u32[]{:S(2)}, u32[]{:S(2)}) collective-permute-start(bf16[6,16,128]{2,1,0:T(8,128)(2,1)S(1)} %get-tuple-element.4), channel_id=1, source_target_pairs={{4,0},{6,2},{8,4},{10,6},{12,8},{14,10},{5,1},{7,3},{9,5},{11,7},{... | collective-permute-start | bytes 73736 | tf_op jit(solution)/shard_map/ppermute | solution.py:13
  55.8 17.7 %collective-permute-start.6 = (bf16[6,16,128]{2,1,0:T(8,128)(2,1)S(1)}, bf16[6,16,128]{2,1,0:T(8,128)(2,1)S(1)}, u32[]{:S(2)}, u32[]{:S(2)}) collective-permute-start(bf16[6,16,128]{2,1,0:T(8,128)(2,1)S(1)} %get-tuple-element.3), channel_id=1, source_target_pairs={{0,4},{2,6},{4,8},{6,10},{8,12},{10,14},{1,5},{3,7},{5,9},{7,11},{... | collective-permute-start | bytes 73736 | tf_op jit(solution)/shard_map/ppermute | solution.py:13
  88.2 3.4 %copy-start.1 = (bf16[256,27,128]{2,1,0:T(8,128)(2,1)S(1)}, bf16[256,27,128]{2,1,0:T(8,128)(2,1)}, u32[]{:S(2)}) copy-start(bf16[256,27,128]{2,1,0:T(8,128)(2,1)} %reshape.76) | copy-start | bytes 5308420
  88.2 3.4 %copy-start.2 = (bf16[27,128,128]{2,1,0:T(8,128)(2,1)S(1)}, bf16[27,128,128]{2,1,0:T(8,128)(2,1)}, u32[]{:S(2)}) copy-start(bf16[27,128,128]{2,1,0:T(8,128)(2,1)} %rev.3) | copy-start | bytes 2654212
  88.2 3.4 %copy-start.4 = (bf16[1,256,128]{2,1,0:T(8,128)(2,1)S(1)}, bf16[1,256,128]{2,1,0:T(8,128)(2,1)}, u32[]{:S(2)}) copy-start(bf16[1,256,128]{2,1,0:T(8,128)(2,1)} %param.7) | copy-start | bytes 196612

commit v2 on v1

v2 whole, which is shorter than its diff:
```python
import functools

import jax
import jax.numpy as jnp
from jax import lax
from jax.experimental import pallas as pl
from jax.experimental.pallas import tpu as pltpu
from jax.sharding import PartitionSpec as P

LAYERS = 16
TILE = 4
STRIP = TILE * LAYERS
HALF = 13
CODE_ROWS = 16
VMEM_BYTES = 48 * 1024 * 1024


def time_embedding(timesteps, width):
    half = width // 2
    freq = jnp.exp(-jnp.log(10000.0) * jnp.arange(half, dtype=jnp.float32) / half)
    angle = timesteps.astype(jnp.float32)[:, None] * freq[None, :]
    return jnp.concatenate([jnp.sin(angle), jnp.cos(angle)], axis=1).astype(jnp.bfloat16)


def strip_codes(neighbours, tiles_y):
    rows_here = TILE * STRIP
    code = (neighbours // rows_here) % tiles_y * STRIP + neighbours % STRIP
    return jnp.where(neighbours < 0, -1, code).astype(jnp.float32)


def pack_kernel(tiles_y, feat_ref, cot_ref, near_ref, temb_ref, cond_ref, wt_ref, pack_ref, shift_ref):
    rows, width = feat_ref.shape
    shift = jnp.dot(temb_ref[...], wt_ref[...], preferred_element_type=jnp.float32)
    shift = shift + cond_ref[...].astype(jnp.float32)
    shift_ref[...] = shift
    z_val = feat_ref[...].astype(jnp.float32) + shift
    pack_ref[:rows, :width] = (z_val * jax.nn.sigmoid(z_val)).astype(jnp.bfloat16)
    pack_ref[:rows, width:] = cot_ref[...]
    pack_ref[rows:, :] = strip_codes(near_ref[:CODE_ROWS, :], tiles_y).astype(jnp.bfloat16)


def weight_kernel(tiles_x, tiles_y, pack_ref, own_ref, sent_ref, ground, turned, codes, gathered):
    width = own_ref.shape[2]
    rows = TILE * STRIP
    span = tiles_y * STRIP
    strips = tiles_x * TILE
    for tile_x in range(tiles_x):
        for tile_y in range(tiles_y):
            tile = tile_x * tiles_y + tile_y
            columns = pack_ref[tile, rows:, :].astype(jnp.float32).T
            for u in range(TILE):
                at = (tile_x * TILE + u) * span + tile_y * STRIP
                ground[at:at + STRIP, :] = pack_ref[tile, u * STRIP:(u + 1) * STRIP, :]
                codes[at:at + STRIP, :] = columns[u * STRIP:(u + 1) * STRIP, :]
    for strip in range(strips):
        at = strip * span
        turned[:, at:at + span] = ground[at:at + span, :].T
    place = lax.broadcasted_iota(jnp.int32, (span, span), 1).astype(jnp.float32)

    def select(strip, carry):
        at = pl.multiple_of(strip * span, span)
        before = pl.multiple_of(jnp.maximum(strip - 1, 0) * span, span)
        code = codes[pl.ds(at, span), :]
        for first, last, source in ((0, 9, before), (9, HALF, at)):
            block = ground[pl.ds(source, span), :]
            for k in range(first, last):
                pick = (code[:, k:k + 1] == place).astype(jnp.bfloat16)
                rows_k = jnp.dot(pick, block, preferred_element_type=jnp.float32)
                gathered[k, pl.ds(at, span), :] = rows_k.astype(jnp.bfloat16)
        return carry

    lax.fori_loop(0, strips, select, 0)

    def multiply(k, carry):
        low = jnp.dot(turned[width:, :], gathered[k, :, :width], preferred_element_type=jnp.float32).T
        high = jnp.dot(turned[:width, :], gathered[k, :, width:], preferred_element_type=jnp.float32)
        own_ref[k] = low
        sent_ref[k] = low.astype(jnp.bfloat16)
        own_ref[2 * HALF - k] = high
        sent_ref[2 * HALF - k] = high.astype(jnp.bfloat16)
        return carry

    lax.fori_loop(0, HALF, multiply, 0)
    centre = jnp.dot(turned[:width, :], ground[:, width:], preferred_element_type=jnp.float32)
    own_ref[HALF] = centre
    sent_ref[HALF] = centre.astype(jnp.bfloat16)


def voxel_kernel(tiles_x, tiles_y, where_ref, pack_ref, near_ref, feat_ref, shift_ref, w_ref,
                 conv_ref, grad_ref, near_act, near_cot, w_back):
    rows, width = feat_ref.shape
    span = tiles_y * STRIP
    strips = tiles_x * TILE
    first = where_ref[0] // tiles_y * TILE
    code = strip_codes(near_ref[...], tiles_y).T
    place = lax.broadcasted_iota(jnp.int32, (STRIP, span), 1).astype(jnp.float32)
    for u in range(TILE):
        here = u * STRIP
        for side in range(3):
            strip = jnp.clip(first + u + side - 1, 0, strips - 1)
            tile = strip // TILE * tiles_y
            at = pl.multiple_of(strip % TILE * STRIP, STRIP)
            block = jnp.concatenate([pack_ref[tile + i, pl.ds(at, STRIP), :] for i in range(tiles_y)], axis=0)
            for k in range(9 * side, 9 * side + 9):
                pick = (code[here:here + STRIP, k:k + 1] == place).astype(jnp.bfloat16)
                rows_k = jnp.dot(pick, block, preferred_element_type=jnp.float32).astype(jnp.bfloat16)
                near_act[here:here + STRIP, k * width:(k + 1) * width] = rows_k[:, :width]
                near_cot[here:here + STRIP, k * width:(k + 1) * width] = rows_k[:, width:]
    for k in range(27):
        w_back[:, k * width:(k + 1) * width] = w_ref[26 - k]
    conv = jnp.dot(near_act[...], w_ref[...].reshape(27 * width, width), preferred_element_type=jnp.float32)
    conv_ref[...] = conv.astype(jnp.bfloat16)
    back = lax.dot_general(near_cot[...], w_back[...], (((1,), (1,)), ((), ())), preferred_element_type=jnp.float32)
    z_val = feat_ref[...].astype(jnp.float32) + shift_ref[...]
    sig = jax.nn.sigmoid(z_val)
    grad_ref[...] = (back * sig * (1.0 + z_val * (1.0 - sig))).astype(jnp.bfloat16)


def whole_scene(features, cotangent, neighbours, timesteps, condition, w_time, w_conv, tiles_x, tiles_y):
    rows, width = features.shape[1:]
    peers = tiles_x * tiles_y
    total = peers * rows
    temb = time_embedding(timesteps, width)
    packed, shift = pl.pallas_call(
        functools.partial(pack_kernel, tiles_y),
        out_shape=(
            jax.ShapeDtypeStruct((rows + CODE_ROWS, 2 * width), jnp.bfloat16),
            jax.ShapeDtypeStruct((1, width), jnp.float32),
        ),
        name="pack_tile",
    )(features[0], cotangent[0], neighbours, temb, condition, w_time)
    scene = lax.all_gather(packed, "brick")
    own, sent = pl.pallas_call(
        functools.partial(weight_kernel, tiles_x, tiles_y),
        out_shape=(
            jax.ShapeDtypeStruct((27, width, width), jnp.float32),
            jax.ShapeDtypeStruct((27, width, width), jnp.bfloat16),
        ),
        scratch_shapes=[
            pltpu.VMEM((total, 2 * width), jnp.bfloat16),
            pltpu.VMEM((2 * width, total), jnp.bfloat16),
            pltpu.VMEM((total, CODE_ROWS), jnp.float32),
            pltpu.VMEM((HALF, total, 2 * width), jnp.bfloat16),
        ],
        compiler_params=pltpu.CompilerParams(vmem_limit_bytes=VMEM_BYTES),
        name="weight_terms",
    )(scene)
    other = lax.ppermute(sent, "batch", [(0, 1), (1, 0)])
    here = lax.axis_index("brick").astype(jnp.int32).reshape(1)
    vmem = pl.BlockSpec(memory_space=pltpu.VMEM)
    conv_out, feature_grad = pl.pallas_call(
        functools.partial(voxel_kernel, tiles_x, tiles_y),
        out_shape=(
            jax.ShapeDtypeStruct((rows, width), jnp.bfloat16),
            jax.ShapeDtypeStruct((rows, width), jnp.bfloat16),
        ),
        in_specs=[pl.BlockSpec(memory_space=pltpu.SMEM)] + [vmem] * 5,
        scratch_shapes=[
            pltpu.VMEM((rows, 27 * width), jnp.bfloat16),
            pltpu.VMEM((rows, 27 * width), jnp.bfloat16),
            pltpu.VMEM((width, 27 * width), jnp.bfloat16),
        ],
        compiler_params=pltpu.CompilerParams(vmem_limit_bytes=VMEM_BYTES),
        cost_estimate=pl.CostEstimate(flops=10**9, bytes_accessed=4 * 10**6, transcendentals=0),
        name="voxel_outputs",
    )(here, scene, neighbours, features[0], shift, w_conv)
    weight_grad = own + other.astype(jnp.float32)
    return (conv_out[None], feature_grad[None], weight_grad)


def passed_along(block, axis, distance):
    devices = range(lax.axis_size(axis))
    route = [(i - distance, i) for i in devices if i - distance in devices]
    return lax.ppermute(block, axis, route)


def slab_rows(block, side_recv, front_recv, width):
    widened = jnp.concatenate([side_recv[0], block, side_recv[1]], axis=1)
    slab = jnp.concatenate([front_recv[0][None], widened, front_recv[1][None]], axis=0)
    flat = slab.reshape(-1, width)
    return jnp.concatenate([flat, jnp.zeros((1, width), jnp.bfloat16)], axis=0)


def with_halo(block, tiles_y):
    width = block.shape[-1]
    side = TILE
    side_recv = tuple(passed_along(block[:, edge], "brick", by)[:, None] for by, edge in ((1, side - 1), (-1, 0)))
    wide = jnp.concatenate([side_recv[0], block, side_recv[1]], axis=1)
    front_recv = tuple(passed_along(wide[edge], "brick", by) for by, edge in ((tiles_y, side - 1), (-tiles_y, 0)))
    return slab_rows(block, side_recv, front_recv, width)


def halo_plan(features, cotangent, neighbours, timesteps, condition, w_time, w_conv, tiles_x, tiles_y):
    rows_here, width = features.shape[1:]
    here = lax.axis_index("brick")
    tile_x = here // tiles_y
    tile_y = here % tiles_y
    side = TILE
    layers = LAYERS
    wide = side + 2
    valid = neighbours >= 0
    safe = jnp.where(valid, neighbours, 0)
    owner = safe // rows_here
    inside = safe % rows_here
    column = inside // layers
    layer = inside % layers
    local_x = (owner // tiles_y - tile_x) * side + column // side + 1
    local_y = (owner % tiles_y - tile_y) * side + column % side + 1
    sentinel = wide * wide * layers
    ext_index = jnp.where(valid, (local_x * wide + local_y) * layers + layer, sentinel).T
    temb = time_embedding(timesteps, width)
    shift = jnp.dot(temb, w_time, preferred_element_type=jnp.float32) + condition.astype(jnp.float32)
    z_val = features[0].astype(jnp.float32) + shift[0][None, :]
    act = jax.nn.silu(z_val).astype(jnp.bfloat16)
    cot = cotangent[0]
    w_forward = w_conv.reshape(27 * width, width)
    w_backward = jnp.transpose(w_conv[::-1], (0, 2, 1)).reshape(27 * width, width)
    act_ext = with_halo(act.reshape(side, side, layers, width), tiles_y)
    gathered = act_ext[ext_index].reshape(rows_here, 27 * width)
    conv_out = jnp.dot(gathered, w_forward, preferred_element_type=jnp.float32).astype(jnp.bfloat16)
    partial_grad = lax.dot_general(
        gathered, cot, (((0,), (0,)), ((), ())), preferred_element_type=jnp.float32
    )
    both = ("brick", "batch")
    parts = tiles_x * tiles_y * lax.axis_size("batch")
    rows = 27 * width
    extra = -rows % (8 * parts)
    pieces = jnp.pad(partial_grad.astype(jnp.bfloat16), ((0, extra), (0, 0))).reshape(parts, -1, width)
    arrived = lax.all_to_all(pieces, both, 0, 0)
    summed = arrived.astype(jnp.float32).sum(0).astype(jnp.bfloat16)
    whole = lax.all_gather(summed, both, axis=0, tiled=True)
    weight_grad = whole[:rows].astype(jnp.float32).reshape(27, width, width)
    cot_ext = with_halo(cot.reshape(side, side, layers, width), tiles_y)
    cot_gathered = cot_ext[ext_index].reshape(rows_here, 27 * width)
    back = jnp.dot(cot_gathered, w_backward, preferred_element_type=jnp.float32)
    sig = jax.nn.sigmoid(z_val)
    feature_grad = (back * sig * (1.0 + z_val * (1.0 - sig))).astype(jnp.bfloat16)
    return (conv_out[None], feature_grad[None], weight_grad)


def shards(*arrays):
    peers = lax.axis_size("brick")
    bits = peers.bit_length() - 1
    tiles_x = 2 ** ((bits + 1) // 2)
    tiles_y = 2 ** (bits // 2)
    plan = whole_scene if tiles_y == 2 else halo_plan
    return plan(*arrays, tiles_x, tiles_y)


def solution(mesh):
    in_specs = (
        P(("groups", "batch"), "brick", None),
        P(("groups", "batch"), "brick", None),
        P(None, ("groups", "brick")),
        P(("groups", "batch")),
        P(("groups", "batch"), None),
        P(),
        P(),
    )
    out_specs = (
        P(("groups", "batch"), "brick", None),
        P(("groups", "batch"), "brick", None),
        P("groups", None, None),
    )
    return jax.shard_map(shards, mesh=mesh, in_specs=in_specs, out_specs=out_specs, check_vma=False)
```

time: 121 us -> 86.8 us (0.72)
  starting transfers between devices: 42.4 us -> 0.11 us
  waiting for transfers between devices: 3.69 us -> 43.9 us
  local copies, waits for them, and re-layouts: 34.8 us -> 5.91 us
  blocking collectives: 26.1 us -> 0 us
  Pallas kernels: 0 us -> 19.8 us
  between operations: 1.51 us -> 14.7 us
  matrix products: 8.58 us -> 0 us
  other arithmetic: 3.46 us -> 2.05 us
    all_gather x0 -> x1, waiting for transfers between devices: none -> 43.8 us  [whole_scene(): scene = lax.all_gather(packed, 'brick')]
    ppermute x8 -> x1, starting transfers between devices: 36.3 us -> 0.07 us  [whole_scene(): other = lax.ppermute(sent, 'batch', [(0, 1), (1, 0)])]
    gather x4 -> x0, local copies, waits for them, and re-layouts: 29.3 us -> none  [the longest x2 14.7 us: shards(): gathered = act_ext[ext_index].reshape(rows_here, 27 * width)]
    all_gather x1 -> x0, blocking collectives: 26.1 us -> none  [shards(): whole = lax.all_gather(summed, both, axis=0, tiled=True)]
    pallas_call x0 -> x3, Pallas kernels: none -> 19.8 us  [the longest x1 14.6 us: whole_scene(): pl.pallas_call(functools.partial(weight_kernel, tiles_x, tiles_y), out_sh...]
    dot_general x4 -> x0, matrix products: 8.58 us -> none  [the longest x1 3.35 us: shards(): jnp.dot(gathered, w_forward, preferred_element_type=jnp.float32)]
    all_to_all x1 -> x0, starting transfers between devices: 6.14 us -> none  [shards(): arrived = lax.all_to_all(pieces, both, 0, 0)]
    unnamed x10 -> x12, local copies, waits for them, and re-layouts: 0.08 us -> 5.91 us
  transfers between devices with their start and end apart: 9 -> 2, of which waited for: 3 -> 1; matrix products, arithmetic and copies ran while one was open for 20% -> 0% of each run, Pallas kernels for 0% -> 4%
where the time goes in v2:
time: 86.8 us; the launch traced here: 86.4 us
  waiting for transfers between devices  43.9 us (51%)
  Pallas kernels  19.8 us (23%)
  between operations  14.7 us (17%)
  local copies, waits for them, and re-layouts  5.91 us (7%)
  other arithmetic  2.05 us (2%)
    all_gather x1, waiting for transfers between devices, whole_scene(): scene = lax.all_gather(packed, 'brick')  43.8 us
    pallas_call x1, Pallas kernels, whole_scene(): pl.pallas_call(functools.partial(weight_kernel, tiles_x, tiles_y), out_sh...  14.6 us
    unnamed x12, local copies, waits for them, and re-layouts  5.91 us
    pallas_call x1, Pallas kernels, whole_scene(): pl.pallas_call(functools.partial(voxel_kernel, tiles_x, tiles_y), out_sha...  3.39 us
  transfers between devices with their start and end apart: 2, of which 1 were waited for; matrix products, arithmetic and copies ran while one was open for 0% of the time, Pallas kernels for 4%

profile of v2, /device:TPU:0, one launch (start us, length us, event | category | flops | bytes accessed | tf_op | source)
XLA Modules:
  0.0 86.4 jit_solution(4135300711188008585)
XLA Ops:
  7.2 0.0 all-gather.3.cloned.1.call-start
  7.9 0.1 convert_bitcast_fusion
  7.9 0.6 pad_maximum_fusion.temb_ref
  8.5 1.7 %pack_tile.1 = (bf16[272,256]{1,0:T(8,128)(2,1)}, f32[1,128]{1,0:T(1,128)}) custom-call(bf16[256,128]{1,0:T(8,128)(2,1)} %bitcast.13, bf16[256,128]{1,0:T(8,128)(2,1)} %bitcast.15, s32[27,256]{1,0:T(8,128)} %near_ref.3, bf16[1,128]{1,0:T(2,128)(2,1)} %pad_maximum_fusion.temb_ref, bf16[1,128]{1,0:T(2,128)(2,1)} %cond_ref.1, bf16[128,128]{1,0:T(8,128)(2,1)} %wt_ref.1), custom_call_target="tpu_custom_call" | custom-call | tf_op jit(solution)/shard_map/pack_tile/pallas_call | solution.py:124
  10.2 0.0 all-gather.3.cloned.1.call-update
  10.2 43.8 %all-gather.3.cloned.1.call-done = bf16[2176,256]{1,0:T(8,128)(2,1)} async-done(((bf16[272,256]{1,0:T(8,128)(2,1)}), bf16[2176,256]{1,0:T(8,128)(2,1)}) %all-gather.3.cloned.1.call-update) | async-done | bytes 1114128 | tf_op jit(solution)/shard_map/all_gather | solution.py:132
  54.1 0.0 copy-start
  54.1 1.2 %copy-done = bf16[2176,256]{1,0:T(8,128)(2,1)S(1)} copy-done((bf16[2176,256]{1,0:T(8,128)(2,1)S(1)}, bf16[2176,256]{1,0:T(8,128)(2,1)}, u32[]{:S(2)}) %copy-start) | copy-done | bytes 1114136
  55.3 14.6 %weight_terms.1 = (f32[27,128,128]{2,1,0:T(8,128)S(1)}, bf16[27,128,128]{2,1,0:T(8,128)(2,1)S(1)}) custom-call(bf16[8,272,256]{2,1,0:T(8,128)(2,1)S(1)} %bitcast.11), custom_call_target="tpu_custom_call" | custom-call | tf_op jit(solution)/shard_map/weight_terms/pallas_call | solution.py:133
  70.0 0.1 collective-permute-start
  70.1 0.0 copy-start.1
  70.1 1.2 %copy-done.1 = bf16[2176,256]{1,0:T(8,128)(2,1)S(1)} copy-done((bf16[2176,256]{1,0:T(8,128)(2,1)S(1)}, bf16[2176,256]{1,0:T(8,128)(2,1)}, u32[]{:S(2)}) %copy-start.1) | copy-done | bytes 1114136
  71.3 0.0 copy-start.2
  71.3 0.8 copy-done.2
  72.2 0.0 copy-start.3
  72.2 0.8 copy-done.3
  72.9 0.0 copy-start.4
  72.9 1.2 %copy-done.4 = bf16[27,128,128]{2,1,0:T(8,128)(2,1)S(1)} copy-done((bf16[27,128,128]{2,1,0:T(8,128)(2,1)S(1)}, bf16[27,128,128]{2,1,0:T(8,128)(2,1)}, u32[]{:S(2)}) %copy-start.4) | copy-done | bytes 884760
  74.1 0.0 copy-start.5
  74.1 0.7 copy-done.5
  74.7 3.4 %voxel_outputs.1 = (bf16[256,128]{1,0:T(8,128)(2,1)}, bf16[256,128]{1,0:T(8,128)(2,1)}) custom-call(s32[1]{0:T(128)} %bitcast.where_ref, bf16[8,272,256]{2,1,0:T(8,128)(2,1)S(1)} %bitcast.12, s32[27,256]{1,0:T(8,128)S(1)} %copy-done.3, bf16[256,128]{1,0:T(8,128)(2,1)S(1)} %bitcast.14, f32[1,128]{1,0:T(1,128)S(1)} %copy-done.5, ...), custom_call_target="tpu_custom_call" | custom-call | flops 1000000000 | bytes 4000000 | tf_op jit(solution)/shard_map/voxel_outputs/pallas_call | solution.py:151
  78.1 0.0 collective-permute-done
  78.1 1.4 %convert_add_fusion = f32[27,128,128]{2,1,0:T(8,128)} fusion(f32[27,128,128]{2,1,0:T(8,128)S(1)} %get-tuple-element.13, bf16[27,128,128]{2,1,0:T(8,128)(2,1)S(1)} %collective-permute-done), kind=kLoop, calls=%fused_computation | loop fusion | flops 884736 | bytes 4423680 | tf_op jit(solution)/shard_map/add | solution.py:167
Async XLA Ops:
  7.2 46.9 %all-gather.3.cloned.1.call-start = ((), (), s32[]{:S(2)}) async-start(), calls=%async_computation | async-start | bytes 1253376 | tf_op jit(solution)/shard_map/all_gather | solution.py:132
  54.1 1.2 %copy-start = (bf16[2176,256]{1,0:T(8,128)(2,1)S(1)}, bf16[2176,256]{1,0:T(8,128)(2,1)}, u32[]{:S(2)}) copy-start(bf16[2176,256]{1,0:T(8,128)(2,1)} %all-gather.3.cloned.1.call-done) | copy-start | bytes 3342340
  70.0 8.2 %collective-permute-start = (bf16[27,128,128]{2,1,0:T(8,128)(2,1)S(1)}, bf16[27,128,128]{2,1,0:T(8,128)(2,1)S(1)}, u32[]{:S(2)}, u32[]{:S(2)}) collective-permute-start(bf16[27,128,128]{2,1,0:T(8,128)(2,1)S(1)} %get-tuple-element.14), channel_id=1, source_target_pairs={{0,1},{1,0},{2,3},{3,2},{4,5},{5,4},{6,7},{7,6},{8,9},{9,8},{10,11... | collective-permute-start | bytes 2654216 | tf_op jit(solution)/shard_map/ppermute | solution.py:148
  70.1 1.2 %copy-start.1 = (bf16[2176,256]{1,0:T(8,128)(2,1)S(1)}, bf16[2176,256]{1,0:T(8,128)(2,1)}, u32[]{:S(2)}) copy-start(bf16[2176,256]{1,0:T(8,128)(2,1)} %all-gather.3.cloned.1.call-done) | copy-start | bytes 3342340
  71.3 0.8 copy-start.2
  72.2 0.8 copy-start.3
  72.9 1.2 %copy-start.4 = (bf16[27,128,128]{2,1,0:T(8,128)(2,1)S(1)}, bf16[27,128,128]{2,1,0:T(8,128)(2,1)}, u32[]{:S(2)}) copy-start(bf16[27,128,128]{2,1,0:T(8,128)(2,1)} %w_ref.1) | copy-start | bytes 2654212
  74.1 0.7 copy-start.5
Sparse Core Ops, SparseCore 0:
  10.8 43.2 all-gather.2

commit v3 on v2

--- a/solution.py
+++ b/solution.py
@@ -12,7 +12,8 @@
 STRIP = TILE * LAYERS
 HALF = 13
 CODE_ROWS = 16
-VMEM_BYTES = 48 * 1024 * 1024
+WEIGHT_VMEM = 32 * 1024 * 1024
+VOXEL_VMEM = 16 * 1024 * 1024
 
 
 def time_embedding(timesteps, width):
@@ -28,18 +29,22 @@
     return jnp.where(neighbours < 0, -1, code).astype(jnp.float32)
 
 
-def pack_kernel(tiles_y, feat_ref, cot_ref, near_ref, temb_ref, cond_ref, wt_ref, pack_ref, shift_ref):
+def pack_kernel(tiles_y, feat_ref, near_ref, temb_ref, cond_ref, wt_ref, pack_ref, z_ref, code_ref):
     rows, width = feat_ref.shape
     shift = jnp.dot(temb_ref[...], wt_ref[...], preferred_element_type=jnp.float32)
     shift = shift + cond_ref[...].astype(jnp.float32)
-    shift_ref[...] = shift
     z_val = feat_ref[...].astype(jnp.float32) + shift
-    pack_ref[:rows, :width] = (z_val * jax.nn.sigmoid(z_val)).astype(jnp.bfloat16)
-    pack_ref[:rows, width:] = cot_ref[...]
-    pack_ref[rows:, :] = strip_codes(near_ref[:CODE_ROWS, :], tiles_y).astype(jnp.bfloat16)
-
-
-def weight_kernel(tiles_x, tiles_y, pack_ref, own_ref, sent_ref, ground, turned, codes, gathered):
+    z_ref[...] = z_val
+    pack_ref[:rows, :] = (z_val * jax.nn.sigmoid(z_val)).astype(jnp.bfloat16)
+    code = strip_codes(near_ref[...], tiles_y)
+    code_ref[...] = code.T
+    for half in range(rows // width):
+        at = rows + half * CODE_ROWS
+        piece = code[:CODE_ROWS, half * width:(half + 1) * width]
+        pack_ref[at:at + CODE_ROWS, :] = piece.astype(jnp.bfloat16)
+
+
+def weight_kernel(tiles_x, tiles_y, act_ref, cot_ref, own_ref, sent_ref, ground, turned, codes, near_act, near_cot):
     width = own_ref.shape[2]
     rows = TILE * STRIP
     span = tiles_y * STRIP
@@ -47,63 +52,82 @@
     for tile_x in range(tiles_x):
         for tile_y in range(tiles_y):
             tile = tile_x * tiles_y + tile_y
-            columns = pack_ref[tile, rows:, :].astype(jnp.float32).T
+            for half in range(rows // width):
+                at = rows + half * CODE_ROWS
+                columns = act_ref[tile, at:at + CODE_ROWS, :].astype(jnp.float32).T
+                for part in range(width // STRIP):
+                    u = half * (width // STRIP) + part
+                    to = (tile_x * TILE + u) * span + tile_y * STRIP
+                    codes[to:to + STRIP, :] = columns[part * STRIP:(part + 1) * STRIP, :]
             for u in range(TILE):
-                at = (tile_x * TILE + u) * span + tile_y * STRIP
-                ground[at:at + STRIP, :] = pack_ref[tile, u * STRIP:(u + 1) * STRIP, :]
-                codes[at:at + STRIP, :] = columns[u * STRIP:(u + 1) * STRIP, :]
+                to = (tile_x * TILE + u) * span + tile_y * STRIP
+                ground[to:to + STRIP, :width] = act_ref[tile, u * STRIP:(u + 1) * STRIP, :]
+                ground[to:to + STRIP, width:] = cot_ref[tile, u * STRIP:(u + 1) * STRIP, :]
     for strip in range(strips):
         at = strip * span
         turned[:, at:at + span] = ground[at:at + span, :].T
     place = lax.broadcasted_iota(jnp.int32, (span, span), 1).astype(jnp.float32)
+    last = HALF // 2
+    near_act[last, :, width:] = ground[:, :width]
+    near_cot[last, :, width:] = ground[:, width:]
 
     def select(strip, carry):
         at = pl.multiple_of(strip * span, span)
         before = pl.multiple_of(jnp.maximum(strip - 1, 0) * span, span)
         code = codes[pl.ds(at, span), :]
-        for first, last, source in ((0, 9, before), (9, HALF, at)):
+        for first, stop, source in ((0, 9, before), (9, HALF, at)):
             block = ground[pl.ds(source, span), :]
-            for k in range(first, last):
-                pick = (code[:, k:k + 1] == place).astype(jnp.bfloat16)
-                rows_k = jnp.dot(pick, block, preferred_element_type=jnp.float32)
-                gathered[k, pl.ds(at, span), :] = rows_k.astype(jnp.bfloat16)
+            picks = [(code[:, k:k + 1] == place).astype(jnp.bfloat16) for k in range(first, stop)]
+            near = jnp.dot(jnp.concatenate(picks, axis=0), block, preferred_element_type=jnp.float32)
+            near = near.astype(jnp.bfloat16)
+            for k in range(first, stop):
+                rows_k = near[(k - first) * span:(k - first + 1) * span, :]
+                side = k % 2 * width
+                near_act[k // 2, pl.ds(at, span), side:side + width] = rows_k[:, :width]
+                near_cot[k // 2, pl.ds(at, span), side:side + width] = rows_k[:, width:]
         return carry
 
     lax.fori_loop(0, strips, select, 0)
 
-    def multiply(k, carry):
-        low = jnp.dot(turned[width:, :], gathered[k, :, :width], preferred_element_type=jnp.float32).T
-        high = jnp.dot(turned[:width, :], gathered[k, :, width:], preferred_element_type=jnp.float32)
-        own_ref[k] = low
-        sent_ref[k] = low.astype(jnp.bfloat16)
-        own_ref[2 * HALF - k] = high
-        sent_ref[2 * HALF - k] = high.astype(jnp.bfloat16)
-        return carry
-
-    lax.fori_loop(0, HALF, multiply, 0)
-    centre = jnp.dot(turned[:width, :], ground[:, width:], preferred_element_type=jnp.float32)
-    own_ref[HALF] = centre
-    sent_ref[HALF] = centre.astype(jnp.bfloat16)
-
-
-def voxel_kernel(tiles_x, tiles_y, where_ref, pack_ref, near_ref, feat_ref, shift_ref, w_ref,
+    for pair in range(last + 1):
+        low = jnp.dot(turned[width:, :], near_act[pair], preferred_element_type=jnp.float32)
+        high = jnp.dot(turned[:width, :], near_cot[pair], preferred_element_type=jnp.float32)
+        for side in range(2):
+            k = 2 * pair + side
+            above = high[:, side * width:(side + 1) * width]
+            own_ref[2 * HALF - k] = above
+            sent_ref[2 * HALF - k] = above.astype(jnp.bfloat16)
+            if k < HALF:
+                below = low[:, side * width:(side + 1) * width].T
+                own_ref[k] = below
+                sent_ref[k] = below.astype(jnp.bfloat16)
+
+
+def voxel_kernel(tiles_x, tiles_y, where_ref, act_ref, cot_ref, code_ref, z_ref, w_ref,
                  conv_ref, grad_ref, near_act, near_cot, w_back):
-    rows, width = feat_ref.shape
+    rows, width = z_ref.shape
     span = tiles_y * STRIP
     strips = tiles_x * TILE
     first = where_ref[0] // tiles_y * TILE
-    code = strip_codes(near_ref[...], tiles_y).T
     place = lax.broadcasted_iota(jnp.int32, (STRIP, span), 1).astype(jnp.float32)
     for u in range(TILE):
         here = u * STRIP
+        code = code_ref[here:here + STRIP, :]
         for side in range(3):
             strip = jnp.clip(first + u + side - 1, 0, strips - 1)
             tile = strip // TILE * tiles_y
             at = pl.multiple_of(strip % TILE * STRIP, STRIP)
-            block = jnp.concatenate([pack_ref[tile + i, pl.ds(at, STRIP), :] for i in range(tiles_y)], axis=0)
-            for k in range(9 * side, 9 * side + 9):
-                pick = (code[here:here + STRIP, k:k + 1] == place).astype(jnp.bfloat16)
-                rows_k = jnp.dot(pick, block, preferred_element_type=jnp.float32).astype(jnp.bfloat16)
+            pieces = [
+                jnp.concatenate([ref[tile + i, pl.ds(at, STRIP), :] for i in range(tiles_y)], axis=0)
+                for ref in (act_ref, cot_ref)
+            ]
+            block = jnp.concatenate(pieces, axis=1)
+            ks = range(9 * side, 9 * side + 9)
+            picks = [(code[:, k:k + 1] == place).astype(jnp.bfloat16) for k in ks]
+            near = jnp.dot(jnp.concatenate(picks, axis=0), block, preferred_element_type=jnp.float32)
+            near = near.astype(jnp.bfloat16)
+            for k in ks:
+                rows_k = near[(k - 9 * side) * STRIP:(k - 9 * side + 1) * STRIP, :]
                 near_act[here:here + STRIP, k * width:(k + 1) * width] = rows_k[:, :width]
                 near_cot[here:here + STRIP, k * width:(k + 1) * width] = rows_k[:, width:]
     for k in range(27):
@@ -111,7 +135,7 @@
     conv = jnp.dot(near_act[...], w_ref[...].reshape(27 * width, width), preferred_element_type=jnp.float32)
     conv_ref[...] = conv.astype(jnp.bfloat16)
     back = lax.dot_general(near_cot[...], w_back[...], (((1,), (1,)), ((), ())), preferred_element_type=jnp.float32)
-    z_val = feat_ref[...].astype(jnp.float32) + shift_ref[...]
+    z_val = z_ref[...]
     sig = jax.nn.sigmoid(z_val)
     grad_ref[...] = (back * sig * (1.0 + z_val * (1.0 - sig))).astype(jnp.bfloat16)
 
@@ -120,34 +144,41 @@
     rows, width = features.shape[1:]
     peers = tiles_x * tiles_y
     total = peers * rows
+    vmem = pl.BlockSpec(memory_space=pltpu.VMEM)
     temb = time_embedding(timesteps, width)
-    packed, shift = pl.pallas_call(
+    packed, z_val, code = pl.pallas_call(
         functools.partial(pack_kernel, tiles_y),
         out_shape=(
-            jax.ShapeDtypeStruct((rows + CODE_ROWS, 2 * width), jnp.bfloat16),
-            jax.ShapeDtypeStruct((1, width), jnp.float32),
+            jax.ShapeDtypeStruct((rows + rows // width * CODE_ROWS, width), jnp.bfloat16),
+            jax.ShapeDtypeStruct((rows, width), jnp.float32),
+            jax.ShapeDtypeStruct((rows, 27), jnp.float32),
         ),
+        out_specs=(vmem, vmem, vmem),
         name="pack_tile",
-    )(features[0], cotangent[0], neighbours, temb, condition, w_time)
-    scene = lax.all_gather(packed, "brick")
+    )(features[0], neighbours, temb, condition, w_time)
+    cot_all = lax.all_gather(cotangent[0], "brick")
+    cot_all, packed = lax.optimization_barrier((cot_all, packed))
+    act_all = lax.all_gather(packed, "brick")
     own, sent = pl.pallas_call(
         functools.partial(weight_kernel, tiles_x, tiles_y),
         out_shape=(
             jax.ShapeDtypeStruct((27, width, width), jnp.float32),
             jax.ShapeDtypeStruct((27, width, width), jnp.bfloat16),
         ),
+        in_specs=[vmem, vmem],
+        out_specs=(vmem, vmem),
         scratch_shapes=[
             pltpu.VMEM((total, 2 * width), jnp.bfloat16),
             pltpu.VMEM((2 * width, total), jnp.bfloat16),
             pltpu.VMEM((total, CODE_ROWS), jnp.float32),
-            pltpu.VMEM((HALF, total, 2 * width), jnp.bfloat16),
+            pltpu.VMEM((HALF // 2 + 1, total, 2 * width), jnp.bfloat16),
+            pltpu.VMEM((HALF // 2 + 1, total, 2 * width), jnp.bfloat16),
         ],
-        compiler_params=pltpu.CompilerParams(vmem_limit_bytes=VMEM_BYTES),
+        compiler_params=pltpu.CompilerParams(vmem_limit_bytes=WEIGHT_VMEM),
         name="weight_terms",
-    )(scene)
+    )(act_all, cot_all)
     other = lax.ppermute(sent, "batch", [(0, 1), (1, 0)])
     here = lax.axis_index("brick").astype(jnp.int32).reshape(1)
-    vmem = pl.BlockSpec(memory_space=pltpu.VMEM)
     conv_out, feature_grad = pl.pallas_call(
         functools.partial(voxel_kernel, tiles_x, tiles_y),
         out_shape=(
@@ -160,10 +191,10 @@
             pltpu.VMEM((rows, 27 * width), jnp.bfloat16),
             pltpu.VMEM((width, 27 * width), jnp.bfloat16),
         ],
-        compiler_params=pltpu.CompilerParams(vmem_limit_bytes=VMEM_BYTES),
+        compiler_params=pltpu.CompilerParams(vmem_limit_bytes=VOXEL_VMEM),
         cost_estimate=pl.CostEstimate(flops=10**9, bytes_accessed=4 * 10**6, transcendentals=0),
         name="voxel_outputs",
-    )(here, scene, neighbours, features[0], shift, w_conv)
+    )(here, act_all, cot_all, code, z_val, w_conv)
     weight_grad = own + other.astype(jnp.float32)
     return (conv_out[None], feature_grad[None], weight_grad)
 

time: 86.8 us -> 87.9 us (1.013)
  blocking collectives: 0 us -> 65 us
  waiting for transfers between devices: 43.9 us -> 0.01 us
  between operations: 14.7 us -> 1.3 us
  local copies, waits for them, and re-layouts: 5.91 us -> 1.17 us
  Pallas kernels: 19.8 us -> 16.8 us
  other arithmetic: 2.05 us -> 3.21 us
    all_gather x0 -> x2, blocking collectives: none -> 65 us  [the longest x1 33.2 us: whole_scene(): cot_all = lax.all_gather(cotangent[0], 'brick')]
    all_gather x1 -> x0, waiting for transfers between devices: 43.8 us -> none  [whole_scene(): scene = lax.all_gather(packed, 'brick')]
    unnamed x12 -> x6, local copies, waits for them, and re-layouts: 5.91 us -> 1.17 us
    pallas_call x1, Pallas kernels: 14.6 us -> 11.7 us  [whole_scene(): pl.pallas_call(functools.partial(weight_kernel, tiles_x, tiles_y), out_sh...]
    add x1, other arithmetic: 1.4 us -> 2.57 us  [whole_scene(): weight_grad = own + other.astype(jnp.float32)]
  transfers between devices with their start and end apart: 2 -> 1, of which waited for: 1 -> 0; matrix products, arithmetic and copies ran while one was open for 0% -> 0% of each run, Pallas kernels for 4% -> 4%
where the time goes in v3:
time: 87.9 us; the launch traced here: 87.5 us
  blocking collectives  65 us (74%)
  Pallas kernels  16.8 us (19%)
  other arithmetic  3.21 us (4%)
  between operations  1.3 us (1%)
  local copies, waits for them, and re-layouts  1.17 us (1%)
    all_gather x1, blocking collectives, whole_scene(): cot_all = lax.all_gather(cotangent[0], 'brick')  33.2 us
    all_gather x1, blocking collectives, whole_scene(): act_all = lax.all_gather(packed, 'brick')  31.8 us
    pallas_call x1, Pallas kernels, whole_scene(): pl.pallas_call(functools.partial(weight_kernel, tiles_x, tiles_y), out_sh...  11.7 us
    pallas_call x1, Pallas kernels, whole_scene(): pl.pallas_call(functools.partial(voxel_kernel, tiles_x, tiles_y), out_sha...  3.34 us
    add x1, other arithmetic, whole_scene(): weight_grad = own + other.astype(jnp.float32)  2.57 us
  transfers between devices with their start and end apart: 1, of which 0 were waited for; matrix products, arithmetic and copies ran while one was open for 0% of the time, Pallas kernels for 4%

profile of v3, /device:TPU:0, one launch (start us, length us, event | category | flops | bytes accessed | tf_op | source)
XLA Modules:
  0.0 87.5 jit_solution(5693810785166089569)
XLA Ops:
  1.3 0.1 convert_bitcast_fusion
  1.3 33.2 %all_gather.9.cot_ref = bf16[8,256,128]{2,1,0:T(8,128)(2,1)S(1)} all-gather(bf16[1,256,128]{2,1,0:T(8,128)(2,1)} %param.8), channel_id=1, replica_groups=mesh['groups'=2,'brick'=8,'batch'=2] {'brick'}, dimensions={0}, use_global_device_ids=true | all-gather | bytes 589824 | tf_op jit(solution)/shard_map/all_gather | solution.py:159
  34.6 0.6 pad_maximum_fusion.temb_ref
  35.1 1.7 %pack_tile.1 = (bf16[288,128]{1,0:T(8,128)(2,1)}, f32[256,128]{1,0:T(8,128)}, f32[256,27]{1,0:T(8,128)}) custom-call(bf16[256,128]{1,0:T(8,128)(2,1)} %bitcast.12, s32[27,256]{1,0:T(8,128)} %near_ref.1, bf16[1,128]{1,0:T(2,128)(2,1)} %pad_maximum_fusion.temb_ref, bf16[1,128]{1,0:T(2,128)(2,1)} %cond_ref.1, bf16[128,128]{1,0:T(8,128)(2,1)} %wt_ref.1), custom_call_target="tpu_custom_call" | custom-call | tf_op jit(solution)/shard_map/pack_tile/pallas_call | solution.py:149
  36.9 0.0 copy-start.1
  36.9 0.0 copy-start.2
  36.9 31.8 %all-gather = bf16[2304,128]{1,0:T(8,128)(2,1)S(1)} all-gather(bf16[288,128]{1,0:T(8,128)(2,1)} %get-tuple-element.13), channel_id=2, replica_groups=mesh['groups'=2,'brick'=8,'batch'=2] {'brick'}, dimensions={0}, use_global_device_ids=true | all-gather | bytes 663552 | tf_op jit(solution)/shard_map/all_gather | solution.py:161
  68.7 11.7 %weight_terms.1 = (f32[27,128,128]{2,1,0:T(8,128)S(1)}, bf16[27,128,128]{2,1,0:T(8,128)(2,1)}) custom-call(bf16[8,288,128]{2,1,0:T(8,128)(2,1)S(1)} %bitcast.10, bf16[8,256,128]{2,1,0:T(8,128)(2,1)S(1)} %all_gather.9.cot_ref), custom_call_target="tpu_custom_call" | custom-call | tf_op jit(solution)/shard_map/weight_terms/pallas_call | solution.py:162
  80.4 0.0 collective-permute-start
  80.4 0.0 copy-done.1
  80.4 0.0 copy-done.2
  80.5 0.0 copy-start
  80.5 1.2 %copy-done = bf16[27,128,128]{2,1,0:T(8,128)(2,1)S(1)} copy-done((bf16[27,128,128]{2,1,0:T(8,128)(2,1)S(1)}, bf16[27,128,128]{2,1,0:T(8,128)(2,1)}, u32[]{:S(2)}) %copy-start) | copy-done | bytes 884760
  81.6 3.3 %voxel_outputs.1 = (bf16[256,128]{1,0:T(8,128)(2,1)}, bf16[256,128]{1,0:T(8,128)(2,1)}) custom-call(s32[1]{0:T(128)} %bitcast.where_ref, bf16[8,288,128]{2,1,0:T(8,128)(2,1)S(1)} %bitcast.11, bf16[8,256,128]{2,1,0:T(8,128)(2,1)S(1)} %all_gather.9.cot_ref, f32[256,27]{1,0:T(8,128)S(1)} %copy-done.2, f32[256,128]{1,0:T(8,128)S(1)} %copy-done.1, ...), custom_call_target="tpu_custom_call" | custom-call | flops 1000000000 | bytes 4000000 | tf_op jit(solution)/shard_map/voxel_outputs/pallas_call | solution.py:182
  85.0 0.0 collective-permute-done
  85.0 2.6 %convert_add_fusion = f32[27,128,128]{2,1,0:T(8,128)} fusion(f32[27,128,128]{2,1,0:T(8,128)S(1)} %get-tuple-element.19, bf16[27,128,128]{2,1,0:T(8,128)(2,1)} %collective-permute-done), kind=kLoop, calls=%fused_computation | loop fusion | flops 884736 | bytes 4423680 | tf_op jit(solution)/shard_map/add | solution.py:198
Async XLA Ops:
  36.9 43.6 %copy-start.1 = (f32[256,128]{1,0:T(8,128)S(1)}, f32[256,128]{1,0:T(8,128)}, u32[]{:S(2)}) copy-start(f32[256,128]{1,0:T(8,128)} %get-tuple-element.16.z_ref) | copy-start | bytes 393220
  36.9 43.6 %copy-start.2 = (f32[256,27]{1,0:T(8,128)S(1)}, f32[256,27]{1,0:T(8,128)}, u32[]{:S(2)}) copy-start(f32[256,27]{1,0:T(8,128)} %get-tuple-element.15.code_ref) | copy-start | bytes 82948
  80.4 4.5 %collective-permute-start = (bf16[27,128,128]{2,1,0:T(8,128)(2,1)}, bf16[27,128,128]{2,1,0:T(8,128)(2,1)}, u32[]{:S(2)}, u32[]{:S(2)}) collective-permute-start(bf16[27,128,128]{2,1,0:T(8,128)(2,1)} %get-tuple-element.20), channel_id=1, source_target_pairs={{0,1},{1,0},{2,3},{3,2},{4,5},{5,4},{6,7},{7,6},{8,9},{9,8},{10,11... | collective-permute-start | bytes 2654216 | tf_op jit(solution)/shard_map/ppermute | solution.py:180
  80.5 1.2 %copy-start = (bf16[27,128,128]{2,1,0:T(8,128)(2,1)S(1)}, bf16[27,128,128]{2,1,0:T(8,128)(2,1)}, u32[]{:S(2)}) copy-start(bf16[27,128,128]{2,1,0:T(8,128)(2,1)} %w_ref.1) | copy-start | bytes 2654212

commit v4 on v2

v4 whole, which is shorter than its diff:
```python
import functools

import jax
import jax.numpy as jnp
from jax import lax
from jax.experimental import pallas as pl
from jax.experimental.pallas import tpu as pltpu
from jax.sharding import PartitionSpec as P

LAYERS = 16
TILE = 4
STRIP = TILE * LAYERS
HALF = 13
CODE_ROWS = 16
KERNEL_VMEM = 24 * 1024 * 1024


def time_embedding(timesteps, width):
    half = width // 2
    freq = jnp.exp(-jnp.log(10000.0) * jnp.arange(half, dtype=jnp.float32) / half)
    angle = timesteps.astype(jnp.float32)[:, None] * freq[None, :]
    return jnp.concatenate([jnp.sin(angle), jnp.cos(angle)], axis=1).astype(jnp.bfloat16)


def strip_codes(neighbours, tiles_y):
    rows_here = TILE * STRIP
    code = (neighbours // rows_here) % tiles_y * STRIP + neighbours % STRIP
    return jnp.where(neighbours < 0, -1, code).astype(jnp.float32)


def pack_kernel(feat_ref, cot_ref, near_ref, temb_ref, cond_ref, wt_ref, pack_ref, z_ref, code_ref):
    rows, width = feat_ref.shape
    shift = jnp.dot(temb_ref[...], wt_ref[...], preferred_element_type=jnp.float32)
    shift = shift + cond_ref[...].astype(jnp.float32)
    z_val = feat_ref[...].astype(jnp.float32) + shift
    z_ref[...] = z_val
    pack_ref[:rows, :width] = (z_val * jax.nn.sigmoid(z_val)).astype(jnp.bfloat16)
    pack_ref[:rows, width:] = cot_ref[...]
    code = strip_codes(near_ref[...], 2)
    code_ref[...] = code.T
    pack_ref[rows:, :] = code[:CODE_ROWS, :].astype(jnp.bfloat16)


def lay_strip(ground, to, tile_y, mine_ref, other_ref, u):
    span = 2 * STRIP
    for ref, place in ((mine_ref, tile_y), (other_ref, 1 - tile_y)):
        at = pl.multiple_of(to * span + place * STRIP, STRIP)
        ground[pl.ds(at, STRIP), :] = ref[u * STRIP:(u + 1) * STRIP, :]


def row_kernel(stage, final, *refs):
    refs = list(refs)
    where_ref = refs.pop(0)
    rows_refs = [refs.pop(0) for _ in range(2 + 2 * (stage > 0) + 2 * final)]
    before = [refs.pop(0) for _ in range(3 * (stage > 0))]
    outs = [refs.pop(0) for _ in range(2 if final else 3)]
    ground, turned, codes, near_act, near_cot = refs
    width = ground.shape[1] // 2
    rows = TILE * STRIP
    span = 2 * STRIP
    tile_y = where_ref[0] % 2
    strips = [(rows_refs[0], rows_refs[1], u) for u in range(TILE)]
    if stage > 0:
        strips.append((rows_refs[2], rows_refs[3], 0))
    for i, (mine, other, u) in enumerate(strips):
        lay_strip(ground, i, tile_y, mine, other, u)
        pair = [ref[rows:, u * STRIP:(u + 1) * STRIP].astype(jnp.float32) for ref in (mine, other)]
        first = jnp.where(tile_y == 0, pair[0], pair[1])
        second = jnp.where(tile_y == 0, pair[1], pair[0])
        codes[i] = jnp.concatenate([first, second], axis=1)
    sources = list(range(TILE))
    if final:
        lay_strip(ground, TILE + 1, tile_y, rows_refs[4], rows_refs[5], TILE - 1)
        sources.append(TILE + 1)
    for i in sources:
        turned[:, i * span:(i + 1) * span] = ground[i * span:(i + 1) * span, :].T
    place = lax.broadcasted_iota(jnp.int32, (span, span), 0).astype(jnp.float32)

    def gather(target, source, start, stop):
        picks = [(place == codes[target, k:k + 1, :]).astype(jnp.bfloat16) for k in range(start, stop)]
        near = jnp.dot(turned[:, source * span:(source + 1) * span], jnp.concatenate(picks, axis=1),
                       preferred_element_type=jnp.float32).astype(jnp.bfloat16)
        for k in range(start, stop):
            one = near[:, (k - start) * span:(k - start + 1) * span]
            near_act[k * width:(k + 1) * width, target * span:(target + 1) * span] = one[:width]
            near_cot[k * width:(k + 1) * width, target * span:(target + 1) * span] = one[width:]

    for u in range(TILE):
        gather(u, u, 9, HALF)
        if u > 0:
            gather(u, u - 1, 0, 9)
    if stage > 0:
        gather(TILE, TILE - 1, 0, 9)
    if final:
        gather(0, TILE + 1, 0, 9)
    low_from = 0 if final else span
    low_to = span * (TILE + (stage > 0))

    def product(near, start, stop, first, last, side):
        return jnp.dot(near[start * width:stop * width, first:last],
                       ground[first:last, side * width:(side + 1) * width], preferred_element_type=jnp.float32)

    pieces = []
    for near, side in ((near_act, 1), (near_cot, 0)):
        pieces.append(((0, 9), product(near, 0, 9, low_from, low_to, side)))
        pieces.append(((9, HALF), product(near, 9, HALF, 0, TILE * span, side)))
    centre = jnp.dot(turned[:width, :TILE * span], ground[:TILE * span, width:], preferred_element_type=jnp.float32)
    if stage > 0:
        centre = centre + before[2][...]
    for i, ((start, stop), value) in enumerate(pieces):
        turn = i // 2
        if stage > 0:
            value = value + before[turn][start * width:stop * width, :]
        if not final:
            outs[turn][start * width:stop * width, :] = value
            continue
        for k in range(start, stop):
            one = value[(k - start) * width:(k - start + 1) * width, :]
            one, to = (one.T, 2 * HALF - k) if turn else (one, k)
            outs[0][to] = one
            outs[1][to] = one.astype(jnp.bfloat16)
    if final:
        outs[0][HALF] = centre
        outs[1][HALF] = centre.astype(jnp.bfloat16)
    else:
        outs[2][...] = centre


def voxel_kernel(where_ref, mine_ref, other_ref, before_mine, before_other, after_mine, after_other,
                 code_ref, z_ref, w_ref, conv_ref, grad_ref, ground, near_act, near_cot, w_back):
    rows, width = z_ref.shape
    span = 2 * STRIP
    tile_y = where_ref[0] % 2
    lay_strip(ground, 0, tile_y, before_mine, before_other, TILE - 1)
    for u in range(TILE):
        lay_strip(ground, u + 1, tile_y, mine_ref, other_ref, u)
    lay_strip(ground, TILE + 1, tile_y, after_mine, after_other, 0)
    place = lax.broadcasted_iota(jnp.int32, (STRIP, span), 1).astype(jnp.float32)
    for u in range(TILE):
        here = u * STRIP
        code = code_ref[here:here + STRIP, :]
        for side in range(3):
            block = ground[(u + side) * span:(u + side + 1) * span, :]
            ks = range(9 * side, 9 * side + 9)
            picks = [(code[:, k:k + 1] == place).astype(jnp.bfloat16) for k in ks]
            near = jnp.dot(jnp.concatenate(picks, axis=0), block, preferred_element_type=jnp.float32)
            near = near.astype(jnp.bfloat16)
            for k in ks:
                rows_k = near[(k - 9 * side) * STRIP:(k - 9 * side + 1) * STRIP, :]
                near_act[here:here + STRIP, k * width:(k + 1) * width] = rows_k[:, :width]
                near_cot[here:here + STRIP, k * width:(k + 1) * width] = rows_k[:, width:]
    for k in range(27):
        w_back[:, k * width:(k + 1) * width] = w_ref[26 - k]
    conv = jnp.dot(near_act[...], w_ref[...].reshape(27 * width, width), preferred_element_type=jnp.float32)
    conv_ref[...] = conv.astype(jnp.bfloat16)
    back = lax.dot_general(near_cot[...], w_back[...], (((1,), (1,)), ((), ())), preferred_element_type=jnp.float32)
    z_val = z_ref[...]
    sig = jax.nn.sigmoid(z_val)
    grad_ref[...] = (back * sig * (1.0 + z_val * (1.0 - sig))).astype(jnp.bfloat16)


def whole_scene(features, cotangent, neighbours, timesteps, condition, w_time, w_conv, tiles_x, tiles_y):
    rows, width = features.shape[1:]
    peers = tiles_x * tiles_y
    span = 2 * STRIP
    vmem = pl.BlockSpec(memory_space=pltpu.VMEM)
    smem = pl.BlockSpec(memory_space=pltpu.SMEM)
    params = pltpu.CompilerParams(vmem_limit_bytes=KERNEL_VMEM)
    temb = time_embedding(timesteps, width)
    packed, z_val, code = pl.pallas_call(
        pack_kernel,
        out_shape=(
            jax.ShapeDtypeStruct((rows + CODE_ROWS, 2 * width), jnp.bfloat16),
            jax.ShapeDtypeStruct((rows, width), jnp.float32),
            jax.ShapeDtypeStruct((rows, 27), jnp.float32),
        ),
        out_specs=(vmem, vmem, vmem),
        name="pack_tile",
    )(features[0], cotangent[0], neighbours, temb, condition, w_time)
    here = lax.axis_index("brick").astype(jnp.int32).reshape(1)
    across = [(i, i ^ 1) for i in range(peers)]
    own_pair = (packed, lax.ppermute(packed, "brick", across))
    pairs = [own_pair]
    for turn in range(1, tiles_x):
        mine = lax.ppermute(packed, "brick", [(i, (i + turn * tiles_y) % peers) for i in range(peers)])
        pairs.append((mine, None))
    sums = ()
    for stage in range(tiles_x):
        final = stage == tiles_x - 1
        blocks = pairs[stage]
        if stage > 0:
            blocks = blocks + pairs[stage - 1]
        if final:
            blocks = blocks + own_pair
            out_shape = (
                jax.ShapeDtypeStruct((27, width, width), jnp.float32),
                jax.ShapeDtypeStruct((27, width, width), jnp.bfloat16),
            )
        else:
            out_shape = (
                jax.ShapeDtypeStruct((HALF * width, width), jnp.float32),
                jax.ShapeDtypeStruct((HALF * width, width), jnp.float32),
                jax.ShapeDtypeStruct((width, width), jnp.float32),
            )
        sums = pl.pallas_call(
            functools.partial(row_kernel, stage, final),
            out_shape=out_shape,
            in_specs=[smem] + [vmem] * (len(blocks) + len(sums)),
            out_specs=(vmem,) * len(out_shape),
            scratch_shapes=[
                pltpu.VMEM(((TILE + 2) * span, 2 * width), jnp.bfloat16),
                pltpu.VMEM((2 * width, (TILE + 2) * span), jnp.bfloat16),
                pltpu.VMEM((TILE + 1, CODE_ROWS, span), jnp.float32),
                pltpu.VMEM((HALF * width, (TILE + 1) * span), jnp.bfloat16),
                pltpu.VMEM((HALF * width, (TILE + 1) * span), jnp.bfloat16),
            ],
            compiler_params=params,
            cost_estimate=pl.CostEstimate(flops=2 * 10**9, bytes_accessed=4 * 10**6, transcendentals=0),
            name=f"weight_row_{stage}",
        )(here, *blocks, *sums)
        if stage == 0:
            for turn in range(1, tiles_x):
                mine, centre = lax.optimization_barrier((pairs[turn][0], sums[2]))
                sums = (sums[0], sums[1], centre)
                pairs[turn] = (mine, lax.ppermute(mine, "brick", across))
    own, sent = sums
    other = lax.ppermute(sent, "batch", [(0, 1), (1, 0)])
    conv_out, feature_grad = pl.pallas_call(
        voxel_kernel,
        out_shape=(
            jax.ShapeDtypeStruct((rows, width), jnp.bfloat16),
            jax.ShapeDtypeStruct((rows, width), jnp.bfloat16),
        ),
        in_specs=[smem] + [vmem] * 9,
        scratch_shapes=[
            pltpu.VMEM(((TILE + 2) * span, 2 * width), jnp.bfloat16),
            pltpu.VMEM((rows, 27 * width), jnp.bfloat16),
            pltpu.VMEM((rows, 27 * width), jnp.bfloat16),
            pltpu.VMEM((width, 27 * width), jnp.bfloat16),
        ],
        compiler_params=params,
        cost_estimate=pl.CostEstimate(flops=10**9, bytes_accessed=4 * 10**6, transcendentals=0),
        name="voxel_outputs",
    )(here, *own_pair, *pairs[1], *pairs[tiles_x - 1], code, z_val, w_conv)
    weight_grad = own + other.astype(jnp.float32)
    return (conv_out[None], feature_grad[None], weight_grad)


def passed_along(block, axis, distance):
    devices = range(lax.axis_size(axis))
    route = [(i - distance, i) for i in devices if i - distance in devices]
    return lax.ppermute(block, axis, route)


def slab_rows(block, side_recv, front_recv, width):
    widened = jnp.concatenate([side_recv[0], block, side_recv[1]], axis=1)
    slab = jnp.concatenate([front_recv[0][None], widened, front_recv[1][None]], axis=0)
    flat = slab.reshape(-1, width)
    return jnp.concatenate([flat, jnp.zeros((1, width), jnp.bfloat16)], axis=0)


def with_halo(block, tiles_y):
    width = block.shape[-1]
    side = TILE
    side_recv = tuple(passed_along(block[:, edge], "brick", by)[:, None] for by, edge in ((1, side - 1), (-1, 0)))
    wide = jnp.concatenate([side_recv[0], block, side_recv[1]], axis=1)
    front_recv = tuple(passed_along(wide[edge], "brick", by) for by, edge in ((tiles_y, side - 1), (-tiles_y, 0)))
    return slab_rows(block, side_recv, front_recv, width)


def halo_plan(features, cotangent, neighbours, timesteps, condition, w_time, w_conv, tiles_x, tiles_y):
    rows_here, width = features.shape[1:]
    here = lax.axis_index("brick")
    tile_x = here // tiles_y
    tile_y = here % tiles_y
    side = TILE
    layers = LAYERS
    wide = side + 2
    valid = neighbours >= 0
    safe = jnp.where(valid, neighbours, 0)
    owner = safe // rows_here
    inside = safe % rows_here
    column = inside // layers
    layer = inside % layers
    local_x = (owner // tiles_y - tile_x) * side + column // side + 1
    local_y = (owner % tiles_y - tile_y) * side + column % side + 1
    sentinel = wide * wide * layers
    ext_index = jnp.where(valid, (local_x * wide + local_y) * layers + layer, sentinel).T
    temb = time_embedding(timesteps, width)
    shift = jnp.dot(temb, w_time, preferred_element_type=jnp.float32) + condition.astype(jnp.float32)
    z_val = features[0].astype(jnp.float32) + shift[0][None, :]
    act = jax.nn.silu(z_val).astype(jnp.bfloat16)
    cot = cotangent[0]
    w_forward = w_conv.reshape(27 * width, width)
    w_backward = jnp.transpose(w_conv[::-1], (0, 2, 1)).reshape(27 * width, width)
    act_ext = with_halo(act.reshape(side, side, layers, width), tiles_y)
    gathered = act_ext[ext_index].reshape(rows_here, 27 * width)
    conv_out = jnp.dot(gathered, w_forward, preferred_element_type=jnp.float32).astype(jnp.bfloat16)
    partial_grad = lax.dot_general(
        gathered, cot, (((0,), (0,)), ((), ())), preferred_element_type=jnp.float32
    )
    both = ("brick", "batch")
    parts = tiles_x * tiles_y * lax.axis_size("batch")
    rows = 27 * width
    extra = -rows % (8 * parts)
    pieces = jnp.pad(partial_grad.astype(jnp.bfloat16), ((0, extra), (0, 0))).reshape(parts, -1, width)
    arrived = lax.all_to_all(pieces, both, 0, 0)
    summed = arrived.astype(jnp.float32).sum(0).astype(jnp.bfloat16)
    whole = lax.all_gather(summed, both, axis=0, tiled=True)
    weight_grad = whole[:rows].astype(jnp.float32).reshape(27, width, width)
    cot_ext = with_halo(cot.reshape(side, side, layers, width), tiles_y)
    cot_gathered = cot_ext[ext_index].reshape(rows_here, 27 * width)
    back = jnp.dot(cot_gathered, w_backward, preferred_element_type=jnp.float32)
    sig = jax.nn.sigmoid(z_val)
    feature_grad = (back * sig * (1.0 + z_val * (1.0 - sig))).astype(jnp.bfloat16)
    return (conv_out[None], feature_grad[None], weight_grad)


def shards(*arrays):
    peers = lax.axis_size("brick")
    bits = peers.bit_length() - 1
    tiles_x = 2 ** ((bits + 1) // 2)
    tiles_y = 2 ** (bits // 2)
    plan = whole_scene if tiles_y == 2 else halo_plan
    return plan(*arrays, tiles_x, tiles_y)


def solution(mesh):
    in_specs = (
        P(("groups", "batch"), "brick", None),
        P(("groups", "batch"), "brick", None),
        P(None, ("groups", "brick")),
        P(("groups", "batch")),
        P(("groups", "batch"), None),
        P(),
        P(),
    )
    out_specs = (
        P(("groups", "batch"), "brick", None),
        P(("groups", "batch"), "brick", None),
        P("groups", None, None),
    )
    return jax.shard_map(shards, mesh=mesh, in_specs=in_specs, out_specs=out_specs, check_vma=False)
```

time: 86.8 us -> 42.4 us (0.49)
  the two profiles are of different devices: /device:TPU:0 before, /device:TPU:17 now
where the time goes in v4:
time: 42.4 us; the launch traced here: 42.2 us
  waiting for transfers between devices  17.5 us (41%)
  Pallas kernels  13.5 us (32%)
  starting transfers between devices  6.82 us (16%)
  other arithmetic  2.09 us (5%)
  between operations  1.36 us (3%)
  local copies, waits for them, and re-layouts  0.93 us (2%)
    ppermute x3, waiting for transfers between devices, whole_scene(): lax.ppermute(packed, 'brick', [(i, (i + turn * tiles_y) % peers) for i in...  9.51 us
    pallas_call x4, Pallas kernels, whole_scene(): pl.pallas_call(functools.partial(row_kernel, stage, final), out_shape=out...  8.41 us
    ppermute x3, waiting for transfers between devices, whole_scene(): pairs[turn] = (mine, lax.ppermute(mine, 'brick', across))  6.9 us
    pallas_call x1, Pallas kernels, whole_scene(): pl.pallas_call(voxel_kernel, out_shape=(jax.ShapeDtypeStruct((rows, width...  3.35 us
    ppermute x3, starting transfers between devices, whole_scene(): lax.ppermute(packed, 'brick', [(i, (i + turn * tiles_y) % peers) for i in...  2.48 us
    pallas_call x1, Pallas kernels, whole_scene(): pl.pallas_call(pack_kernel, out_shape=(jax.ShapeDtypeStruct((rows + CODE_...  1.78 us
    ppermute x3, starting transfers between devices, whole_scene(): pairs[turn] = (mine, lax.ppermute(mine, 'brick', across))  1.72 us
    add x1, other arithmetic, whole_scene(): weight_grad = own + other.astype(jnp.float32)  1.45 us
  transfers between devices with their start and end apart: 8, of which 4 were waited for; matrix products, arithmetic and copies ran while one was open for 0% of the time, Pallas kernels for 22%

profile of v4, /device:TPU:17, one launch (start us, length us, event | category | flops | bytes accessed | tf_op | source)
XLA Modules:
  0.0 42.2 jit_solution(11311082554157563333)
XLA Ops:
  1.3 0.1 convert_bitcast_fusion
  1.3 0.6 %pad_maximum_fusion.temb_ref = bf16[1,128]{1,0:T(2,128)(2,1)} fusion(bf16[1,64]{1,0:T(2,128)(2,1)S(1)} %get-tuple-element.47, bf16[1,64]{1,0:T(2,128)(2,1)S(1)} %get-tuple-element.48), kind=kLoop, calls=%fused_computation.1 | loop fusion | flops 512 | bytes 512 | tf_op jit(solution)/shard_map/concatenate | solution.py:22
  1.9 1.8 %pack_tile.1 = (bf16[272,256]{1,0:T(8,128)(2,1)}, f32[256,128]{1,0:T(8,128)}, f32[256,27]{1,0:T(8,128)}) custom-call(bf16[256,128]{1,0:T(8,128)(2,1)} %bitcast.10, bf16[256,128]{1,0:T(8,128)(2,1)} %bitcast.11, s32[27,256]{1,0:T(8,128)} %near_ref.1, bf16[1,128]{1,0:T(2,128)(2,1)} %pad_maximum_fusion.temb_ref, bf16[1,128]{1,0:T(2,128)(2,1)} %cond_ref.1, ...), custom_call_target="tpu_custom_call" | custom-call | tf_op jit(solution)/shard_map/pack_tile/pallas_call | solution.py:170
  3.7 1.2 %collective-permute-start = (bf16[272,256]{1,0:T(8,128)(2,1)}, bf16[272,256]{1,0:T(8,128)(2,1)S(1)}, u32[]{:S(2)}, u32[]{:S(2)}) collective-permute-start(bf16[272,256]{1,0:T(8,128)(2,1)} %get-tuple-element.25.refs_1_.mine_ref.refs_3_.refs_5_), channel_id=1, source_target_pairs={{0,2},{2,0},{4,6},{6,4},{8,10},{10,8},{12,14},{14,12},{1,3},{3,1},... | collective-permute-start | bytes 417800 | tf_op jit(solution)/shard_map/ppermute | solution.py:182
  4.9 0.1 collective-permute-start.4
  5.0 2.4 %collective-permute-start.3 = (bf16[272,256]{1,0:T(8,128)(2,1)}, bf16[272,256]{1,0:T(8,128)(2,1)S(1)}, u32[]{:S(2)}, u32[]{:S(2)}) collective-permute-start(bf16[272,256]{1,0:T(8,128)(2,1)} %get-tuple-element.25.refs_1_.mine_ref.refs_3_.refs_5_), channel_id=1, source_target_pairs={{0,12},{2,14},{4,0},{6,2},{8,4},{10,6},{12,8},{14,10},{1,13},{3,15... | collective-permute-start | bytes 417800 | tf_op jit(solution)/shard_map/ppermute | solution.py:185
  7.4 0.0 collective-permute-start.1
  7.4 1.1 %collective-permute-done.refs_2_.other_ref.refs_4_.refs_6_ = bf16[272,256]{1,0:T(8,128)(2,1)S(1)} collective-permute-done((bf16[272,256]{1,0:T(8,128)(2,1)}, bf16[272,256]{1,0:T(8,128)(2,1)S(1)}, u32[]{:S(2)}, u32[]{:S(2)}) %collective-permute-start) | collective-permute-done | bytes 139296 | tf_op jit(solution)/shard_map/ppermute | solution.py:182
  8.5 0.0 copy-start.1
  8.5 0.9 %copy-done.1 = bf16[272,256]{1,0:T(8,128)(2,1)S(1)} copy-done((bf16[272,256]{1,0:T(8,128)(2,1)S(1)}, bf16[272,256]{1,0:T(8,128)(2,1)}, u32[]{:S(2)}) %copy-start.1) | copy-done | bytes 139288
  9.4 1.8 %weight_row_0.1 = (f32[1664,128]{1,0:T(8,128)S(1)}, f32[1664,128]{1,0:T(8,128)S(1)}, f32[128,128]{1,0:T(8,128)S(1)}) custom-call(s32[1]{0:T(128)} %bitcast.refs_0_.where_ref, bf16[272,256]{1,0:T(8,128)(2,1)S(1)} %copy-done.1, bf16[272,256]{1,0:T(8,128)(2,1)S(1)} %collective-permute-done.refs_2_.other_ref.refs_4_.refs_6_), custom_call_target="tpu_custom_call" | custom-call | flops 2000000000 | bytes 4000000 | tf_op jit(solution)/shard_map/weight_row_0/pallas_call | solution.py:205
  11.1 9.5 %collective-permute-done.1.before_mine.refs_1_.refs_3_ = bf16[272,256]{1,0:T(8,128)(2,1)S(1)} collective-permute-done((bf16[272,256]{1,0:T(8,128)(2,1)}, bf16[272,256]{1,0:T(8,128)(2,1)S(1)}, u32[]{:S(2)}, u32[]{:S(2)}) %collective-permute-start.1) | collective-permute-done | bytes 139296 | tf_op jit(solution)/shard_map/ppermute | solution.py:185
  20.6 0.3 collective-permute-start.2
  20.9 0.0 collective-permute-done.4.refs_1_.refs_3_
  20.9 0.0 collective-permute-done.3.after_mine.refs_1_
  20.9 1.2 %collective-permute-start.5 = (bf16[272,256]{1,0:T(8,128)(2,1)S(1)}, bf16[272,256]{1,0:T(8,128)(2,1)S(1)}, u32[]{:S(2)}, u32[]{:S(2)}) collective-permute-start(bf16[272,256]{1,0:T(8,128)(2,1)S(1)} %collective-permute-done.3.after_mine.refs_1_), channel_id=1, source_target_pairs={{0,2},{2,0},{4,6},{6,4},{8,10},{10,8},{12,14},{14,12},{1,3},{3,1},... | collective-permute-start | bytes 417800 | tf_op jit(solution)/shard_map/ppermute | solution.py:225
  22.1 0.3 collective-permute-start.6
  22.4 3.0 %collective-permute-done.2.before_other.refs_2_.refs_4_ = bf16[272,256]{1,0:T(8,128)(2,1)S(1)} collective-permute-done((bf16[272,256]{1,0:T(8,128)(2,1)S(1)}, bf16[272,256]{1,0:T(8,128)(2,1)S(1)}, u32[]{:S(2)}, u32[]{:S(2)}) %collective-permute-start.2) | collective-permute-done | bytes 139296 | tf_op jit(solution)/shard_map/ppermute | solution.py:225
  25.4 2.1 %weight_row_1.1 = (f32[1664,128]{1,0:T(8,128)S(1)}, f32[1664,128]{1,0:T(8,128)S(1)}, f32[128,128]{1,0:T(8,128)S(1)}) custom-call(s32[1]{0:T(128)} %bitcast.refs_0_.where_ref, bf16[272,256]{1,0:T(8,128)(2,1)S(1)} %collective-permute-done.1.before_mine.refs_1_.refs_3_, bf16[272,256]{1,0:T(8,128)(2,1)S(1)} %collective-permute-done.2.before_other.refs_2_.refs_4_, ...), custom_call_target="tpu_custom_call" | custom-call | flops 2000000000 | bytes 4000000 | tf_op jit(solution)/shard_map/weight_row_1/pallas_call | solution.py:205
  27.5 3.9 %collective-permute-done.6.refs_2_.refs_4_ = bf16[272,256]{1,0:T(8,128)(2,1)S(1)} collective-permute-done((bf16[272,256]{1,0:T(8,128)(2,1)S(1)}, bf16[272,256]{1,0:T(8,128)(2,1)S(1)}, u32[]{:S(2)}, u32[]{:S(2)}) %collective-permute-start.6) | collective-permute-done | bytes 139296 | tf_op jit(solution)/shard_map/ppermute | solution.py:225
  31.3 0.0 copy-start.2
  31.3 2.1 %weight_row_2.1 = (f32[1664,128]{1,0:T(8,128)S(1)}, f32[1664,128]{1,0:T(8,128)S(1)}, f32[128,128]{1,0:T(8,128)S(1)}) custom-call(s32[1]{0:T(128)} %bitcast.refs_0_.where_ref, bf16[272,256]{1,0:T(8,128)(2,1)S(1)} %collective-permute-done.4.refs_1_.refs_3_, bf16[272,256]{1,0:T(8,128)(2,1)S(1)} %collective-permute-done.6.refs_2_.refs_4_, ...), custom_call_target="tpu_custom_call" | custom-call | flops 2000000000 | bytes 4000000 | tf_op jit(solution)/shard_map/weight_row_2/pallas_call | solution.py:205
  33.4 0.0 collective-permute-done.5.after_other.refs_2_
  33.4 0.0 copy-done.2
  33.5 0.0 copy-start
  33.5 0.0 copy-start.3
  33.5 0.0 copy-start.4
  33.5 2.5 %weight_row_3.1 = (f32[27,128,128]{2,1,0:T(8,128)S(1)}, bf16[27,128,128]{2,1,0:T(8,128)(2,1)S(1)}) custom-call(s32[1]{0:T(128)} %bitcast.refs_0_.where_ref, bf16[272,256]{1,0:T(8,128)(2,1)S(1)} %collective-permute-done.3.after_mine.refs_1_, bf16[272,256]{1,0:T(8,128)(2,1)S(1)} %collective-permute-done.5.after_other.refs_2_, ...), custom_call_target="tpu_custom_call" | custom-call | flops 2000000000 | bytes 4000000 | tf_op jit(solution)/shard_map/weight_row_3/pallas_call | solution.py:205
  36.0 1.4 %collective-permute-start.7 = (bf16[27,128,128]{2,1,0:T(8,128)(2,1)S(1)}, bf16[27,128,128]{2,1,0:T(8,128)(2,1)S(1)}, u32[]{:S(2)}, u32[]{:S(2)}) collective-permute-start(bf16[27,128,128]{2,1,0:T(8,128)(2,1)S(1)} %get-tuple-element.46), channel_id=1, source_target_pairs={{0,1},{1,0},{2,3},{3,2},{4,5},{5,4},{6,7},{7,6},{8,9},{9,8},{10,11... | collective-permute-start | bytes 2654216 | tf_op jit(solution)/shard_map/ppermute | solution.py:227
  37.4 0.0 copy-done
  37.4 0.0 copy-done.3
  37.4 0.0 copy-done.4
  37.4 3.3 %voxel_outputs.1 = (bf16[256,128]{1,0:T(8,128)(2,1)}, bf16[256,128]{1,0:T(8,128)(2,1)}) custom-call(s32[1]{0:T(128)} %bitcast.refs_0_.where_ref, bf16[272,256]{1,0:T(8,128)(2,1)S(1)} %copy-done.2, bf16[272,256]{1,0:T(8,128)(2,1)S(1)} %collective-permute-done.refs_2_.other_ref.refs_4_.refs_6_, ...), custom_call_target="tpu_custom_call" | custom-call | flops 1000000000 | bytes 4000000 | tf_op jit(solution)/shard_map/voxel_outputs/pallas_call | solution.py:228
  40.8 0.0 collective-permute-done.7
  40.8 1.4 %convert_add_fusion = f32[27,128,128]{2,1,0:T(8,128)} fusion(f32[27,128,128]{2,1,0:T(8,128)S(1)} %get-tuple-element.45, bf16[27,128,128]{2,1,0:T(8,128)(2,1)S(1)} %collective-permute-done.7), kind=kLoop, calls=%fused_computation | loop fusion | flops 884736 | bytes 4423680 | tf_op jit(solution)/shard_map/add | solution.py:245
Async XLA Ops:
  3.7 4.8 %collective-permute-start = (bf16[272,256]{1,0:T(8,128)(2,1)}, bf16[272,256]{1,0:T(8,128)(2,1)S(1)}, u32[]{:S(2)}, u32[]{:S(2)}) collective-permute-start(bf16[272,256]{1,0:T(8,128)(2,1)} %get-tuple-element.25.refs_1_.mine_ref.refs_3_.refs_5_), channel_id=1, source_target_pairs={{0,2},{2,0},{4,6},{6,4},{8,10},{10,8},{12,14},{14,12},{1,3},{3,1},... | collective-permute-start | bytes 417800 | tf_op jit(solution)/shard_map/ppermute | solution.py:182
  4.9 16.0 %collective-permute-start.4 = (bf16[272,256]{1,0:T(8,128)(2,1)}, bf16[272,256]{1,0:T(8,128)(2,1)S(1)}, u32[]{:S(2)}, u32[]{:S(2)}) collective-permute-start(bf16[272,256]{1,0:T(8,128)(2,1)} %get-tuple-element.25.refs_1_.mine_ref.refs_3_.refs_5_), channel_id=1, source_target_pairs={{0,8},{2,10},{4,12},{6,14},{8,0},{10,2},{12,4},{14,6},{1,9},{3,11}... | collective-permute-start | bytes 417800 | tf_op jit(solution)/shard_map/ppermute | solution.py:185
  5.0 15.9 %collective-permute-start.3 = (bf16[272,256]{1,0:T(8,128)(2,1)}, bf16[272,256]{1,0:T(8,128)(2,1)S(1)}, u32[]{:S(2)}, u32[]{:S(2)}) collective-permute-start(bf16[272,256]{1,0:T(8,128)(2,1)} %get-tuple-element.25.refs_1_.mine_ref.refs_3_.refs_5_), channel_id=1, source_target_pairs={{0,12},{2,14},{4,0},{6,2},{8,4},{10,6},{12,8},{14,10},{1,13},{3,15... | collective-permute-start | bytes 417800 | tf_op jit(solution)/shard_map/ppermute | solution.py:185
  7.4 13.2 %collective-permute-start.1 = (bf16[272,256]{1,0:T(8,128)(2,1)}, bf16[272,256]{1,0:T(8,128)(2,1)S(1)}, u32[]{:S(2)}, u32[]{:S(2)}) collective-permute-start(bf16[272,256]{1,0:T(8,128)(2,1)} %get-tuple-element.25.refs_1_.mine_ref.refs_3_.refs_5_), channel_id=1, source_target_pairs={{0,4},{2,6},{4,8},{6,10},{8,12},{10,14},{12,0},{14,2},{1,5},{3,7},... | collective-permute-start | bytes 417800 | tf_op jit(solution)/shard_map/ppermute | solution.py:185
  8.5 0.9 %copy-start.1 = (bf16[272,256]{1,0:T(8,128)(2,1)S(1)}, bf16[272,256]{1,0:T(8,128)(2,1)}, u32[]{:S(2)}) copy-start(bf16[272,256]{1,0:T(8,128)(2,1)} %get-tuple-element.25.refs_1_.mine_ref.refs_3_.refs_5_) | copy-start | bytes 417796
  20.6 4.7 %collective-permute-start.2 = (bf16[272,256]{1,0:T(8,128)(2,1)S(1)}, bf16[272,256]{1,0:T(8,128)(2,1)S(1)}, u32[]{:S(2)}, u32[]{:S(2)}) collective-permute-start(bf16[272,256]{1,0:T(8,128)(2,1)S(1)} %collective-permute-done.1.before_mine.refs_1_.refs_3_), channel_id=1, source_target_pairs={{0,2},{2,0},{4,6},{6,4},{8,10},{10,8},{12,14},{14,12},{1,3},{3,1},... | collective-permute-start | bytes 417800 | tf_op jit(solution)/shard_map/ppermute | solution.py:225
  20.9 12.5 %collective-permute-start.5 = (bf16[272,256]{1,0:T(8,128)(2,1)S(1)}, bf16[272,256]{1,0:T(8,128)(2,1)S(1)}, u32[]{:S(2)}, u32[]{:S(2)}) collective-permute-start(bf16[272,256]{1,0:T(8,128)(2,1)S(1)} %collective-permute-done.3.after_mine.refs_1_), channel_id=1, source_target_pairs={{0,2},{2,0},{4,6},{6,4},{8,10},{10,8},{12,14},{14,12},{1,3},{3,1},... | collective-permute-start | bytes 417800 | tf_op jit(solution)/shard_map/ppermute | solution.py:225
  22.1 9.2 %collective-permute-start.6 = (bf16[272,256]{1,0:T(8,128)(2,1)S(1)}, bf16[272,256]{1,0:T(8,128)(2,1)S(1)}, u32[]{:S(2)}, u32[]{:S(2)}) collective-permute-start(bf16[272,256]{1,0:T(8,128)(2,1)S(1)} %collective-permute-done.4.refs_1_.refs_3_), channel_id=1, source_target_pairs={{0,2},{2,0},{4,6},{6,4},{8,10},{10,8},{12,14},{14,12},{1,3},{3,1},... | collective-permute-start | bytes 417800 | tf_op jit(solution)/shard_map/ppermute | solution.py:225
  31.3 2.1 %copy-start.2 = (bf16[272,256]{1,0:T(8,128)(2,1)S(1)}, bf16[272,256]{1,0:T(8,128)(2,1)}, u32[]{:S(2)}) copy-start(bf16[272,256]{1,0:T(8,128)(2,1)} %get-tuple-element.25.refs_1_.mine_ref.refs_3_.refs_5_) | copy-start | bytes 417796
  33.5 3.9 %copy-start = (bf16[27,128,128]{2,1,0:T(8,128)(2,1)S(1)}, bf16[27,128,128]{2,1,0:T(8,128)(2,1)}, u32[]{:S(2)}) copy-start(bf16[27,128,128]{2,1,0:T(8,128)(2,1)} %w_ref.1) | copy-start | bytes 2654212
  33.5 3.9 %copy-start.3 = (f32[256,128]{1,0:T(8,128)S(1)}, f32[256,128]{1,0:T(8,128)}, u32[]{:S(2)}) copy-start(f32[256,128]{1,0:T(8,128)} %get-tuple-element.32.z_ref) | copy-start | bytes 393220
  33.5 3.9 %copy-start.4 = (f32[256,27]{1,0:T(8,128)S(1)}, f32[256,27]{1,0:T(8,128)}, u32[]{:S(2)}) copy-start(f32[256,27]{1,0:T(8,128)} %get-tuple-element.31.code_ref) | copy-start | bytes 82948
  36.0 4.8 %collective-permute-start.7 = (bf16[27,128,128]{2,1,0:T(8,128)(2,1)S(1)}, bf16[27,128,128]{2,1,0:T(8,128)(2,1)S(1)}, u32[]{:S(2)}, u32[]{:S(2)}) collective-permute-start(bf16[27,128,128]{2,1,0:T(8,128)(2,1)S(1)} %get-tuple-element.46), channel_id=1, source_target_pairs={{0,1},{1,0},{2,3},{3,2},{4,5},{5,4},{6,7},{7,6},{8,9},{9,8},{10,11... | collective-permute-start | bytes 2654216 | tf_op jit(solution)/shard_map/ppermute | solution.py:227

commit v5 on v4

--- a/solution.py
+++ b/solution.py
@@ -12,7 +12,9 @@
 STRIP = TILE * LAYERS
 HALF = 13
 CODE_ROWS = 16
+ROW_STAGES = 4
 KERNEL_VMEM = 24 * 1024 * 1024
+PACK_VMEM = 4 * 1024 * 1024
 
 
 def time_embedding(timesteps, width):
@@ -28,17 +30,37 @@
     return jnp.where(neighbours < 0, -1, code).astype(jnp.float32)
 
 
-def pack_kernel(feat_ref, cot_ref, near_ref, temb_ref, cond_ref, wt_ref, pack_ref, z_ref, code_ref):
+def pack_kernel(time_ref, feat_hbm, cot_hbm, near_hbm, cond_hbm, wt_hbm, pack_ref, z_ref, code_ref,
+                feat_ref, near_ref, cond_ref, wt_ref, sems):
     rows, width = feat_ref.shape
-    shift = jnp.dot(temb_ref[...], wt_ref[...], preferred_element_type=jnp.float32)
+    half = width // 2
+    moves = (
+        (wt_hbm, wt_ref),
+        (cond_hbm, cond_ref),
+        (feat_hbm.at[0], feat_ref),
+        (near_hbm, near_ref),
+        (cot_hbm.at[0], pack_ref.at[:rows, width:]),
+    )
+    copies = [pltpu.make_async_copy(source, to, sems.at[i]) for i, (source, to) in enumerate(moves)]
+    for copy in copies:
+        copy.start()
+    lane = lax.broadcasted_iota(jnp.int32, (1, width), 1)
+    freq = jnp.exp(-jnp.log(10000.0) * (lane % half).astype(jnp.float32) / half)
+    angle = time_ref[0].astype(jnp.float32) * freq
+    temb = jnp.where(lane < half, jnp.sin(angle), jnp.cos(angle)).astype(jnp.bfloat16)
+    copies[0].wait()
+    copies[1].wait()
+    shift = jnp.dot(temb, wt_ref[...], preferred_element_type=jnp.float32)
     shift = shift + cond_ref[...].astype(jnp.float32)
+    copies[2].wait()
     z_val = feat_ref[...].astype(jnp.float32) + shift
     z_ref[...] = z_val
     pack_ref[:rows, :width] = (z_val * jax.nn.sigmoid(z_val)).astype(jnp.bfloat16)
-    pack_ref[:rows, width:] = cot_ref[...]
+    copies[3].wait()
     code = strip_codes(near_ref[...], 2)
     code_ref[...] = code.T
     pack_ref[rows:, :] = code[:CODE_ROWS, :].astype(jnp.bfloat16)
+    copies[4].wait()
 
 
 def lay_strip(ground, to, tile_y, mine_ref, other_ref, u):
@@ -48,32 +70,29 @@
         ground[pl.ds(at, STRIP), :] = ref[u * STRIP:(u + 1) * STRIP, :]
 
 
-def row_kernel(stage, final, *refs):
+def row_kernel(stage, strips, borders, *refs):
     refs = list(refs)
+    first_stage, final = stage == 0, stage == ROW_STAGES - 1
     where_ref = refs.pop(0)
-    rows_refs = [refs.pop(0) for _ in range(2 + 2 * (stage > 0) + 2 * final)]
-    before = [refs.pop(0) for _ in range(3 * (stage > 0))]
+    pairs = [(refs.pop(0), refs.pop(0)) for _ in range(1 + max(pair for pair, _ in strips))]
+    before = [refs.pop(0) for _ in range(0 if first_stage else 3)]
     outs = [refs.pop(0) for _ in range(2 if final else 3)]
     ground, turned, codes, near_act, near_cot = refs
     width = ground.shape[1] // 2
     rows = TILE * STRIP
     span = 2 * STRIP
     tile_y = where_ref[0] % 2
-    strips = [(rows_refs[0], rows_refs[1], u) for u in range(TILE)]
-    if stage > 0:
-        strips.append((rows_refs[2], rows_refs[3], 0))
-    for i, (mine, other, u) in enumerate(strips):
-        lay_strip(ground, i, tile_y, mine, other, u)
-        pair = [ref[rows:, u * STRIP:(u + 1) * STRIP].astype(jnp.float32) for ref in (mine, other)]
-        first = jnp.where(tile_y == 0, pair[0], pair[1])
-        second = jnp.where(tile_y == 0, pair[1], pair[0])
-        codes[i] = jnp.concatenate([first, second], axis=1)
-    sources = list(range(TILE))
-    if final:
-        lay_strip(ground, TILE + 1, tile_y, rows_refs[4], rows_refs[5], TILE - 1)
-        sources.append(TILE + 1)
-    for i in sources:
-        turned[:, i * span:(i + 1) * span] = ground[i * span:(i + 1) * span, :].T
+    borders = [(u, u - 1) for u in range(1, TILE)] + borders
+    targets = sorted({target for target, _ in borders})
+    for i, (pair, u) in enumerate(strips):
+        lay_strip(ground, i, tile_y, *pairs[pair], u)
+        if i < TILE or i in targets:
+            both = [ref[rows:, u * STRIP:(u + 1) * STRIP].astype(jnp.float32) for ref in pairs[pair]]
+            first = jnp.where(tile_y == 0, both[0], both[1])
+            second = jnp.where(tile_y == 0, both[1], both[0])
+            codes[i] = jnp.concatenate([first, second], axis=1)
+        if i < TILE or i in [source for _, source in borders]:
+            turned[:, i * span:(i + 1) * span] = ground[i * span:(i + 1) * span, :].T
     place = lax.broadcasted_iota(jnp.int32, (span, span), 0).astype(jnp.float32)
 
     def gather(target, source, start, stop):
@@ -87,14 +106,10 @@
 
     for u in range(TILE):
         gather(u, u, 9, HALF)
-        if u > 0:
-            gather(u, u - 1, 0, 9)
-    if stage > 0:
-        gather(TILE, TILE - 1, 0, 9)
-    if final:
-        gather(0, TILE + 1, 0, 9)
-    low_from = 0 if final else span
-    low_to = span * (TILE + (stage > 0))
+    for target, source in borders:
+        gather(target, source, 0, 9)
+    low_from = span * targets[0]
+    low_to = span * (targets[-1] + 1)
 
     def product(near, start, stop, first, last, side):
         return jnp.dot(near[start * width:stop * width, first:last],
@@ -105,11 +120,11 @@
         pieces.append(((0, 9), product(near, 0, 9, low_from, low_to, side)))
         pieces.append(((9, HALF), product(near, 9, HALF, 0, TILE * span, side)))
     centre = jnp.dot(turned[:width, :TILE * span], ground[:TILE * span, width:], preferred_element_type=jnp.float32)
-    if stage > 0:
+    if not first_stage:
         centre = centre + before[2][...]
     for i, ((start, stop), value) in enumerate(pieces):
         turn = i // 2
-        if stage > 0:
+        if not first_stage:
             value = value + before[turn][start * width:stop * width, :]
         if not final:
             outs[turn][start * width:stop * width, :] = value
@@ -166,7 +181,6 @@
     vmem = pl.BlockSpec(memory_space=pltpu.VMEM)
     smem = pl.BlockSpec(memory_space=pltpu.SMEM)
     params = pltpu.CompilerParams(vmem_limit_bytes=KERNEL_VMEM)
-    temb = time_embedding(timesteps, width)
     packed, z_val, code = pl.pallas_call(
         pack_kernel,
         out_shape=(
@@ -174,24 +188,43 @@
             jax.ShapeDtypeStruct((rows, width), jnp.float32),
             jax.ShapeDtypeStruct((rows, 27), jnp.float32),
         ),
+        in_specs=[smem] + [pl.BlockSpec(memory_space=pltpu.HBM)] * 5,
         out_specs=(vmem, vmem, vmem),
+        scratch_shapes=[
+            pltpu.VMEM((rows, width), jnp.bfloat16),
+            pltpu.VMEM(neighbours.shape, jnp.int32),
+            pltpu.VMEM((1, width), jnp.bfloat16),
+            pltpu.VMEM((width, width), jnp.bfloat16),
+            pltpu.SemaphoreType.DMA((5,)),
+        ],
+        compiler_params=pltpu.CompilerParams(vmem_limit_bytes=PACK_VMEM),
         name="pack_tile",
-    )(features[0], cotangent[0], neighbours, temb, condition, w_time)
+    )(timesteps, features, cotangent, neighbours, condition, w_time)
     here = lax.axis_index("brick").astype(jnp.int32).reshape(1)
-    across = [(i, i ^ 1) for i in range(peers)]
-    own_pair = (packed, lax.ppermute(packed, "brick", across))
-    pairs = [own_pair]
-    for turn in range(1, tiles_x):
-        mine = lax.ppermute(packed, "brick", [(i, (i + turn * tiles_y) % peers) for i in range(peers)])
-        pairs.append((mine, None))
+
+    def across(block):
+        return lax.ppermute(block, "brick", [(i, i ^ 1) for i in range(peers)])
+
+    def along(block, turn):
+        return lax.ppermute(block, "brick", [(i, (i + turn * tiles_y) % peers) for i in range(peers)])
+
+    before, after = along(packed, 1), along(packed, -1)
+    far = along(before, 1)
+    own_pair = (packed, across(packed))
+    before_pair = (before, across(before))
+    after_pair = (after, across(after))
+    far_pair = (far, across(far))
+    line = [(0, u) for u in range(TILE)]
+    stages = (
+        ((own_pair,), line, []),
+        ((before_pair, own_pair), line + [(1, 0)], [(TILE, TILE - 1)]),
+        ((after_pair, own_pair), line + [(1, TILE - 1)], [(0, TILE)]),
+        ((far_pair, before_pair, after_pair), line + [(1, 0), (2, TILE - 1)], [(TILE, TILE - 1), (0, TILE + 1)]),
+    )
     sums = ()
-    for stage in range(tiles_x):
-        final = stage == tiles_x - 1
-        blocks = pairs[stage]
-        if stage > 0:
-            blocks = blocks + pairs[stage - 1]
-        if final:
-            blocks = blocks + own_pair
+    for stage, (pairs, strips, borders) in enumerate(stages):
+        blocks = [block for pair in pairs for block in pair]
+        if stage == ROW_STAGES - 1:
             out_shape = (
                 jax.ShapeDtypeStruct((27, width, width), jnp.float32),
                 jax.ShapeDtypeStruct((27, width, width), jnp.bfloat16),
@@ -203,7 +236,7 @@
                 jax.ShapeDtypeStruct((width, width), jnp.float32),
             )
         sums = pl.pallas_call(
-            functools.partial(row_kernel, stage, final),
+            functools.partial(row_kernel, stage, strips, borders),
             out_shape=out_shape,
             in_specs=[smem] + [vmem] * (len(blocks) + len(sums)),
             out_specs=(vmem,) * len(out_shape),
@@ -218,11 +251,6 @@
             cost_estimate=pl.CostEstimate(flops=2 * 10**9, bytes_accessed=4 * 10**6, transcendentals=0),
             name=f"weight_row_{stage}",
         )(here, *blocks, *sums)
-        if stage == 0:
-            for turn in range(1, tiles_x):
-                mine, centre = lax.optimization_barrier((pairs[turn][0], sums[2]))
-                sums = (sums[0], sums[1], centre)
-                pairs[turn] = (mine, lax.ppermute(mine, "brick", across))
     own, sent = sums
     other = lax.ppermute(sent, "batch", [(0, 1), (1, 0)])
     conv_out, feature_grad = pl.pallas_call(
@@ -241,7 +269,7 @@
         compiler_params=params,
         cost_estimate=pl.CostEstimate(flops=10**9, bytes_accessed=4 * 10**6, transcendentals=0),
         name="voxel_outputs",
-    )(here, *own_pair, *pairs[1], *pairs[tiles_x - 1], code, z_val, w_conv)
+    )(here, *own_pair, *before_pair, *after_pair, code, z_val, w_conv)
     weight_grad = own + other.astype(jnp.float32)
     return (conv_out[None], feature_grad[None], weight_grad)
 
@@ -321,7 +349,7 @@
     bits = peers.bit_length() - 1
     tiles_x = 2 ** ((bits + 1) // 2)
     tiles_y = 2 ** (bits // 2)
-    plan = whole_scene if tiles_y == 2 else halo_plan
+    plan = whole_scene if (tiles_x, tiles_y) == (ROW_STAGES, 2) else halo_plan
     return plan(*arrays, tiles_x, tiles_y)
 
 

time: 42.4 us -> 35.9 us (0.85)
  the two profiles are of different devices: /device:TPU:17 before, /device:TPU:0 now
where the time goes in v5:
time: 35.9 us; the launch traced here: 35.5 us
  Pallas kernels  12.4 us (35%)
  starting transfers between devices  11.6 us (32%)
  waiting for transfers between devices  4.85 us (14%)
  local copies, waits for them, and re-layouts  3.85 us (11%)
  other arithmetic  1.45 us (4%)
  between operations  1.37 us (4%)
    pallas_call x4, Pallas kernels, whole_scene(): pl.pallas_call(functools.partial(row_kernel, stage, strips, borders), out...  8.47 us
    ppermute x4, starting transfers between devices, across(): return lax.ppermute(block, 'brick', [(i, i ^ 1) for i in range(peers)])  6.4 us
    ppermute x3, starting transfers between devices, along(): lax.ppermute(block, 'brick', [(i, (i + turn * tiles_y) % peers) for i in...  5.17 us
    ppermute x3, waiting for transfers between devices, along(): lax.ppermute(block, 'brick', [(i, (i + turn * tiles_y) % peers) for i in...  4.84 us
    unnamed x12, local copies, waits for them, and re-layouts  3.85 us
    pallas_call x1, Pallas kernels, whole_scene(): pl.pallas_call(voxel_kernel, out_shape=(jax.ShapeDtypeStruct((rows, width...  3.35 us
    add x1, other arithmetic, whole_scene(): weight_grad = own + other.astype(jnp.float32)  1.45 us
  transfers between devices with their start and end apart: 8, of which 2 were waited for; matrix products, arithmetic and copies ran while one was open for 0% of the time, Pallas kernels for 26%

profile of v5, /device:TPU:0, one launch (start us, length us, event | category | flops | bytes accessed | tf_op | source)
XLA Modules:
  0.0 35.5 jit_solution(1610703768107782413)
XLA Ops:
  1.3 0.0 copy-start
  1.3 0.8 %copy-done = bf16[1,256,128]{2,1,0:T(8,128)(2,1)S(1)} copy-done((bf16[1,256,128]{2,1,0:T(8,128)(2,1)S(1)}, bf16[1,256,128]{2,1,0:T(8,128)(2,1)}, u32[]{:S(2)}) %copy-start) | copy-done | bytes 65560
  2.1 0.0 copy-start.1
  2.1 0.8 %copy-done.1 = bf16[1,256,128]{2,1,0:T(8,128)(2,1)S(1)} copy-done((bf16[1,256,128]{2,1,0:T(8,128)(2,1)S(1)}, bf16[1,256,128]{2,1,0:T(8,128)(2,1)}, u32[]{:S(2)}) %copy-start.1) | copy-done | bytes 65560
  3.0 0.0 copy-start.2
  3.0 0.8 %copy-done.2 = s32[27,256]{1,0:T(8,128)S(1)} copy-done((s32[27,256]{1,0:T(8,128)S(1)}, s32[27,256]{1,0:T(8,128)}, u32[]{:S(2)}) %copy-start.2) | copy-done | bytes 27672
  3.7 0.0 copy-start.3
  3.7 0.8 %copy-done.3 = bf16[128,128]{1,0:T(8,128)(2,1)S(1)} copy-done((bf16[128,128]{1,0:T(8,128)(2,1)S(1)}, bf16[128,128]{1,0:T(8,128)(2,1)}, u32[]{:S(2)}) %copy-start.3) | copy-done | bytes 32792
  4.5 0.0 copy-start.4
  4.5 0.7 %copy-done.4 = bf16[1,128]{1,0:T(2,128)(2,1)S(1)} copy-done((bf16[1,128]{1,0:T(2,128)(2,1)S(1)}, bf16[1,128]{1,0:T(2,128)(2,1)}, u32[]{:S(2)}) %copy-start.4) | copy-done | bytes 280
  5.1 0.6 %pack_tile.1 = (bf16[272,256]{1,0:T(8,128)(2,1)S(1)}, f32[256,128]{1,0:T(8,128)S(1)}, f32[256,27]{1,0:T(8,128)S(1)}) custom-call(s32[1]{0:T(128)S(6)} %copy.10.time_ref, bf16[1,256,128]{2,1,0:T(8,128)(2,1)S(1)} %copy-done, bf16[1,256,128]{2,1,0:T(8,128)(2,1)S(1)} %copy-done.1, s32[27,256]{1,0:T(8,128)S(1)} %copy-done.2, bf16[1,128]{1,0:T(2,128)(2,1)S(1)} %copy-done.4, ...), custom_call_target="tpu_custom_call" | custom-call | tf_op jit(solution)/shard_map/pack_tile/pallas_call | solution.py:184
  5.7 3.1 %collective-permute-start.1 = (bf16[272,256]{1,0:T(8,128)(2,1)S(1)}, bf16[272,256]{1,0:T(8,128)(2,1)S(1)}, u32[]{:S(2)}, u32[]{:S(2)}) collective-permute-start(bf16[272,256]{1,0:T(8,128)(2,1)S(1)} %get-tuple-element.19.mine_ref.refs_1_.refs_3_), channel_id=1, source_target_pairs={{0,4},{2,6},{4,8},{6,10},{8,12},{10,14},{12,0},{14,2},{1,5},{3,7},... | collective-permute-start | bytes 417800 | tf_op jit(solution)/shard_map/ppermute | solution.py:209
  8.8 2.1 %collective-permute-start.3 = (bf16[272,256]{1,0:T(8,128)(2,1)S(1)}, bf16[272,256]{1,0:T(8,128)(2,1)S(1)}, u32[]{:S(2)}, u32[]{:S(2)}) collective-permute-start(bf16[272,256]{1,0:T(8,128)(2,1)S(1)} %get-tuple-element.19.mine_ref.refs_1_.refs_3_), channel_id=1, source_target_pairs={{0,12},{2,14},{4,0},{6,2},{8,4},{10,6},{12,8},{14,10},{1,13},{3,15... | collective-permute-start | bytes 417800 | tf_op jit(solution)/shard_map/ppermute | solution.py:209
  10.9 1.6 %collective-permute-start = (bf16[272,256]{1,0:T(8,128)(2,1)S(1)}, bf16[272,256]{1,0:T(8,128)(2,1)S(1)}, u32[]{:S(2)}, u32[]{:S(2)}) collective-permute-start(bf16[272,256]{1,0:T(8,128)(2,1)S(1)} %get-tuple-element.19.mine_ref.refs_1_.refs_3_), channel_id=1, source_target_pairs={{0,2},{2,0},{4,6},{6,4},{8,10},{10,8},{12,14},{14,12},{1,3},{3,1},... | collective-permute-start | bytes 417800 | tf_op jit(solution)/shard_map/ppermute | solution.py:206
  12.5 2.8 %collective-permute-done.1.before_mine.refs_1_.refs_3_ = bf16[272,256]{1,0:T(8,128)(2,1)S(1)} collective-permute-done((bf16[272,256]{1,0:T(8,128)(2,1)S(1)}, bf16[272,256]{1,0:T(8,128)(2,1)S(1)}, u32[]{:S(2)}, u32[]{:S(2)}) %collective-permute-start.1) | collective-permute-done | bytes 139296 | tf_op jit(solution)/shard_map/ppermute | solution.py:209
  15.3 0.0 collective-permute-start.5
  15.3 1.7 %collective-permute-start.2 = (bf16[272,256]{1,0:T(8,128)(2,1)S(1)}, bf16[272,256]{1,0:T(8,128)(2,1)S(1)}, u32[]{:S(2)}, u32[]{:S(2)}) collective-permute-start(bf16[272,256]{1,0:T(8,128)(2,1)S(1)} %collective-permute-done.1.before_mine.refs_1_.refs_3_), channel_id=1, source_target_pairs={{0,2},{2,0},{4,6},{6,4},{8,10},{10,8},{12,14},{14,12},{1,3},{3,1},... | collective-permute-start | bytes 417800 | tf_op jit(solution)/shard_map/ppermute | solution.py:206
  17.0 0.0 collective-permute-done.3.after_mine.refs_1_.refs_5_
  17.1 1.3 %collective-permute-start.4 = (bf16[272,256]{1,0:T(8,128)(2,1)S(1)}, bf16[272,256]{1,0:T(8,128)(2,1)S(1)}, u32[]{:S(2)}, u32[]{:S(2)}) collective-permute-start(bf16[272,256]{1,0:T(8,128)(2,1)S(1)} %collective-permute-done.3.after_mine.refs_1_.refs_5_), channel_id=1, source_target_pairs={{0,2},{2,0},{4,6},{6,4},{8,10},{10,8},{12,14},{14,12},{1,3},{3,1},... | collective-permute-start | bytes 417800 | tf_op jit(solution)/shard_map/ppermute | solution.py:206
  18.4 0.0 collective-permute-done.other_ref.refs_2_.refs_4_
  18.4 1.8 %weight_row_0.1 = (f32[1664,128]{1,0:T(8,128)S(1)}, f32[1664,128]{1,0:T(8,128)S(1)}, f32[128,128]{1,0:T(8,128)S(1)}) custom-call(s32[1]{0:T(128)} %bitcast.where_ref.refs_0_, bf16[272,256]{1,0:T(8,128)(2,1)S(1)} %get-tuple-element.19.mine_ref.refs_1_.refs_3_, bf16[272,256]{1,0:T(8,128)(2,1)S(1)} %collective-permute-done.other_ref.refs_2_.refs_4_), custom_call_target="tpu_custom_call" | custom-call | flops 2000000000 | bytes 4000000 | tf_op jit(solution)/shard_map/weight_row_0/pallas_call | solution.py:238
  20.2 2.0 %collective-permute-done.5.refs_1_ = bf16[272,256]{1,0:T(8,128)(2,1)S(1)} collective-permute-done((bf16[272,256]{1,0:T(8,128)(2,1)S(1)}, bf16[272,256]{1,0:T(8,128)(2,1)S(1)}, u32[]{:S(2)}, u32[]{:S(2)}) %collective-permute-start.5) | collective-permute-done | bytes 139296 | tf_op jit(solution)/shard_map/ppermute | solution.py:209
  22.2 1.7 %collective-permute-start.6 = (bf16[272,256]{1,0:T(8,128)(2,1)S(1)}, bf16[272,256]{1,0:T(8,128)(2,1)S(1)}, u32[]{:S(2)}, u32[]{:S(2)}) collective-permute-start(bf16[272,256]{1,0:T(8,128)(2,1)S(1)} %collective-permute-done.5.refs_1_), channel_id=1, source_target_pairs={{0,2},{2,0},{4,6},{6,4},{8,10},{10,8},{12,14},{14,12},{1,3},{3,1},... | collective-permute-start | bytes 417800 | tf_op jit(solution)/shard_map/ppermute | solution.py:206
  23.9 0.0 collective-permute-done.2.before_other.refs_2_.refs_4_
  23.9 2.1 %weight_row_1.1 = (f32[1664,128]{1,0:T(8,128)S(1)}, f32[1664,128]{1,0:T(8,128)S(1)}, f32[128,128]{1,0:T(8,128)S(1)}) custom-call(s32[1]{0:T(128)} %bitcast.where_ref.refs_0_, bf16[272,256]{1,0:T(8,128)(2,1)S(1)} %collective-permute-done.1.before_mine.refs_1_.refs_3_, bf16[272,256]{1,0:T(8,128)(2,1)S(1)} %collective-permute-done.2.before_other.refs_2_.refs_4_, ...), custom_call_target="tpu_custom_call" | custom-call | flops 2000000000 | bytes 4000000 | tf_op jit(solution)/shard_map/weight_row_1/pallas_call | solution.py:238
  26.0 0.0 collective-permute-done.4.after_other.refs_2_.refs_6_
  26.0 2.1 %weight_row_2.1 = (f32[1664,128]{1,0:T(8,128)S(1)}, f32[1664,128]{1,0:T(8,128)S(1)}, f32[128,128]{1,0:T(8,128)S(1)}) custom-call(s32[1]{0:T(128)} %bitcast.where_ref.refs_0_, bf16[272,256]{1,0:T(8,128)(2,1)S(1)} %collective-permute-done.3.after_mine.refs_1_.refs_5_, bf16[272,256]{1,0:T(8,128)(2,1)S(1)} %collective-permute-done.4.after_other.refs_2_.refs_6_, ...), custom_call_target="tpu_custom_call" | custom-call | flops 2000000000 | bytes 4000000 | tf_op jit(solution)/shard_map/weight_row_2/pallas_call | solution.py:238
  28.1 0.0 collective-permute-done.6.refs_2_
  28.1 0.0 copy-start.5
  28.1 2.5 %weight_row_3.1 = (f32[27,128,128]{2,1,0:T(8,128)S(1)}, bf16[27,128,128]{2,1,0:T(8,128)(2,1)S(1)}) custom-call(s32[1]{0:T(128)} %bitcast.where_ref.refs_0_, bf16[272,256]{1,0:T(8,128)(2,1)S(1)} %collective-permute-done.5.refs_1_, bf16[272,256]{1,0:T(8,128)(2,1)S(1)} %collective-permute-done.6.refs_2_, ...), custom_call_target="tpu_custom_call" | custom-call | flops 2000000000 | bytes 4000000 | tf_op jit(solution)/shard_map/weight_row_3/pallas_call | solution.py:238
  30.7 0.1 collective-permute-start.7
  30.7 0.0 copy-done.5
  30.7 3.4 %voxel_outputs.1 = (bf16[256,128]{1,0:T(8,128)(2,1)}, bf16[256,128]{1,0:T(8,128)(2,1)}) custom-call(s32[1]{0:T(128)} %bitcast.where_ref.refs_0_, bf16[272,256]{1,0:T(8,128)(2,1)S(1)} %get-tuple-element.19.mine_ref.refs_1_.refs_3_, bf16[272,256]{1,0:T(8,128)(2,1)S(1)} %collective-permute-done.other_ref.refs_2_.refs_4_, ...), custom_call_target="tpu_custom_call" | custom-call | flops 1000000000 | bytes 4000000 | tf_op jit(solution)/shard_map/voxel_outputs/pallas_call | solution.py:256
  34.1 0.0 collective-permute-done.7
  34.1 1.4 %convert_add_fusion = f32[27,128,128]{2,1,0:T(8,128)} fusion(f32[27,128,128]{2,1,0:T(8,128)S(1)} %get-tuple-element.33, bf16[27,128,128]{2,1,0:T(8,128)(2,1)S(1)} %collective-permute-done.7), kind=kLoop, calls=%fused_computation | loop fusion | flops 884736 | bytes 4423680 | tf_op jit(solution)/shard_map/add | solution.py:273
Async XLA Ops:
  1.3 0.8 %copy-start = (bf16[1,256,128]{2,1,0:T(8,128)(2,1)S(1)}, bf16[1,256,128]{2,1,0:T(8,128)(2,1)}, u32[]{:S(2)}) copy-start(bf16[1,256,128]{2,1,0:T(8,128)(2,1)} %feat_hbm.1) | copy-start | bytes 196612
  2.1 0.8 %copy-start.1 = (bf16[1,256,128]{2,1,0:T(8,128)(2,1)S(1)}, bf16[1,256,128]{2,1,0:T(8,128)(2,1)}, u32[]{:S(2)}) copy-start(bf16[1,256,128]{2,1,0:T(8,128)(2,1)} %cot_hbm.1) | copy-start | bytes 196612
  3.0 0.8 %copy-start.2 = (s32[27,256]{1,0:T(8,128)S(1)}, s32[27,256]{1,0:T(8,128)}, u32[]{:S(2)}) copy-start(s32[27,256]{1,0:T(8,128)} %near_hbm.1) | copy-start | bytes 82948
  3.7 0.8 %copy-start.3 = (bf16[128,128]{1,0:T(8,128)(2,1)S(1)}, bf16[128,128]{1,0:T(8,128)(2,1)}, u32[]{:S(2)}) copy-start(bf16[128,128]{1,0:T(8,128)(2,1)} %wt_hbm.1) | copy-start | bytes 98308
  4.5 0.7 %copy-start.4 = (bf16[1,128]{1,0:T(2,128)(2,1)S(1)}, bf16[1,128]{1,0:T(2,128)(2,1)}, u32[]{:S(2)}) copy-start(bf16[1,128]{1,0:T(2,128)(2,1)} %cond_hbm.1) | copy-start | bytes 772
  5.7 9.6 %collective-permute-start.1 = (bf16[272,256]{1,0:T(8,128)(2,1)S(1)}, bf16[272,256]{1,0:T(8,128)(2,1)S(1)}, u32[]{:S(2)}, u32[]{:S(2)}) collective-permute-start(bf16[272,256]{1,0:T(8,128)(2,1)S(1)} %get-tuple-element.19.mine_ref.refs_1_.refs_3_), channel_id=1, source_target_pairs={{0,4},{2,6},{4,8},{6,10},{8,12},{10,14},{12,0},{14,2},{1,5},{3,7},... | collective-permute-start | bytes 417800 | tf_op jit(solution)/shard_map/ppermute | solution.py:209
  8.8 8.3 %collective-permute-start.3 = (bf16[272,256]{1,0:T(8,128)(2,1)S(1)}, bf16[272,256]{1,0:T(8,128)(2,1)S(1)}, u32[]{:S(2)}, u32[]{:S(2)}) collective-permute-start(bf16[272,256]{1,0:T(8,128)(2,1)S(1)} %get-tuple-element.19.mine_ref.refs_1_.refs_3_), channel_id=1, source_target_pairs={{0,12},{2,14},{4,0},{6,2},{8,4},{10,6},{12,8},{14,10},{1,13},{3,15... | collective-permute-start | bytes 417800 | tf_op jit(solution)/shard_map/ppermute | solution.py:209
  10.9 7.5 %collective-permute-start = (bf16[272,256]{1,0:T(8,128)(2,1)S(1)}, bf16[272,256]{1,0:T(8,128)(2,1)S(1)}, u32[]{:S(2)}, u32[]{:S(2)}) collective-permute-start(bf16[272,256]{1,0:T(8,128)(2,1)S(1)} %get-tuple-element.19.mine_ref.refs_1_.refs_3_), channel_id=1, source_target_pairs={{0,2},{2,0},{4,6},{6,4},{8,10},{10,8},{12,14},{14,12},{1,3},{3,1},... | collective-permute-start | bytes 417800 | tf_op jit(solution)/shard_map/ppermute | solution.py:206
  15.3 6.9 %collective-permute-start.5 = (bf16[272,256]{1,0:T(8,128)(2,1)S(1)}, bf16[272,256]{1,0:T(8,128)(2,1)S(1)}, u32[]{:S(2)}, u32[]{:S(2)}) collective-permute-start(bf16[272,256]{1,0:T(8,128)(2,1)S(1)} %collective-permute-done.1.before_mine.refs_1_.refs_3_), channel_id=1, source_target_pairs={{0,4},{2,6},{4,8},{6,10},{8,12},{10,14},{12,0},{14,2},{1,5},{3,7},... | collective-permute-start | bytes 417800 | tf_op jit(solution)/shard_map/ppermute | solution.py:209
  15.3 8.6 %collective-permute-start.2 = (bf16[272,256]{1,0:T(8,128)(2,1)S(1)}, bf16[272,256]{1,0:T(8,128)(2,1)S(1)}, u32[]{:S(2)}, u32[]{:S(2)}) collective-permute-start(bf16[272,256]{1,0:T(8,128)(2,1)S(1)} %collective-permute-done.1.before_mine.refs_1_.refs_3_), channel_id=1, source_target_pairs={{0,2},{2,0},{4,6},{6,4},{8,10},{10,8},{12,14},{14,12},{1,3},{3,1},... | collective-permute-start | bytes 417800 | tf_op jit(solution)/shard_map/ppermute | solution.py:206
  17.1 8.9 %collective-permute-start.4 = (bf16[272,256]{1,0:T(8,128)(2,1)S(1)}, bf16[272,256]{1,0:T(8,128)(2,1)S(1)}, u32[]{:S(2)}, u32[]{:S(2)}) collective-permute-start(bf16[272,256]{1,0:T(8,128)(2,1)S(1)} %collective-permute-done.3.after_mine.refs_1_.refs_5_), channel_id=1, source_target_pairs={{0,2},{2,0},{4,6},{6,4},{8,10},{10,8},{12,14},{14,12},{1,3},{3,1},... | collective-permute-start | bytes 417800 | tf_op jit(solution)/shard_map/ppermute | solution.py:206
  22.2 5.9 %collective-permute-start.6 = (bf16[272,256]{1,0:T(8,128)(2,1)S(1)}, bf16[272,256]{1,0:T(8,128)(2,1)S(1)}, u32[]{:S(2)}, u32[]{:S(2)}) collective-permute-start(bf16[272,256]{1,0:T(8,128)(2,1)S(1)} %collective-permute-done.5.refs_1_), channel_id=1, source_target_pairs={{0,2},{2,0},{4,6},{6,4},{8,10},{10,8},{12,14},{14,12},{1,3},{3,1},... | collective-permute-start | bytes 417800 | tf_op jit(solution)/shard_map/ppermute | solution.py:206
  28.1 2.6 %copy-start.5 = (bf16[27,128,128]{2,1,0:T(8,128)(2,1)S(1)}, bf16[27,128,128]{2,1,0:T(8,128)(2,1)}, u32[]{:S(2)}) copy-start(bf16[27,128,128]{2,1,0:T(8,128)(2,1)} %w_ref.1) | copy-start | bytes 2654212
  30.7 3.4 %collective-permute-start.7 = (bf16[27,128,128]{2,1,0:T(8,128)(2,1)S(1)}, bf16[27,128,128]{2,1,0:T(8,128)(2,1)S(1)}, u32[]{:S(2)}, u32[]{:S(2)}) collective-permute-start(bf16[27,128,128]{2,1,0:T(8,128)(2,1)S(1)} %get-tuple-element.34), channel_id=1, source_target_pairs={{0,1},{1,0},{2,3},{3,2},{4,5},{5,4},{6,7},{7,6},{8,9},{9,8},{10,11... | collective-permute-start | bytes 2654216 | tf_op jit(solution)/shard_map/ppermute | solution.py:255

commit v6 on v5

--- a/solution.py
+++ b/solution.py
@@ -14,7 +14,6 @@
 CODE_ROWS = 16
 ROW_STAGES = 4
 KERNEL_VMEM = 24 * 1024 * 1024
-PACK_VMEM = 4 * 1024 * 1024
 
 
 def time_embedding(timesteps, width):
@@ -30,7 +29,7 @@
     return jnp.where(neighbours < 0, -1, code).astype(jnp.float32)
 
 
-def pack_kernel(time_ref, feat_hbm, cot_hbm, near_hbm, cond_hbm, wt_hbm, pack_ref, z_ref, code_ref,
+def pack_kernel(time_ref, feat_hbm, cot_hbm, near_hbm, cond_hbm, wt_hbm, pack_ref, shift_ref,
                 feat_ref, near_ref, cond_ref, wt_ref, sems):
     rows, width = feat_ref.shape
     half = width // 2
@@ -54,12 +53,10 @@
     shift = shift + cond_ref[...].astype(jnp.float32)
     copies[2].wait()
     z_val = feat_ref[...].astype(jnp.float32) + shift
-    z_ref[...] = z_val
+    shift_ref[...] = shift
     pack_ref[:rows, :width] = (z_val * jax.nn.sigmoid(z_val)).astype(jnp.bfloat16)
     copies[3].wait()
-    code = strip_codes(near_ref[...], 2)
-    code_ref[...] = code.T
-    pack_ref[rows:, :] = code[:CODE_ROWS, :].astype(jnp.bfloat16)
+    pack_ref[rows:, :] = strip_codes(near_ref[:CODE_ROWS, :], 2).astype(jnp.bfloat16)
     copies[4].wait()
 
 
@@ -141,35 +138,45 @@
         outs[2][...] = centre
 
 
+def turn_kernel(w_ref, forward_ref, back_ref):
+    width = w_ref.shape[1]
+    for k in range(27):
+        forward_ref[:, k * width:(k + 1) * width] = w_ref[k].T
+        back_ref[:, k * width:(k + 1) * width] = w_ref[26 - k]
+
+
 def voxel_kernel(where_ref, mine_ref, other_ref, before_mine, before_other, after_mine, after_other,
-                 code_ref, z_ref, w_ref, conv_ref, grad_ref, ground, near_act, near_cot, w_back):
-    rows, width = z_ref.shape
+                 near_ref, feat_ref, shift_ref, forward_ref, back_ref, conv_ref, grad_ref,
+                 ground, turned, codes, near_act, near_cot):
+    width = feat_ref.shape[1]
     span = 2 * STRIP
     tile_y = where_ref[0] % 2
     lay_strip(ground, 0, tile_y, before_mine, before_other, TILE - 1)
     for u in range(TILE):
         lay_strip(ground, u + 1, tile_y, mine_ref, other_ref, u)
     lay_strip(ground, TILE + 1, tile_y, after_mine, after_other, 0)
-    place = lax.broadcasted_iota(jnp.int32, (STRIP, span), 1).astype(jnp.float32)
-    for u in range(TILE):
-        here = u * STRIP
-        code = code_ref[here:here + STRIP, :]
+    for i in range(TILE + 2):
+        turned[:, i * span:(i + 1) * span] = ground[i * span:(i + 1) * span, :].T
+    code = strip_codes(near_ref[...], 2)
+    lane = lax.broadcasted_iota(jnp.int32, code.shape, 1)
+    codes[...] = jnp.where((code >= 0) & (lane // STRIP % 2 == 1), code + span, code)
+    place = lax.broadcasted_iota(jnp.int32, (2 * span, span), 0).astype(jnp.float32)
+    for half in range(TILE // 2):
+        at = half * span
         for side in range(3):
-            block = ground[(u + side) * span:(u + side + 1) * span, :]
+            source = (2 * half + side) * span
             ks = range(9 * side, 9 * side + 9)
-            picks = [(code[:, k:k + 1] == place).astype(jnp.bfloat16) for k in ks]
-            near = jnp.dot(jnp.concatenate(picks, axis=0), block, preferred_element_type=jnp.float32)
-            near = near.astype(jnp.bfloat16)
+            picks = [(place == codes[k:k + 1, at:at + span]).astype(jnp.bfloat16) for k in ks]
+            near = jnp.dot(turned[:, source:source + 2 * span], jnp.concatenate(picks, axis=1),
+                           preferred_element_type=jnp.float32).astype(jnp.bfloat16)
             for k in ks:
-                rows_k = near[(k - 9 * side) * STRIP:(k - 9 * side + 1) * STRIP, :]
-                near_act[here:here + STRIP, k * width:(k + 1) * width] = rows_k[:, :width]
-                near_cot[here:here + STRIP, k * width:(k + 1) * width] = rows_k[:, width:]
-    for k in range(27):
-        w_back[:, k * width:(k + 1) * width] = w_ref[26 - k]
-    conv = jnp.dot(near_act[...], w_ref[...].reshape(27 * width, width), preferred_element_type=jnp.float32)
-    conv_ref[...] = conv.astype(jnp.bfloat16)
-    back = lax.dot_general(near_cot[...], w_back[...], (((1,), (1,)), ((), ())), preferred_element_type=jnp.float32)
-    z_val = z_ref[...]
+                one = near[:, (k - 9 * side) * span:(k - 9 * side + 1) * span]
+                near_act[k * width:(k + 1) * width, at:at + span] = one[:width]
+                near_cot[k * width:(k + 1) * width, at:at + span] = one[width:]
+    conv = jnp.dot(forward_ref[...], near_act[...], preferred_element_type=jnp.float32)
+    conv_ref[...] = conv.T.astype(jnp.bfloat16)
+    back = jnp.dot(back_ref[...], near_cot[...], preferred_element_type=jnp.float32).T
+    z_val = feat_ref[...].astype(jnp.float32) + shift_ref[...]
     sig = jax.nn.sigmoid(z_val)
     grad_ref[...] = (back * sig * (1.0 + z_val * (1.0 - sig))).astype(jnp.bfloat16)
 
@@ -181,15 +188,14 @@
     vmem = pl.BlockSpec(memory_space=pltpu.VMEM)
     smem = pl.BlockSpec(memory_space=pltpu.SMEM)
     params = pltpu.CompilerParams(vmem_limit_bytes=KERNEL_VMEM)
-    packed, z_val, code = pl.pallas_call(
+    packed, shift = pl.pallas_call(
         pack_kernel,
         out_shape=(
             jax.ShapeDtypeStruct((rows + CODE_ROWS, 2 * width), jnp.bfloat16),
-            jax.ShapeDtypeStruct((rows, width), jnp.float32),
-            jax.ShapeDtypeStruct((rows, 27), jnp.float32),
+            jax.ShapeDtypeStruct((1, width), jnp.float32),
         ),
         in_specs=[smem] + [pl.BlockSpec(memory_space=pltpu.HBM)] * 5,
-        out_specs=(vmem, vmem, vmem),
+        out_specs=(vmem, vmem),
         scratch_shapes=[
             pltpu.VMEM((rows, width), jnp.bfloat16),
             pltpu.VMEM(neighbours.shape, jnp.int32),
@@ -197,7 +203,6 @@
             pltpu.VMEM((width, width), jnp.bfloat16),
             pltpu.SemaphoreType.DMA((5,)),
         ],
-        compiler_params=pltpu.CompilerParams(vmem_limit_bytes=PACK_VMEM),
         name="pack_tile",
     )(timesteps, features, cotangent, neighbours, condition, w_time)
     here = lax.axis_index("brick").astype(jnp.int32).reshape(1)
@@ -208,7 +213,18 @@
     def along(block, turn):
         return lax.ppermute(block, "brick", [(i, (i + turn * tiles_y) % peers) for i in range(peers)])
 
+    w_conv, packed = lax.optimization_barrier((w_conv, packed))
+    w_forward, w_back = pl.pallas_call(
+        turn_kernel,
+        out_shape=(jax.ShapeDtypeStruct((width, 27 * width), jnp.bfloat16),) * 2,
+        in_specs=[vmem],
+        out_specs=(vmem, vmem),
+        compiler_params=params,
+        cost_estimate=pl.CostEstimate(flops=2 * 10**8, bytes_accessed=3 * 10**6, transcendentals=0),
+        name="turn_weights",
+    )(w_conv)
     before, after = along(packed, 1), along(packed, -1)
+    before, w_forward = lax.optimization_barrier((before, w_forward))
     far = along(before, 1)
     own_pair = (packed, across(packed))
     before_pair = (before, across(before))
@@ -259,17 +275,18 @@
             jax.ShapeDtypeStruct((rows, width), jnp.bfloat16),
             jax.ShapeDtypeStruct((rows, width), jnp.bfloat16),
         ),
-        in_specs=[smem] + [vmem] * 9,
+        in_specs=[smem] + [vmem] * 11,
         scratch_shapes=[
             pltpu.VMEM(((TILE + 2) * span, 2 * width), jnp.bfloat16),
-            pltpu.VMEM((rows, 27 * width), jnp.bfloat16),
-            pltpu.VMEM((rows, 27 * width), jnp.bfloat16),
-            pltpu.VMEM((width, 27 * width), jnp.bfloat16),
+            pltpu.VMEM((2 * width, (TILE + 2) * span), jnp.bfloat16),
+            pltpu.VMEM((27, rows), jnp.float32),
+            pltpu.VMEM((27 * width, rows), jnp.bfloat16),
+            pltpu.VMEM((27 * width, rows), jnp.bfloat16),
         ],
         compiler_params=params,
         cost_estimate=pl.CostEstimate(flops=10**9, bytes_accessed=4 * 10**6, transcendentals=0),
         name="voxel_outputs",
-    )(here, *own_pair, *before_pair, *after_pair, code, z_val, w_conv)
+    )(here, *own_pair, *before_pair, *after_pair, neighbours, features[0], shift, w_forward, w_back)
     weight_grad = own + other.astype(jnp.float32)
     return (conv_out[None], feature_grad[None], weight_grad)
 

time: 35.9 us -> 32.6 us (0.908)
  waiting for transfers between devices: 4.85 us -> 2.62 us
  local copies, waits for them, and re-layouts: 3.85 us -> 2.1 us
  Pallas kernels: 12.4 us -> 13.2 us
    ppermute x3, waiting for transfers between devices: 4.84 us -> 2.6 us  [along(): lax.ppermute(block, 'brick', [(i, (i + turn * tiles_y) % peers) for i in...]
    unnamed x12, local copies, waits for them, and re-layouts: 3.85 us -> 2.1 us
    pallas_call x1, Pallas kernels: 0.56 us -> 1.66 us  [whole_scene(): pl.pallas_call(pack_kernel, out_shape=(jax.ShapeDtypeStruct((rows + CODE_...]
    pallas_call x1, Pallas kernels: 3.35 us -> 2.66 us  [whole_scene(): pl.pallas_call(voxel_kernel, out_shape=(jax.ShapeDtypeStruct((rows, width...]
    pallas_call x0 -> x1, Pallas kernels: none -> 0.37 us  [whole_scene(): pl.pallas_call(turn_kernel, out_shape=(jax.ShapeDtypeStruct((width, 27 *...]
  transfers between devices with their start and end apart: 8 -> 8, of which waited for: 2 -> 2; matrix products, arithmetic and copies ran while one was open for 0% -> 0% of each run, Pallas kernels for 26% -> 28%
where the time goes in v6:
time: 32.6 us; the launch traced here: 32.3 us
  Pallas kernels  13.2 us (40%)
  starting transfers between devices  11.6 us (36%)
  waiting for transfers between devices  2.62 us (8%)
  local copies, waits for them, and re-layouts  2.1 us (6%)
  other arithmetic  1.42 us (4%)
  between operations  1.41 us (4%)
    pallas_call x4, Pallas kernels, whole_scene(): pl.pallas_call(functools.partial(row_kernel, stage, strips, borders), out...  8.47 us
    ppermute x4, starting transfers between devices, across(): return lax.ppermute(block, 'brick', [(i, i ^ 1) for i in range(peers)])  6.41 us
    ppermute x3, starting transfers between devices, along(): lax.ppermute(block, 'brick', [(i, (i + turn * tiles_y) % peers) for i in...  5.17 us
    pallas_call x1, Pallas kernels, whole_scene(): pl.pallas_call(voxel_kernel, out_shape=(jax.ShapeDtypeStruct((rows, width...  2.66 us
    ppermute x3, waiting for transfers between devices, along(): lax.ppermute(block, 'brick', [(i, (i + turn * tiles_y) % peers) for i in...  2.6 us
    unnamed x12, local copies, waits for them, and re-layouts  2.1 us
    pallas_call x1, Pallas kernels, whole_scene(): pl.pallas_call(pack_kernel, out_shape=(jax.ShapeDtypeStruct((rows + CODE_...  1.66 us
    add x1, other arithmetic, whole_scene(): weight_grad = own + other.astype(jnp.float32)  1.42 us
  transfers between devices with their start and end apart: 8, of which 2 were waited for; matrix products, arithmetic and copies ran while one was open for 0% of the time, Pallas kernels for 28%

profile of v6, /device:TPU:0, one launch (start us, length us, event | category | flops | bytes accessed | tf_op | source)
XLA Modules:
  0.0 32.3 jit_solution(826432514897155191)
XLA Ops:
  1.3 1.7 %pack_tile.1 = (bf16[272,256]{1,0:T(8,128)(2,1)}, f32[1,128]{1,0:T(1,128)}) custom-call(s32[1]{0:T(128)S(6)} %copy.10.time_ref, bf16[1,256,128]{2,1,0:T(8,128)(2,1)} %feat_hbm.1, bf16[1,256,128]{2,1,0:T(8,128)(2,1)} %cot_hbm.1, s32[27,256]{1,0:T(8,128)} %near_ref.1, bf16[1,128]{1,0:T(2,128)(2,1)} %cond_hbm.1, bf16[128,128]{1,0:T(8,128)(2,1)} %wt_hbm.1), custom_call_target="tpu_custom_call" | custom-call | tf_op jit(solution)/shard_map/pack_tile/pallas_call | solution.py:191
  2.9 3.1 %collective-permute-start.1 = (bf16[272,256]{1,0:T(8,128)(2,1)}, bf16[272,256]{1,0:T(8,128)(2,1)S(1)}, u32[]{:S(2)}, u32[]{:S(2)}) collective-permute-start(bf16[272,256]{1,0:T(8,128)(2,1)} %get-tuple-element.25.mine_ref.refs_1_.refs_3_), channel_id=1, source_target_pairs={{0,4},{2,6},{4,8},{6,10},{8,12},{10,14},{12,0},{14,2},{1,5},{3,7},... | collective-permute-start | bytes 417800 | tf_op jit(solution)/shard_map/ppermute | solution.py:214
  6.0 2.1 %collective-permute-start.3 = (bf16[272,256]{1,0:T(8,128)(2,1)}, bf16[272,256]{1,0:T(8,128)(2,1)S(1)}, u32[]{:S(2)}, u32[]{:S(2)}) collective-permute-start(bf16[272,256]{1,0:T(8,128)(2,1)} %get-tuple-element.25.mine_ref.refs_1_.refs_3_), channel_id=1, source_target_pairs={{0,12},{2,14},{4,0},{6,2},{8,4},{10,6},{12,8},{14,10},{1,13},{3,15... | collective-permute-start | bytes 417800 | tf_op jit(solution)/shard_map/ppermute | solution.py:214
  8.1 1.6 %collective-permute-start = (bf16[272,256]{1,0:T(8,128)(2,1)}, bf16[272,256]{1,0:T(8,128)(2,1)S(1)}, u32[]{:S(2)}, u32[]{:S(2)}) collective-permute-start(bf16[272,256]{1,0:T(8,128)(2,1)} %get-tuple-element.25.mine_ref.refs_1_.refs_3_), channel_id=1, source_target_pairs={{0,2},{2,0},{4,6},{6,4},{8,10},{10,8},{12,14},{14,12},{1,3},{3,1},... | collective-permute-start | bytes 417800 | tf_op jit(solution)/shard_map/ppermute | solution.py:211
  9.8 0.0 copy-start
  9.8 1.2 %copy-done = bf16[27,128,128]{2,1,0:T(8,128)(2,1)S(1)} copy-done((bf16[27,128,128]{2,1,0:T(8,128)(2,1)S(1)}, bf16[27,128,128]{2,1,0:T(8,128)(2,1)}, u32[]{:S(2)}) %copy-start) | copy-done | bytes 884760
  10.9 0.4 %turn_weights.1 = (bf16[128,3456]{1,0:T(8,128)(2,1)S(1)}, bf16[128,3456]{1,0:T(8,128)(2,1)S(1)}) custom-call(bf16[27,128,128]{2,1,0:T(8,128)(2,1)S(1)} %copy-done), custom_call_target="tpu_custom_call" | custom-call | flops 200000000 | bytes 3000000 | tf_op jit(solution)/shard_map/turn_weights/pallas_call | solution.py:217
  11.3 1.5 %collective-permute-done.1.before_mine.refs_1_.refs_3_ = bf16[272,256]{1,0:T(8,128)(2,1)S(1)} collective-permute-done((bf16[272,256]{1,0:T(8,128)(2,1)}, bf16[272,256]{1,0:T(8,128)(2,1)S(1)}, u32[]{:S(2)}, u32[]{:S(2)}) %collective-permute-start.1) | collective-permute-done | bytes 139296 | tf_op jit(solution)/shard_map/ppermute | solution.py:214
  12.8 0.0 collective-permute-start.5
  12.8 1.7 %collective-permute-start.2 = (bf16[272,256]{1,0:T(8,128)(2,1)S(1)}, bf16[272,256]{1,0:T(8,128)(2,1)S(1)}, u32[]{:S(2)}, u32[]{:S(2)}) collective-permute-start(bf16[272,256]{1,0:T(8,128)(2,1)S(1)} %collective-permute-done.1.before_mine.refs_1_.refs_3_), channel_id=1, source_target_pairs={{0,2},{2,0},{4,6},{6,4},{8,10},{10,8},{12,14},{14,12},{1,3},{3,1},... | collective-permute-start | bytes 417800 | tf_op jit(solution)/shard_map/ppermute | solution.py:211
  14.5 0.0 collective-permute-done.3.after_mine.refs_1_.refs_5_
  14.5 1.3 %collective-permute-start.4 = (bf16[272,256]{1,0:T(8,128)(2,1)S(1)}, bf16[272,256]{1,0:T(8,128)(2,1)S(1)}, u32[]{:S(2)}, u32[]{:S(2)}) collective-permute-start(bf16[272,256]{1,0:T(8,128)(2,1)S(1)} %collective-permute-done.3.after_mine.refs_1_.refs_5_), channel_id=1, source_target_pairs={{0,2},{2,0},{4,6},{6,4},{8,10},{10,8},{12,14},{14,12},{1,3},{3,1},... | collective-permute-start | bytes 417800 | tf_op jit(solution)/shard_map/ppermute | solution.py:211
  15.8 0.0 collective-permute-done.other_ref.refs_2_.refs_4_
  15.8 0.0 copy-start.3
  15.8 0.9 %copy-done.3 = bf16[272,256]{1,0:T(8,128)(2,1)S(1)} copy-done((bf16[272,256]{1,0:T(8,128)(2,1)S(1)}, bf16[272,256]{1,0:T(8,128)(2,1)}, u32[]{:S(2)}) %copy-start.3) | copy-done | bytes 139288
  16.8 1.8 %weight_row_0.1 = (f32[1664,128]{1,0:T(8,128)S(1)}, f32[1664,128]{1,0:T(8,128)S(1)}, f32[128,128]{1,0:T(8,128)S(1)}) custom-call(s32[1]{0:T(128)} %bitcast.where_ref.refs_0_, bf16[272,256]{1,0:T(8,128)(2,1)S(1)} %copy-done.3, bf16[272,256]{1,0:T(8,128)(2,1)S(1)} %collective-permute-done.other_ref.refs_2_.refs_4_), custom_call_target="tpu_custom_call" | custom-call | flops 2000000000 | bytes 4000000 | tf_op jit(solution)/shard_map/weight_row_0/pallas_call | solution.py:254
  18.5 1.1 %collective-permute-done.5.refs_1_ = bf16[272,256]{1,0:T(8,128)(2,1)S(1)} collective-permute-done((bf16[272,256]{1,0:T(8,128)(2,1)S(1)}, bf16[272,256]{1,0:T(8,128)(2,1)S(1)}, u32[]{:S(2)}, u32[]{:S(2)}) %collective-permute-start.5) | collective-permute-done | bytes 139296 | tf_op jit(solution)/shard_map/ppermute | solution.py:214
  19.6 1.7 %collective-permute-start.6 = (bf16[272,256]{1,0:T(8,128)(2,1)S(1)}, bf16[272,256]{1,0:T(8,128)(2,1)S(1)}, u32[]{:S(2)}, u32[]{:S(2)}) collective-permute-start(bf16[272,256]{1,0:T(8,128)(2,1)S(1)} %collective-permute-done.5.refs_1_), channel_id=1, source_target_pairs={{0,2},{2,0},{4,6},{6,4},{8,10},{10,8},{12,14},{14,12},{1,3},{3,1},... | collective-permute-start | bytes 417800 | tf_op jit(solution)/shard_map/ppermute | solution.py:211
  21.4 0.0 collective-permute-done.2.before_other.refs_2_.refs_4_
  21.4 2.1 %weight_row_1.1 = (f32[1664,128]{1,0:T(8,128)S(1)}, f32[1664,128]{1,0:T(8,128)S(1)}, f32[128,128]{1,0:T(8,128)S(1)}) custom-call(s32[1]{0:T(128)} %bitcast.where_ref.refs_0_, bf16[272,256]{1,0:T(8,128)(2,1)S(1)} %collective-permute-done.1.before_mine.refs_1_.refs_3_, bf16[272,256]{1,0:T(8,128)(2,1)S(1)} %collective-permute-done.2.before_other.refs_2_.refs_4_, ...), custom_call_target="tpu_custom_call" | custom-call | flops 2000000000 | bytes 4000000 | tf_op jit(solution)/shard_map/weight_row_1/pallas_call | solution.py:254
  23.4 0.0 collective-permute-done.4.after_other.refs_2_.refs_6_
  23.5 2.1 %weight_row_2.1 = (f32[1664,128]{1,0:T(8,128)S(1)}, f32[1664,128]{1,0:T(8,128)S(1)}, f32[128,128]{1,0:T(8,128)S(1)}) custom-call(s32[1]{0:T(128)} %bitcast.where_ref.refs_0_, bf16[272,256]{1,0:T(8,128)(2,1)S(1)} %collective-permute-done.3.after_mine.refs_1_.refs_5_, bf16[272,256]{1,0:T(8,128)(2,1)S(1)} %collective-permute-done.4.after_other.refs_2_.refs_6_, ...), custom_call_target="tpu_custom_call" | custom-call | flops 2000000000 | bytes 4000000 | tf_op jit(solution)/shard_map/weight_row_2/pallas_call | solution.py:254
  25.6 0.0 collective-permute-done.6.refs_2_
  25.6 0.0 copy-start.1
  25.6 0.0 copy-start.2
  25.6 0.0 copy-start.4
  25.6 0.0 copy-start.5
  25.6 2.5 %weight_row_3.1 = (f32[27,128,128]{2,1,0:T(8,128)S(1)}, bf16[27,128,128]{2,1,0:T(8,128)(2,1)S(1)}) custom-call(s32[1]{0:T(128)} %bitcast.where_ref.refs_0_, bf16[272,256]{1,0:T(8,128)(2,1)S(1)} %collective-permute-done.5.refs_1_, bf16[272,256]{1,0:T(8,128)(2,1)S(1)} %collective-permute-done.6.refs_2_, ...), custom_call_target="tpu_custom_call" | custom-call | flops 2000000000 | bytes 4000000 | tf_op jit(solution)/shard_map/weight_row_3/pallas_call | solution.py:254
  28.1 0.1 collective-permute-start.7
  28.2 0.0 copy-done.1
  28.2 0.0 copy-done.2
  28.2 0.0 copy-done.4
  28.3 0.0 copy-done.5
  28.3 2.7 %voxel_outputs.1 = (bf16[256,128]{1,0:T(8,128)(2,1)}, bf16[256,128]{1,0:T(8,128)(2,1)}) custom-call(s32[1]{0:T(128)} %bitcast.where_ref.refs_0_, bf16[272,256]{1,0:T(8,128)(2,1)S(1)} %copy-done.4, bf16[272,256]{1,0:T(8,128)(2,1)S(1)} %collective-permute-done.other_ref.refs_2_.refs_4_, ...), custom_call_target="tpu_custom_call" | custom-call | flops 1000000000 | bytes 4000000 | tf_op jit(solution)/shard_map/voxel_outputs/pallas_call | solution.py:272
  30.9 0.0 collective-permute-done.7
  30.9 1.4 %convert_add_fusion = f32[27,128,128]{2,1,0:T(8,128)} fusion(f32[27,128,128]{2,1,0:T(8,128)S(1)} %get-tuple-element.43, bf16[27,128,128]{2,1,0:T(8,128)(2,1)S(1)} %collective-permute-done.7), kind=kLoop, calls=%fused_computation | loop fusion | flops 884736 | bytes 4423680 | tf_op jit(solution)/shard_map/add | solution.py:290
Async XLA Ops:
  2.9 9.8 %collective-permute-start.1 = (bf16[272,256]{1,0:T(8,128)(2,1)}, bf16[272,256]{1,0:T(8,128)(2,1)S(1)}, u32[]{:S(2)}, u32[]{:S(2)}) collective-permute-start(bf16[272,256]{1,0:T(8,128)(2,1)} %get-tuple-element.25.mine_ref.refs_1_.refs_3_), channel_id=1, source_target_pairs={{0,4},{2,6},{4,8},{6,10},{8,12},{10,14},{12,0},{14,2},{1,5},{3,7},... | collective-permute-start | bytes 417800 | tf_op jit(solution)/shard_map/ppermute | solution.py:214
  6.0 8.5 %collective-permute-start.3 = (bf16[272,256]{1,0:T(8,128)(2,1)}, bf16[272,256]{1,0:T(8,128)(2,1)S(1)}, u32[]{:S(2)}, u32[]{:S(2)}) collective-permute-start(bf16[272,256]{1,0:T(8,128)(2,1)} %get-tuple-element.25.mine_ref.refs_1_.refs_3_), channel_id=1, source_target_pairs={{0,12},{2,14},{4,0},{6,2},{8,4},{10,6},{12,8},{14,10},{1,13},{3,15... | collective-permute-start | bytes 417800 | tf_op jit(solution)/shard_map/ppermute | solution.py:214
  8.1 7.7 %collective-permute-start = (bf16[272,256]{1,0:T(8,128)(2,1)}, bf16[272,256]{1,0:T(8,128)(2,1)S(1)}, u32[]{:S(2)}, u32[]{:S(2)}) collective-permute-start(bf16[272,256]{1,0:T(8,128)(2,1)} %get-tuple-element.25.mine_ref.refs_1_.refs_3_), channel_id=1, source_target_pairs={{0,2},{2,0},{4,6},{6,4},{8,10},{10,8},{12,14},{14,12},{1,3},{3,1},... | collective-permute-start | bytes 417800 | tf_op jit(solution)/shard_map/ppermute | solution.py:211
  9.8 1.2 %copy-start = (bf16[27,128,128]{2,1,0:T(8,128)(2,1)S(1)}, bf16[27,128,128]{2,1,0:T(8,128)(2,1)}, u32[]{:S(2)}) copy-start(bf16[27,128,128]{2,1,0:T(8,128)(2,1)} %w_ref) | copy-start | bytes 2654212
  12.8 6.9 %collective-permute-start.5 = (bf16[272,256]{1,0:T(8,128)(2,1)S(1)}, bf16[272,256]{1,0:T(8,128)(2,1)S(1)}, u32[]{:S(2)}, u32[]{:S(2)}) collective-permute-start(bf16[272,256]{1,0:T(8,128)(2,1)S(1)} %collective-permute-done.1.before_mine.refs_1_.refs_3_), channel_id=1, source_target_pairs={{0,4},{2,6},{4,8},{6,10},{8,12},{10,14},{12,0},{14,2},{1,5},{3,7},... | collective-permute-start | bytes 417800 | tf_op jit(solution)/shard_map/ppermute | solution.py:214
  12.8 8.6 %collective-permute-start.2 = (bf16[272,256]{1,0:T(8,128)(2,1)S(1)}, bf16[272,256]{1,0:T(8,128)(2,1)S(1)}, u32[]{:S(2)}, u32[]{:S(2)}) collective-permute-start(bf16[272,256]{1,0:T(8,128)(2,1)S(1)} %collective-permute-done.1.before_mine.refs_1_.refs_3_), channel_id=1, source_target_pairs={{0,2},{2,0},{4,6},{6,4},{8,10},{10,8},{12,14},{14,12},{1,3},{3,1},... | collective-permute-start | bytes 417800 | tf_op jit(solution)/shard_map/ppermute | solution.py:211
  14.5 8.9 %collective-permute-start.4 = (bf16[272,256]{1,0:T(8,128)(2,1)S(1)}, bf16[272,256]{1,0:T(8,128)(2,1)S(1)}, u32[]{:S(2)}, u32[]{:S(2)}) collective-permute-start(bf16[272,256]{1,0:T(8,128)(2,1)S(1)} %collective-permute-done.3.after_mine.refs_1_.refs_5_), channel_id=1, source_target_pairs={{0,2},{2,0},{4,6},{6,4},{8,10},{10,8},{12,14},{14,12},{1,3},{3,1},... | collective-permute-start | bytes 417800 | tf_op jit(solution)/shard_map/ppermute | solution.py:211
  15.8 0.9 %copy-start.3 = (bf16[272,256]{1,0:T(8,128)(2,1)S(1)}, bf16[272,256]{1,0:T(8,128)(2,1)}, u32[]{:S(2)}) copy-start(bf16[272,256]{1,0:T(8,128)(2,1)} %get-tuple-element.25.mine_ref.refs_1_.refs_3_) | copy-start | bytes 417796
  19.6 5.9 %collective-permute-start.6 = (bf16[272,256]{1,0:T(8,128)(2,1)S(1)}, bf16[272,256]{1,0:T(8,128)(2,1)S(1)}, u32[]{:S(2)}, u32[]{:S(2)}) collective-permute-start(bf16[272,256]{1,0:T(8,128)(2,1)S(1)} %collective-permute-done.5.refs_1_), channel_id=1, source_target_pairs={{0,2},{2,0},{4,6},{6,4},{8,10},{10,8},{12,14},{14,12},{1,3},{3,1},... | collective-permute-start | bytes 417800 | tf_op jit(solution)/shard_map/ppermute | solution.py:211
  25.6 2.7 %copy-start.1 = (bf16[1,256,128]{2,1,0:T(8,128)(2,1)S(1)}, bf16[1,256,128]{2,1,0:T(8,128)(2,1)}, u32[]{:S(2)}) copy-start(bf16[1,256,128]{2,1,0:T(8,128)(2,1)} %feat_hbm.1) | copy-start | bytes 196612
  25.6 2.7 %copy-start.2 = (s32[27,256]{1,0:T(8,128)S(1)}, s32[27,256]{1,0:T(8,128)}, u32[]{:S(2)}) copy-start(s32[27,256]{1,0:T(8,128)} %near_ref.1) | copy-start | bytes 82948
  25.6 2.7 %copy-start.4 = (bf16[272,256]{1,0:T(8,128)(2,1)S(1)}, bf16[272,256]{1,0:T(8,128)(2,1)}, u32[]{:S(2)}) copy-start(bf16[272,256]{1,0:T(8,128)(2,1)} %get-tuple-element.25.mine_ref.refs_1_.refs_3_) | copy-start | bytes 417796
  25.6 2.7 %copy-start.5 = (f32[1,128]{1,0:T(1,128)S(1)}, f32[1,128]{1,0:T(1,128)}, u32[]{:S(2)}) copy-start(f32[1,128]{1,0:T(1,128)} %get-tuple-element.29.shift_ref) | copy-start | bytes 1540
  28.1 2.8 %collective-permute-start.7 = (bf16[27,128,128]{2,1,0:T(8,128)(2,1)S(1)}, bf16[27,128,128]{2,1,0:T(8,128)(2,1)S(1)}, u32[]{:S(2)}, u32[]{:S(2)}) collective-permute-start(bf16[27,128,128]{2,1,0:T(8,128)(2,1)S(1)} %get-tuple-element.44), channel_id=1, source_target_pairs={{0,1},{1,0},{2,3},{3,2},{4,5},{5,4},{6,7},{7,6},{8,9},{9,8},{10,11... | collective-permute-start | bytes 2654216 | tf_op jit(solution)/shard_map/ppermute | solution.py:271

commit v7 on v6

--- a/solution.py
+++ b/solution.py
@@ -138,8 +138,9 @@
         outs[2][...] = centre
 
 
-def turn_kernel(w_ref, forward_ref, back_ref):
+def turn_kernel(w_ref, pack_ref, forward_ref, back_ref, own_ref):
     width = w_ref.shape[1]
+    own_ref[...] = pack_ref[...]
     for k in range(27):
         forward_ref[:, k * width:(k + 1) * width] = w_ref[k].T
         back_ref[:, k * width:(k + 1) * width] = w_ref[26 - k]
@@ -214,31 +215,23 @@
         return lax.ppermute(block, "brick", [(i, (i + turn * tiles_y) % peers) for i in range(peers)])
 
     w_conv, packed = lax.optimization_barrier((w_conv, packed))
-    w_forward, w_back = pl.pallas_call(
+    w_forward, w_back, own = pl.pallas_call(
         turn_kernel,
-        out_shape=(jax.ShapeDtypeStruct((width, 27 * width), jnp.bfloat16),) * 2,
-        in_specs=[vmem],
-        out_specs=(vmem, vmem),
+        out_shape=(
+            jax.ShapeDtypeStruct((width, 27 * width), jnp.bfloat16),
+            jax.ShapeDtypeStruct((width, 27 * width), jnp.bfloat16),
+            jax.ShapeDtypeStruct(packed.shape, jnp.bfloat16),
+        ),
+        in_specs=[vmem, vmem],
+        out_specs=(vmem, vmem, vmem),
         compiler_params=params,
         cost_estimate=pl.CostEstimate(flops=2 * 10**8, bytes_accessed=3 * 10**6, transcendentals=0),
         name="turn_weights",
-    )(w_conv)
-    before, after = along(packed, 1), along(packed, -1)
-    before, w_forward = lax.optimization_barrier((before, w_forward))
-    far = along(before, 1)
-    own_pair = (packed, across(packed))
-    before_pair = (before, across(before))
-    after_pair = (after, across(after))
-    far_pair = (far, across(far))
-    line = [(0, u) for u in range(TILE)]
-    stages = (
-        ((own_pair,), line, []),
-        ((before_pair, own_pair), line + [(1, 0)], [(TILE, TILE - 1)]),
-        ((after_pair, own_pair), line + [(1, TILE - 1)], [(0, TILE)]),
-        ((far_pair, before_pair, after_pair), line + [(1, 0), (2, TILE - 1)], [(TILE, TILE - 1), (0, TILE + 1)]),
-    )
-    sums = ()
-    for stage, (pairs, strips, borders) in enumerate(stages):
+    )(w_conv, packed)
+    after, before = along(packed, -1), along(packed, 1)
+    own_pair = (own, across(packed))
+
+    def row_sums(stage, pairs, strips, borders, sums):
         blocks = [block for pair in pairs for block in pair]
         if stage == ROW_STAGES - 1:
             out_shape = (
@@ -251,7 +244,7 @@
                 jax.ShapeDtypeStruct((HALF * width, width), jnp.float32),
                 jax.ShapeDtypeStruct((width, width), jnp.float32),
             )
-        sums = pl.pallas_call(
+        return pl.pallas_call(
             functools.partial(row_kernel, stage, strips, borders),
             out_shape=out_shape,
             in_specs=[smem] + [vmem] * (len(blocks) + len(sums)),
@@ -267,7 +260,20 @@
             cost_estimate=pl.CostEstimate(flops=2 * 10**9, bytes_accessed=4 * 10**6, transcendentals=0),
             name=f"weight_row_{stage}",
         )(here, *blocks, *sums)
-    own, sent = sums
+
+    line = [(0, u) for u in range(TILE)]
+    low, high, centre = row_sums(0, (own_pair,), line, [], ())
+    before, w_forward, centre = lax.optimization_barrier((before, w_forward, centre))
+    sums = (low, high, centre)
+    far = along(before, 1)
+    before_pair = (before, across(before))
+    after_pair = (after, across(after))
+    far_pair = (far, across(far))
+    sums = row_sums(1, (before_pair, own_pair), line + [(1, 0)], [(TILE, TILE - 1)], sums)
+    sums = row_sums(2, (after_pair, own_pair), line + [(1, TILE - 1)], [(0, TILE)], sums)
+    sums = row_sums(3, (far_pair, before_pair, after_pair), line + [(1, 0), (2, TILE - 1)],
+                    [(TILE, TILE - 1), (0, TILE + 1)], sums)
+    kept, sent = sums
     other = lax.ppermute(sent, "batch", [(0, 1), (1, 0)])
     conv_out, feature_grad = pl.pallas_call(
         voxel_kernel,
@@ -287,7 +293,7 @@
         cost_estimate=pl.CostEstimate(flops=10**9, bytes_accessed=4 * 10**6, transcendentals=0),
         name="voxel_outputs",
     )(here, *own_pair, *before_pair, *after_pair, neighbours, features[0], shift, w_forward, w_back)
-    weight_grad = own + other.astype(jnp.float32)
+    weight_grad = kept + other.astype(jnp.float32)
     return (conv_out[None], feature_grad[None], weight_grad)
 
 

time: 32.6 us -> 35.5 us (1.089)
  waiting for transfers between devices: 2.62 us -> 6.67 us
  starting transfers between devices: 11.6 us -> 10.5 us
    ppermute x3, waiting for transfers between devices: 2.6 us -> 6.33 us  [along(): lax.ppermute(block, 'brick', [(i, (i + turn * tiles_y) % peers) for i in...]
    ppermute x4, starting transfers between devices: 6.41 us -> 5.56 us  [across(): return lax.ppermute(block, 'brick', [(i, i ^ 1) for i in range(peers)])]
    unnamed x12 -> x10, local copies, waits for them, and re-layouts: 2.1 us -> 2.08 us
  transfers between devices with their start and end apart: 8 -> 8, of which waited for: 2 -> 3; matrix products, arithmetic and copies ran while one was open for 0% -> 0% of each run, Pallas kernels for 28% -> 25%
where the time goes in v7:
time: 35.5 us; the launch traced here: 35.3 us
  Pallas kernels  13.2 us (37%)
  starting transfers between devices  10.5 us (30%)
  waiting for transfers between devices  6.67 us (19%)
  local copies, waits for them, and re-layouts  2.08 us (6%)
  other arithmetic  1.45 us (4%)
  between operations  1.36 us (4%)
    pallas_call x4, Pallas kernels, row_sums(): pl.pallas_call(functools.partial(row_kernel, stage, strips, borders), out...  8.46 us
    ppermute x3, waiting for transfers between devices, along(): lax.ppermute(block, 'brick', [(i, (i + turn * tiles_y) % peers) for i in...  6.33 us
    ppermute x4, starting transfers between devices, across(): return lax.ppermute(block, 'brick', [(i, i ^ 1) for i in range(peers)])  5.56 us
    ppermute x3, starting transfers between devices, along(): lax.ppermute(block, 'brick', [(i, (i + turn * tiles_y) % peers) for i in...  4.91 us
    pallas_call x1, Pallas kernels, whole_scene(): pl.pallas_call(voxel_kernel, out_shape=(jax.ShapeDtypeStruct((rows, width...  2.67 us
    unnamed x10, local copies, waits for them, and re-layouts  2.08 us
    pallas_call x1, Pallas kernels, whole_scene(): pl.pallas_call(pack_kernel, out_shape=(jax.ShapeDtypeStruct((rows + CODE_...  1.66 us
    add x1, other arithmetic, whole_scene(): weight_grad = kept + other.astype(jnp.float32)  1.45 us
  transfers between devices with their start and end apart: 8, of which 3 were waited for; matrix products, arithmetic and copies ran while one was open for 0% of the time, Pallas kernels for 25%

profile of v7, /device:TPU:0, one launch (start us, length us, event | category | flops | bytes accessed | tf_op | source)
XLA Modules:
  0.0 35.3 jit_solution(3616294444927911052)
XLA Ops:
  1.3 1.7 %pack_tile.1 = (bf16[272,256]{1,0:T(8,128)(2,1)}, f32[1,128]{1,0:T(1,128)}) custom-call(s32[1]{0:T(128)S(6)} %copy.10.time_ref, bf16[1,256,128]{2,1,0:T(8,128)(2,1)} %feat_hbm.1, bf16[1,256,128]{2,1,0:T(8,128)(2,1)} %cot_hbm.1, s32[27,256]{1,0:T(8,128)} %near_ref.1, bf16[1,128]{1,0:T(2,128)(2,1)} %cond_hbm.1, bf16[128,128]{1,0:T(8,128)(2,1)} %wt_hbm.1), custom_call_target="tpu_custom_call" | custom-call | tf_op jit(solution)/shard_map/pack_tile/pallas_call | solution.py:192
  2.9 3.0 %collective-permute-start = (bf16[272,256]{1,0:T(8,128)(2,1)}, bf16[272,256]{1,0:T(8,128)(2,1)S(1)}, u32[]{:S(2)}, u32[]{:S(2)}) collective-permute-start(bf16[272,256]{1,0:T(8,128)(2,1)} %get-tuple-element.28.pack_ref), channel_id=1, source_target_pairs={{0,2},{2,0},{4,6},{6,4},{8,10},{10,8},{12,14},{14,12},{1,3},{3,1},... | collective-permute-start | bytes 417800 | tf_op jit(solution)/shard_map/ppermute | solution.py:212
  6.0 3.6 %collective-permute-start.3 = (bf16[272,256]{1,0:T(8,128)(2,1)}, bf16[272,256]{1,0:T(8,128)(2,1)S(1)}, u32[]{:S(2)}, u32[]{:S(2)}) collective-permute-start(bf16[272,256]{1,0:T(8,128)(2,1)} %get-tuple-element.28.pack_ref), channel_id=1, source_target_pairs={{0,12},{2,14},{4,0},{6,2},{8,4},{10,6},{12,8},{14,10},{1,13},{3,15... | collective-permute-start | bytes 417800 | tf_op jit(solution)/shard_map/ppermute | solution.py:215
  9.6 0.0 collective-permute-start.1
  9.6 0.0 copy-start
  9.6 1.2 %copy-done = bf16[27,128,128]{2,1,0:T(8,128)(2,1)S(1)} copy-done((bf16[27,128,128]{2,1,0:T(8,128)(2,1)S(1)}, bf16[27,128,128]{2,1,0:T(8,128)(2,1)}, u32[]{:S(2)}) %copy-start) | copy-done | bytes 884760
  10.7 0.0 copy-start.1
  10.7 0.9 %copy-done.1 = bf16[272,256]{1,0:T(8,128)(2,1)S(1)} copy-done((bf16[272,256]{1,0:T(8,128)(2,1)S(1)}, bf16[272,256]{1,0:T(8,128)(2,1)}, u32[]{:S(2)}) %copy-start.1) | copy-done | bytes 139288
  11.6 0.4 %turn_weights.1 = (bf16[128,3456]{1,0:T(8,128)(2,1)S(1)}, bf16[128,3456]{1,0:T(8,128)(2,1)S(1)}, bf16[272,256]{1,0:T(8,128)(2,1)S(1)}) custom-call(bf16[27,128,128]{2,1,0:T(8,128)(2,1)S(1)} %copy-done, bf16[272,256]{1,0:T(8,128)(2,1)S(1)} %copy-done.1), custom_call_target="tpu_custom_call" | custom-call | flops 200000000 | bytes 3000000 | tf_op jit(solution)/shard_map/turn_weights/pallas_call | solution.py:218
  12.0 0.0 collective-permute-done.refs_2_.other_ref.refs_4_
  12.0 1.8 %weight_row_0.1 = (f32[1664,128]{1,0:T(8,128)S(1)}, f32[1664,128]{1,0:T(8,128)S(1)}, f32[128,128]{1,0:T(8,128)S(1)}) custom-call(s32[1]{0:T(128)} %bitcast.refs_0_.where_ref, bf16[272,256]{1,0:T(8,128)(2,1)S(1)} %get-tuple-element.29.refs_1_.mine_ref.refs_3_, bf16[272,256]{1,0:T(8,128)(2,1)S(1)} %collective-permute-done.refs_2_.other_ref.refs_4_), custom_call_target="tpu_custom_call" | custom-call | flops 2000000000 | bytes 4000000 | tf_op jit(solution)/shard_map/weight_row_0/pallas_call | solution.py:247
  13.8 2.8 %collective-permute-done.1.before_mine.refs_1_.refs_3_ = bf16[272,256]{1,0:T(8,128)(2,1)S(1)} collective-permute-done((bf16[272,256]{1,0:T(8,128)(2,1)}, bf16[272,256]{1,0:T(8,128)(2,1)S(1)}, u32[]{:S(2)}, u32[]{:S(2)}) %collective-permute-start.1) | collective-permute-done | bytes 139296 | tf_op jit(solution)/shard_map/ppermute | solution.py:215
  16.6 1.3 %collective-permute-start.5 = (bf16[272,256]{1,0:T(8,128)(2,1)S(1)}, bf16[272,256]{1,0:T(8,128)(2,1)S(1)}, u32[]{:S(2)}, u32[]{:S(2)}) collective-permute-start(bf16[272,256]{1,0:T(8,128)(2,1)S(1)} %collective-permute-done.1.before_mine.refs_1_.refs_3_), channel_id=1, source_target_pairs={{0,4},{2,6},{4,8},{6,10},{8,12},{10,14},{12,0},{14,2},{1,5},{3,7},... | collective-permute-start | bytes 417800 | tf_op jit(solution)/shard_map/ppermute | solution.py:215
  17.9 0.5 %collective-permute-start.2 = (bf16[272,256]{1,0:T(8,128)(2,1)S(1)}, bf16[272,256]{1,0:T(8,128)(2,1)S(1)}, u32[]{:S(2)}, u32[]{:S(2)}) collective-permute-start(bf16[272,256]{1,0:T(8,128)(2,1)S(1)} %collective-permute-done.1.before_mine.refs_1_.refs_3_), channel_id=1, source_target_pairs={{0,2},{2,0},{4,6},{6,4},{8,10},{10,8},{12,14},{14,12},{1,3},{3,1},... | collective-permute-start | bytes 417800 | tf_op jit(solution)/shard_map/ppermute | solution.py:212
  18.5 0.0 collective-permute-done.3.after_mine.refs_1_.refs_5_
  18.5 1.5 %collective-permute-start.4 = (bf16[272,256]{1,0:T(8,128)(2,1)S(1)}, bf16[272,256]{1,0:T(8,128)(2,1)S(1)}, u32[]{:S(2)}, u32[]{:S(2)}) collective-permute-start(bf16[272,256]{1,0:T(8,128)(2,1)S(1)} %collective-permute-done.3.after_mine.refs_1_.refs_5_), channel_id=1, source_target_pairs={{0,2},{2,0},{4,6},{6,4},{8,10},{10,8},{12,14},{14,12},{1,3},{3,1},... | collective-permute-start | bytes 417800 | tf_op jit(solution)/shard_map/ppermute | solution.py:212
  20.0 3.5 %collective-permute-done.5.refs_1_ = bf16[272,256]{1,0:T(8,128)(2,1)S(1)} collective-permute-done((bf16[272,256]{1,0:T(8,128)(2,1)S(1)}, bf16[272,256]{1,0:T(8,128)(2,1)S(1)}, u32[]{:S(2)}, u32[]{:S(2)}) %collective-permute-start.5) | collective-permute-done | bytes 139296 | tf_op jit(solution)/shard_map/ppermute | solution.py:215
  23.5 0.5 %collective-permute-start.6 = (bf16[272,256]{1,0:T(8,128)(2,1)S(1)}, bf16[272,256]{1,0:T(8,128)(2,1)S(1)}, u32[]{:S(2)}, u32[]{:S(2)}) collective-permute-start(bf16[272,256]{1,0:T(8,128)(2,1)S(1)} %collective-permute-done.5.refs_1_), channel_id=1, source_target_pairs={{0,2},{2,0},{4,6},{6,4},{8,10},{10,8},{12,14},{14,12},{1,3},{3,1},... | collective-permute-start | bytes 417800 | tf_op jit(solution)/shard_map/ppermute | solution.py:212
  24.0 0.0 collective-permute-done.2.before_other.refs_2_.refs_4_
  24.0 2.1 %weight_row_1.1 = (f32[1664,128]{1,0:T(8,128)S(1)}, f32[1664,128]{1,0:T(8,128)S(1)}, f32[128,128]{1,0:T(8,128)S(1)}) custom-call(s32[1]{0:T(128)} %bitcast.refs_0_.where_ref, bf16[272,256]{1,0:T(8,128)(2,1)S(1)} %collective-permute-done.1.before_mine.refs_1_.refs_3_, bf16[272,256]{1,0:T(8,128)(2,1)S(1)} %collective-permute-done.2.before_other.refs_2_.refs_4_, ...), custom_call_target="tpu_custom_call" | custom-call | flops 2000000000 | bytes 4000000 | tf_op jit(solution)/shard_map/weight_row_1/pallas_call | solution.py:247
  26.1 0.3 collective-permute-done.4.after_other.refs_2_.refs_6_
  26.4 2.1 %weight_row_2.1 = (f32[1664,128]{1,0:T(8,128)S(1)}, f32[1664,128]{1,0:T(8,128)S(1)}, f32[128,128]{1,0:T(8,128)S(1)}) custom-call(s32[1]{0:T(128)} %bitcast.refs_0_.where_ref, bf16[272,256]{1,0:T(8,128)(2,1)S(1)} %collective-permute-done.3.after_mine.refs_1_.refs_5_, bf16[272,256]{1,0:T(8,128)(2,1)S(1)} %collective-permute-done.4.after_other.refs_2_.refs_6_, ...), custom_call_target="tpu_custom_call" | custom-call | flops 2000000000 | bytes 4000000 | tf_op jit(solution)/shard_map/weight_row_2/pallas_call | solution.py:247
  28.5 0.0 collective-permute-done.6.refs_2_
  28.5 0.0 copy-start.2
  28.5 0.0 copy-start.3
  28.5 0.0 copy-start.4
  28.5 2.5 %weight_row_3.1 = (f32[27,128,128]{2,1,0:T(8,128)S(1)}, bf16[27,128,128]{2,1,0:T(8,128)(2,1)S(1)}) custom-call(s32[1]{0:T(128)} %bitcast.refs_0_.where_ref, bf16[272,256]{1,0:T(8,128)(2,1)S(1)} %collective-permute-done.5.refs_1_, bf16[272,256]{1,0:T(8,128)(2,1)S(1)} %collective-permute-done.6.refs_2_, ...), custom_call_target="tpu_custom_call" | custom-call | flops 2000000000 | bytes 4000000 | tf_op jit(solution)/shard_map/weight_row_3/pallas_call | solution.py:247
  31.1 0.1 collective-permute-start.7
  31.1 0.0 copy-done.2
  31.1 0.0 copy-done.3
  31.2 0.0 copy-done.4
  31.2 2.7 %voxel_outputs.1 = (bf16[256,128]{1,0:T(8,128)(2,1)}, bf16[256,128]{1,0:T(8,128)(2,1)}) custom-call(s32[1]{0:T(128)} %bitcast.refs_0_.where_ref, bf16[272,256]{1,0:T(8,128)(2,1)S(1)} %get-tuple-element.29.refs_1_.mine_ref.refs_3_, bf16[272,256]{1,0:T(8,128)(2,1)S(1)} %collective-permute-done.refs_2_.other_ref.refs_4_, ...), custom_call_target="tpu_custom_call" | custom-call | flops 1000000000 | bytes 4000000 | tf_op jit(solution)/shard_map/voxel_outputs/pallas_call | solution.py:278
  33.8 0.0 collective-permute-done.7
  33.8 1.4 %convert_add_fusion = f32[27,128,128]{2,1,0:T(8,128)} fusion(f32[27,128,128]{2,1,0:T(8,128)S(1)} %get-tuple-element.47, bf16[27,128,128]{2,1,0:T(8,128)(2,1)S(1)} %collective-permute-done.7), kind=kLoop, calls=%fused_computation | loop fusion | flops 884736 | bytes 4423680 | tf_op jit(solution)/shard_map/add | solution.py:296
Async XLA Ops:
  2.9 9.1 %collective-permute-start = (bf16[272,256]{1,0:T(8,128)(2,1)}, bf16[272,256]{1,0:T(8,128)(2,1)S(1)}, u32[]{:S(2)}, u32[]{:S(2)}) collective-permute-start(bf16[272,256]{1,0:T(8,128)(2,1)} %get-tuple-element.28.pack_ref), channel_id=1, source_target_pairs={{0,2},{2,0},{4,6},{6,4},{8,10},{10,8},{12,14},{14,12},{1,3},{3,1},... | collective-permute-start | bytes 417800 | tf_op jit(solution)/shard_map/ppermute | solution.py:212
  6.0 12.5 %collective-permute-start.3 = (bf16[272,256]{1,0:T(8,128)(2,1)}, bf16[272,256]{1,0:T(8,128)(2,1)S(1)}, u32[]{:S(2)}, u32[]{:S(2)}) collective-permute-start(bf16[272,256]{1,0:T(8,128)(2,1)} %get-tuple-element.28.pack_ref), channel_id=1, source_target_pairs={{0,12},{2,14},{4,0},{6,2},{8,4},{10,6},{12,8},{14,10},{1,13},{3,15... | collective-permute-start | bytes 417800 | tf_op jit(solution)/shard_map/ppermute | solution.py:215
  9.6 7.1 %collective-permute-start.1 = (bf16[272,256]{1,0:T(8,128)(2,1)}, bf16[272,256]{1,0:T(8,128)(2,1)S(1)}, u32[]{:S(2)}, u32[]{:S(2)}) collective-permute-start(bf16[272,256]{1,0:T(8,128)(2,1)} %get-tuple-element.28.pack_ref), channel_id=1, source_target_pairs={{0,4},{2,6},{4,8},{6,10},{8,12},{10,14},{12,0},{14,2},{1,5},{3,7},... | collective-permute-start | bytes 417800 | tf_op jit(solution)/shard_map/ppermute | solution.py:215
  9.6 1.2 %copy-start = (bf16[27,128,128]{2,1,0:T(8,128)(2,1)S(1)}, bf16[27,128,128]{2,1,0:T(8,128)(2,1)}, u32[]{:S(2)}) copy-start(bf16[27,128,128]{2,1,0:T(8,128)(2,1)} %w_ref) | copy-start | bytes 2654212
  10.7 0.9 %copy-start.1 = (bf16[272,256]{1,0:T(8,128)(2,1)S(1)}, bf16[272,256]{1,0:T(8,128)(2,1)}, u32[]{:S(2)}) copy-start(bf16[272,256]{1,0:T(8,128)(2,1)} %get-tuple-element.28.pack_ref) | copy-start | bytes 417796
  16.6 6.9 %collective-permute-start.5 = (bf16[272,256]{1,0:T(8,128)(2,1)S(1)}, bf16[272,256]{1,0:T(8,128)(2,1)S(1)}, u32[]{:S(2)}, u32[]{:S(2)}) collective-permute-start(bf16[272,256]{1,0:T(8,128)(2,1)S(1)} %collective-permute-done.1.before_mine.refs_1_.refs_3_), channel_id=1, source_target_pairs={{0,4},{2,6},{4,8},{6,10},{8,12},{10,14},{12,0},{14,2},{1,5},{3,7},... | collective-permute-start | bytes 417800 | tf_op jit(solution)/shard_map/ppermute | solution.py:215
  17.9 6.1 %collective-permute-start.2 = (bf16[272,256]{1,0:T(8,128)(2,1)S(1)}, bf16[272,256]{1,0:T(8,128)(2,1)S(1)}, u32[]{:S(2)}, u32[]{:S(2)}) collective-permute-start(bf16[272,256]{1,0:T(8,128)(2,1)S(1)} %collective-permute-done.1.before_mine.refs_1_.refs_3_), channel_id=1, source_target_pairs={{0,2},{2,0},{4,6},{6,4},{8,10},{10,8},{12,14},{14,12},{1,3},{3,1},... | collective-permute-start | bytes 417800 | tf_op jit(solution)/shard_map/ppermute | solution.py:212
  18.5 7.9 %collective-permute-start.4 = (bf16[272,256]{1,0:T(8,128)(2,1)S(1)}, bf16[272,256]{1,0:T(8,128)(2,1)S(1)}, u32[]{:S(2)}, u32[]{:S(2)}) collective-permute-start(bf16[272,256]{1,0:T(8,128)(2,1)S(1)} %collective-permute-done.3.after_mine.refs_1_.refs_5_), channel_id=1, source_target_pairs={{0,2},{2,0},{4,6},{6,4},{8,10},{10,8},{12,14},{14,12},{1,3},{3,1},... | collective-permute-start | bytes 417800 | tf_op jit(solution)/shard_map/ppermute | solution.py:212
  23.5 5.1 %collective-permute-start.6 = (bf16[272,256]{1,0:T(8,128)(2,1)S(1)}, bf16[272,256]{1,0:T(8,128)(2,1)S(1)}, u32[]{:S(2)}, u32[]{:S(2)}) collective-permute-start(bf16[272,256]{1,0:T(8,128)(2,1)S(1)} %collective-permute-done.5.refs_1_), channel_id=1, source_target_pairs={{0,2},{2,0},{4,6},{6,4},{8,10},{10,8},{12,14},{14,12},{1,3},{3,1},... | collective-permute-start | bytes 417800 | tf_op jit(solution)/shard_map/ppermute | solution.py:212
  28.5 2.6 %copy-start.2 = (bf16[1,256,128]{2,1,0:T(8,128)(2,1)S(1)}, bf16[1,256,128]{2,1,0:T(8,128)(2,1)}, u32[]{:S(2)}) copy-start(bf16[1,256,128]{2,1,0:T(8,128)(2,1)} %feat_hbm.1) | copy-start | bytes 196612
  28.5 2.6 %copy-start.3 = (s32[27,256]{1,0:T(8,128)S(1)}, s32[27,256]{1,0:T(8,128)}, u32[]{:S(2)}) copy-start(s32[27,256]{1,0:T(8,128)} %near_ref.1) | copy-start | bytes 82948
  28.5 2.6 %copy-start.4 = (f32[1,128]{1,0:T(1,128)S(1)}, f32[1,128]{1,0:T(1,128)}, u32[]{:S(2)}) copy-start(f32[1,128]{1,0:T(1,128)} %get-tuple-element.33.shift_ref) | copy-start | bytes 1540
  31.1 2.8 %collective-permute-start.7 = (bf16[27,128,128]{2,1,0:T(8,128)(2,1)S(1)}, bf16[27,128,128]{2,1,0:T(8,128)(2,1)S(1)}, u32[]{:S(2)}, u32[]{:S(2)}) collective-permute-start(bf16[27,128,128]{2,1,0:T(8,128)(2,1)S(1)} %get-tuple-element.48), channel_id=1, source_target_pairs={{0,1},{1,0},{2,3},{3,2},{4,5},{5,4},{6,7},{7,6},{8,9},{9,8},{10,11... | collective-permute-start | bytes 2654216 | tf_op jit(solution)/shard_map/ppermute | solution.py:277

commit v8 on v7

--- a/solution.py
+++ b/solution.py
@@ -225,7 +225,7 @@
         in_specs=[vmem, vmem],
         out_specs=(vmem, vmem, vmem),
         compiler_params=params,
-        cost_estimate=pl.CostEstimate(flops=2 * 10**8, bytes_accessed=3 * 10**6, transcendentals=0),
+        cost_estimate=pl.CostEstimate(flops=10**6, bytes_accessed=10**4, transcendentals=0),
         name="turn_weights",
     )(w_conv, packed)
     after, before = along(packed, -1), along(packed, 1)
@@ -257,7 +257,7 @@
                 pltpu.VMEM((HALF * width, (TILE + 1) * span), jnp.bfloat16),
             ],
             compiler_params=params,
-            cost_estimate=pl.CostEstimate(flops=2 * 10**9, bytes_accessed=4 * 10**6, transcendentals=0),
+            cost_estimate=pl.CostEstimate(flops=2 * 10**9 if stage else 10**8, bytes_accessed=10**4, transcendentals=0),
             name=f"weight_row_{stage}",
         )(here, *blocks, *sums)
 

time: 35.5 us -> 33.4 us (0.941)
  starting transfers between devices: 10.5 us -> 8.68 us
    ppermute x3, starting transfers between devices: 4.91 us -> 3.83 us  [along(): lax.ppermute(block, 'brick', [(i, (i + turn * tiles_y) % peers) for i in...]
    ppermute x4, starting transfers between devices: 5.56 us -> 4.78 us  [across(): return lax.ppermute(block, 'brick', [(i, i ^ 1) for i in range(peers)])]
    ppermute x3, waiting for transfers between devices: 6.33 us -> 5.92 us  [along(): lax.ppermute(block, 'brick', [(i, (i + turn * tiles_y) % peers) for i in...]
  transfers between devices with their start and end apart: 8 -> 8, of which waited for: 3 -> 4; matrix products, arithmetic and copies ran while one was open for 0% -> 0% of each run, Pallas kernels for 25% -> 27%
where the time goes in v8:
time: 33.4 us; the launch traced here: 33.2 us
  Pallas kernels  13.2 us (40%)
  starting transfers between devices  8.68 us (26%)
  waiting for transfers between devices  6.46 us (19%)
  local copies, waits for them, and re-layouts  2.08 us (6%)
  other arithmetic  1.45 us (4%)
  between operations  1.37 us (4%)
    pallas_call x4, Pallas kernels, row_sums(): pl.pallas_call(functools.partial(row_kernel, stage, strips, borders), out...  8.46 us
    ppermute x3, waiting for transfers between devices, along(): lax.ppermute(block, 'brick', [(i, (i + turn * tiles_y) % peers) for i in...  5.92 us
    ppermute x4, starting transfers between devices, across(): return lax.ppermute(block, 'brick', [(i, i ^ 1) for i in range(peers)])  4.78 us
    ppermute x3, starting transfers between devices, along(): lax.ppermute(block, 'brick', [(i, (i + turn * tiles_y) % peers) for i in...  3.83 us
    pallas_call x1, Pallas kernels, whole_scene(): pl.pallas_call(voxel_kernel, out_shape=(jax.ShapeDtypeStruct((rows, width...  2.65 us
    unnamed x10, local copies, waits for them, and re-layouts  2.08 us
    pallas_call x1, Pallas kernels, whole_scene(): pl.pallas_call(pack_kernel, out_shape=(jax.ShapeDtypeStruct((rows + CODE_...  1.66 us
    add x1, other arithmetic, whole_scene(): weight_grad = kept + other.astype(jnp.float32)  1.45 us
  transfers between devices with their start and end apart: 8, of which 4 were waited for; matrix products, arithmetic and copies ran while one was open for 0% of the time, Pallas kernels for 27%

profile of v8, /device:TPU:0, one launch (start us, length us, event | category | flops | bytes accessed | tf_op | source)
XLA Modules:
  0.0 33.2 jit_solution(595084085031677106)
XLA Ops:
  1.3 1.7 %pack_tile.1 = (bf16[272,256]{1,0:T(8,128)(2,1)}, f32[1,128]{1,0:T(1,128)}) custom-call(s32[1]{0:T(128)S(6)} %copy.10.time_ref, bf16[1,256,128]{2,1,0:T(8,128)(2,1)} %feat_hbm.1, bf16[1,256,128]{2,1,0:T(8,128)(2,1)} %cot_hbm.1, s32[27,256]{1,0:T(8,128)} %near_ref.1, bf16[1,128]{1,0:T(2,128)(2,1)} %cond_hbm.1, bf16[128,128]{1,0:T(8,128)(2,1)} %wt_hbm.1), custom_call_target="tpu_custom_call" | custom-call | tf_op jit(solution)/shard_map/pack_tile/pallas_call | solution.py:192
  2.9 3.0 %collective-permute-start = (bf16[272,256]{1,0:T(8,128)(2,1)}, bf16[272,256]{1,0:T(8,128)(2,1)S(1)}, u32[]{:S(2)}, u32[]{:S(2)}) collective-permute-start(bf16[272,256]{1,0:T(8,128)(2,1)} %get-tuple-element.28.pack_ref), channel_id=1, source_target_pairs={{0,2},{2,0},{4,6},{6,4},{8,10},{10,8},{12,14},{14,12},{1,3},{3,1},... | collective-permute-start | bytes 417800 | tf_op jit(solution)/shard_map/ppermute | solution.py:212
  6.0 1.6 %collective-permute-start.1 = (bf16[272,256]{1,0:T(8,128)(2,1)}, bf16[272,256]{1,0:T(8,128)(2,1)S(1)}, u32[]{:S(2)}, u32[]{:S(2)}) collective-permute-start(bf16[272,256]{1,0:T(8,128)(2,1)} %get-tuple-element.28.pack_ref), channel_id=1, source_target_pairs={{0,4},{2,6},{4,8},{6,10},{8,12},{10,14},{12,0},{14,2},{1,5},{3,7},... | collective-permute-start | bytes 417800 | tf_op jit(solution)/shard_map/ppermute | solution.py:215
  7.5 2.2 %collective-permute-start.3 = (bf16[272,256]{1,0:T(8,128)(2,1)}, bf16[272,256]{1,0:T(8,128)(2,1)S(1)}, u32[]{:S(2)}, u32[]{:S(2)}) collective-permute-start(bf16[272,256]{1,0:T(8,128)(2,1)} %get-tuple-element.28.pack_ref), channel_id=1, source_target_pairs={{0,12},{2,14},{4,0},{6,2},{8,4},{10,6},{12,8},{14,10},{1,13},{3,15... | collective-permute-start | bytes 417800 | tf_op jit(solution)/shard_map/ppermute | solution.py:215
  9.8 0.0 copy-start
  9.8 1.2 %copy-done = bf16[27,128,128]{2,1,0:T(8,128)(2,1)S(1)} copy-done((bf16[27,128,128]{2,1,0:T(8,128)(2,1)S(1)}, bf16[27,128,128]{2,1,0:T(8,128)(2,1)}, u32[]{:S(2)}) %copy-start) | copy-done | bytes 884760
  10.9 0.0 copy-start.1
  10.9 0.9 %copy-done.1 = bf16[272,256]{1,0:T(8,128)(2,1)S(1)} copy-done((bf16[272,256]{1,0:T(8,128)(2,1)S(1)}, bf16[272,256]{1,0:T(8,128)(2,1)}, u32[]{:S(2)}) %copy-start.1) | copy-done | bytes 139288
  11.9 0.4 %turn_weights.1 = (bf16[128,3456]{1,0:T(8,128)(2,1)S(1)}, bf16[128,3456]{1,0:T(8,128)(2,1)S(1)}, bf16[272,256]{1,0:T(8,128)(2,1)S(1)}) custom-call(bf16[27,128,128]{2,1,0:T(8,128)(2,1)S(1)} %copy-done, bf16[272,256]{1,0:T(8,128)(2,1)S(1)} %copy-done.1), custom_call_target="tpu_custom_call" | custom-call | flops 1000000 | bytes 10000 | tf_op jit(solution)/shard_map/turn_weights/pallas_call | solution.py:218
  12.2 0.0 collective-permute-done.refs_2_.other_ref.refs_4_
  12.2 1.8 %weight_row_0.1 = (f32[1664,128]{1,0:T(8,128)S(1)}, f32[1664,128]{1,0:T(8,128)S(1)}, f32[128,128]{1,0:T(8,128)S(1)}) custom-call(s32[1]{0:T(128)} %bitcast.refs_0_.where_ref, bf16[272,256]{1,0:T(8,128)(2,1)S(1)} %get-tuple-element.29.refs_1_.mine_ref.refs_3_, bf16[272,256]{1,0:T(8,128)(2,1)S(1)} %collective-permute-done.refs_2_.other_ref.refs_4_), custom_call_target="tpu_custom_call" | custom-call | flops 100000000 | bytes 10000 | tf_op jit(solution)/shard_map/weight_row_0/pallas_call | solution.py:247
  14.0 0.5 %collective-permute-done.1.before_mine.refs_1_.refs_3_ = bf16[272,256]{1,0:T(8,128)(2,1)S(1)} collective-permute-done((bf16[272,256]{1,0:T(8,128)(2,1)}, bf16[272,256]{1,0:T(8,128)(2,1)S(1)}, u32[]{:S(2)}, u32[]{:S(2)}) %collective-permute-start.1) | collective-permute-done | bytes 139296 | tf_op jit(solution)/shard_map/ppermute | solution.py:215
  14.6 0.0 collective-permute-start.5
  14.6 0.4 %collective-permute-start.2 = (bf16[272,256]{1,0:T(8,128)(2,1)S(1)}, bf16[272,256]{1,0:T(8,128)(2,1)S(1)}, u32[]{:S(2)}, u32[]{:S(2)}) collective-permute-start(bf16[272,256]{1,0:T(8,128)(2,1)S(1)} %collective-permute-done.1.before_mine.refs_1_.refs_3_), channel_id=1, source_target_pairs={{0,2},{2,0},{4,6},{6,4},{8,10},{10,8},{12,14},{14,12},{1,3},{3,1},... | collective-permute-start | bytes 417800 | tf_op jit(solution)/shard_map/ppermute | solution.py:212
  15.0 0.6 %collective-permute-done.3.after_mine.refs_1_.refs_5_ = bf16[272,256]{1,0:T(8,128)(2,1)S(1)} collective-permute-done((bf16[272,256]{1,0:T(8,128)(2,1)}, bf16[272,256]{1,0:T(8,128)(2,1)S(1)}, u32[]{:S(2)}, u32[]{:S(2)}) %collective-permute-start.3) | collective-permute-done | bytes 139296 | tf_op jit(solution)/shard_map/ppermute | solution.py:215
  15.6 1.0 %collective-permute-start.4 = (bf16[272,256]{1,0:T(8,128)(2,1)S(1)}, bf16[272,256]{1,0:T(8,128)(2,1)S(1)}, u32[]{:S(2)}, u32[]{:S(2)}) collective-permute-start(bf16[272,256]{1,0:T(8,128)(2,1)S(1)} %collective-permute-done.3.after_mine.refs_1_.refs_5_), channel_id=1, source_target_pairs={{0,2},{2,0},{4,6},{6,4},{8,10},{10,8},{12,14},{14,12},{1,3},{3,1},... | collective-permute-start | bytes 417800 | tf_op jit(solution)/shard_map/ppermute | solution.py:212
  16.6 4.8 %collective-permute-done.5.refs_1_ = bf16[272,256]{1,0:T(8,128)(2,1)S(1)} collective-permute-done((bf16[272,256]{1,0:T(8,128)(2,1)S(1)}, bf16[272,256]{1,0:T(8,128)(2,1)S(1)}, u32[]{:S(2)}, u32[]{:S(2)}) %collective-permute-start.5) | collective-permute-done | bytes 139296 | tf_op jit(solution)/shard_map/ppermute | solution.py:215
  21.4 0.3 collective-permute-start.6
  21.7 0.0 collective-permute-done.2.before_other.refs_2_.refs_4_
  21.7 2.1 %weight_row_1.1 = (f32[1664,128]{1,0:T(8,128)S(1)}, f32[1664,128]{1,0:T(8,128)S(1)}, f32[128,128]{1,0:T(8,128)S(1)}) custom-call(s32[1]{0:T(128)} %bitcast.refs_0_.where_ref, bf16[272,256]{1,0:T(8,128)(2,1)S(1)} %collective-permute-done.1.before_mine.refs_1_.refs_3_, bf16[272,256]{1,0:T(8,128)(2,1)S(1)} %collective-permute-done.2.before_other.refs_2_.refs_4_, ...), custom_call_target="tpu_custom_call" | custom-call | flops 2000000000 | bytes 10000 | tf_op jit(solution)/shard_map/weight_row_1/pallas_call | solution.py:247
  23.8 0.0 collective-permute-done.4.after_other.refs_2_.refs_6_
  23.8 2.1 %weight_row_2.1 = (f32[1664,128]{1,0:T(8,128)S(1)}, f32[1664,128]{1,0:T(8,128)S(1)}, f32[128,128]{1,0:T(8,128)S(1)}) custom-call(s32[1]{0:T(128)} %bitcast.refs_0_.where_ref, bf16[272,256]{1,0:T(8,128)(2,1)S(1)} %collective-permute-done.3.after_mine.refs_1_.refs_5_, bf16[272,256]{1,0:T(8,128)(2,1)S(1)} %collective-permute-done.4.after_other.refs_2_.refs_6_, ...), custom_call_target="tpu_custom_call" | custom-call | flops 2000000000 | bytes 10000 | tf_op jit(solution)/shard_map/weight_row_2/pallas_call | solution.py:247
  25.9 0.5 %collective-permute-done.6.refs_2_ = bf16[272,256]{1,0:T(8,128)(2,1)S(1)} collective-permute-done((bf16[272,256]{1,0:T(8,128)(2,1)S(1)}, bf16[272,256]{1,0:T(8,128)(2,1)S(1)}, u32[]{:S(2)}, u32[]{:S(2)}) %collective-permute-start.6) | collective-permute-done | bytes 139296 | tf_op jit(solution)/shard_map/ppermute | solution.py:212
  26.5 0.0 copy-start.2
  26.5 0.0 copy-start.3
  26.5 0.0 copy-start.4
  26.5 2.5 %weight_row_3.1 = (f32[27,128,128]{2,1,0:T(8,128)S(1)}, bf16[27,128,128]{2,1,0:T(8,128)(2,1)S(1)}) custom-call(s32[1]{0:T(128)} %bitcast.refs_0_.where_ref, bf16[272,256]{1,0:T(8,128)(2,1)S(1)} %collective-permute-done.5.refs_1_, bf16[272,256]{1,0:T(8,128)(2,1)S(1)} %collective-permute-done.6.refs_2_, ...), custom_call_target="tpu_custom_call" | custom-call | flops 2000000000 | bytes 10000 | tf_op jit(solution)/shard_map/weight_row_3/pallas_call | solution.py:247
  29.0 0.1 collective-permute-start.7
  29.1 0.0 copy-done.2
  29.1 0.0 copy-done.3
  29.1 0.0 copy-done.4
  29.1 2.7 %voxel_outputs.1 = (bf16[256,128]{1,0:T(8,128)(2,1)}, bf16[256,128]{1,0:T(8,128)(2,1)}) custom-call(s32[1]{0:T(128)} %bitcast.refs_0_.where_ref, bf16[272,256]{1,0:T(8,128)(2,1)S(1)} %get-tuple-element.29.refs_1_.mine_ref.refs_3_, bf16[272,256]{1,0:T(8,128)(2,1)S(1)} %collective-permute-done.refs_2_.other_ref.refs_4_, ...), custom_call_target="tpu_custom_call" | custom-call | flops 1000000000 | bytes 4000000 | tf_op jit(solution)/shard_map/voxel_outputs/pallas_call | solution.py:278
  31.8 0.0 collective-permute-done.7
  31.8 1.4 %convert_add_fusion = f32[27,128,128]{2,1,0:T(8,128)} fusion(f32[27,128,128]{2,1,0:T(8,128)S(1)} %get-tuple-element.47, bf16[27,128,128]{2,1,0:T(8,128)(2,1)S(1)} %collective-permute-done.7), kind=kLoop, calls=%fused_computation | loop fusion | flops 884736 | bytes 4423680 | tf_op jit(solution)/shard_map/add | solution.py:296
Async XLA Ops:
  2.9 9.3 %collective-permute-start = (bf16[272,256]{1,0:T(8,128)(2,1)}, bf16[272,256]{1,0:T(8,128)(2,1)S(1)}, u32[]{:S(2)}, u32[]{:S(2)}) collective-permute-start(bf16[272,256]{1,0:T(8,128)(2,1)} %get-tuple-element.28.pack_ref), channel_id=1, source_target_pairs={{0,2},{2,0},{4,6},{6,4},{8,10},{10,8},{12,14},{14,12},{1,3},{3,1},... | collective-permute-start | bytes 417800 | tf_op jit(solution)/shard_map/ppermute | solution.py:212
  6.0 8.6 %collective-permute-start.1 = (bf16[272,256]{1,0:T(8,128)(2,1)}, bf16[272,256]{1,0:T(8,128)(2,1)S(1)}, u32[]{:S(2)}, u32[]{:S(2)}) collective-permute-start(bf16[272,256]{1,0:T(8,128)(2,1)} %get-tuple-element.28.pack_ref), channel_id=1, source_target_pairs={{0,4},{2,6},{4,8},{6,10},{8,12},{10,14},{12,0},{14,2},{1,5},{3,7},... | collective-permute-start | bytes 417800 | tf_op jit(solution)/shard_map/ppermute | solution.py:215
  7.5 8.0 %collective-permute-start.3 = (bf16[272,256]{1,0:T(8,128)(2,1)}, bf16[272,256]{1,0:T(8,128)(2,1)S(1)}, u32[]{:S(2)}, u32[]{:S(2)}) collective-permute-start(bf16[272,256]{1,0:T(8,128)(2,1)} %get-tuple-element.28.pack_ref), channel_id=1, source_target_pairs={{0,12},{2,14},{4,0},{6,2},{8,4},{10,6},{12,8},{14,10},{1,13},{3,15... | collective-permute-start | bytes 417800 | tf_op jit(solution)/shard_map/ppermute | solution.py:215
  9.8 1.2 %copy-start = (bf16[27,128,128]{2,1,0:T(8,128)(2,1)S(1)}, bf16[27,128,128]{2,1,0:T(8,128)(2,1)}, u32[]{:S(2)}) copy-start(bf16[27,128,128]{2,1,0:T(8,128)(2,1)} %w_ref) | copy-start | bytes 2654212
  10.9 0.9 %copy-start.1 = (bf16[272,256]{1,0:T(8,128)(2,1)S(1)}, bf16[272,256]{1,0:T(8,128)(2,1)}, u32[]{:S(2)}) copy-start(bf16[272,256]{1,0:T(8,128)(2,1)} %get-tuple-element.28.pack_ref) | copy-start | bytes 417796
  14.6 6.9 %collective-permute-start.5 = (bf16[272,256]{1,0:T(8,128)(2,1)S(1)}, bf16[272,256]{1,0:T(8,128)(2,1)S(1)}, u32[]{:S(2)}, u32[]{:S(2)}) collective-permute-start(bf16[272,256]{1,0:T(8,128)(2,1)S(1)} %collective-permute-done.1.before_mine.refs_1_.refs_3_), channel_id=1, source_target_pairs={{0,4},{2,6},{4,8},{6,10},{8,12},{10,14},{12,0},{14,2},{1,5},{3,7},... | collective-permute-start | bytes 417800 | tf_op jit(solution)/shard_map/ppermute | solution.py:215
  14.6 7.2 %collective-permute-start.2 = (bf16[272,256]{1,0:T(8,128)(2,1)S(1)}, bf16[272,256]{1,0:T(8,128)(2,1)S(1)}, u32[]{:S(2)}, u32[]{:S(2)}) collective-permute-start(bf16[272,256]{1,0:T(8,128)(2,1)S(1)} %collective-permute-done.1.before_mine.refs_1_.refs_3_), channel_id=1, source_target_pairs={{0,2},{2,0},{4,6},{6,4},{8,10},{10,8},{12,14},{14,12},{1,3},{3,1},... | collective-permute-start | bytes 417800 | tf_op jit(solution)/shard_map/ppermute | solution.py:212
  15.6 8.2 %collective-permute-start.4 = (bf16[272,256]{1,0:T(8,128)(2,1)S(1)}, bf16[272,256]{1,0:T(8,128)(2,1)S(1)}, u32[]{:S(2)}, u32[]{:S(2)}) collective-permute-start(bf16[272,256]{1,0:T(8,128)(2,1)S(1)} %collective-permute-done.3.after_mine.refs_1_.refs_5_), channel_id=1, source_target_pairs={{0,2},{2,0},{4,6},{6,4},{8,10},{10,8},{12,14},{14,12},{1,3},{3,1},... | collective-permute-start | bytes 417800 | tf_op jit(solution)/shard_map/ppermute | solution.py:212
  21.4 5.1 %collective-permute-start.6 = (bf16[272,256]{1,0:T(8,128)(2,1)S(1)}, bf16[272,256]{1,0:T(8,128)(2,1)S(1)}, u32[]{:S(2)}, u32[]{:S(2)}) collective-permute-start(bf16[272,256]{1,0:T(8,128)(2,1)S(1)} %collective-permute-done.5.refs_1_), channel_id=1, source_target_pairs={{0,2},{2,0},{4,6},{6,4},{8,10},{10,8},{12,14},{14,12},{1,3},{3,1},... | collective-permute-start | bytes 417800 | tf_op jit(solution)/shard_map/ppermute | solution.py:212
  26.5 2.6 %copy-start.2 = (bf16[1,256,128]{2,1,0:T(8,128)(2,1)S(1)}, bf16[1,256,128]{2,1,0:T(8,128)(2,1)}, u32[]{:S(2)}) copy-start(bf16[1,256,128]{2,1,0:T(8,128)(2,1)} %feat_hbm.1) | copy-start | bytes 196612
  26.5 2.6 %copy-start.3 = (s32[27,256]{1,0:T(8,128)S(1)}, s32[27,256]{1,0:T(8,128)}, u32[]{:S(2)}) copy-start(s32[27,256]{1,0:T(8,128)} %near_ref.1) | copy-start | bytes 82948
  26.5 2.6 %copy-start.4 = (f32[1,128]{1,0:T(1,128)S(1)}, f32[1,128]{1,0:T(1,128)}, u32[]{:S(2)}) copy-start(f32[1,128]{1,0:T(1,128)} %get-tuple-element.33.shift_ref) | copy-start | bytes 1540
  29.0 2.8 %collective-permute-start.7 = (bf16[27,128,128]{2,1,0:T(8,128)(2,1)S(1)}, bf16[27,128,128]{2,1,0:T(8,128)(2,1)S(1)}, u32[]{:S(2)}, u32[]{:S(2)}) collective-permute-start(bf16[27,128,128]{2,1,0:T(8,128)(2,1)S(1)} %get-tuple-element.48), channel_id=1, source_target_pairs={{0,1},{1,0},{2,3},{3,2},{4,5},{5,4},{6,7},{7,6},{8,9},{9,8},{10,11... | collective-permute-start | bytes 2654216 | tf_op jit(solution)/shard_map/ppermute | solution.py:277

commit v9 on v6

--- a/solution.py
+++ b/solution.py
@@ -13,6 +13,7 @@
 HALF = 13
 CODE_ROWS = 16
 ROW_STAGES = 4
+PACK_VMEM = 8 * 1024 * 1024
 KERNEL_VMEM = 24 * 1024 * 1024
 
 
@@ -27,6 +28,10 @@
     rows_here = TILE * STRIP
     code = (neighbours // rows_here) % tiles_y * STRIP + neighbours % STRIP
     return jnp.where(neighbours < 0, -1, code).astype(jnp.float32)
+
+
+def in_hbm(array):
+    return pltpu.with_memory_space_constraint(array, pltpu.HBM)
 
 
 def pack_kernel(time_ref, feat_hbm, cot_hbm, near_hbm, cond_hbm, wt_hbm, pack_ref, shift_ref,
@@ -203,8 +208,9 @@
             pltpu.VMEM((width, width), jnp.bfloat16),
             pltpu.SemaphoreType.DMA((5,)),
         ],
+        compiler_params=pltpu.CompilerParams(vmem_limit_bytes=PACK_VMEM),
         name="pack_tile",
-    )(timesteps, features, cotangent, neighbours, condition, w_time)
+    )(timesteps, *[in_hbm(array) for array in (features, cotangent, neighbours, condition, w_time)])
     here = lax.axis_index("brick").astype(jnp.int32).reshape(1)
 
     def across(block):

time: 32.6 us -> 31.7 us (0.972)
  local copies, waits for them, and re-layouts: 2.1 us -> 1.18 us
  Pallas kernels: 13.2 us -> 12.5 us
  waiting for transfers between devices: 2.62 us -> 3.31 us
    unnamed x12 -> x6, local copies, waits for them, and re-layouts: 2.1 us -> 1.18 us
    ppermute x3, waiting for transfers between devices: 2.6 us -> 3.3 us  [along(): lax.ppermute(block, 'brick', [(i, (i + turn * tiles_y) % peers) for i in...]
    pallas_call x1, Pallas kernels: 1.66 us -> 1 us  [whole_scene(): pl.pallas_call(pack_kernel, out_shape=(jax.ShapeDtypeStruct((rows + CODE_...]
  transfers between devices with their start and end apart: 8 -> 8, of which waited for: 2 -> 2; matrix products, arithmetic and copies ran while one was open for 0% -> 0% of each run, Pallas kernels for 28% -> 29%
where the time goes in v9:
time: 31.7 us; the launch traced here: 31.4 us
  Pallas kernels  12.5 us (39%)
  starting transfers between devices  11.6 us (37%)
  waiting for transfers between devices  3.31 us (10%)
  other arithmetic  1.42 us (4%)
  between operations  1.38 us (4%)
  local copies, waits for them, and re-layouts  1.18 us (4%)
    pallas_call x4, Pallas kernels, whole_scene(): pl.pallas_call(functools.partial(row_kernel, stage, strips, borders), out...  8.47 us
    ppermute x4, starting transfers between devices, across(): return lax.ppermute(block, 'brick', [(i, i ^ 1) for i in range(peers)])  6.4 us
    ppermute x3, starting transfers between devices, along(): lax.ppermute(block, 'brick', [(i, (i + turn * tiles_y) % peers) for i in...  5.17 us
    ppermute x3, waiting for transfers between devices, along(): lax.ppermute(block, 'brick', [(i, (i + turn * tiles_y) % peers) for i in...  3.3 us
    pallas_call x1, Pallas kernels, whole_scene(): pl.pallas_call(voxel_kernel, out_shape=(jax.ShapeDtypeStruct((rows, width...  2.65 us
    add x1, other arithmetic, whole_scene(): weight_grad = own + other.astype(jnp.float32)  1.42 us
    unnamed x6, local copies, waits for them, and re-layouts  1.18 us
    pallas_call x1, Pallas kernels, whole_scene(): pl.pallas_call(pack_kernel, out_shape=(jax.ShapeDtypeStruct((rows + CODE_...  1 us
  transfers between devices with their start and end apart: 8, of which 2 were waited for; matrix products, arithmetic and copies ran while one was open for 0% of the time, Pallas kernels for 29%

profile of v9, /device:TPU:0, one launch (start us, length us, event | category | flops | bytes accessed | tf_op | source)
XLA Modules:
  0.0 31.4 jit_solution(5443752569596361443)
XLA Ops:
  1.3 1.0 %pack_tile.1 = (bf16[272,256]{1,0:T(8,128)(2,1)S(1)}, f32[1,128]{1,0:T(1,128)S(1)}) custom-call(s32[1]{0:T(128)S(6)} %copy.10.time_ref, bf16[1,256,128]{2,1,0:T(8,128)(2,1)} %feat_hbm.1, bf16[1,256,128]{2,1,0:T(8,128)(2,1)} %cot_hbm.1, s32[27,256]{1,0:T(8,128)} %near_ref.1, bf16[1,128]{1,0:T(2,128)(2,1)} %cond_hbm.1, bf16[128,128]{1,0:T(8,128)(2,1)} %wt_hbm.1), custom_call_target="tpu_custom_call" | custom-call | tf_op jit(solution)/shard_map/pack_tile/pallas_call | solution.py:196
  2.3 3.1 %collective-permute-start.1 = (bf16[272,256]{1,0:T(8,128)(2,1)S(1)}, bf16[272,256]{1,0:T(8,128)(2,1)S(1)}, u32[]{:S(2)}, u32[]{:S(2)}) collective-permute-start(bf16[272,256]{1,0:T(8,128)(2,1)S(1)} %get-tuple-element.25.mine_ref.refs_1_.refs_3_), channel_id=1, source_target_pairs={{0,4},{2,6},{4,8},{6,10},{8,12},{10,14},{12,0},{14,2},{1,5},{3,7},... | collective-permute-start | bytes 417800 | tf_op jit(solution)/shard_map/ppermute | solution.py:220
  5.4 2.1 %collective-permute-start.3 = (bf16[272,256]{1,0:T(8,128)(2,1)S(1)}, bf16[272,256]{1,0:T(8,128)(2,1)S(1)}, u32[]{:S(2)}, u32[]{:S(2)}) collective-permute-start(bf16[272,256]{1,0:T(8,128)(2,1)S(1)} %get-tuple-element.25.mine_ref.refs_1_.refs_3_), channel_id=1, source_target_pairs={{0,12},{2,14},{4,0},{6,2},{8,4},{10,6},{12,8},{14,10},{1,13},{3,15... | collective-permute-start | bytes 417800 | tf_op jit(solution)/shard_map/ppermute | solution.py:220
  7.5 1.6 %collective-permute-start = (bf16[272,256]{1,0:T(8,128)(2,1)S(1)}, bf16[272,256]{1,0:T(8,128)(2,1)S(1)}, u32[]{:S(2)}, u32[]{:S(2)}) collective-permute-start(bf16[272,256]{1,0:T(8,128)(2,1)S(1)} %get-tuple-element.25.mine_ref.refs_1_.refs_3_), channel_id=1, source_target_pairs={{0,2},{2,0},{4,6},{6,4},{8,10},{10,8},{12,14},{14,12},{1,3},{3,1},... | collective-permute-start | bytes 417800 | tf_op jit(solution)/shard_map/ppermute | solution.py:217
  9.1 0.0 copy-start
  9.1 1.2 %copy-done = bf16[27,128,128]{2,1,0:T(8,128)(2,1)S(1)} copy-done((bf16[27,128,128]{2,1,0:T(8,128)(2,1)S(1)}, bf16[27,128,128]{2,1,0:T(8,128)(2,1)}, u32[]{:S(2)}) %copy-start) | copy-done | bytes 884760
  10.3 0.4 %turn_weights.1 = (bf16[128,3456]{1,0:T(8,128)(2,1)S(1)}, bf16[128,3456]{1,0:T(8,128)(2,1)S(1)}) custom-call(bf16[27,128,128]{2,1,0:T(8,128)(2,1)S(1)} %copy-done), custom_call_target="tpu_custom_call" | custom-call | flops 200000000 | bytes 3000000 | tf_op jit(solution)/shard_map/turn_weights/pallas_call | solution.py:223
  10.6 1.3 %collective-permute-done.1.before_mine.refs_1_.refs_3_ = bf16[272,256]{1,0:T(8,128)(2,1)S(1)} collective-permute-done((bf16[272,256]{1,0:T(8,128)(2,1)S(1)}, bf16[272,256]{1,0:T(8,128)(2,1)S(1)}, u32[]{:S(2)}, u32[]{:S(2)}) %collective-permute-start.1) | collective-permute-done | bytes 139296 | tf_op jit(solution)/shard_map/ppermute | solution.py:220
  11.9 0.0 collective-permute-start.5
  11.9 1.7 %collective-permute-start.2 = (bf16[272,256]{1,0:T(8,128)(2,1)S(1)}, bf16[272,256]{1,0:T(8,128)(2,1)S(1)}, u32[]{:S(2)}, u32[]{:S(2)}) collective-permute-start(bf16[272,256]{1,0:T(8,128)(2,1)S(1)} %collective-permute-done.1.before_mine.refs_1_.refs_3_), channel_id=1, source_target_pairs={{0,2},{2,0},{4,6},{6,4},{8,10},{10,8},{12,14},{14,12},{1,3},{3,1},... | collective-permute-start | bytes 417800 | tf_op jit(solution)/shard_map/ppermute | solution.py:217
  13.6 0.0 collective-permute-done.3.after_mine.refs_1_.refs_5_
  13.6 1.3 %collective-permute-start.4 = (bf16[272,256]{1,0:T(8,128)(2,1)S(1)}, bf16[272,256]{1,0:T(8,128)(2,1)S(1)}, u32[]{:S(2)}, u32[]{:S(2)}) collective-permute-start(bf16[272,256]{1,0:T(8,128)(2,1)S(1)} %collective-permute-done.3.after_mine.refs_1_.refs_5_), channel_id=1, source_target_pairs={{0,2},{2,0},{4,6},{6,4},{8,10},{10,8},{12,14},{14,12},{1,3},{3,1},... | collective-permute-start | bytes 417800 | tf_op jit(solution)/shard_map/ppermute | solution.py:217
  15.0 0.0 collective-permute-done.other_ref.refs_2_.refs_4_
  15.0 1.8 %weight_row_0.1 = (f32[1664,128]{1,0:T(8,128)S(1)}, f32[1664,128]{1,0:T(8,128)S(1)}, f32[128,128]{1,0:T(8,128)S(1)}) custom-call(s32[1]{0:T(128)} %bitcast.where_ref.refs_0_, bf16[272,256]{1,0:T(8,128)(2,1)S(1)} %get-tuple-element.25.mine_ref.refs_1_.refs_3_, bf16[272,256]{1,0:T(8,128)(2,1)S(1)} %collective-permute-done.other_ref.refs_2_.refs_4_), custom_call_target="tpu_custom_call" | custom-call | flops 2000000000 | bytes 4000000 | tf_op jit(solution)/shard_map/weight_row_0/pallas_call | solution.py:260
  16.7 2.0 %collective-permute-done.5.refs_1_ = bf16[272,256]{1,0:T(8,128)(2,1)S(1)} collective-permute-done((bf16[272,256]{1,0:T(8,128)(2,1)S(1)}, bf16[272,256]{1,0:T(8,128)(2,1)S(1)}, u32[]{:S(2)}, u32[]{:S(2)}) %collective-permute-start.5) | collective-permute-done | bytes 139296 | tf_op jit(solution)/shard_map/ppermute | solution.py:220
  18.8 1.7 %collective-permute-start.6 = (bf16[272,256]{1,0:T(8,128)(2,1)S(1)}, bf16[272,256]{1,0:T(8,128)(2,1)S(1)}, u32[]{:S(2)}, u32[]{:S(2)}) collective-permute-start(bf16[272,256]{1,0:T(8,128)(2,1)S(1)} %collective-permute-done.5.refs_1_), channel_id=1, source_target_pairs={{0,2},{2,0},{4,6},{6,4},{8,10},{10,8},{12,14},{14,12},{1,3},{3,1},... | collective-permute-start | bytes 417800 | tf_op jit(solution)/shard_map/ppermute | solution.py:217
  20.5 0.0 collective-permute-done.2.before_other.refs_2_.refs_4_
  20.5 2.1 %weight_row_1.1 = (f32[1664,128]{1,0:T(8,128)S(1)}, f32[1664,128]{1,0:T(8,128)S(1)}, f32[128,128]{1,0:T(8,128)S(1)}) custom-call(s32[1]{0:T(128)} %bitcast.where_ref.refs_0_, bf16[272,256]{1,0:T(8,128)(2,1)S(1)} %collective-permute-done.1.before_mine.refs_1_.refs_3_, bf16[272,256]{1,0:T(8,128)(2,1)S(1)} %collective-permute-done.2.before_other.refs_2_.refs_4_, ...), custom_call_target="tpu_custom_call" | custom-call | flops 2000000000 | bytes 4000000 | tf_op jit(solution)/shard_map/weight_row_1/pallas_call | solution.py:260
  22.6 0.0 collective-permute-done.4.after_other.refs_2_.refs_6_
  22.6 2.1 %weight_row_2.1 = (f32[1664,128]{1,0:T(8,128)S(1)}, f32[1664,128]{1,0:T(8,128)S(1)}, f32[128,128]{1,0:T(8,128)S(1)}) custom-call(s32[1]{0:T(128)} %bitcast.where_ref.refs_0_, bf16[272,256]{1,0:T(8,128)(2,1)S(1)} %collective-permute-done.3.after_mine.refs_1_.refs_5_, bf16[272,256]{1,0:T(8,128)(2,1)S(1)} %collective-permute-done.4.after_other.refs_2_.refs_6_, ...), custom_call_target="tpu_custom_call" | custom-call | flops 2000000000 | bytes 4000000 | tf_op jit(solution)/shard_map/weight_row_2/pallas_call | solution.py:260
  24.7 0.0 collective-permute-done.6.refs_2_
  24.7 0.0 copy-start.1
  24.7 0.0 copy-start.2
  24.7 2.5 %weight_row_3.1 = (f32[27,128,128]{2,1,0:T(8,128)S(1)}, bf16[27,128,128]{2,1,0:T(8,128)(2,1)S(1)}) custom-call(s32[1]{0:T(128)} %bitcast.where_ref.refs_0_, bf16[272,256]{1,0:T(8,128)(2,1)S(1)} %collective-permute-done.5.refs_1_, bf16[272,256]{1,0:T(8,128)(2,1)S(1)} %collective-permute-done.6.refs_2_, ...), custom_call_target="tpu_custom_call" | custom-call | flops 2000000000 | bytes 4000000 | tf_op jit(solution)/shard_map/weight_row_3/pallas_call | solution.py:260
  27.3 0.1 collective-permute-start.7
  27.3 0.0 copy-done.1
  27.3 0.0 copy-done.2
  27.4 2.7 %voxel_outputs.1 = (bf16[256,128]{1,0:T(8,128)(2,1)}, bf16[256,128]{1,0:T(8,128)(2,1)}) custom-call(s32[1]{0:T(128)} %bitcast.where_ref.refs_0_, bf16[272,256]{1,0:T(8,128)(2,1)S(1)} %get-tuple-element.25.mine_ref.refs_1_.refs_3_, bf16[272,256]{1,0:T(8,128)(2,1)S(1)} %collective-permute-done.other_ref.refs_2_.refs_4_, ...), custom_call_target="tpu_custom_call" | custom-call | flops 1000000000 | bytes 4000000 | tf_op jit(solution)/shard_map/voxel_outputs/pallas_call | solution.py:278
  30.0 0.0 collective-permute-done.7
  30.0 1.4 %convert_add_fusion = f32[27,128,128]{2,1,0:T(8,128)} fusion(f32[27,128,128]{2,1,0:T(8,128)S(1)} %get-tuple-element.43, bf16[27,128,128]{2,1,0:T(8,128)(2,1)S(1)} %collective-permute-done.7), kind=kLoop, calls=%fused_computation | loop fusion | flops 884736 | bytes 4423680 | tf_op jit(solution)/shard_map/add | solution.py:296
Async XLA Ops:
  2.3 9.6 %collective-permute-start.1 = (bf16[272,256]{1,0:T(8,128)(2,1)S(1)}, bf16[272,256]{1,0:T(8,128)(2,1)S(1)}, u32[]{:S(2)}, u32[]{:S(2)}) collective-permute-start(bf16[272,256]{1,0:T(8,128)(2,1)S(1)} %get-tuple-element.25.mine_ref.refs_1_.refs_3_), channel_id=1, source_target_pairs={{0,4},{2,6},{4,8},{6,10},{8,12},{10,14},{12,0},{14,2},{1,5},{3,7},... | collective-permute-start | bytes 417800 | tf_op jit(solution)/shard_map/ppermute | solution.py:220
  5.4 8.3 %collective-permute-start.3 = (bf16[272,256]{1,0:T(8,128)(2,1)S(1)}, bf16[272,256]{1,0:T(8,128)(2,1)S(1)}, u32[]{:S(2)}, u32[]{:S(2)}) collective-permute-start(bf16[272,256]{1,0:T(8,128)(2,1)S(1)} %get-tuple-element.25.mine_ref.refs_1_.refs_3_), channel_id=1, source_target_pairs={{0,12},{2,14},{4,0},{6,2},{8,4},{10,6},{12,8},{14,10},{1,13},{3,15... | collective-permute-start | bytes 417800 | tf_op jit(solution)/shard_map/ppermute | solution.py:220
  7.5 7.5 %collective-permute-start = (bf16[272,256]{1,0:T(8,128)(2,1)S(1)}, bf16[272,256]{1,0:T(8,128)(2,1)S(1)}, u32[]{:S(2)}, u32[]{:S(2)}) collective-permute-start(bf16[272,256]{1,0:T(8,128)(2,1)S(1)} %get-tuple-element.25.mine_ref.refs_1_.refs_3_), channel_id=1, source_target_pairs={{0,2},{2,0},{4,6},{6,4},{8,10},{10,8},{12,14},{14,12},{1,3},{3,1},... | collective-permute-start | bytes 417800 | tf_op jit(solution)/shard_map/ppermute | solution.py:217
  9.1 1.2 %copy-start = (bf16[27,128,128]{2,1,0:T(8,128)(2,1)S(1)}, bf16[27,128,128]{2,1,0:T(8,128)(2,1)}, u32[]{:S(2)}) copy-start(bf16[27,128,128]{2,1,0:T(8,128)(2,1)} %w_ref) | copy-start | bytes 2654212
  11.9 6.9 %collective-permute-start.5 = (bf16[272,256]{1,0:T(8,128)(2,1)S(1)}, bf16[272,256]{1,0:T(8,128)(2,1)S(1)}, u32[]{:S(2)}, u32[]{:S(2)}) collective-permute-start(bf16[272,256]{1,0:T(8,128)(2,1)S(1)} %collective-permute-done.1.before_mine.refs_1_.refs_3_), channel_id=1, source_target_pairs={{0,4},{2,6},{4,8},{6,10},{8,12},{10,14},{12,0},{14,2},{1,5},{3,7},... | collective-permute-start | bytes 417800 | tf_op jit(solution)/shard_map/ppermute | solution.py:220
  11.9 8.6 %collective-permute-start.2 = (bf16[272,256]{1,0:T(8,128)(2,1)S(1)}, bf16[272,256]{1,0:T(8,128)(2,1)S(1)}, u32[]{:S(2)}, u32[]{:S(2)}) collective-permute-start(bf16[272,256]{1,0:T(8,128)(2,1)S(1)} %collective-permute-done.1.before_mine.refs_1_.refs_3_), channel_id=1, source_target_pairs={{0,2},{2,0},{4,6},{6,4},{8,10},{10,8},{12,14},{14,12},{1,3},{3,1},... | collective-permute-start | bytes 417800 | tf_op jit(solution)/shard_map/ppermute | solution.py:217
  13.6 8.9 %collective-permute-start.4 = (bf16[272,256]{1,0:T(8,128)(2,1)S(1)}, bf16[272,256]{1,0:T(8,128)(2,1)S(1)}, u32[]{:S(2)}, u32[]{:S(2)}) collective-permute-start(bf16[272,256]{1,0:T(8,128)(2,1)S(1)} %collective-permute-done.3.after_mine.refs_1_.refs_5_), channel_id=1, source_target_pairs={{0,2},{2,0},{4,6},{6,4},{8,10},{10,8},{12,14},{14,12},{1,3},{3,1},... | collective-permute-start | bytes 417800 | tf_op jit(solution)/shard_map/ppermute | solution.py:217
  18.8 5.9 %collective-permute-start.6 = (bf16[272,256]{1,0:T(8,128)(2,1)S(1)}, bf16[272,256]{1,0:T(8,128)(2,1)S(1)}, u32[]{:S(2)}, u32[]{:S(2)}) collective-permute-start(bf16[272,256]{1,0:T(8,128)(2,1)S(1)} %collective-permute-done.5.refs_1_), channel_id=1, source_target_pairs={{0,2},{2,0},{4,6},{6,4},{8,10},{10,8},{12,14},{14,12},{1,3},{3,1},... | collective-permute-start | bytes 417800 | tf_op jit(solution)/shard_map/ppermute | solution.py:217
  24.7 2.6 %copy-start.1 = (bf16[1,256,128]{2,1,0:T(8,128)(2,1)S(1)}, bf16[1,256,128]{2,1,0:T(8,128)(2,1)}, u32[]{:S(2)}) copy-start(bf16[1,256,128]{2,1,0:T(8,128)(2,1)} %feat_hbm.1) | copy-start | bytes 196612
  24.7 2.6 %copy-start.2 = (s32[27,256]{1,0:T(8,128)S(1)}, s32[27,256]{1,0:T(8,128)}, u32[]{:S(2)}) copy-start(s32[27,256]{1,0:T(8,128)} %near_ref.1) | copy-start | bytes 82948
  27.3 2.8 %collective-permute-start.7 = (bf16[27,128,128]{2,1,0:T(8,128)(2,1)S(1)}, bf16[27,128,128]{2,1,0:T(8,128)(2,1)S(1)}, u32[]{:S(2)}, u32[]{:S(2)}) collective-permute-start(bf16[27,128,128]{2,1,0:T(8,128)(2,1)S(1)} %get-tuple-element.44), channel_id=1, source_target_pairs={{0,1},{1,0},{2,3},{3,2},{4,5},{5,4},{6,7},{7,6},{8,9},{9,8},{10,11... | collective-permute-start | bytes 2654216 | tf_op jit(solution)/shard_map/ppermute | solution.py:277

commit v10 on v9

--- a/solution.py
+++ b/solution.py
@@ -93,7 +93,7 @@
             first = jnp.where(tile_y == 0, both[0], both[1])
             second = jnp.where(tile_y == 0, both[1], both[0])
             codes[i] = jnp.concatenate([first, second], axis=1)
-        if i < TILE or i in [source for _, source in borders]:
+        if i < TILE or i in [strip for border in borders for strip in border]:
             turned[:, i * span:(i + 1) * span] = ground[i * span:(i + 1) * span, :].T
     place = lax.broadcasted_iota(jnp.int32, (span, span), 0).astype(jnp.float32)
 
@@ -114,8 +114,9 @@
     low_to = span * (targets[-1] + 1)
 
     def product(near, start, stop, first, last, side):
-        return jnp.dot(near[start * width:stop * width, first:last],
-                       ground[first:last, side * width:(side + 1) * width], preferred_element_type=jnp.float32)
+        return lax.dot_general(turned[side * width:(side + 1) * width, first:last],
+                               near[start * width:stop * width, first:last],
+                               (((1,), (1,)), ((), ())), preferred_element_type=jnp.float32)
 
     pieces = []
     for near, side in ((near_act, 1), (near_cot, 0)):
@@ -127,13 +128,13 @@
     for i, ((start, stop), value) in enumerate(pieces):
         turn = i // 2
         if not first_stage:
-            value = value + before[turn][start * width:stop * width, :]
+            value = value + before[turn][:, start * width:stop * width]
         if not final:
-            outs[turn][start * width:stop * width, :] = value
+            outs[turn][:, start * width:stop * width] = value
             continue
         for k in range(start, stop):
-            one = value[(k - start) * width:(k - start + 1) * width, :]
-            one, to = (one.T, 2 * HALF - k) if turn else (one, k)
+            one = value[:, (k - start) * width:(k - start + 1) * width]
+            one, to = (one, 2 * HALF - k) if turn else (one.T, k)
             outs[0][to] = one
             outs[1][to] = one.astype(jnp.bfloat16)
     if final:
@@ -253,8 +254,8 @@
             )
         else:
             out_shape = (
-                jax.ShapeDtypeStruct((HALF * width, width), jnp.float32),
-                jax.ShapeDtypeStruct((HALF * width, width), jnp.float32),
+                jax.ShapeDtypeStruct((width, HALF * width), jnp.float32),
+                jax.ShapeDtypeStruct((width, HALF * width), jnp.float32),
                 jax.ShapeDtypeStruct((width, width), jnp.float32),
             )
         sums = pl.pallas_call(

time: 31.7 us -> 32.1 us (1.013)
  Pallas kernels: 12.5 us -> 13.1 us
    pallas_call x4, Pallas kernels: 8.47 us -> 9.05 us  [whole_scene(): pl.pallas_call(functools.partial(row_kernel, stage, strips, borders), out...]
  transfers between devices with their start and end apart: 8 -> 8, of which waited for: 2 -> 2; matrix products, arithmetic and copies ran while one was open for 0% -> 0% of each run, Pallas kernels for 29% -> 30%
where the time goes in v10:
time: 32.1 us; the launch traced here: 31.9 us
  Pallas kernels  13.1 us (41%)
  starting transfers between devices  11.6 us (36%)
  waiting for transfers between devices  3.19 us (10%)
  other arithmetic  1.42 us (4%)
  between operations  1.39 us (4%)
  local copies, waits for them, and re-layouts  1.18 us (4%)
    pallas_call x4, Pallas kernels, whole_scene(): pl.pallas_call(functools.partial(row_kernel, stage, strips, borders), out...  9.05 us
    ppermute x4, starting transfers between devices, across(): return lax.ppermute(block, 'brick', [(i, i ^ 1) for i in range(peers)])  6.4 us
    ppermute x3, starting transfers between devices, along(): lax.ppermute(block, 'brick', [(i, (i + turn * tiles_y) % peers) for i in...  5.17 us
    ppermute x3, waiting for transfers between devices, along(): lax.ppermute(block, 'brick', [(i, (i + turn * tiles_y) % peers) for i in...  3.17 us
    pallas_call x1, Pallas kernels, whole_scene(): pl.pallas_call(voxel_kernel, out_shape=(jax.ShapeDtypeStruct((rows, width...  2.66 us
    add x1, other arithmetic, whole_scene(): weight_grad = own + other.astype(jnp.float32)  1.42 us
    unnamed x6, local copies, waits for them, and re-layouts  1.18 us
    pallas_call x1, Pallas kernels, whole_scene(): pl.pallas_call(pack_kernel, out_shape=(jax.ShapeDtypeStruct((rows + CODE_...  1 us
  transfers between devices with their start and end apart: 8, of which 2 were waited for; matrix products, arithmetic and copies ran while one was open for 0% of the time, Pallas kernels for 30%

profile of v10, /device:TPU:0, one launch (start us, length us, event | category | flops | bytes accessed | tf_op | source)
XLA Modules:
  0.0 31.9 jit_solution(8598337693241255911)
XLA Ops:
  1.3 1.0 %pack_tile.1 = (bf16[272,256]{1,0:T(8,128)(2,1)S(1)}, f32[1,128]{1,0:T(1,128)S(1)}) custom-call(s32[1]{0:T(128)S(6)} %copy.10.time_ref, bf16[1,256,128]{2,1,0:T(8,128)(2,1)} %feat_hbm.1, bf16[1,256,128]{2,1,0:T(8,128)(2,1)} %cot_hbm.1, s32[27,256]{1,0:T(8,128)} %near_ref.1, bf16[1,128]{1,0:T(2,128)(2,1)} %cond_hbm.1, bf16[128,128]{1,0:T(8,128)(2,1)} %wt_hbm.1), custom_call_target="tpu_custom_call" | custom-call | tf_op jit(solution)/shard_map/pack_tile/pallas_call | solution.py:197
  2.3 3.1 %collective-permute-start.1 = (bf16[272,256]{1,0:T(8,128)(2,1)S(1)}, bf16[272,256]{1,0:T(8,128)(2,1)S(1)}, u32[]{:S(2)}, u32[]{:S(2)}) collective-permute-start(bf16[272,256]{1,0:T(8,128)(2,1)S(1)} %get-tuple-element.25.mine_ref.refs_1_.refs_3_), channel_id=1, source_target_pairs={{0,4},{2,6},{4,8},{6,10},{8,12},{10,14},{12,0},{14,2},{1,5},{3,7},... | collective-permute-start | bytes 417800 | tf_op jit(solution)/shard_map/ppermute | solution.py:221
  5.4 2.1 %collective-permute-start.3 = (bf16[272,256]{1,0:T(8,128)(2,1)S(1)}, bf16[272,256]{1,0:T(8,128)(2,1)S(1)}, u32[]{:S(2)}, u32[]{:S(2)}) collective-permute-start(bf16[272,256]{1,0:T(8,128)(2,1)S(1)} %get-tuple-element.25.mine_ref.refs_1_.refs_3_), channel_id=1, source_target_pairs={{0,12},{2,14},{4,0},{6,2},{8,4},{10,6},{12,8},{14,10},{1,13},{3,15... | collective-permute-start | bytes 417800 | tf_op jit(solution)/shard_map/ppermute | solution.py:221
  7.5 1.6 %collective-permute-start = (bf16[272,256]{1,0:T(8,128)(2,1)S(1)}, bf16[272,256]{1,0:T(8,128)(2,1)S(1)}, u32[]{:S(2)}, u32[]{:S(2)}) collective-permute-start(bf16[272,256]{1,0:T(8,128)(2,1)S(1)} %get-tuple-element.25.mine_ref.refs_1_.refs_3_), channel_id=1, source_target_pairs={{0,2},{2,0},{4,6},{6,4},{8,10},{10,8},{12,14},{14,12},{1,3},{3,1},... | collective-permute-start | bytes 417800 | tf_op jit(solution)/shard_map/ppermute | solution.py:218
  9.1 0.0 copy-start
  9.1 1.2 %copy-done = bf16[27,128,128]{2,1,0:T(8,128)(2,1)S(1)} copy-done((bf16[27,128,128]{2,1,0:T(8,128)(2,1)S(1)}, bf16[27,128,128]{2,1,0:T(8,128)(2,1)}, u32[]{:S(2)}) %copy-start) | copy-done | bytes 884760
  10.3 0.4 %turn_weights.1 = (bf16[128,3456]{1,0:T(8,128)(2,1)S(1)}, bf16[128,3456]{1,0:T(8,128)(2,1)S(1)}) custom-call(bf16[27,128,128]{2,1,0:T(8,128)(2,1)S(1)} %copy-done), custom_call_target="tpu_custom_call" | custom-call | flops 200000000 | bytes 3000000 | tf_op jit(solution)/shard_map/turn_weights/pallas_call | solution.py:224
  10.6 1.3 %collective-permute-done.1.before_mine.refs_1_.refs_3_ = bf16[272,256]{1,0:T(8,128)(2,1)S(1)} collective-permute-done((bf16[272,256]{1,0:T(8,128)(2,1)S(1)}, bf16[272,256]{1,0:T(8,128)(2,1)S(1)}, u32[]{:S(2)}, u32[]{:S(2)}) %collective-permute-start.1) | collective-permute-done | bytes 139296 | tf_op jit(solution)/shard_map/ppermute | solution.py:221
  11.9 0.0 collective-permute-start.5
  11.9 1.7 %collective-permute-start.2 = (bf16[272,256]{1,0:T(8,128)(2,1)S(1)}, bf16[272,256]{1,0:T(8,128)(2,1)S(1)}, u32[]{:S(2)}, u32[]{:S(2)}) collective-permute-start(bf16[272,256]{1,0:T(8,128)(2,1)S(1)} %collective-permute-done.1.before_mine.refs_1_.refs_3_), channel_id=1, source_target_pairs={{0,2},{2,0},{4,6},{6,4},{8,10},{10,8},{12,14},{14,12},{1,3},{3,1},... | collective-permute-start | bytes 417800 | tf_op jit(solution)/shard_map/ppermute | solution.py:218
  13.6 0.0 collective-permute-done.3.after_mine.refs_1_.refs_5_
  13.6 1.3 %collective-permute-start.4 = (bf16[272,256]{1,0:T(8,128)(2,1)S(1)}, bf16[272,256]{1,0:T(8,128)(2,1)S(1)}, u32[]{:S(2)}, u32[]{:S(2)}) collective-permute-start(bf16[272,256]{1,0:T(8,128)(2,1)S(1)} %collective-permute-done.3.after_mine.refs_1_.refs_5_), channel_id=1, source_target_pairs={{0,2},{2,0},{4,6},{6,4},{8,10},{10,8},{12,14},{14,12},{1,3},{3,1},... | collective-permute-start | bytes 417800 | tf_op jit(solution)/shard_map/ppermute | solution.py:218
  15.0 0.0 collective-permute-done.other_ref.refs_2_.refs_4_
  15.0 1.9 %weight_row_0.1 = (f32[128,1664]{1,0:T(8,128)S(1)}, f32[128,1664]{1,0:T(8,128)S(1)}, f32[128,128]{1,0:T(8,128)S(1)}) custom-call(s32[1]{0:T(128)} %bitcast.where_ref.refs_0_, bf16[272,256]{1,0:T(8,128)(2,1)S(1)} %get-tuple-element.25.mine_ref.refs_1_.refs_3_, bf16[272,256]{1,0:T(8,128)(2,1)S(1)} %collective-permute-done.other_ref.refs_2_.refs_4_), custom_call_target="tpu_custom_call" | custom-call | flops 2000000000 | bytes 4000000 | tf_op jit(solution)/shard_map/weight_row_0/pallas_call | solution.py:261
  16.9 1.9 %collective-permute-done.5.refs_1_ = bf16[272,256]{1,0:T(8,128)(2,1)S(1)} collective-permute-done((bf16[272,256]{1,0:T(8,128)(2,1)S(1)}, bf16[272,256]{1,0:T(8,128)(2,1)S(1)}, u32[]{:S(2)}, u32[]{:S(2)}) %collective-permute-start.5) | collective-permute-done | bytes 139296 | tf_op jit(solution)/shard_map/ppermute | solution.py:221
  18.8 1.7 %collective-permute-start.6 = (bf16[272,256]{1,0:T(8,128)(2,1)S(1)}, bf16[272,256]{1,0:T(8,128)(2,1)S(1)}, u32[]{:S(2)}, u32[]{:S(2)}) collective-permute-start(bf16[272,256]{1,0:T(8,128)(2,1)S(1)} %collective-permute-done.5.refs_1_), channel_id=1, source_target_pairs={{0,2},{2,0},{4,6},{6,4},{8,10},{10,8},{12,14},{14,12},{1,3},{3,1},... | collective-permute-start | bytes 417800 | tf_op jit(solution)/shard_map/ppermute | solution.py:218
  20.5 0.0 collective-permute-done.2.before_other.refs_2_.refs_4_
  20.5 2.3 %weight_row_1.1 = (f32[128,1664]{1,0:T(8,128)S(1)}, f32[128,1664]{1,0:T(8,128)S(1)}, f32[128,128]{1,0:T(8,128)S(1)}) custom-call(s32[1]{0:T(128)} %bitcast.where_ref.refs_0_, bf16[272,256]{1,0:T(8,128)(2,1)S(1)} %collective-permute-done.1.before_mine.refs_1_.refs_3_, bf16[272,256]{1,0:T(8,128)(2,1)S(1)} %collective-permute-done.2.before_other.refs_2_.refs_4_, ...), custom_call_target="tpu_custom_call" | custom-call | flops 2000000000 | bytes 4000000 | tf_op jit(solution)/shard_map/weight_row_1/pallas_call | solution.py:261
  22.8 0.0 collective-permute-done.4.after_other.refs_2_.refs_6_
  22.8 2.3 %weight_row_2.1 = (f32[128,1664]{1,0:T(8,128)S(1)}, f32[128,1664]{1,0:T(8,128)S(1)}, f32[128,128]{1,0:T(8,128)S(1)}) custom-call(s32[1]{0:T(128)} %bitcast.where_ref.refs_0_, bf16[272,256]{1,0:T(8,128)(2,1)S(1)} %collective-permute-done.3.after_mine.refs_1_.refs_5_, bf16[272,256]{1,0:T(8,128)(2,1)S(1)} %collective-permute-done.4.after_other.refs_2_.refs_6_, ...), custom_call_target="tpu_custom_call" | custom-call | flops 2000000000 | bytes 4000000 | tf_op jit(solution)/shard_map/weight_row_2/pallas_call | solution.py:261
  25.1 0.0 collective-permute-done.6.refs_2_
  25.1 0.0 copy-start.1
  25.1 0.0 copy-start.2
  25.1 2.6 %weight_row_3.1 = (f32[27,128,128]{2,1,0:T(8,128)S(1)}, bf16[27,128,128]{2,1,0:T(8,128)(2,1)S(1)}) custom-call(s32[1]{0:T(128)} %bitcast.where_ref.refs_0_, bf16[272,256]{1,0:T(8,128)(2,1)S(1)} %collective-permute-done.5.refs_1_, bf16[272,256]{1,0:T(8,128)(2,1)S(1)} %collective-permute-done.6.refs_2_, ...), custom_call_target="tpu_custom_call" | custom-call | flops 2000000000 | bytes 4000000 | tf_op jit(solution)/shard_map/weight_row_3/pallas_call | solution.py:261
  27.7 0.1 collective-permute-start.7
  27.8 0.0 copy-done.1
  27.8 0.0 copy-done.2
  27.8 2.7 %voxel_outputs.1 = (bf16[256,128]{1,0:T(8,128)(2,1)}, bf16[256,128]{1,0:T(8,128)(2,1)}) custom-call(s32[1]{0:T(128)} %bitcast.where_ref.refs_0_, bf16[272,256]{1,0:T(8,128)(2,1)S(1)} %get-tuple-element.25.mine_ref.refs_1_.refs_3_, bf16[272,256]{1,0:T(8,128)(2,1)S(1)} %collective-permute-done.other_ref.refs_2_.refs_4_, ...), custom_call_target="tpu_custom_call" | custom-call | flops 1000000000 | bytes 4000000 | tf_op jit(solution)/shard_map/voxel_outputs/pallas_call | solution.py:279
  30.5 0.0 collective-permute-done.7
  30.5 1.4 %convert_add_fusion = f32[27,128,128]{2,1,0:T(8,128)} fusion(f32[27,128,128]{2,1,0:T(8,128)S(1)} %get-tuple-element.43, bf16[27,128,128]{2,1,0:T(8,128)(2,1)S(1)} %collective-permute-done.7), kind=kLoop, calls=%fused_computation | loop fusion | flops 884736 | bytes 4423680 | tf_op jit(solution)/shard_map/add | solution.py:297
Async XLA Ops:
  2.3 9.6 %collective-permute-start.1 = (bf16[272,256]{1,0:T(8,128)(2,1)S(1)}, bf16[272,256]{1,0:T(8,128)(2,1)S(1)}, u32[]{:S(2)}, u32[]{:S(2)}) collective-permute-start(bf16[272,256]{1,0:T(8,128)(2,1)S(1)} %get-tuple-element.25.mine_ref.refs_1_.refs_3_), channel_id=1, source_target_pairs={{0,4},{2,6},{4,8},{6,10},{8,12},{10,14},{12,0},{14,2},{1,5},{3,7},... | collective-permute-start | bytes 417800 | tf_op jit(solution)/shard_map/ppermute | solution.py:221
  5.4 8.3 %collective-permute-start.3 = (bf16[272,256]{1,0:T(8,128)(2,1)S(1)}, bf16[272,256]{1,0:T(8,128)(2,1)S(1)}, u32[]{:S(2)}, u32[]{:S(2)}) collective-permute-start(bf16[272,256]{1,0:T(8,128)(2,1)S(1)} %get-tuple-element.25.mine_ref.refs_1_.refs_3_), channel_id=1, source_target_pairs={{0,12},{2,14},{4,0},{6,2},{8,4},{10,6},{12,8},{14,10},{1,13},{3,15... | collective-permute-start | bytes 417800 | tf_op jit(solution)/shard_map/ppermute | solution.py:221
  7.5 7.5 %collective-permute-start = (bf16[272,256]{1,0:T(8,128)(2,1)S(1)}, bf16[272,256]{1,0:T(8,128)(2,1)S(1)}, u32[]{:S(2)}, u32[]{:S(2)}) collective-permute-start(bf16[272,256]{1,0:T(8,128)(2,1)S(1)} %get-tuple-element.25.mine_ref.refs_1_.refs_3_), channel_id=1, source_target_pairs={{0,2},{2,0},{4,6},{6,4},{8,10},{10,8},{12,14},{14,12},{1,3},{3,1},... | collective-permute-start | bytes 417800 | tf_op jit(solution)/shard_map/ppermute | solution.py:218
  9.1 1.2 %copy-start = (bf16[27,128,128]{2,1,0:T(8,128)(2,1)S(1)}, bf16[27,128,128]{2,1,0:T(8,128)(2,1)}, u32[]{:S(2)}) copy-start(bf16[27,128,128]{2,1,0:T(8,128)(2,1)} %w_ref) | copy-start | bytes 2654212
  11.9 6.9 %collective-permute-start.5 = (bf16[272,256]{1,0:T(8,128)(2,1)S(1)}, bf16[272,256]{1,0:T(8,128)(2,1)S(1)}, u32[]{:S(2)}, u32[]{:S(2)}) collective-permute-start(bf16[272,256]{1,0:T(8,128)(2,1)S(1)} %collective-permute-done.1.before_mine.refs_1_.refs_3_), channel_id=1, source_target_pairs={{0,4},{2,6},{4,8},{6,10},{8,12},{10,14},{12,0},{14,2},{1,5},{3,7},... | collective-permute-start | bytes 417800 | tf_op jit(solution)/shard_map/ppermute | solution.py:221
  11.9 8.6 %collective-permute-start.2 = (bf16[272,256]{1,0:T(8,128)(2,1)S(1)}, bf16[272,256]{1,0:T(8,128)(2,1)S(1)}, u32[]{:S(2)}, u32[]{:S(2)}) collective-permute-start(bf16[272,256]{1,0:T(8,128)(2,1)S(1)} %collective-permute-done.1.before_mine.refs_1_.refs_3_), channel_id=1, source_target_pairs={{0,2},{2,0},{4,6},{6,4},{8,10},{10,8},{12,14},{14,12},{1,3},{3,1},... | collective-permute-start | bytes 417800 | tf_op jit(solution)/shard_map/ppermute | solution.py:218
  13.6 9.2 %collective-permute-start.4 = (bf16[272,256]{1,0:T(8,128)(2,1)S(1)}, bf16[272,256]{1,0:T(8,128)(2,1)S(1)}, u32[]{:S(2)}, u32[]{:S(2)}) collective-permute-start(bf16[272,256]{1,0:T(8,128)(2,1)S(1)} %collective-permute-done.3.after_mine.refs_1_.refs_5_), channel_id=1, source_target_pairs={{0,2},{2,0},{4,6},{6,4},{8,10},{10,8},{12,14},{14,12},{1,3},{3,1},... | collective-permute-start | bytes 417800 | tf_op jit(solution)/shard_map/ppermute | solution.py:218
  18.8 6.3 %collective-permute-start.6 = (bf16[272,256]{1,0:T(8,128)(2,1)S(1)}, bf16[272,256]{1,0:T(8,128)(2,1)S(1)}, u32[]{:S(2)}, u32[]{:S(2)}) collective-permute-start(bf16[272,256]{1,0:T(8,128)(2,1)S(1)} %collective-permute-done.5.refs_1_), channel_id=1, source_target_pairs={{0,2},{2,0},{4,6},{6,4},{8,10},{10,8},{12,14},{14,12},{1,3},{3,1},... | collective-permute-start | bytes 417800 | tf_op jit(solution)/shard_map/ppermute | solution.py:218
  25.1 2.7 %copy-start.1 = (bf16[1,256,128]{2,1,0:T(8,128)(2,1)S(1)}, bf16[1,256,128]{2,1,0:T(8,128)(2,1)}, u32[]{:S(2)}) copy-start(bf16[1,256,128]{2,1,0:T(8,128)(2,1)} %feat_hbm.1) | copy-start | bytes 196612
  25.1 2.7 %copy-start.2 = (s32[27,256]{1,0:T(8,128)S(1)}, s32[27,256]{1,0:T(8,128)}, u32[]{:S(2)}) copy-start(s32[27,256]{1,0:T(8,128)} %near_ref.1) | copy-start | bytes 82948
  27.7 2.8 %collective-permute-start.7 = (bf16[27,128,128]{2,1,0:T(8,128)(2,1)S(1)}, bf16[27,128,128]{2,1,0:T(8,128)(2,1)S(1)}, u32[]{:S(2)}, u32[]{:S(2)}) collective-permute-start(bf16[27,128,128]{2,1,0:T(8,128)(2,1)S(1)} %get-tuple-element.44), channel_id=1, source_target_pairs={{0,1},{1,0},{2,3},{3,2},{4,5},{5,4},{6,7},{7,6},{8,9},{9,8},{10,11... | collective-permute-start | bytes 2654216 | tf_op jit(solution)/shard_map/ppermute | solution.py:278

commit v11 on v9

--- a/solution.py
+++ b/solution.py
@@ -13,6 +13,7 @@
 HALF = 13
 CODE_ROWS = 16
 ROW_STAGES = 4
+FINISH_STEP = 3
 PACK_VMEM = 8 * 1024 * 1024
 KERNEL_VMEM = 24 * 1024 * 1024
 
@@ -150,10 +151,9 @@
         back_ref[:, k * width:(k + 1) * width] = w_ref[26 - k]
 
 
-def voxel_kernel(where_ref, mine_ref, other_ref, before_mine, before_other, after_mine, after_other,
-                 near_ref, feat_ref, shift_ref, forward_ref, back_ref, conv_ref, grad_ref,
-                 ground, turned, codes, near_act, near_cot):
-    width = feat_ref.shape[1]
+def conv_kernel(where_ref, mine_ref, other_ref, before_mine, before_other, after_mine, after_other,
+                near_ref, forward_ref, conv_ref, near_cot, ground, turned, codes, near_act):
+    width = conv_ref.shape[1]
     span = 2 * STRIP
     tile_y = where_ref[0] % 2
     lay_strip(ground, 0, tile_y, before_mine, before_other, TILE - 1)
@@ -180,10 +180,24 @@
                 near_cot[k * width:(k + 1) * width, at:at + span] = one[width:]
     conv = jnp.dot(forward_ref[...], near_act[...], preferred_element_type=jnp.float32)
     conv_ref[...] = conv.T.astype(jnp.bfloat16)
-    back = jnp.dot(back_ref[...], near_cot[...], preferred_element_type=jnp.float32).T
+
+
+def finish_kernel(kept_ref, sent_ref, near_ref, back_ref, feat_ref, shift_ref, weight_hbm, grad_hbm,
+                  weight, grad, sems):
+    copies = []
+    for i, first in enumerate(range(0, 27, FINISH_STEP)):
+        part = slice(first, first + FINISH_STEP)
+        weight[part] = kept_ref[part] + sent_ref[part].astype(jnp.float32)
+        copies.append(pltpu.make_async_copy(weight.at[part], weight_hbm.at[part], sems.at[i]))
+        copies[-1].start()
+    back = jnp.dot(back_ref[...], near_ref[...], preferred_element_type=jnp.float32).T
     z_val = feat_ref[...].astype(jnp.float32) + shift_ref[...]
     sig = jax.nn.sigmoid(z_val)
-    grad_ref[...] = (back * sig * (1.0 + z_val * (1.0 - sig))).astype(jnp.bfloat16)
+    grad[...] = (back * sig * (1.0 + z_val * (1.0 - sig))).astype(jnp.bfloat16)
+    copies.append(pltpu.make_async_copy(grad, grad_hbm, sems.at[len(copies)]))
+    copies[-1].start()
+    for copy in copies:
+        copy.wait()
 
 
 def whole_scene(features, cotangent, neighbours, timesteps, condition, w_time, w_conv, tiles_x, tiles_y):
@@ -275,25 +289,42 @@
         )(here, *blocks, *sums)
     own, sent = sums
     other = lax.ppermute(sent, "batch", [(0, 1), (1, 0)])
-    conv_out, feature_grad = pl.pallas_call(
-        voxel_kernel,
+    conv_out, near_cot = pl.pallas_call(
+        conv_kernel,
         out_shape=(
             jax.ShapeDtypeStruct((rows, width), jnp.bfloat16),
-            jax.ShapeDtypeStruct((rows, width), jnp.bfloat16),
+            jax.ShapeDtypeStruct((27 * width, rows), jnp.bfloat16),
         ),
-        in_specs=[smem] + [vmem] * 11,
+        in_specs=[smem] + [vmem] * 8,
+        out_specs=(vmem, vmem),
         scratch_shapes=[
             pltpu.VMEM(((TILE + 2) * span, 2 * width), jnp.bfloat16),
             pltpu.VMEM((2 * width, (TILE + 2) * span), jnp.bfloat16),
             pltpu.VMEM((27, rows), jnp.float32),
             pltpu.VMEM((27 * width, rows), jnp.bfloat16),
-            pltpu.VMEM((27 * width, rows), jnp.bfloat16),
         ],
         compiler_params=params,
         cost_estimate=pl.CostEstimate(flops=10**9, bytes_accessed=4 * 10**6, transcendentals=0),
-        name="voxel_outputs",
-    )(here, *own_pair, *before_pair, *after_pair, neighbours, features[0], shift, w_forward, w_back)
-    weight_grad = own + other.astype(jnp.float32)
+        name="conv_out",
+    )(here, *own_pair, *before_pair, *after_pair, neighbours, w_forward)
+    other, near_cot = lax.optimization_barrier((other, near_cot))
+    hbm = pl.BlockSpec(memory_space=pltpu.HBM)
+    weight_grad, feature_grad = pl.pallas_call(
+        finish_kernel,
+        out_shape=(
+            jax.ShapeDtypeStruct((27, width, width), jnp.float32),
+            jax.ShapeDtypeStruct((rows, width), jnp.bfloat16),
+        ),
+        in_specs=[vmem] * 6,
+        out_specs=(hbm, hbm),
+        scratch_shapes=[
+            pltpu.VMEM((27, width, width), jnp.float32),
+            pltpu.VMEM((rows, width), jnp.bfloat16),
+            pltpu.SemaphoreType.DMA((27 // FINISH_STEP + 1,)),
+        ],
+        compiler_params=pltpu.CompilerParams(vmem_limit_bytes=PACK_VMEM),
+        name="finish",
+    )(own, other, near_cot, w_back, features[0], shift)
     return (conv_out[None], feature_grad[None], weight_grad)
 
 

time: 31.7 us -> 31.8 us (level)
  Pallas kernels: 12.5 us -> 14 us
  other arithmetic: 1.42 us -> 0 us
    pallas_call x1 -> x2, Pallas kernels: 2.65 us -> 4.18 us  [the longest x1 2.45 us: whole_scene(): pl.pallas_call(conv_kernel, out_shape=(jax.ShapeDtypeStruct((rows, width)...]
    add x1 -> x0, other arithmetic: 1.42 us -> none  [whole_scene(): weight_grad = own + other.astype(jnp.float32)]
  transfers between devices with their start and end apart: 8 -> 8, of which waited for: 2 -> 2; matrix products, arithmetic and copies ran while one was open for 0% -> 0% of each run, Pallas kernels for 29% -> 28%
where the time goes in v11:
time: 31.8 us; the launch traced here: 31.5 us
  Pallas kernels  14 us (44%)
  starting transfers between devices  11.6 us (36%)
  waiting for transfers between devices  3.31 us (10%)
  between operations  1.37 us (4%)
  local copies, waits for them, and re-layouts  1.18 us (4%)
    pallas_call x4, Pallas kernels, whole_scene(): pl.pallas_call(functools.partial(row_kernel, stage, strips, borders), out...  8.47 us
    ppermute x4, starting transfers between devices, across(): return lax.ppermute(block, 'brick', [(i, i ^ 1) for i in range(peers)])  6.4 us
    ppermute x3, starting transfers between devices, along(): lax.ppermute(block, 'brick', [(i, (i + turn * tiles_y) % peers) for i in...  5.17 us
    ppermute x3, waiting for transfers between devices, along(): lax.ppermute(block, 'brick', [(i, (i + turn * tiles_y) % peers) for i in...  3.3 us
    pallas_call x1, Pallas kernels, whole_scene(): pl.pallas_call(conv_kernel, out_shape=(jax.ShapeDtypeStruct((rows, width)...  2.45 us
    pallas_call x1, Pallas kernels, whole_scene(): pl.pallas_call(finish_kernel, out_shape=(jax.ShapeDtypeStruct((27, width,...  1.73 us
    unnamed x6, local copies, waits for them, and re-layouts  1.18 us
    pallas_call x1, Pallas kernels, whole_scene(): pl.pallas_call(pack_kernel, out_shape=(jax.ShapeDtypeStruct((rows + CODE_...  1 us
  transfers between devices with their start and end apart: 8, of which 2 were waited for; matrix products, arithmetic and copies ran while one was open for 0% of the time, Pallas kernels for 28%

profile of v11, /device:TPU:0, one launch (start us, length us, event | category | flops | bytes accessed | tf_op | source)
XLA Modules:
  0.0 31.5 jit_solution(14067621488265668996)
XLA Ops:
  1.3 1.0 %pack_tile.1 = (bf16[272,256]{1,0:T(8,128)(2,1)S(1)}, f32[1,128]{1,0:T(1,128)S(1)}) custom-call(s32[1]{0:T(128)S(6)} %copy.10.time_ref, bf16[1,256,128]{2,1,0:T(8,128)(2,1)} %feat_hbm.1, bf16[1,256,128]{2,1,0:T(8,128)(2,1)} %cot_hbm.1, s32[27,256]{1,0:T(8,128)} %near_ref.1, bf16[1,128]{1,0:T(2,128)(2,1)} %cond_hbm.1, bf16[128,128]{1,0:T(8,128)(2,1)} %wt_hbm.1), custom_call_target="tpu_custom_call" | custom-call | tf_op jit(solution)/shard_map/pack_tile/pallas_call | solution.py:210
  2.3 3.1 %collective-permute-start.1 = (bf16[272,256]{1,0:T(8,128)(2,1)S(1)}, bf16[272,256]{1,0:T(8,128)(2,1)S(1)}, u32[]{:S(2)}, u32[]{:S(2)}) collective-permute-start(bf16[272,256]{1,0:T(8,128)(2,1)S(1)} %get-tuple-element.29.mine_ref.refs_1_.refs_3_), channel_id=1, source_target_pairs={{0,4},{2,6},{4,8},{6,10},{8,12},{10,14},{12,0},{14,2},{1,5},{3,7},... | collective-permute-start | bytes 417800 | tf_op jit(solution)/shard_map/ppermute | solution.py:234
  5.4 2.1 %collective-permute-start.3 = (bf16[272,256]{1,0:T(8,128)(2,1)S(1)}, bf16[272,256]{1,0:T(8,128)(2,1)S(1)}, u32[]{:S(2)}, u32[]{:S(2)}) collective-permute-start(bf16[272,256]{1,0:T(8,128)(2,1)S(1)} %get-tuple-element.29.mine_ref.refs_1_.refs_3_), channel_id=1, source_target_pairs={{0,12},{2,14},{4,0},{6,2},{8,4},{10,6},{12,8},{14,10},{1,13},{3,15... | collective-permute-start | bytes 417800 | tf_op jit(solution)/shard_map/ppermute | solution.py:234
  7.5 1.6 %collective-permute-start = (bf16[272,256]{1,0:T(8,128)(2,1)S(1)}, bf16[272,256]{1,0:T(8,128)(2,1)S(1)}, u32[]{:S(2)}, u32[]{:S(2)}) collective-permute-start(bf16[272,256]{1,0:T(8,128)(2,1)S(1)} %get-tuple-element.29.mine_ref.refs_1_.refs_3_), channel_id=1, source_target_pairs={{0,2},{2,0},{4,6},{6,4},{8,10},{10,8},{12,14},{14,12},{1,3},{3,1},... | collective-permute-start | bytes 417800 | tf_op jit(solution)/shard_map/ppermute | solution.py:231
  9.1 0.0 copy-start
  9.1 1.2 %copy-done = bf16[27,128,128]{2,1,0:T(8,128)(2,1)S(1)} copy-done((bf16[27,128,128]{2,1,0:T(8,128)(2,1)S(1)}, bf16[27,128,128]{2,1,0:T(8,128)(2,1)}, u32[]{:S(2)}) %copy-start) | copy-done | bytes 884760
  10.3 0.4 %turn_weights.1 = (bf16[128,3456]{1,0:T(8,128)(2,1)S(1)}, bf16[128,3456]{1,0:T(8,128)(2,1)S(1)}) custom-call(bf16[27,128,128]{2,1,0:T(8,128)(2,1)S(1)} %copy-done), custom_call_target="tpu_custom_call" | custom-call | flops 200000000 | bytes 3000000 | tf_op jit(solution)/shard_map/turn_weights/pallas_call | solution.py:237
  10.6 1.3 %collective-permute-done.1.before_mine.refs_1_.refs_3_ = bf16[272,256]{1,0:T(8,128)(2,1)S(1)} collective-permute-done((bf16[272,256]{1,0:T(8,128)(2,1)S(1)}, bf16[272,256]{1,0:T(8,128)(2,1)S(1)}, u32[]{:S(2)}, u32[]{:S(2)}) %collective-permute-start.1) | collective-permute-done | bytes 139296 | tf_op jit(solution)/shard_map/ppermute | solution.py:234
  11.9 0.0 collective-permute-start.5
  11.9 1.7 %collective-permute-start.2 = (bf16[272,256]{1,0:T(8,128)(2,1)S(1)}, bf16[272,256]{1,0:T(8,128)(2,1)S(1)}, u32[]{:S(2)}, u32[]{:S(2)}) collective-permute-start(bf16[272,256]{1,0:T(8,128)(2,1)S(1)} %collective-permute-done.1.before_mine.refs_1_.refs_3_), channel_id=1, source_target_pairs={{0,2},{2,0},{4,6},{6,4},{8,10},{10,8},{12,14},{14,12},{1,3},{3,1},... | collective-permute-start | bytes 417800 | tf_op jit(solution)/shard_map/ppermute | solution.py:231
  13.6 0.0 collective-permute-done.3.after_mine.refs_1_.refs_5_
  13.6 1.3 %collective-permute-start.4 = (bf16[272,256]{1,0:T(8,128)(2,1)S(1)}, bf16[272,256]{1,0:T(8,128)(2,1)S(1)}, u32[]{:S(2)}, u32[]{:S(2)}) collective-permute-start(bf16[272,256]{1,0:T(8,128)(2,1)S(1)} %collective-permute-done.3.after_mine.refs_1_.refs_5_), channel_id=1, source_target_pairs={{0,2},{2,0},{4,6},{6,4},{8,10},{10,8},{12,14},{14,12},{1,3},{3,1},... | collective-permute-start | bytes 417800 | tf_op jit(solution)/shard_map/ppermute | solution.py:231
  15.0 0.0 collective-permute-done.other_ref.refs_2_.refs_4_
  15.0 1.8 %weight_row_0.1 = (f32[1664,128]{1,0:T(8,128)S(1)}, f32[1664,128]{1,0:T(8,128)S(1)}, f32[128,128]{1,0:T(8,128)S(1)}) custom-call(s32[1]{0:T(128)} %bitcast.where_ref.refs_0_, bf16[272,256]{1,0:T(8,128)(2,1)S(1)} %get-tuple-element.29.mine_ref.refs_1_.refs_3_, bf16[272,256]{1,0:T(8,128)(2,1)S(1)} %collective-permute-done.other_ref.refs_2_.refs_4_), custom_call_target="tpu_custom_call" | custom-call | flops 2000000000 | bytes 4000000 | tf_op jit(solution)/shard_map/weight_row_0/pallas_call | solution.py:274
  16.7 2.0 %collective-permute-done.5.refs_1_ = bf16[272,256]{1,0:T(8,128)(2,1)S(1)} collective-permute-done((bf16[272,256]{1,0:T(8,128)(2,1)S(1)}, bf16[272,256]{1,0:T(8,128)(2,1)S(1)}, u32[]{:S(2)}, u32[]{:S(2)}) %collective-permute-start.5) | collective-permute-done | bytes 139296 | tf_op jit(solution)/shard_map/ppermute | solution.py:234
  18.8 1.7 %collective-permute-start.6 = (bf16[272,256]{1,0:T(8,128)(2,1)S(1)}, bf16[272,256]{1,0:T(8,128)(2,1)S(1)}, u32[]{:S(2)}, u32[]{:S(2)}) collective-permute-start(bf16[272,256]{1,0:T(8,128)(2,1)S(1)} %collective-permute-done.5.refs_1_), channel_id=1, source_target_pairs={{0,2},{2,0},{4,6},{6,4},{8,10},{10,8},{12,14},{14,12},{1,3},{3,1},... | collective-permute-start | bytes 417800 | tf_op jit(solution)/shard_map/ppermute | solution.py:231
  20.5 0.0 collective-permute-done.2.before_other.refs_2_.refs_4_
  20.5 2.1 %weight_row_1.1 = (f32[1664,128]{1,0:T(8,128)S(1)}, f32[1664,128]{1,0:T(8,128)S(1)}, f32[128,128]{1,0:T(8,128)S(1)}) custom-call(s32[1]{0:T(128)} %bitcast.where_ref.refs_0_, bf16[272,256]{1,0:T(8,128)(2,1)S(1)} %collective-permute-done.1.before_mine.refs_1_.refs_3_, bf16[272,256]{1,0:T(8,128)(2,1)S(1)} %collective-permute-done.2.before_other.refs_2_.refs_4_, ...), custom_call_target="tpu_custom_call" | custom-call | flops 2000000000 | bytes 4000000 | tf_op jit(solution)/shard_map/weight_row_1/pallas_call | solution.py:274
  22.6 0.0 collective-permute-done.4.after_other.refs_2_.refs_6_
  22.6 2.1 %weight_row_2.1 = (f32[1664,128]{1,0:T(8,128)S(1)}, f32[1664,128]{1,0:T(8,128)S(1)}, f32[128,128]{1,0:T(8,128)S(1)}) custom-call(s32[1]{0:T(128)} %bitcast.where_ref.refs_0_, bf16[272,256]{1,0:T(8,128)(2,1)S(1)} %collective-permute-done.3.after_mine.refs_1_.refs_5_, bf16[272,256]{1,0:T(8,128)(2,1)S(1)} %collective-permute-done.4.after_other.refs_2_.refs_6_, ...), custom_call_target="tpu_custom_call" | custom-call | flops 2000000000 | bytes 4000000 | tf_op jit(solution)/shard_map/weight_row_2/pallas_call | solution.py:274
  24.7 0.0 collective-permute-done.6.refs_2_
  24.7 0.0 copy-start.2
  24.7 2.5 %weight_row_3.1 = (f32[27,128,128]{2,1,0:T(8,128)S(1)}, bf16[27,128,128]{2,1,0:T(8,128)(2,1)S(1)}) custom-call(s32[1]{0:T(128)} %bitcast.where_ref.refs_0_, bf16[272,256]{1,0:T(8,128)(2,1)S(1)} %collective-permute-done.5.refs_1_, bf16[272,256]{1,0:T(8,128)(2,1)S(1)} %collective-permute-done.6.refs_2_, ...), custom_call_target="tpu_custom_call" | custom-call | flops 2000000000 | bytes 4000000 | tf_op jit(solution)/shard_map/weight_row_3/pallas_call | solution.py:274
  27.2 0.0 copy-start.1
  27.3 0.1 collective-permute-start.7
  27.3 0.0 copy-done.2
  27.3 2.5 %conv_out.1 = (bf16[256,128]{1,0:T(8,128)(2,1)}, bf16[3456,256]{1,0:T(8,128)(2,1)S(1)}) custom-call(s32[1]{0:T(128)} %bitcast.where_ref.refs_0_, bf16[272,256]{1,0:T(8,128)(2,1)S(1)} %get-tuple-element.29.mine_ref.refs_1_.refs_3_, bf16[272,256]{1,0:T(8,128)(2,1)S(1)} %collective-permute-done.other_ref.refs_2_.refs_4_, ...), custom_call_target="tpu_custom_call" | custom-call | flops 1000000000 | bytes 4000000 | tf_op jit(solution)/shard_map/conv_out/pallas_call | solution.py:292
  29.8 0.0 collective-permute-done.7.sent_ref
  29.8 0.0 copy-done.1
  29.8 1.7 %finish.1 = (f32[27,128,128]{2,1,0:T(8,128)}, bf16[256,128]{1,0:T(8,128)(2,1)}) custom-call(f32[27,128,128]{2,1,0:T(8,128)S(1)} %get-tuple-element.44.kept_ref, bf16[27,128,128]{2,1,0:T(8,128)(2,1)S(1)} %collective-permute-done.7.sent_ref, bf16[3456,256]{1,0:T(8,128)(2,1)S(1)} %get-tuple-element.48.near_ref, ...), custom_call_target="tpu_custom_call" | custom-call | tf_op jit(solution)/shard_map/finish/pallas_call | solution.py:312
Async XLA Ops:
  2.3 9.6 %collective-permute-start.1 = (bf16[272,256]{1,0:T(8,128)(2,1)S(1)}, bf16[272,256]{1,0:T(8,128)(2,1)S(1)}, u32[]{:S(2)}, u32[]{:S(2)}) collective-permute-start(bf16[272,256]{1,0:T(8,128)(2,1)S(1)} %get-tuple-element.29.mine_ref.refs_1_.refs_3_), channel_id=1, source_target_pairs={{0,4},{2,6},{4,8},{6,10},{8,12},{10,14},{12,0},{14,2},{1,5},{3,7},... | collective-permute-start | bytes 417800 | tf_op jit(solution)/shard_map/ppermute | solution.py:234
  5.4 8.3 %collective-permute-start.3 = (bf16[272,256]{1,0:T(8,128)(2,1)S(1)}, bf16[272,256]{1,0:T(8,128)(2,1)S(1)}, u32[]{:S(2)}, u32[]{:S(2)}) collective-permute-start(bf16[272,256]{1,0:T(8,128)(2,1)S(1)} %get-tuple-element.29.mine_ref.refs_1_.refs_3_), channel_id=1, source_target_pairs={{0,12},{2,14},{4,0},{6,2},{8,4},{10,6},{12,8},{14,10},{1,13},{3,15... | collective-permute-start | bytes 417800 | tf_op jit(solution)/shard_map/ppermute | solution.py:234
  7.5 7.5 %collective-permute-start = (bf16[272,256]{1,0:T(8,128)(2,1)S(1)}, bf16[272,256]{1,0:T(8,128)(2,1)S(1)}, u32[]{:S(2)}, u32[]{:S(2)}) collective-permute-start(bf16[272,256]{1,0:T(8,128)(2,1)S(1)} %get-tuple-element.29.mine_ref.refs_1_.refs_3_), channel_id=1, source_target_pairs={{0,2},{2,0},{4,6},{6,4},{8,10},{10,8},{12,14},{14,12},{1,3},{3,1},... | collective-permute-start | bytes 417800 | tf_op jit(solution)/shard_map/ppermute | solution.py:231
  9.1 1.2 %copy-start = (bf16[27,128,128]{2,1,0:T(8,128)(2,1)S(1)}, bf16[27,128,128]{2,1,0:T(8,128)(2,1)}, u32[]{:S(2)}) copy-start(bf16[27,128,128]{2,1,0:T(8,128)(2,1)} %w_ref) | copy-start | bytes 2654212
  11.9 6.9 %collective-permute-start.5 = (bf16[272,256]{1,0:T(8,128)(2,1)S(1)}, bf16[272,256]{1,0:T(8,128)(2,1)S(1)}, u32[]{:S(2)}, u32[]{:S(2)}) collective-permute-start(bf16[272,256]{1,0:T(8,128)(2,1)S(1)} %collective-permute-done.1.before_mine.refs_1_.refs_3_), channel_id=1, source_target_pairs={{0,4},{2,6},{4,8},{6,10},{8,12},{10,14},{12,0},{14,2},{1,5},{3,7},... | collective-permute-start | bytes 417800 | tf_op jit(solution)/shard_map/ppermute | solution.py:234
  11.9 8.6 %collective-permute-start.2 = (bf16[272,256]{1,0:T(8,128)(2,1)S(1)}, bf16[272,256]{1,0:T(8,128)(2,1)S(1)}, u32[]{:S(2)}, u32[]{:S(2)}) collective-permute-start(bf16[272,256]{1,0:T(8,128)(2,1)S(1)} %collective-permute-done.1.before_mine.refs_1_.refs_3_), channel_id=1, source_target_pairs={{0,2},{2,0},{4,6},{6,4},{8,10},{10,8},{12,14},{14,12},{1,3},{3,1},... | collective-permute-start | bytes 417800 | tf_op jit(solution)/shard_map/ppermute | solution.py:231
  13.6 8.9 %collective-permute-start.4 = (bf16[272,256]{1,0:T(8,128)(2,1)S(1)}, bf16[272,256]{1,0:T(8,128)(2,1)S(1)}, u32[]{:S(2)}, u32[]{:S(2)}) collective-permute-start(bf16[272,256]{1,0:T(8,128)(2,1)S(1)} %collective-permute-done.3.after_mine.refs_1_.refs_5_), channel_id=1, source_target_pairs={{0,2},{2,0},{4,6},{6,4},{8,10},{10,8},{12,14},{14,12},{1,3},{3,1},... | collective-permute-start | bytes 417800 | tf_op jit(solution)/shard_map/ppermute | solution.py:231
  18.8 5.9 %collective-permute-start.6 = (bf16[272,256]{1,0:T(8,128)(2,1)S(1)}, bf16[272,256]{1,0:T(8,128)(2,1)S(1)}, u32[]{:S(2)}, u32[]{:S(2)}) collective-permute-start(bf16[272,256]{1,0:T(8,128)(2,1)S(1)} %collective-permute-done.5.refs_1_), channel_id=1, source_target_pairs={{0,2},{2,0},{4,6},{6,4},{8,10},{10,8},{12,14},{14,12},{1,3},{3,1},... | collective-permute-start | bytes 417800 | tf_op jit(solution)/shard_map/ppermute | solution.py:231
  24.7 2.6 %copy-start.2 = (s32[27,256]{1,0:T(8,128)S(1)}, s32[27,256]{1,0:T(8,128)}, u32[]{:S(2)}) copy-start(s32[27,256]{1,0:T(8,128)} %near_ref.1) | copy-start | bytes 82948
  27.2 2.6 %copy-start.1 = (bf16[1,256,128]{2,1,0:T(8,128)(2,1)S(1)}, bf16[1,256,128]{2,1,0:T(8,128)(2,1)}, u32[]{:S(2)}) copy-start(bf16[1,256,128]{2,1,0:T(8,128)(2,1)} %feat_hbm.1) | copy-start | bytes 196612
  27.3 2.5 %collective-permute-start.7 = (bf16[27,128,128]{2,1,0:T(8,128)(2,1)S(1)}, bf16[27,128,128]{2,1,0:T(8,128)(2,1)S(1)}, u32[]{:S(2)}, u32[]{:S(2)}) collective-permute-start(bf16[27,128,128]{2,1,0:T(8,128)(2,1)S(1)} %get-tuple-element.45), channel_id=1, source_target_pairs={{0,1},{1,0},{2,3},{3,2},{4,5},{5,4},{6,7},{7,6},{8,9},{9,8},{10,11... | collective-permute-start | bytes 2654216 | tf_op jit(solution)/shard_map/ppermute | solution.py:291

commit v12 on v9

--- a/solution.py
+++ b/solution.py
@@ -13,6 +13,7 @@
 HALF = 13
 CODE_ROWS = 16
 ROW_STAGES = 4
+FINISH_STEP = 3
 PACK_VMEM = 8 * 1024 * 1024
 KERNEL_VMEM = 24 * 1024 * 1024
 
@@ -34,7 +35,7 @@
     return pltpu.with_memory_space_constraint(array, pltpu.HBM)
 
 
-def pack_kernel(time_ref, feat_hbm, cot_hbm, near_hbm, cond_hbm, wt_hbm, pack_ref, shift_ref,
+def pack_kernel(time_ref, feat_hbm, cot_hbm, near_hbm, cond_hbm, wt_hbm, pack_ref, z_ref, code_ref,
                 feat_ref, near_ref, cond_ref, wt_ref, sems):
     rows, width = feat_ref.shape
     half = width // 2
@@ -58,10 +59,12 @@
     shift = shift + cond_ref[...].astype(jnp.float32)
     copies[2].wait()
     z_val = feat_ref[...].astype(jnp.float32) + shift
-    shift_ref[...] = shift
+    z_ref[...] = z_val
     pack_ref[:rows, :width] = (z_val * jax.nn.sigmoid(z_val)).astype(jnp.bfloat16)
     copies[3].wait()
-    pack_ref[rows:, :] = strip_codes(near_ref[:CODE_ROWS, :], 2).astype(jnp.bfloat16)
+    code = strip_codes(near_ref[...], 2)
+    code_ref[...] = code
+    pack_ref[rows:, :] = code[:CODE_ROWS, :].astype(jnp.bfloat16)
     copies[4].wait()
 
 
@@ -150,19 +153,17 @@
         back_ref[:, k * width:(k + 1) * width] = w_ref[26 - k]
 
 
-def voxel_kernel(where_ref, mine_ref, other_ref, before_mine, before_other, after_mine, after_other,
-                 near_ref, feat_ref, shift_ref, forward_ref, back_ref, conv_ref, grad_ref,
-                 ground, turned, codes, near_act, near_cot):
-    width = feat_ref.shape[1]
+def own_kernel(where_ref, mine_ref, other_ref, code_ref, forward_ref, back_ref, conv_ref, grad_ref,
+               ground, turned, codes, near_act, near_cot):
+    width = conv_ref.shape[0]
     span = 2 * STRIP
     tile_y = where_ref[0] % 2
-    lay_strip(ground, 0, tile_y, before_mine, before_other, TILE - 1)
     for u in range(TILE):
-        lay_strip(ground, u + 1, tile_y, mine_ref, other_ref, u)
-    lay_strip(ground, TILE + 1, tile_y, after_mine, after_other, 0)
-    for i in range(TILE + 2):
-        turned[:, i * span:(i + 1) * span] = ground[i * span:(i + 1) * span, :].T
-    code = strip_codes(near_ref[...], 2)
+        lay_strip(ground, u, tile_y, mine_ref, other_ref, u)
+        turned[:, (u + 1) * span:(u + 2) * span] = ground[u * span:(u + 1) * span, :].T
+    for i in (0, TILE + 1):
+        turned[:, i * span:(i + 1) * span] = jnp.zeros((2 * width, span), jnp.bfloat16)
+    code = code_ref[...]
     lane = lax.broadcasted_iota(jnp.int32, code.shape, 1)
     codes[...] = jnp.where((code >= 0) & (lane // STRIP % 2 == 1), code + span, code)
     place = lax.broadcasted_iota(jnp.int32, (2 * span, span), 0).astype(jnp.float32)
@@ -178,12 +179,54 @@
                 one = near[:, (k - 9 * side) * span:(k - 9 * side + 1) * span]
                 near_act[k * width:(k + 1) * width, at:at + span] = one[:width]
                 near_cot[k * width:(k + 1) * width, at:at + span] = one[width:]
-    conv = jnp.dot(forward_ref[...], near_act[...], preferred_element_type=jnp.float32)
-    conv_ref[...] = conv.T.astype(jnp.bfloat16)
-    back = jnp.dot(back_ref[...], near_cot[...], preferred_element_type=jnp.float32).T
-    z_val = feat_ref[...].astype(jnp.float32) + shift_ref[...]
+    conv_ref[...] = jnp.dot(forward_ref[...], near_act[...], preferred_element_type=jnp.float32)
+    grad_ref[...] = jnp.dot(back_ref[...], near_cot[...], preferred_element_type=jnp.float32)
+
+
+def edge_kernel(where_ref, before_mine, before_other, after_mine, after_other, code_ref, forward_ref, back_ref,
+                own_conv, own_grad, z_ref, conv_ref, grad_ref, ground, turned, near):
+    width = z_ref.shape[1]
+    span = 2 * STRIP
+    tile_y = where_ref[0] % 2
+    lay_strip(ground, 0, tile_y, before_mine, before_other, TILE - 1)
+    lay_strip(ground, 1, tile_y, after_mine, after_other, 0)
+    for i in range(2):
+        turned[:, i * span:(i + 1) * span] = ground[i * span:(i + 1) * span, :].T
+    first = code_ref[:9, :span]
+    last = code_ref[18:, span:]
+    lane = lax.broadcasted_iota(jnp.int32, first.shape, 1)
+    code = jnp.where(lane < STRIP, first, jnp.where(last >= 0, last + span, last))
+    place = lax.broadcasted_iota(jnp.int32, (2 * span, span), 0).astype(jnp.float32)
+    picks = [(place == code[k:k + 1, :]).astype(jnp.bfloat16) for k in range(9)]
+    found = jnp.dot(turned[...], jnp.concatenate(picks, axis=1), preferred_element_type=jnp.float32)
+    found = found.astype(jnp.bfloat16)
+    for k in range(9):
+        near[:, k * width:(k + 1) * width, :] = found[:, k * span:(k + 1) * span].reshape(2, width, span)
+    lane = lax.broadcasted_iota(jnp.int32, (width, span), 1)
+
+    def total(own_ref, weights, side):
+        low = jnp.dot(weights[:, :9 * width], near[side], preferred_element_type=jnp.float32)
+        high = jnp.dot(weights[:, 18 * width:], near[side], preferred_element_type=jnp.float32)
+        low = own_ref[:, :span] + jnp.where(lane < STRIP, low, 0.0)
+        high = own_ref[:, span:] + jnp.where(lane < STRIP, 0.0, high)
+        return jnp.concatenate([low, high], axis=1).T
+
+    conv_ref[...] = total(own_conv, forward_ref, 0).astype(jnp.bfloat16)
+    back = total(own_grad, back_ref, 1)
+    z_val = z_ref[...]
     sig = jax.nn.sigmoid(z_val)
     grad_ref[...] = (back * sig * (1.0 + z_val * (1.0 - sig))).astype(jnp.bfloat16)
+
+
+def finish_kernel(kept_ref, sent_ref, weight_hbm, weight, sems):
+    copies = []
+    for i, first in enumerate(range(0, 27, FINISH_STEP)):
+        part = slice(first, first + FINISH_STEP)
+        weight[part] = kept_ref[part] + sent_ref[part].astype(jnp.float32)
+        copies.append(pltpu.make_async_copy(weight.at[part], weight_hbm.at[part], sems.at[i]))
+        copies[-1].start()
+    for copy in copies:
+        copy.wait()
 
 
 def whole_scene(features, cotangent, neighbours, timesteps, condition, w_time, w_conv, tiles_x, tiles_y):
@@ -193,14 +236,15 @@
     vmem = pl.BlockSpec(memory_space=pltpu.VMEM)
     smem = pl.BlockSpec(memory_space=pltpu.SMEM)
     params = pltpu.CompilerParams(vmem_limit_bytes=KERNEL_VMEM)
-    packed, shift = pl.pallas_call(
+    packed, z_val, code = pl.pallas_call(
         pack_kernel,
         out_shape=(
             jax.ShapeDtypeStruct((rows + CODE_ROWS, 2 * width), jnp.bfloat16),
-            jax.ShapeDtypeStruct((1, width), jnp.float32),
+            jax.ShapeDtypeStruct((rows, width), jnp.float32),
+            jax.ShapeDtypeStruct(neighbours.shape, jnp.float32),
         ),
         in_specs=[smem] + [pl.BlockSpec(memory_space=pltpu.HBM)] * 5,
-        out_specs=(vmem, vmem),
+        out_specs=(vmem, vmem, vmem),
         scratch_shapes=[
             pltpu.VMEM((rows, width), jnp.bfloat16),
             pltpu.VMEM(neighbours.shape, jnp.int32),
@@ -233,6 +277,23 @@
     before, w_forward = lax.optimization_barrier((before, w_forward))
     far = along(before, 1)
     own_pair = (packed, across(packed))
+    own_conv, own_grad = pl.pallas_call(
+        own_kernel,
+        out_shape=(jax.ShapeDtypeStruct((width, rows), jnp.float32),) * 2,
+        in_specs=[smem] + [vmem] * 5,
+        out_specs=(vmem, vmem),
+        scratch_shapes=[
+            pltpu.VMEM((TILE * span, 2 * width), jnp.bfloat16),
+            pltpu.VMEM((2 * width, (TILE + 2) * span), jnp.bfloat16),
+            pltpu.VMEM((27, rows), jnp.float32),
+            pltpu.VMEM((27 * width, rows), jnp.bfloat16),
+            pltpu.VMEM((27 * width, rows), jnp.bfloat16),
+        ],
+        compiler_params=params,
+        cost_estimate=pl.CostEstimate(flops=2 * 10**9, bytes_accessed=4 * 10**6, transcendentals=0),
+        name="voxels_own_row",
+    )(here, *own_pair, code, w_forward, w_back)
+    far, own_conv = lax.optimization_barrier((far, own_conv))
     before_pair = (before, across(before))
     after_pair = (after, across(after))
     far_pair = (far, across(far))
@@ -276,24 +337,32 @@
     own, sent = sums
     other = lax.ppermute(sent, "batch", [(0, 1), (1, 0)])
     conv_out, feature_grad = pl.pallas_call(
-        voxel_kernel,
-        out_shape=(
-            jax.ShapeDtypeStruct((rows, width), jnp.bfloat16),
-            jax.ShapeDtypeStruct((rows, width), jnp.bfloat16),
-        ),
-        in_specs=[smem] + [vmem] * 11,
+        edge_kernel,
+        out_shape=(jax.ShapeDtypeStruct((rows, width), jnp.bfloat16),) * 2,
+        in_specs=[smem] + [vmem] * 10,
+        out_specs=(vmem, vmem),
         scratch_shapes=[
-            pltpu.VMEM(((TILE + 2) * span, 2 * width), jnp.bfloat16),
-            pltpu.VMEM((2 * width, (TILE + 2) * span), jnp.bfloat16),
-            pltpu.VMEM((27, rows), jnp.float32),
-            pltpu.VMEM((27 * width, rows), jnp.bfloat16),
-            pltpu.VMEM((27 * width, rows), jnp.bfloat16),
+            pltpu.VMEM((2 * span, 2 * width), jnp.bfloat16),
+            pltpu.VMEM((2 * width, 2 * span), jnp.bfloat16),
+            pltpu.VMEM((2, 9 * width, span), jnp.bfloat16),
         ],
         compiler_params=params,
         cost_estimate=pl.CostEstimate(flops=10**9, bytes_accessed=4 * 10**6, transcendentals=0),
-        name="voxel_outputs",
-    )(here, *own_pair, *before_pair, *after_pair, neighbours, features[0], shift, w_forward, w_back)
-    weight_grad = own + other.astype(jnp.float32)
+        name="voxel_edges",
+    )(here, *before_pair, *after_pair, code, w_forward, w_back, own_conv, own_grad, z_val)
+    other, conv_out = lax.optimization_barrier((other, conv_out))
+    weight_grad = pl.pallas_call(
+        finish_kernel,
+        out_shape=jax.ShapeDtypeStruct((27, width, width), jnp.float32),
+        in_specs=[vmem] * 2,
+        out_specs=pl.BlockSpec(memory_space=pltpu.HBM),
+        scratch_shapes=[
+            pltpu.VMEM((27, width, width), jnp.float32),
+            pltpu.SemaphoreType.DMA((27 // FINISH_STEP,)),
+        ],
+        compiler_params=pltpu.CompilerParams(vmem_limit_bytes=PACK_VMEM),
+        name="finish",
+    )(own, other)
     return (conv_out[None], feature_grad[None], weight_grad)
 
 

time: 31.7 us -> 31.3 us (0.987)
  Pallas kernels: 12.5 us -> 14.6 us
  other arithmetic: 1.42 us -> 0 us
  waiting for transfers between devices: 3.31 us -> 2.31 us
    pallas_call x1 -> x3, Pallas kernels: 2.65 us -> 4.69 us  [the longest x1 1.86 us: whole_scene(): pl.pallas_call(own_kernel, out_shape=(jax.ShapeDtypeStruct((width, rows),...]
    ppermute x3, waiting for transfers between devices: 3.3 us -> 1.43 us  [along(): lax.ppermute(block, 'brick', [(i, (i + turn * tiles_y) % peers) for i in...]
    add x1 -> x0, other arithmetic: 1.42 us -> none  [whole_scene(): weight_grad = own + other.astype(jnp.float32)]
    ppermute x1, waiting for transfers between devices: 0.01 us -> 0.86 us  [whole_scene(): other = lax.ppermute(sent, 'batch', [(0, 1), (1, 0)])]
    unnamed x6 -> x2, local copies, waits for them, and re-layouts: 1.18 us -> 1.17 us
  transfers between devices with their start and end apart: 8 -> 8, of which waited for: 2 -> 3; matrix products, arithmetic and copies ran while one was open for 0% -> 0% of each run, Pallas kernels for 29% -> 31%
where the time goes in v12:
time: 31.3 us; the launch traced here: 31 us
  Pallas kernels  14.6 us (47%)
  starting transfers between devices  11.6 us (37%)
  waiting for transfers between devices  2.31 us (7%)
  between operations  1.35 us (4%)
  local copies, waits for them, and re-layouts  1.17 us (4%)
    pallas_call x4, Pallas kernels, whole_scene(): pl.pallas_call(functools.partial(row_kernel, stage, strips, borders), out...  8.48 us
    ppermute x4, starting transfers between devices, across(): return lax.ppermute(block, 'brick', [(i, i ^ 1) for i in range(peers)])  6.4 us
    ppermute x3, starting transfers between devices, along(): lax.ppermute(block, 'brick', [(i, (i + turn * tiles_y) % peers) for i in...  5.17 us
    pallas_call x1, Pallas kernels, whole_scene(): pl.pallas_call(own_kernel, out_shape=(jax.ShapeDtypeStruct((width, rows),...  1.86 us
    pallas_call x1, Pallas kernels, whole_scene(): pl.pallas_call(edge_kernel, out_shape=(jax.ShapeDtypeStruct((rows, width)...  1.55 us
    ppermute x3, waiting for transfers between devices, along(): lax.ppermute(block, 'brick', [(i, (i + turn * tiles_y) % peers) for i in...  1.43 us
    pallas_call x1, Pallas kernels, whole_scene(): pl.pallas_call(finish_kernel, out_shape=jax.ShapeDtypeStruct((27, width,...  1.29 us
    unnamed x2, local copies, waits for them, and re-layouts  1.17 us
  transfers between devices with their start and end apart: 8, of which 3 were waited for; matrix products, arithmetic and copies ran while one was open for 0% of the time, Pallas kernels for 31%

profile of v12, /device:TPU:0, one launch (start us, length us, event | category | flops | bytes accessed | tf_op | source)
XLA Modules:
  0.0 31.0 jit_solution(12624038171743366924)
XLA Ops:
  1.3 1.0 %pack_tile.1 = (bf16[272,256]{1,0:T(8,128)(2,1)S(1)}, f32[256,128]{1,0:T(8,128)S(1)}, f32[27,256]{1,0:T(8,128)S(1)}) custom-call(s32[1]{0:T(128)S(6)} %copy.10.time_ref, bf16[1,256,128]{2,1,0:T(8,128)(2,1)} %feat_hbm.1, bf16[1,256,128]{2,1,0:T(8,128)(2,1)} %cot_hbm.1, s32[27,256]{1,0:T(8,128)} %near_hbm.1, bf16[1,128]{1,0:T(2,128)(2,1)} %cond_hbm.1, ...), custom_call_target="tpu_custom_call" | custom-call | tf_op jit(solution)/shard_map/pack_tile/pallas_call | solution.py:239
  2.3 3.1 %collective-permute-start = (bf16[272,256]{1,0:T(8,128)(2,1)S(1)}, bf16[272,256]{1,0:T(8,128)(2,1)S(1)}, u32[]{:S(2)}, u32[]{:S(2)}) collective-permute-start(bf16[272,256]{1,0:T(8,128)(2,1)S(1)} %get-tuple-element.32.mine_ref.refs_1_.refs_3_), channel_id=1, source_target_pairs={{0,4},{2,6},{4,8},{6,10},{8,12},{10,14},{12,0},{14,2},{1,5},{3,7},... | collective-permute-start | bytes 417800 | tf_op jit(solution)/shard_map/ppermute | solution.py:264
  5.4 2.1 %collective-permute-start.5 = (bf16[272,256]{1,0:T(8,128)(2,1)S(1)}, bf16[272,256]{1,0:T(8,128)(2,1)S(1)}, u32[]{:S(2)}, u32[]{:S(2)}) collective-permute-start(bf16[272,256]{1,0:T(8,128)(2,1)S(1)} %get-tuple-element.32.mine_ref.refs_1_.refs_3_), channel_id=1, source_target_pairs={{0,12},{2,14},{4,0},{6,2},{8,4},{10,6},{12,8},{14,10},{1,13},{3,15... | collective-permute-start | bytes 417800 | tf_op jit(solution)/shard_map/ppermute | solution.py:264
  7.5 1.6 %collective-permute-start.2 = (bf16[272,256]{1,0:T(8,128)(2,1)S(1)}, bf16[272,256]{1,0:T(8,128)(2,1)S(1)}, u32[]{:S(2)}, u32[]{:S(2)}) collective-permute-start(bf16[272,256]{1,0:T(8,128)(2,1)S(1)} %get-tuple-element.32.mine_ref.refs_1_.refs_3_), channel_id=1, source_target_pairs={{0,2},{2,0},{4,6},{6,4},{8,10},{10,8},{12,14},{14,12},{1,3},{3,1},... | collective-permute-start | bytes 417800 | tf_op jit(solution)/shard_map/ppermute | solution.py:261
  9.1 0.0 copy-start
  9.1 1.2 %copy-done = bf16[27,128,128]{2,1,0:T(8,128)(2,1)S(1)} copy-done((bf16[27,128,128]{2,1,0:T(8,128)(2,1)S(1)}, bf16[27,128,128]{2,1,0:T(8,128)(2,1)}, u32[]{:S(2)}) %copy-start) | copy-done | bytes 884760
  10.3 0.4 %turn_weights.1 = (bf16[128,3456]{1,0:T(8,128)(2,1)S(1)}, bf16[128,3456]{1,0:T(8,128)(2,1)S(1)}) custom-call(bf16[27,128,128]{2,1,0:T(8,128)(2,1)S(1)} %copy-done), custom_call_target="tpu_custom_call" | custom-call | flops 200000000 | bytes 3000000 | tf_op jit(solution)/shard_map/turn_weights/pallas_call | solution.py:267
  10.7 1.3 %collective-permute-done.refs_1_.refs_3_.before_mine = bf16[272,256]{1,0:T(8,128)(2,1)S(1)} collective-permute-done((bf16[272,256]{1,0:T(8,128)(2,1)S(1)}, bf16[272,256]{1,0:T(8,128)(2,1)S(1)}, u32[]{:S(2)}, u32[]{:S(2)}) %collective-permute-start) | collective-permute-done | bytes 139296 | tf_op jit(solution)/shard_map/ppermute | solution.py:264
  11.9 0.0 collective-permute-start.1
  11.9 1.7 %collective-permute-start.4 = (bf16[272,256]{1,0:T(8,128)(2,1)S(1)}, bf16[272,256]{1,0:T(8,128)(2,1)S(1)}, u32[]{:S(2)}, u32[]{:S(2)}) collective-permute-start(bf16[272,256]{1,0:T(8,128)(2,1)S(1)} %collective-permute-done.refs_1_.refs_3_.before_mine), channel_id=1, source_target_pairs={{0,2},{2,0},{4,6},{6,4},{8,10},{10,8},{12,14},{14,12},{1,3},{3,1},... | collective-permute-start | bytes 417800 | tf_op jit(solution)/shard_map/ppermute | solution.py:261
  13.7 0.0 collective-permute-done.5.refs_1_.refs_5_.after_mine
  13.7 1.3 %collective-permute-start.6 = (bf16[272,256]{1,0:T(8,128)(2,1)S(1)}, bf16[272,256]{1,0:T(8,128)(2,1)S(1)}, u32[]{:S(2)}, u32[]{:S(2)}) collective-permute-start(bf16[272,256]{1,0:T(8,128)(2,1)S(1)} %collective-permute-done.5.refs_1_.refs_5_.after_mine), channel_id=1, source_target_pairs={{0,2},{2,0},{4,6},{6,4},{8,10},{10,8},{12,14},{14,12},{1,3},{3,1},... | collective-permute-start | bytes 417800 | tf_op jit(solution)/shard_map/ppermute | solution.py:261
  15.0 0.0 collective-permute-done.2.other_ref.refs_2_.refs_4_
  15.0 1.8 %weight_row_0.1 = (f32[1664,128]{1,0:T(8,128)S(1)}, f32[1664,128]{1,0:T(8,128)S(1)}, f32[128,128]{1,0:T(8,128)S(1)}) custom-call(s32[1]{0:T(128)} %bitcast.where_ref.refs_0_, bf16[272,256]{1,0:T(8,128)(2,1)S(1)} %get-tuple-element.32.mine_ref.refs_1_.refs_3_, bf16[272,256]{1,0:T(8,128)(2,1)S(1)} %collective-permute-done.2.other_ref.refs_2_.refs_4_), custom_call_target="tpu_custom_call" | custom-call | flops 2000000000 | bytes 4000000 | tf_op jit(solution)/shard_map/weight_row_0/pallas_call | solution.py:321
  16.8 1.9 %voxels_own_row.1 = (f32[128,256]{1,0:T(8,128)S(1)}, f32[128,256]{1,0:T(8,128)S(1)}) custom-call(s32[1]{0:T(128)} %bitcast.where_ref.refs_0_, bf16[272,256]{1,0:T(8,128)(2,1)S(1)} %get-tuple-element.32.mine_ref.refs_1_.refs_3_, bf16[272,256]{1,0:T(8,128)(2,1)S(1)} %collective-permute-done.2.other_ref.refs_2_.refs_4_, ...), custom_call_target="tpu_custom_call" | custom-call | flops 2000000000 | bytes 4000000 | tf_op jit(solution)/shard_map/voxels_own_row/pallas_call | solution.py:280
  18.6 0.2 collective-permute-done.1.refs_1_
  18.8 1.7 %collective-permute-start.3 = (bf16[272,256]{1,0:T(8,128)(2,1)S(1)}, bf16[272,256]{1,0:T(8,128)(2,1)S(1)}, u32[]{:S(2)}, u32[]{:S(2)}) collective-permute-start(bf16[272,256]{1,0:T(8,128)(2,1)S(1)} %collective-permute-done.1.refs_1_), channel_id=1, source_target_pairs={{0,2},{2,0},{4,6},{6,4},{8,10},{10,8},{12,14},{14,12},{1,3},{3,1},... | collective-permute-start | bytes 417800 | tf_op jit(solution)/shard_map/ppermute | solution.py:261
  20.5 0.0 collective-permute-done.4.refs_2_.refs_4_.before_other
  20.5 2.1 %weight_row_1.1 = (f32[1664,128]{1,0:T(8,128)S(1)}, f32[1664,128]{1,0:T(8,128)S(1)}, f32[128,128]{1,0:T(8,128)S(1)}) custom-call(s32[1]{0:T(128)} %bitcast.where_ref.refs_0_, bf16[272,256]{1,0:T(8,128)(2,1)S(1)} %collective-permute-done.refs_1_.refs_3_.before_mine, bf16[272,256]{1,0:T(8,128)(2,1)S(1)} %collective-permute-done.4.refs_2_.refs_4_.before_other, ...), custom_call_target="tpu_custom_call" | custom-call | flops 2000000000 | bytes 4000000 | tf_op jit(solution)/shard_map/weight_row_1/pallas_call | solution.py:321
  22.6 0.0 collective-permute-done.6.refs_2_.refs_6_.after_other
  22.6 2.1 %weight_row_2.1 = (f32[1664,128]{1,0:T(8,128)S(1)}, f32[1664,128]{1,0:T(8,128)S(1)}, f32[128,128]{1,0:T(8,128)S(1)}) custom-call(s32[1]{0:T(128)} %bitcast.where_ref.refs_0_, bf16[272,256]{1,0:T(8,128)(2,1)S(1)} %collective-permute-done.5.refs_1_.refs_5_.after_mine, bf16[272,256]{1,0:T(8,128)(2,1)S(1)} %collective-permute-done.6.refs_2_.refs_6_.after_other, ...), custom_call_target="tpu_custom_call" | custom-call | flops 2000000000 | bytes 4000000 | tf_op jit(solution)/shard_map/weight_row_2/pallas_call | solution.py:321
  24.7 0.0 collective-permute-done.3.refs_2_
  24.7 2.5 %weight_row_3.1 = (f32[27,128,128]{2,1,0:T(8,128)S(1)}, bf16[27,128,128]{2,1,0:T(8,128)(2,1)S(1)}) custom-call(s32[1]{0:T(128)} %bitcast.where_ref.refs_0_, bf16[272,256]{1,0:T(8,128)(2,1)S(1)} %collective-permute-done.1.refs_1_, bf16[272,256]{1,0:T(8,128)(2,1)S(1)} %collective-permute-done.3.refs_2_, ...), custom_call_target="tpu_custom_call" | custom-call | flops 2000000000 | bytes 4000000 | tf_op jit(solution)/shard_map/weight_row_3/pallas_call | solution.py:321
  27.3 0.1 collective-permute-start.7
  27.3 1.5 %voxel_edges.1 = (bf16[256,128]{1,0:T(8,128)(2,1)}, bf16[256,128]{1,0:T(8,128)(2,1)}) custom-call(s32[1]{0:T(128)} %bitcast.where_ref.refs_0_, bf16[272,256]{1,0:T(8,128)(2,1)S(1)} %collective-permute-done.refs_1_.refs_3_.before_mine, bf16[272,256]{1,0:T(8,128)(2,1)S(1)} %collective-permute-done.4.refs_2_.refs_4_.before_other, ...), custom_call_target="tpu_custom_call" | custom-call | flops 1000000000 | bytes 4000000 | tf_op jit(solution)/shard_map/voxel_edges/pallas_call | solution.py:339
  28.9 0.9 %collective-permute-done.7.sent_ref = bf16[27,128,128]{2,1,0:T(8,128)(2,1)S(1)} collective-permute-done((bf16[27,128,128]{2,1,0:T(8,128)(2,1)S(1)}, bf16[27,128,128]{2,1,0:T(8,128)(2,1)S(1)}, u32[]{:S(2)}, u32[]{:S(2)}) %collective-permute-start.7) | collective-permute-done | bytes 884768 | tf_op jit(solution)/shard_map/ppermute | solution.py:338
  29.7 1.3 %finish.1 = f32[27,128,128]{2,1,0:T(8,128)} custom-call(f32[27,128,128]{2,1,0:T(8,128)S(1)} %get-tuple-element.57.kept_ref, bf16[27,128,128]{2,1,0:T(8,128)(2,1)S(1)} %collective-permute-done.7.sent_ref), custom_call_target="tpu_custom_call" | custom-call | tf_op jit(solution)/shard_map/finish/pallas_call | solution.py:354
Async XLA Ops:
  2.3 9.6 %collective-permute-start = (bf16[272,256]{1,0:T(8,128)(2,1)S(1)}, bf16[272,256]{1,0:T(8,128)(2,1)S(1)}, u32[]{:S(2)}, u32[]{:S(2)}) collective-permute-start(bf16[272,256]{1,0:T(8,128)(2,1)S(1)} %get-tuple-element.32.mine_ref.refs_1_.refs_3_), channel_id=1, source_target_pairs={{0,4},{2,6},{4,8},{6,10},{8,12},{10,14},{12,0},{14,2},{1,5},{3,7},... | collective-permute-start | bytes 417800 | tf_op jit(solution)/shard_map/ppermute | solution.py:264
  5.4 8.3 %collective-permute-start.5 = (bf16[272,256]{1,0:T(8,128)(2,1)S(1)}, bf16[272,256]{1,0:T(8,128)(2,1)S(1)}, u32[]{:S(2)}, u32[]{:S(2)}) collective-permute-start(bf16[272,256]{1,0:T(8,128)(2,1)S(1)} %get-tuple-element.32.mine_ref.refs_1_.refs_3_), channel_id=1, source_target_pairs={{0,12},{2,14},{4,0},{6,2},{8,4},{10,6},{12,8},{14,10},{1,13},{3,15... | collective-permute-start | bytes 417800 | tf_op jit(solution)/shard_map/ppermute | solution.py:264
  7.5 7.5 %collective-permute-start.2 = (bf16[272,256]{1,0:T(8,128)(2,1)S(1)}, bf16[272,256]{1,0:T(8,128)(2,1)S(1)}, u32[]{:S(2)}, u32[]{:S(2)}) collective-permute-start(bf16[272,256]{1,0:T(8,128)(2,1)S(1)} %get-tuple-element.32.mine_ref.refs_1_.refs_3_), channel_id=1, source_target_pairs={{0,2},{2,0},{4,6},{6,4},{8,10},{10,8},{12,14},{14,12},{1,3},{3,1},... | collective-permute-start | bytes 417800 | tf_op jit(solution)/shard_map/ppermute | solution.py:261
  9.1 1.2 %copy-start = (bf16[27,128,128]{2,1,0:T(8,128)(2,1)S(1)}, bf16[27,128,128]{2,1,0:T(8,128)(2,1)}, u32[]{:S(2)}) copy-start(bf16[27,128,128]{2,1,0:T(8,128)(2,1)} %w_ref) | copy-start | bytes 2654212
  11.9 6.9 %collective-permute-start.1 = (bf16[272,256]{1,0:T(8,128)(2,1)S(1)}, bf16[272,256]{1,0:T(8,128)(2,1)S(1)}, u32[]{:S(2)}, u32[]{:S(2)}) collective-permute-start(bf16[272,256]{1,0:T(8,128)(2,1)S(1)} %collective-permute-done.refs_1_.refs_3_.before_mine), channel_id=1, source_target_pairs={{0,4},{2,6},{4,8},{6,10},{8,12},{10,14},{12,0},{14,2},{1,5},{3,7},... | collective-permute-start | bytes 417800 | tf_op jit(solution)/shard_map/ppermute | solution.py:264
  11.9 8.6 %collective-permute-start.4 = (bf16[272,256]{1,0:T(8,128)(2,1)S(1)}, bf16[272,256]{1,0:T(8,128)(2,1)S(1)}, u32[]{:S(2)}, u32[]{:S(2)}) collective-permute-start(bf16[272,256]{1,0:T(8,128)(2,1)S(1)} %collective-permute-done.refs_1_.refs_3_.before_mine), channel_id=1, source_target_pairs={{0,2},{2,0},{4,6},{6,4},{8,10},{10,8},{12,14},{14,12},{1,3},{3,1},... | collective-permute-start | bytes 417800 | tf_op jit(solution)/shard_map/ppermute | solution.py:261
  13.7 9.0 %collective-permute-start.6 = (bf16[272,256]{1,0:T(8,128)(2,1)S(1)}, bf16[272,256]{1,0:T(8,128)(2,1)S(1)}, u32[]{:S(2)}, u32[]{:S(2)}) collective-permute-start(bf16[272,256]{1,0:T(8,128)(2,1)S(1)} %collective-permute-done.5.refs_1_.refs_5_.after_mine), channel_id=1, source_target_pairs={{0,2},{2,0},{4,6},{6,4},{8,10},{10,8},{12,14},{14,12},{1,3},{3,1},... | collective-permute-start | bytes 417800 | tf_op jit(solution)/shard_map/ppermute | solution.py:261
  18.8 5.9 %collective-permute-start.3 = (bf16[272,256]{1,0:T(8,128)(2,1)S(1)}, bf16[272,256]{1,0:T(8,128)(2,1)S(1)}, u32[]{:S(2)}, u32[]{:S(2)}) collective-permute-start(bf16[272,256]{1,0:T(8,128)(2,1)S(1)} %collective-permute-done.1.refs_1_), channel_id=1, source_target_pairs={{0,2},{2,0},{4,6},{6,4},{8,10},{10,8},{12,14},{14,12},{1,3},{3,1},... | collective-permute-start | bytes 417800 | tf_op jit(solution)/shard_map/ppermute | solution.py:261
  27.3 2.5 %collective-permute-start.7 = (bf16[27,128,128]{2,1,0:T(8,128)(2,1)S(1)}, bf16[27,128,128]{2,1,0:T(8,128)(2,1)S(1)}, u32[]{:S(2)}, u32[]{:S(2)}) collective-permute-start(bf16[27,128,128]{2,1,0:T(8,128)(2,1)S(1)} %get-tuple-element.50), channel_id=1, source_target_pairs={{0,1},{1,0},{2,3},{3,2},{4,5},{5,4},{6,7},{7,6},{8,9},{9,8},{10,11... | collective-permute-start | bytes 2654216 | tf_op jit(solution)/shard_map/ppermute | solution.py:338

commit v13 on v12

--- a/solution.py
+++ b/solution.py
@@ -153,6 +153,24 @@
         back_ref[:, k * width:(k + 1) * width] = w_ref[26 - k]
 
 
+def paired_codes(code_ref):
+    code = code_ref[...]
+    lane = lax.broadcasted_iota(jnp.int32, code.shape, 1)
+    return jnp.where((code >= 0) & (lane // STRIP % 2 == 1), code + 2 * STRIP, code)
+
+
+def look_up(window, codes, to_act, to_cot, columns):
+    width = window.shape[0] // 2
+    span = codes.shape[1]
+    place = lax.broadcasted_iota(jnp.int32, (window.shape[1], span), 0).astype(jnp.float32)
+    picks = [(place == codes[k:k + 1, :]).astype(jnp.bfloat16) for k in range(codes.shape[0])]
+    near = jnp.dot(window, jnp.concatenate(picks, axis=1), preferred_element_type=jnp.float32).astype(jnp.bfloat16)
+    for k in range(codes.shape[0]):
+        one = near[:, k * span:(k + 1) * span]
+        to_act[k * width:(k + 1) * width, columns:columns + span] = one[:width]
+        to_cot[k * width:(k + 1) * width, columns:columns + span] = one[width:]
+
+
 def own_kernel(where_ref, mine_ref, other_ref, code_ref, forward_ref, back_ref, conv_ref, grad_ref,
                ground, turned, codes, near_act, near_cot):
     width = conv_ref.shape[0]
@@ -161,58 +179,44 @@
     for u in range(TILE):
         lay_strip(ground, u, tile_y, mine_ref, other_ref, u)
         turned[:, (u + 1) * span:(u + 2) * span] = ground[u * span:(u + 1) * span, :].T
-    for i in (0, TILE + 1):
-        turned[:, i * span:(i + 1) * span] = jnp.zeros((2 * width, span), jnp.bfloat16)
-    code = code_ref[...]
-    lane = lax.broadcasted_iota(jnp.int32, code.shape, 1)
-    codes[...] = jnp.where((code >= 0) & (lane // STRIP % 2 == 1), code + span, code)
-    place = lax.broadcasted_iota(jnp.int32, (2 * span, span), 0).astype(jnp.float32)
+    turned[:, :span] = jnp.zeros((2 * width, span), jnp.bfloat16)
+    codes[...] = paired_codes(code_ref)
     for half in range(TILE // 2):
-        at = half * span
-        for side in range(3):
+        for side in range(2):
             source = (2 * half + side) * span
-            ks = range(9 * side, 9 * side + 9)
-            picks = [(place == codes[k:k + 1, at:at + span]).astype(jnp.bfloat16) for k in ks]
-            near = jnp.dot(turned[:, source:source + 2 * span], jnp.concatenate(picks, axis=1),
-                           preferred_element_type=jnp.float32).astype(jnp.bfloat16)
-            for k in ks:
-                one = near[:, (k - 9 * side) * span:(k - 9 * side + 1) * span]
-                near_act[k * width:(k + 1) * width, at:at + span] = one[:width]
-                near_cot[k * width:(k + 1) * width, at:at + span] = one[width:]
-    conv_ref[...] = jnp.dot(forward_ref[...], near_act[...], preferred_element_type=jnp.float32)
-    grad_ref[...] = jnp.dot(back_ref[...], near_cot[...], preferred_element_type=jnp.float32)
-
-
-def edge_kernel(where_ref, before_mine, before_other, after_mine, after_other, code_ref, forward_ref, back_ref,
-                own_conv, own_grad, z_ref, conv_ref, grad_ref, ground, turned, near):
+            rows = slice(9 * side * width, 9 * (side + 1) * width)
+            look_up(turned[:, source:source + 2 * span], codes[9 * side:9 * side + 9, half * span:(half + 1) * span],
+                    near_act.at[rows], near_cot.at[rows], half * span)
+    conv_ref[...] = jnp.dot(forward_ref[:, :18 * width], near_act[...], preferred_element_type=jnp.float32)
+    grad_ref[...] = jnp.dot(back_ref[:, :18 * width], near_cot[...], preferred_element_type=jnp.float32)
+
+
+def edge_kernel(where_ref, mine_ref, other_ref, before_mine, before_other, after_mine, after_other,
+                code_ref, forward_ref, back_ref, own_conv, own_grad, z_ref, conv_ref, grad_ref,
+                ground, turned, codes, near_act, near_cot, edge_act, edge_cot):
     width = z_ref.shape[1]
     span = 2 * STRIP
     tile_y = where_ref[0] % 2
-    lay_strip(ground, 0, tile_y, before_mine, before_other, TILE - 1)
-    lay_strip(ground, 1, tile_y, after_mine, after_other, 0)
-    for i in range(2):
+    strips = [(mine_ref, other_ref, u) for u in range(1, TILE)]
+    strips += [(after_mine, after_other, 0), (before_mine, before_other, TILE - 1)]
+    for i, strip in enumerate(strips):
+        lay_strip(ground, i, tile_y, *strip)
         turned[:, i * span:(i + 1) * span] = ground[i * span:(i + 1) * span, :].T
-    first = code_ref[:9, :span]
-    last = code_ref[18:, span:]
-    lane = lax.broadcasted_iota(jnp.int32, first.shape, 1)
-    code = jnp.where(lane < STRIP, first, jnp.where(last >= 0, last + span, last))
-    place = lax.broadcasted_iota(jnp.int32, (2 * span, span), 0).astype(jnp.float32)
-    picks = [(place == code[k:k + 1, :]).astype(jnp.bfloat16) for k in range(9)]
-    found = jnp.dot(turned[...], jnp.concatenate(picks, axis=1), preferred_element_type=jnp.float32)
-    found = found.astype(jnp.bfloat16)
-    for k in range(9):
-        near[:, k * width:(k + 1) * width, :] = found[:, k * span:(k + 1) * span].reshape(2, width, span)
-    lane = lax.broadcasted_iota(jnp.int32, (width, span), 1)
-
-    def total(own_ref, weights, side):
-        low = jnp.dot(weights[:, :9 * width], near[side], preferred_element_type=jnp.float32)
-        high = jnp.dot(weights[:, 18 * width:], near[side], preferred_element_type=jnp.float32)
-        low = own_ref[:, :span] + jnp.where(lane < STRIP, low, 0.0)
-        high = own_ref[:, span:] + jnp.where(lane < STRIP, 0.0, high)
-        return jnp.concatenate([low, high], axis=1).T
-
-    conv_ref[...] = total(own_conv, forward_ref, 0).astype(jnp.bfloat16)
-    back = total(own_grad, back_ref, 1)
+    codes[...] = paired_codes(code_ref)
+    for half in range(TILE // 2):
+        columns = slice(half * span, (half + 1) * span)
+        look_up(turned[:, 2 * half * span:2 * (half + 1) * span], codes[18:, columns], near_act, near_cot, half * span)
+    code = codes[:9, :span]
+    lane = lax.broadcasted_iota(jnp.int32, code.shape, 1)
+    look_up(turned[:, TILE * span:], jnp.where(lane < STRIP, code, -1.0), edge_act, edge_cot, 0)
+
+    def total(own_ref, weights, near, edge):
+        value = own_ref[...] + jnp.dot(weights[:, 18 * width:], near[...], preferred_element_type=jnp.float32)
+        first = value[:, :span] + jnp.dot(weights[:, :9 * width], edge[...], preferred_element_type=jnp.float32)
+        return jnp.concatenate([first, value[:, span:]], axis=1).T
+
+    conv_ref[...] = total(own_conv, forward_ref, near_act, edge_act).astype(jnp.bfloat16)
+    back = total(own_grad, back_ref, near_cot, edge_cot)
     z_val = z_ref[...]
     sig = jax.nn.sigmoid(z_val)
     grad_ref[...] = (back * sig * (1.0 + z_val * (1.0 - sig))).astype(jnp.bfloat16)
@@ -284,10 +288,10 @@
         out_specs=(vmem, vmem),
         scratch_shapes=[
             pltpu.VMEM((TILE * span, 2 * width), jnp.bfloat16),
-            pltpu.VMEM((2 * width, (TILE + 2) * span), jnp.bfloat16),
+            pltpu.VMEM((2 * width, (TILE + 1) * span), jnp.bfloat16),
             pltpu.VMEM((27, rows), jnp.float32),
-            pltpu.VMEM((27 * width, rows), jnp.bfloat16),
-            pltpu.VMEM((27 * width, rows), jnp.bfloat16),
+            pltpu.VMEM((18 * width, rows), jnp.bfloat16),
+            pltpu.VMEM((18 * width, rows), jnp.bfloat16),
         ],
         compiler_params=params,
         cost_estimate=pl.CostEstimate(flops=2 * 10**9, bytes_accessed=4 * 10**6, transcendentals=0),
@@ -339,17 +343,21 @@
     conv_out, feature_grad = pl.pallas_call(
         edge_kernel,
         out_shape=(jax.ShapeDtypeStruct((rows, width), jnp.bfloat16),) * 2,
-        in_specs=[smem] + [vmem] * 10,
+        in_specs=[smem] + [vmem] * 12,
         out_specs=(vmem, vmem),
         scratch_shapes=[
-            pltpu.VMEM((2 * span, 2 * width), jnp.bfloat16),
-            pltpu.VMEM((2 * width, 2 * span), jnp.bfloat16),
-            pltpu.VMEM((2, 9 * width, span), jnp.bfloat16),
+            pltpu.VMEM(((TILE + 1) * span, 2 * width), jnp.bfloat16),
+            pltpu.VMEM((2 * width, (TILE + 1) * span), jnp.bfloat16),
+            pltpu.VMEM((27, rows), jnp.float32),
+            pltpu.VMEM((9 * width, rows), jnp.bfloat16),
+            pltpu.VMEM((9 * width, rows), jnp.bfloat16),
+            pltpu.VMEM((9 * width, span), jnp.bfloat16),
+            pltpu.VMEM((9 * width, span), jnp.bfloat16),
         ],
         compiler_params=params,
         cost_estimate=pl.CostEstimate(flops=10**9, bytes_accessed=4 * 10**6, transcendentals=0),
         name="voxel_edges",
-    )(here, *before_pair, *after_pair, code, w_forward, w_back, own_conv, own_grad, z_val)
+    )(here, *own_pair, *before_pair, *after_pair, code, w_forward, w_back, own_conv, own_grad, z_val)
     other, conv_out = lax.optimization_barrier((other, conv_out))
     weight_grad = pl.pallas_call(
         finish_kernel,

time: 31.3 us -> 31.3 us (level)
    pallas_call x1, Pallas kernels: 1.86 us -> 1.29 us  [whole_scene(): pl.pallas_call(own_kernel, out_shape=(jax.ShapeDtypeStruct((width, rows),...]
    ppermute x3, waiting for transfers between devices: 1.43 us -> 2 us  [along(): lax.ppermute(block, 'brick', [(i, (i + turn * tiles_y) % peers) for i in...]
    pallas_call x1, Pallas kernels: 1.55 us -> 1.88 us  [whole_scene(): pl.pallas_call(edge_kernel, out_shape=(jax.ShapeDtypeStruct((rows, width)...]
    ppermute x1, waiting for transfers between devices: 0.86 us -> 0.53 us  [whole_scene(): other = lax.ppermute(sent, 'batch', [(0, 1), (1, 0)])]
where the time goes in v13:
time: 31.3 us; the launch traced here: 31 us
  Pallas kernels  14.3 us (46%)
  starting transfers between devices  11.6 us (37%)
  waiting for transfers between devices  2.54 us (8%)
  between operations  1.35 us (4%)
  local copies, waits for them, and re-layouts  1.17 us (4%)
    pallas_call x4, Pallas kernels, whole_scene(): pl.pallas_call(functools.partial(row_kernel, stage, strips, borders), out...  8.48 us
    ppermute x4, starting transfers between devices, across(): return lax.ppermute(block, 'brick', [(i, i ^ 1) for i in range(peers)])  6.4 us
    ppermute x3, starting transfers between devices, along(): lax.ppermute(block, 'brick', [(i, (i + turn * tiles_y) % peers) for i in...  5.17 us
    ppermute x3, waiting for transfers between devices, along(): lax.ppermute(block, 'brick', [(i, (i + turn * tiles_y) % peers) for i in...  2 us
    pallas_call x1, Pallas kernels, whole_scene(): pl.pallas_call(edge_kernel, out_shape=(jax.ShapeDtypeStruct((rows, width)...  1.88 us
    pallas_call x1, Pallas kernels, whole_scene(): pl.pallas_call(finish_kernel, out_shape=jax.ShapeDtypeStruct((27, width,...  1.29 us
    pallas_call x1, Pallas kernels, whole_scene(): pl.pallas_call(own_kernel, out_shape=(jax.ShapeDtypeStruct((width, rows),...  1.29 us
    unnamed x2, local copies, waits for them, and re-layouts  1.17 us
  transfers between devices with their start and end apart: 8, of which 3 were waited for; matrix products, arithmetic and copies ran while one was open for 0% of the time, Pallas kernels for 31%

profile of v13, /device:TPU:0, one launch (start us, length us, event | category | flops | bytes accessed | tf_op | source)
XLA Modules:
  0.0 31.0 jit_solution(2772557536926093404)
XLA Ops:
  1.3 1.0 %pack_tile.1 = (bf16[272,256]{1,0:T(8,128)(2,1)S(1)}, f32[256,128]{1,0:T(8,128)S(1)}, f32[27,256]{1,0:T(8,128)S(1)}) custom-call(s32[1]{0:T(128)S(6)} %copy.10.time_ref, bf16[1,256,128]{2,1,0:T(8,128)(2,1)} %feat_hbm.1, bf16[1,256,128]{2,1,0:T(8,128)(2,1)} %cot_hbm.1, s32[27,256]{1,0:T(8,128)} %near_hbm.1, bf16[1,128]{1,0:T(2,128)(2,1)} %cond_hbm.1, ...), custom_call_target="tpu_custom_call" | custom-call | tf_op jit(solution)/shard_map/pack_tile/pallas_call | solution.py:243
  2.3 3.1 %collective-permute-start = (bf16[272,256]{1,0:T(8,128)(2,1)S(1)}, bf16[272,256]{1,0:T(8,128)(2,1)S(1)}, u32[]{:S(2)}, u32[]{:S(2)}) collective-permute-start(bf16[272,256]{1,0:T(8,128)(2,1)S(1)} %get-tuple-element.32.mine_ref.refs_1_.refs_3_), channel_id=1, source_target_pairs={{0,4},{2,6},{4,8},{6,10},{8,12},{10,14},{12,0},{14,2},{1,5},{3,7},... | collective-permute-start | bytes 417800 | tf_op jit(solution)/shard_map/ppermute | solution.py:268
  5.4 2.1 %collective-permute-start.5 = (bf16[272,256]{1,0:T(8,128)(2,1)S(1)}, bf16[272,256]{1,0:T(8,128)(2,1)S(1)}, u32[]{:S(2)}, u32[]{:S(2)}) collective-permute-start(bf16[272,256]{1,0:T(8,128)(2,1)S(1)} %get-tuple-element.32.mine_ref.refs_1_.refs_3_), channel_id=1, source_target_pairs={{0,12},{2,14},{4,0},{6,2},{8,4},{10,6},{12,8},{14,10},{1,13},{3,15... | collective-permute-start | bytes 417800 | tf_op jit(solution)/shard_map/ppermute | solution.py:268
  7.5 1.6 %collective-permute-start.2 = (bf16[272,256]{1,0:T(8,128)(2,1)S(1)}, bf16[272,256]{1,0:T(8,128)(2,1)S(1)}, u32[]{:S(2)}, u32[]{:S(2)}) collective-permute-start(bf16[272,256]{1,0:T(8,128)(2,1)S(1)} %get-tuple-element.32.mine_ref.refs_1_.refs_3_), channel_id=1, source_target_pairs={{0,2},{2,0},{4,6},{6,4},{8,10},{10,8},{12,14},{14,12},{1,3},{3,1},... | collective-permute-start | bytes 417800 | tf_op jit(solution)/shard_map/ppermute | solution.py:265
  9.1 0.0 copy-start
  9.1 1.2 %copy-done = bf16[27,128,128]{2,1,0:T(8,128)(2,1)S(1)} copy-done((bf16[27,128,128]{2,1,0:T(8,128)(2,1)S(1)}, bf16[27,128,128]{2,1,0:T(8,128)(2,1)}, u32[]{:S(2)}) %copy-start) | copy-done | bytes 884760
  10.3 0.4 %turn_weights.1 = (bf16[128,3456]{1,0:T(8,128)(2,1)S(1)}, bf16[128,3456]{1,0:T(8,128)(2,1)S(1)}) custom-call(bf16[27,128,128]{2,1,0:T(8,128)(2,1)S(1)} %copy-done), custom_call_target="tpu_custom_call" | custom-call | flops 200000000 | bytes 3000000 | tf_op jit(solution)/shard_map/turn_weights/pallas_call | solution.py:271
  10.7 1.3 %collective-permute-done.refs_1_.refs_3_.before_mine = bf16[272,256]{1,0:T(8,128)(2,1)S(1)} collective-permute-done((bf16[272,256]{1,0:T(8,128)(2,1)S(1)}, bf16[272,256]{1,0:T(8,128)(2,1)S(1)}, u32[]{:S(2)}, u32[]{:S(2)}) %collective-permute-start) | collective-permute-done | bytes 139296 | tf_op jit(solution)/shard_map/ppermute | solution.py:268
  11.9 0.0 collective-permute-start.1
  11.9 1.7 %collective-permute-start.4 = (bf16[272,256]{1,0:T(8,128)(2,1)S(1)}, bf16[272,256]{1,0:T(8,128)(2,1)S(1)}, u32[]{:S(2)}, u32[]{:S(2)}) collective-permute-start(bf16[272,256]{1,0:T(8,128)(2,1)S(1)} %collective-permute-done.refs_1_.refs_3_.before_mine), channel_id=1, source_target_pairs={{0,2},{2,0},{4,6},{6,4},{8,10},{10,8},{12,14},{14,12},{1,3},{3,1},... | collective-permute-start | bytes 417800 | tf_op jit(solution)/shard_map/ppermute | solution.py:265
  13.7 0.0 collective-permute-done.5.refs_1_.refs_5_.after_mine
  13.7 1.3 %collective-permute-start.6 = (bf16[272,256]{1,0:T(8,128)(2,1)S(1)}, bf16[272,256]{1,0:T(8,128)(2,1)S(1)}, u32[]{:S(2)}, u32[]{:S(2)}) collective-permute-start(bf16[272,256]{1,0:T(8,128)(2,1)S(1)} %collective-permute-done.5.refs_1_.refs_5_.after_mine), channel_id=1, source_target_pairs={{0,2},{2,0},{4,6},{6,4},{8,10},{10,8},{12,14},{14,12},{1,3},{3,1},... | collective-permute-start | bytes 417800 | tf_op jit(solution)/shard_map/ppermute | solution.py:265
  15.0 0.0 collective-permute-done.2.other_ref.refs_2_.refs_4_
  15.0 1.8 %weight_row_0.1 = (f32[1664,128]{1,0:T(8,128)S(1)}, f32[1664,128]{1,0:T(8,128)S(1)}, f32[128,128]{1,0:T(8,128)S(1)}) custom-call(s32[1]{0:T(128)} %bitcast.where_ref.refs_0_, bf16[272,256]{1,0:T(8,128)(2,1)S(1)} %get-tuple-element.32.mine_ref.refs_1_.refs_3_, bf16[272,256]{1,0:T(8,128)(2,1)S(1)} %collective-permute-done.2.other_ref.refs_2_.refs_4_), custom_call_target="tpu_custom_call" | custom-call | flops 2000000000 | bytes 4000000 | tf_op jit(solution)/shard_map/weight_row_0/pallas_call | solution.py:325
  16.8 1.3 %voxels_own_row.1 = (f32[128,256]{1,0:T(8,128)S(1)}, f32[128,256]{1,0:T(8,128)S(1)}) custom-call(s32[1]{0:T(128)} %bitcast.where_ref.refs_0_, bf16[272,256]{1,0:T(8,128)(2,1)S(1)} %get-tuple-element.32.mine_ref.refs_1_.refs_3_, bf16[272,256]{1,0:T(8,128)(2,1)S(1)} %collective-permute-done.2.other_ref.refs_2_.refs_4_, ...), custom_call_target="tpu_custom_call" | custom-call | flops 2000000000 | bytes 4000000 | tf_op jit(solution)/shard_map/voxels_own_row/pallas_call | solution.py:284
  18.1 0.7 %collective-permute-done.1.refs_1_ = bf16[272,256]{1,0:T(8,128)(2,1)S(1)} collective-permute-done((bf16[272,256]{1,0:T(8,128)(2,1)S(1)}, bf16[272,256]{1,0:T(8,128)(2,1)S(1)}, u32[]{:S(2)}, u32[]{:S(2)}) %collective-permute-start.1) | collective-permute-done | bytes 139296 | tf_op jit(solution)/shard_map/ppermute | solution.py:268
  18.8 1.7 %collective-permute-start.3 = (bf16[272,256]{1,0:T(8,128)(2,1)S(1)}, bf16[272,256]{1,0:T(8,128)(2,1)S(1)}, u32[]{:S(2)}, u32[]{:S(2)}) collective-permute-start(bf16[272,256]{1,0:T(8,128)(2,1)S(1)} %collective-permute-done.1.refs_1_), channel_id=1, source_target_pairs={{0,2},{2,0},{4,6},{6,4},{8,10},{10,8},{12,14},{14,12},{1,3},{3,1},... | collective-permute-start | bytes 417800 | tf_op jit(solution)/shard_map/ppermute | solution.py:265
  20.5 0.0 collective-permute-done.4.refs_2_.refs_4_.before_other
  20.5 2.1 %weight_row_1.1 = (f32[1664,128]{1,0:T(8,128)S(1)}, f32[1664,128]{1,0:T(8,128)S(1)}, f32[128,128]{1,0:T(8,128)S(1)}) custom-call(s32[1]{0:T(128)} %bitcast.where_ref.refs_0_, bf16[272,256]{1,0:T(8,128)(2,1)S(1)} %collective-permute-done.refs_1_.refs_3_.before_mine, bf16[272,256]{1,0:T(8,128)(2,1)S(1)} %collective-permute-done.4.refs_2_.refs_4_.before_other, ...), custom_call_target="tpu_custom_call" | custom-call | flops 2000000000 | bytes 4000000 | tf_op jit(solution)/shard_map/weight_row_1/pallas_call | solution.py:325
  22.6 0.0 collective-permute-done.6.refs_2_.refs_6_.after_other
  22.6 2.1 %weight_row_2.1 = (f32[1664,128]{1,0:T(8,128)S(1)}, f32[1664,128]{1,0:T(8,128)S(1)}, f32[128,128]{1,0:T(8,128)S(1)}) custom-call(s32[1]{0:T(128)} %bitcast.where_ref.refs_0_, bf16[272,256]{1,0:T(8,128)(2,1)S(1)} %collective-permute-done.5.refs_1_.refs_5_.after_mine, bf16[272,256]{1,0:T(8,128)(2,1)S(1)} %collective-permute-done.6.refs_2_.refs_6_.after_other, ...), custom_call_target="tpu_custom_call" | custom-call | flops 2000000000 | bytes 4000000 | tf_op jit(solution)/shard_map/weight_row_2/pallas_call | solution.py:325
  24.7 0.0 collective-permute-done.3.refs_2_
  24.7 2.5 %weight_row_3.1 = (f32[27,128,128]{2,1,0:T(8,128)S(1)}, bf16[27,128,128]{2,1,0:T(8,128)(2,1)S(1)}) custom-call(s32[1]{0:T(128)} %bitcast.where_ref.refs_0_, bf16[272,256]{1,0:T(8,128)(2,1)S(1)} %collective-permute-done.1.refs_1_, bf16[272,256]{1,0:T(8,128)(2,1)S(1)} %collective-permute-done.3.refs_2_, ...), custom_call_target="tpu_custom_call" | custom-call | flops 2000000000 | bytes 4000000 | tf_op jit(solution)/shard_map/weight_row_3/pallas_call | solution.py:325
  27.3 0.1 collective-permute-start.7
  27.3 1.9 %voxel_edges.1 = (bf16[256,128]{1,0:T(8,128)(2,1)}, bf16[256,128]{1,0:T(8,128)(2,1)}) custom-call(s32[1]{0:T(128)} %bitcast.where_ref.refs_0_, bf16[272,256]{1,0:T(8,128)(2,1)S(1)} %get-tuple-element.32.mine_ref.refs_1_.refs_3_, bf16[272,256]{1,0:T(8,128)(2,1)S(1)} %collective-permute-done.2.other_ref.refs_2_.refs_4_, ...), custom_call_target="tpu_custom_call" | custom-call | flops 1000000000 | bytes 4000000 | tf_op jit(solution)/shard_map/voxel_edges/pallas_call | solution.py:343
  29.2 0.5 %collective-permute-done.7.sent_ref = bf16[27,128,128]{2,1,0:T(8,128)(2,1)S(1)} collective-permute-done((bf16[27,128,128]{2,1,0:T(8,128)(2,1)S(1)}, bf16[27,128,128]{2,1,0:T(8,128)(2,1)S(1)}, u32[]{:S(2)}, u32[]{:S(2)}) %collective-permute-start.7) | collective-permute-done | bytes 884768 | tf_op jit(solution)/shard_map/ppermute | solution.py:342
  29.7 1.3 %finish.1 = f32[27,128,128]{2,1,0:T(8,128)} custom-call(f32[27,128,128]{2,1,0:T(8,128)S(1)} %get-tuple-element.57.kept_ref, bf16[27,128,128]{2,1,0:T(8,128)(2,1)S(1)} %collective-permute-done.7.sent_ref), custom_call_target="tpu_custom_call" | custom-call | tf_op jit(solution)/shard_map/finish/pallas_call | solution.py:362
Async XLA Ops:
  2.3 9.6 %collective-permute-start = (bf16[272,256]{1,0:T(8,128)(2,1)S(1)}, bf16[272,256]{1,0:T(8,128)(2,1)S(1)}, u32[]{:S(2)}, u32[]{:S(2)}) collective-permute-start(bf16[272,256]{1,0:T(8,128)(2,1)S(1)} %get-tuple-element.32.mine_ref.refs_1_.refs_3_), channel_id=1, source_target_pairs={{0,4},{2,6},{4,8},{6,10},{8,12},{10,14},{12,0},{14,2},{1,5},{3,7},... | collective-permute-start | bytes 417800 | tf_op jit(solution)/shard_map/ppermute | solution.py:268
  5.4 8.3 %collective-permute-start.5 = (bf16[272,256]{1,0:T(8,128)(2,1)S(1)}, bf16[272,256]{1,0:T(8,128)(2,1)S(1)}, u32[]{:S(2)}, u32[]{:S(2)}) collective-permute-start(bf16[272,256]{1,0:T(8,128)(2,1)S(1)} %get-tuple-element.32.mine_ref.refs_1_.refs_3_), channel_id=1, source_target_pairs={{0,12},{2,14},{4,0},{6,2},{8,4},{10,6},{12,8},{14,10},{1,13},{3,15... | collective-permute-start | bytes 417800 | tf_op jit(solution)/shard_map/ppermute | solution.py:268
  7.5 7.5 %collective-permute-start.2 = (bf16[272,256]{1,0:T(8,128)(2,1)S(1)}, bf16[272,256]{1,0:T(8,128)(2,1)S(1)}, u32[]{:S(2)}, u32[]{:S(2)}) collective-permute-start(bf16[272,256]{1,0:T(8,128)(2,1)S(1)} %get-tuple-element.32.mine_ref.refs_1_.refs_3_), channel_id=1, source_target_pairs={{0,2},{2,0},{4,6},{6,4},{8,10},{10,8},{12,14},{14,12},{1,3},{3,1},... | collective-permute-start | bytes 417800 | tf_op jit(solution)/shard_map/ppermute | solution.py:265
  9.1 1.2 %copy-start = (bf16[27,128,128]{2,1,0:T(8,128)(2,1)S(1)}, bf16[27,128,128]{2,1,0:T(8,128)(2,1)}, u32[]{:S(2)}) copy-start(bf16[27,128,128]{2,1,0:T(8,128)(2,1)} %w_ref) | copy-start | bytes 2654212
  11.9 6.9 %collective-permute-start.1 = (bf16[272,256]{1,0:T(8,128)(2,1)S(1)}, bf16[272,256]{1,0:T(8,128)(2,1)S(1)}, u32[]{:S(2)}, u32[]{:S(2)}) collective-permute-start(bf16[272,256]{1,0:T(8,128)(2,1)S(1)} %collective-permute-done.refs_1_.refs_3_.before_mine), channel_id=1, source_target_pairs={{0,4},{2,6},{4,8},{6,10},{8,12},{10,14},{12,0},{14,2},{1,5},{3,7},... | collective-permute-start | bytes 417800 | tf_op jit(solution)/shard_map/ppermute | solution.py:268
  11.9 8.6 %collective-permute-start.4 = (bf16[272,256]{1,0:T(8,128)(2,1)S(1)}, bf16[272,256]{1,0:T(8,128)(2,1)S(1)}, u32[]{:S(2)}, u32[]{:S(2)}) collective-permute-start(bf16[272,256]{1,0:T(8,128)(2,1)S(1)} %collective-permute-done.refs_1_.refs_3_.before_mine), channel_id=1, source_target_pairs={{0,2},{2,0},{4,6},{6,4},{8,10},{10,8},{12,14},{14,12},{1,3},{3,1},... | collective-permute-start | bytes 417800 | tf_op jit(solution)/shard_map/ppermute | solution.py:265
  13.7 9.0 %collective-permute-start.6 = (bf16[272,256]{1,0:T(8,128)(2,1)S(1)}, bf16[272,256]{1,0:T(8,128)(2,1)S(1)}, u32[]{:S(2)}, u32[]{:S(2)}) collective-permute-start(bf16[272,256]{1,0:T(8,128)(2,1)S(1)} %collective-permute-done.5.refs_1_.refs_5_.after_mine), channel_id=1, source_target_pairs={{0,2},{2,0},{4,6},{6,4},{8,10},{10,8},{12,14},{14,12},{1,3},{3,1},... | collective-permute-start | bytes 417800 | tf_op jit(solution)/shard_map/ppermute | solution.py:265
  18.8 5.9 %collective-permute-start.3 = (bf16[272,256]{1,0:T(8,128)(2,1)S(1)}, bf16[272,256]{1,0:T(8,128)(2,1)S(1)}, u32[]{:S(2)}, u32[]{:S(2)}) collective-permute-start(bf16[272,256]{1,0:T(8,128)(2,1)S(1)} %collective-permute-done.1.refs_1_), channel_id=1, source_target_pairs={{0,2},{2,0},{4,6},{6,4},{8,10},{10,8},{12,14},{14,12},{1,3},{3,1},... | collective-permute-start | bytes 417800 | tf_op jit(solution)/shard_map/ppermute | solution.py:265
  27.3 2.5 %collective-permute-start.7 = (bf16[27,128,128]{2,1,0:T(8,128)(2,1)S(1)}, bf16[27,128,128]{2,1,0:T(8,128)(2,1)S(1)}, u32[]{:S(2)}, u32[]{:S(2)}) collective-permute-start(bf16[27,128,128]{2,1,0:T(8,128)(2,1)S(1)} %get-tuple-element.50), channel_id=1, source_target_pairs={{0,1},{1,0},{2,3},{3,2},{4,5},{5,4},{6,7},{7,6},{8,9},{9,8},{10,11... | collective-permute-start | bytes 2654216 | tf_op jit(solution)/shard_map/ppermute | solution.py:342

commit v14 on v13

--- a/solution.py
+++ b/solution.py
@@ -277,9 +277,9 @@
         cost_estimate=pl.CostEstimate(flops=2 * 10**8, bytes_accessed=3 * 10**6, transcendentals=0),
         name="turn_weights",
     )(w_conv)
-    before, after = along(packed, 1), along(packed, -1)
-    before, w_forward = lax.optimization_barrier((before, w_forward))
-    far = along(before, 1)
+    after, before = along(packed, -1), along(packed, 1)
+    after, w_forward = lax.optimization_barrier((after, w_forward))
+    far = along(after, -1)
     own_pair = (packed, across(packed))
     own_conv, own_grad = pl.pallas_call(
         own_kernel,
@@ -298,14 +298,14 @@
         name="voxels_own_row",
     )(here, *own_pair, code, w_forward, w_back)
     far, own_conv = lax.optimization_barrier((far, own_conv))
+    after_pair = (after, across(after))
     before_pair = (before, across(before))
-    after_pair = (after, across(after))
     far_pair = (far, across(far))
     line = [(0, u) for u in range(TILE)]
     stages = (
         ((own_pair,), line, []),
+        ((after_pair, own_pair), line + [(1, TILE - 1)], [(0, TILE)]),
         ((before_pair, own_pair), line + [(1, 0)], [(TILE, TILE - 1)]),
-        ((after_pair, own_pair), line + [(1, TILE - 1)], [(0, TILE)]),
         ((far_pair, before_pair, after_pair), line + [(1, 0), (2, TILE - 1)], [(TILE, TILE - 1), (0, TILE + 1)]),
     )
     sums = ()

time: 31.3 us -> 33.2 us (1.061)
  starting transfers between devices: 11.6 us -> 14.5 us
  waiting for transfers between devices: 2.54 us -> 1.59 us
    ppermute x3, starting transfers between devices: 5.17 us -> 9.39 us  [along(): lax.ppermute(block, 'brick', [(i, (i + turn * tiles_y) % peers) for i in...]
    ppermute x4, starting transfers between devices: 6.4 us -> 5.07 us  [across(): return lax.ppermute(block, 'brick', [(i, i ^ 1) for i in range(peers)])]
    ppermute x3, waiting for transfers between devices: 2 us -> 1.05 us  [along(): lax.ppermute(block, 'brick', [(i, (i + turn * tiles_y) % peers) for i in...]
  transfers between devices with their start and end apart: 8 -> 8, of which waited for: 3 -> 2; matrix products, arithmetic and copies ran while one was open for 0% -> 0% of each run, Pallas kernels for 31% -> 29%
where the time goes in v14:
time: 33.2 us; the launch traced here: 33 us
  starting transfers between devices  14.5 us (44%)
  Pallas kernels  14.3 us (43%)
  waiting for transfers between devices  1.59 us (5%)
  between operations  1.36 us (4%)
  local copies, waits for them, and re-layouts  1.17 us (4%)
    ppermute x3, starting transfers between devices, along(): lax.ppermute(block, 'brick', [(i, (i + turn * tiles_y) % peers) for i in...  9.39 us
    pallas_call x4, Pallas kernels, whole_scene(): pl.pallas_call(functools.partial(row_kernel, stage, strips, borders), out...  8.47 us
    ppermute x4, starting transfers between devices, across(): return lax.ppermute(block, 'brick', [(i, i ^ 1) for i in range(peers)])  5.07 us
    pallas_call x1, Pallas kernels, whole_scene(): pl.pallas_call(edge_kernel, out_shape=(jax.ShapeDtypeStruct((rows, width)...  1.88 us
    pallas_call x1, Pallas kernels, whole_scene(): pl.pallas_call(own_kernel, out_shape=(jax.ShapeDtypeStruct((width, rows),...  1.29 us
    pallas_call x1, Pallas kernels, whole_scene(): pl.pallas_call(finish_kernel, out_shape=jax.ShapeDtypeStruct((27, width,...  1.29 us
    unnamed x2, local copies, waits for them, and re-layouts  1.17 us
    ppermute x3, waiting for transfers between devices, along(): lax.ppermute(block, 'brick', [(i, (i + turn * tiles_y) % peers) for i in...  1.05 us
  transfers between devices with their start and end apart: 8, of which 2 were waited for; matrix products, arithmetic and copies ran while one was open for 0% of the time, Pallas kernels for 29%

profile of v14, /device:TPU:0, one launch (start us, length us, event | category | flops | bytes accessed | tf_op | source)
XLA Modules:
  0.0 33.0 jit_solution(6127912105505502173)
XLA Ops:
  1.3 1.0 %pack_tile.1 = (bf16[272,256]{1,0:T(8,128)(2,1)S(1)}, f32[256,128]{1,0:T(8,128)S(1)}, f32[27,256]{1,0:T(8,128)S(1)}) custom-call(s32[1]{0:T(128)S(6)} %copy.10.time_ref, bf16[1,256,128]{2,1,0:T(8,128)(2,1)} %feat_hbm.1, bf16[1,256,128]{2,1,0:T(8,128)(2,1)} %cot_hbm.1, s32[27,256]{1,0:T(8,128)} %near_hbm.1, bf16[1,128]{1,0:T(2,128)(2,1)} %cond_hbm.1, ...), custom_call_target="tpu_custom_call" | custom-call | tf_op jit(solution)/shard_map/pack_tile/pallas_call | solution.py:243
  2.3 5.1 %collective-permute-start = (bf16[272,256]{1,0:T(8,128)(2,1)S(1)}, bf16[272,256]{1,0:T(8,128)(2,1)S(1)}, u32[]{:S(2)}, u32[]{:S(2)}) collective-permute-start(bf16[272,256]{1,0:T(8,128)(2,1)S(1)} %get-tuple-element.32.mine_ref.refs_1_.refs_3_), channel_id=1, source_target_pairs={{0,12},{2,14},{4,0},{6,2},{8,4},{10,6},{12,8},{14,10},{1,13},{3,15... | collective-permute-start | bytes 417800 | tf_op jit(solution)/shard_map/ppermute | solution.py:268
  7.4 0.0 collective-permute-start.4
  7.4 1.5 %collective-permute-start.2 = (bf16[272,256]{1,0:T(8,128)(2,1)S(1)}, bf16[272,256]{1,0:T(8,128)(2,1)S(1)}, u32[]{:S(2)}, u32[]{:S(2)}) collective-permute-start(bf16[272,256]{1,0:T(8,128)(2,1)S(1)} %get-tuple-element.32.mine_ref.refs_1_.refs_3_), channel_id=1, source_target_pairs={{0,2},{2,0},{4,6},{6,4},{8,10},{10,8},{12,14},{14,12},{1,3},{3,1},... | collective-permute-start | bytes 417800 | tf_op jit(solution)/shard_map/ppermute | solution.py:265
  8.9 0.0 copy-start
  8.9 1.2 %copy-done = bf16[27,128,128]{2,1,0:T(8,128)(2,1)S(1)} copy-done((bf16[27,128,128]{2,1,0:T(8,128)(2,1)S(1)}, bf16[27,128,128]{2,1,0:T(8,128)(2,1)}, u32[]{:S(2)}) %copy-start) | copy-done | bytes 884760
  10.1 0.4 %turn_weights.1 = (bf16[128,3456]{1,0:T(8,128)(2,1)S(1)}, bf16[128,3456]{1,0:T(8,128)(2,1)S(1)}) custom-call(bf16[27,128,128]{2,1,0:T(8,128)(2,1)S(1)} %copy-done), custom_call_target="tpu_custom_call" | custom-call | flops 200000000 | bytes 3000000 | tf_op jit(solution)/shard_map/turn_weights/pallas_call | solution.py:271
  10.5 1.0 %collective-permute-done.refs_1_.refs_5_.after_mine = bf16[272,256]{1,0:T(8,128)(2,1)S(1)} collective-permute-done((bf16[272,256]{1,0:T(8,128)(2,1)S(1)}, bf16[272,256]{1,0:T(8,128)(2,1)S(1)}, u32[]{:S(2)}, u32[]{:S(2)}) %collective-permute-start) | collective-permute-done | bytes 139296 | tf_op jit(solution)/shard_map/ppermute | solution.py:268
  11.5 4.3 %collective-permute-start.1 = (bf16[272,256]{1,0:T(8,128)(2,1)S(1)}, bf16[272,256]{1,0:T(8,128)(2,1)S(1)}, u32[]{:S(2)}, u32[]{:S(2)}) collective-permute-start(bf16[272,256]{1,0:T(8,128)(2,1)S(1)} %collective-permute-done.refs_1_.refs_5_.after_mine), channel_id=1, source_target_pairs={{0,12},{2,14},{4,0},{6,2},{8,4},{10,6},{12,8},{14,10},{1,13},{3,15... | collective-permute-start | bytes 417800 | tf_op jit(solution)/shard_map/ppermute | solution.py:268
  15.8 1.5 %collective-permute-start.6 = (bf16[272,256]{1,0:T(8,128)(2,1)S(1)}, bf16[272,256]{1,0:T(8,128)(2,1)S(1)}, u32[]{:S(2)}, u32[]{:S(2)}) collective-permute-start(bf16[272,256]{1,0:T(8,128)(2,1)S(1)} %collective-permute-done.refs_1_.refs_5_.after_mine), channel_id=1, source_target_pairs={{0,2},{2,0},{4,6},{6,4},{8,10},{10,8},{12,14},{14,12},{1,3},{3,1},... | collective-permute-start | bytes 417800 | tf_op jit(solution)/shard_map/ppermute | solution.py:265
  17.3 0.0 collective-permute-done.4.refs_1_.refs_3_.before_mine
  17.3 0.5 %collective-permute-start.5 = (bf16[272,256]{1,0:T(8,128)(2,1)S(1)}, bf16[272,256]{1,0:T(8,128)(2,1)S(1)}, u32[]{:S(2)}, u32[]{:S(2)}) collective-permute-start(bf16[272,256]{1,0:T(8,128)(2,1)S(1)} %collective-permute-done.4.refs_1_.refs_3_.before_mine), channel_id=1, source_target_pairs={{0,2},{2,0},{4,6},{6,4},{8,10},{10,8},{12,14},{14,12},{1,3},{3,1},... | collective-permute-start | bytes 417800 | tf_op jit(solution)/shard_map/ppermute | solution.py:265
  17.8 0.0 collective-permute-done.2.other_ref.refs_2_.refs_4_
  17.8 1.8 %weight_row_0.1 = (f32[1664,128]{1,0:T(8,128)S(1)}, f32[1664,128]{1,0:T(8,128)S(1)}, f32[128,128]{1,0:T(8,128)S(1)}) custom-call(s32[1]{0:T(128)} %bitcast.where_ref.refs_0_, bf16[272,256]{1,0:T(8,128)(2,1)S(1)} %get-tuple-element.32.mine_ref.refs_1_.refs_3_, bf16[272,256]{1,0:T(8,128)(2,1)S(1)} %collective-permute-done.2.other_ref.refs_2_.refs_4_), custom_call_target="tpu_custom_call" | custom-call | flops 2000000000 | bytes 4000000 | tf_op jit(solution)/shard_map/weight_row_0/pallas_call | solution.py:325
  19.6 1.3 %voxels_own_row.1 = (f32[128,256]{1,0:T(8,128)S(1)}, f32[128,256]{1,0:T(8,128)S(1)}) custom-call(s32[1]{0:T(128)} %bitcast.where_ref.refs_0_, bf16[272,256]{1,0:T(8,128)(2,1)S(1)} %get-tuple-element.32.mine_ref.refs_1_.refs_3_, bf16[272,256]{1,0:T(8,128)(2,1)S(1)} %collective-permute-done.2.other_ref.refs_2_.refs_4_, ...), custom_call_target="tpu_custom_call" | custom-call | flops 2000000000 | bytes 4000000 | tf_op jit(solution)/shard_map/voxels_own_row/pallas_call | solution.py:284
  20.9 0.0 collective-permute-done.1.refs_1_
  20.9 1.6 %collective-permute-start.3 = (bf16[272,256]{1,0:T(8,128)(2,1)S(1)}, bf16[272,256]{1,0:T(8,128)(2,1)S(1)}, u32[]{:S(2)}, u32[]{:S(2)}) collective-permute-start(bf16[272,256]{1,0:T(8,128)(2,1)S(1)} %collective-permute-done.1.refs_1_), channel_id=1, source_target_pairs={{0,2},{2,0},{4,6},{6,4},{8,10},{10,8},{12,14},{14,12},{1,3},{3,1},... | collective-permute-start | bytes 417800 | tf_op jit(solution)/shard_map/ppermute | solution.py:265
  22.4 0.0 collective-permute-done.6.refs_2_.refs_6_.after_other
  22.4 2.1 %weight_row_1.1 = (f32[1664,128]{1,0:T(8,128)S(1)}, f32[1664,128]{1,0:T(8,128)S(1)}, f32[128,128]{1,0:T(8,128)S(1)}) custom-call(s32[1]{0:T(128)} %bitcast.where_ref.refs_0_, bf16[272,256]{1,0:T(8,128)(2,1)S(1)} %collective-permute-done.refs_1_.refs_5_.after_mine, bf16[272,256]{1,0:T(8,128)(2,1)S(1)} %collective-permute-done.6.refs_2_.refs_6_.after_other, ...), custom_call_target="tpu_custom_call" | custom-call | flops 2000000000 | bytes 4000000 | tf_op jit(solution)/shard_map/weight_row_1/pallas_call | solution.py:325
  24.5 0.0 collective-permute-done.5.refs_2_.refs_4_.before_other
  24.6 2.1 %weight_row_2.1 = (f32[1664,128]{1,0:T(8,128)S(1)}, f32[1664,128]{1,0:T(8,128)S(1)}, f32[128,128]{1,0:T(8,128)S(1)}) custom-call(s32[1]{0:T(128)} %bitcast.where_ref.refs_0_, bf16[272,256]{1,0:T(8,128)(2,1)S(1)} %collective-permute-done.4.refs_1_.refs_3_.before_mine, bf16[272,256]{1,0:T(8,128)(2,1)S(1)} %collective-permute-done.5.refs_2_.refs_4_.before_other, ...), custom_call_target="tpu_custom_call" | custom-call | flops 2000000000 | bytes 4000000 | tf_op jit(solution)/shard_map/weight_row_2/pallas_call | solution.py:325
  26.6 0.0 collective-permute-done.3.refs_2_
  26.7 2.5 %weight_row_3.1 = (f32[27,128,128]{2,1,0:T(8,128)S(1)}, bf16[27,128,128]{2,1,0:T(8,128)(2,1)S(1)}) custom-call(s32[1]{0:T(128)} %bitcast.where_ref.refs_0_, bf16[272,256]{1,0:T(8,128)(2,1)S(1)} %collective-permute-done.1.refs_1_, bf16[272,256]{1,0:T(8,128)(2,1)S(1)} %collective-permute-done.3.refs_2_, ...), custom_call_target="tpu_custom_call" | custom-call | flops 2000000000 | bytes 4000000 | tf_op jit(solution)/shard_map/weight_row_3/pallas_call | solution.py:325
  29.2 0.1 collective-permute-start.7
  29.3 1.9 %voxel_edges.1 = (bf16[256,128]{1,0:T(8,128)(2,1)}, bf16[256,128]{1,0:T(8,128)(2,1)}) custom-call(s32[1]{0:T(128)} %bitcast.where_ref.refs_0_, bf16[272,256]{1,0:T(8,128)(2,1)S(1)} %get-tuple-element.32.mine_ref.refs_1_.refs_3_, bf16[272,256]{1,0:T(8,128)(2,1)S(1)} %collective-permute-done.2.other_ref.refs_2_.refs_4_, ...), custom_call_target="tpu_custom_call" | custom-call | flops 1000000000 | bytes 4000000 | tf_op jit(solution)/shard_map/voxel_edges/pallas_call | solution.py:343
  31.2 0.5 %collective-permute-done.7.sent_ref = bf16[27,128,128]{2,1,0:T(8,128)(2,1)S(1)} collective-permute-done((bf16[27,128,128]{2,1,0:T(8,128)(2,1)S(1)}, bf16[27,128,128]{2,1,0:T(8,128)(2,1)S(1)}, u32[]{:S(2)}, u32[]{:S(2)}) %collective-permute-start.7) | collective-permute-done | bytes 884768 | tf_op jit(solution)/shard_map/ppermute | solution.py:342
  31.7 1.3 %finish.1 = f32[27,128,128]{2,1,0:T(8,128)} custom-call(f32[27,128,128]{2,1,0:T(8,128)S(1)} %get-tuple-element.57.kept_ref, bf16[27,128,128]{2,1,0:T(8,128)(2,1)S(1)} %collective-permute-done.7.sent_ref), custom_call_target="tpu_custom_call" | custom-call | tf_op jit(solution)/shard_map/finish/pallas_call | solution.py:362
Async XLA Ops:
  2.3 9.2 %collective-permute-start = (bf16[272,256]{1,0:T(8,128)(2,1)S(1)}, bf16[272,256]{1,0:T(8,128)(2,1)S(1)}, u32[]{:S(2)}, u32[]{:S(2)}) collective-permute-start(bf16[272,256]{1,0:T(8,128)(2,1)S(1)} %get-tuple-element.32.mine_ref.refs_1_.refs_3_), channel_id=1, source_target_pairs={{0,12},{2,14},{4,0},{6,2},{8,4},{10,6},{12,8},{14,10},{1,13},{3,15... | collective-permute-start | bytes 417800 | tf_op jit(solution)/shard_map/ppermute | solution.py:268
  7.4 9.9 %collective-permute-start.4 = (bf16[272,256]{1,0:T(8,128)(2,1)S(1)}, bf16[272,256]{1,0:T(8,128)(2,1)S(1)}, u32[]{:S(2)}, u32[]{:S(2)}) collective-permute-start(bf16[272,256]{1,0:T(8,128)(2,1)S(1)} %get-tuple-element.32.mine_ref.refs_1_.refs_3_), channel_id=1, source_target_pairs={{0,4},{2,6},{4,8},{6,10},{8,12},{10,14},{12,0},{14,2},{1,5},{3,7},... | collective-permute-start | bytes 417800 | tf_op jit(solution)/shard_map/ppermute | solution.py:268
  7.4 10.4 %collective-permute-start.2 = (bf16[272,256]{1,0:T(8,128)(2,1)S(1)}, bf16[272,256]{1,0:T(8,128)(2,1)S(1)}, u32[]{:S(2)}, u32[]{:S(2)}) collective-permute-start(bf16[272,256]{1,0:T(8,128)(2,1)S(1)} %get-tuple-element.32.mine_ref.refs_1_.refs_3_), channel_id=1, source_target_pairs={{0,2},{2,0},{4,6},{6,4},{8,10},{10,8},{12,14},{14,12},{1,3},{3,1},... | collective-permute-start | bytes 417800 | tf_op jit(solution)/shard_map/ppermute | solution.py:265
  8.9 1.2 %copy-start = (bf16[27,128,128]{2,1,0:T(8,128)(2,1)S(1)}, bf16[27,128,128]{2,1,0:T(8,128)(2,1)}, u32[]{:S(2)}) copy-start(bf16[27,128,128]{2,1,0:T(8,128)(2,1)} %w_ref) | copy-start | bytes 2654212
  11.5 9.4 %collective-permute-start.1 = (bf16[272,256]{1,0:T(8,128)(2,1)S(1)}, bf16[272,256]{1,0:T(8,128)(2,1)S(1)}, u32[]{:S(2)}, u32[]{:S(2)}) collective-permute-start(bf16[272,256]{1,0:T(8,128)(2,1)S(1)} %collective-permute-done.refs_1_.refs_5_.after_mine), channel_id=1, source_target_pairs={{0,12},{2,14},{4,0},{6,2},{8,4},{10,6},{12,8},{14,10},{1,13},{3,15... | collective-permute-start | bytes 417800 | tf_op jit(solution)/shard_map/ppermute | solution.py:268
  15.8 6.7 %collective-permute-start.6 = (bf16[272,256]{1,0:T(8,128)(2,1)S(1)}, bf16[272,256]{1,0:T(8,128)(2,1)S(1)}, u32[]{:S(2)}, u32[]{:S(2)}) collective-permute-start(bf16[272,256]{1,0:T(8,128)(2,1)S(1)} %collective-permute-done.refs_1_.refs_5_.after_mine), channel_id=1, source_target_pairs={{0,2},{2,0},{4,6},{6,4},{8,10},{10,8},{12,14},{14,12},{1,3},{3,1},... | collective-permute-start | bytes 417800 | tf_op jit(solution)/shard_map/ppermute | solution.py:265
  17.3 7.3 %collective-permute-start.5 = (bf16[272,256]{1,0:T(8,128)(2,1)S(1)}, bf16[272,256]{1,0:T(8,128)(2,1)S(1)}, u32[]{:S(2)}, u32[]{:S(2)}) collective-permute-start(bf16[272,256]{1,0:T(8,128)(2,1)S(1)} %collective-permute-done.4.refs_1_.refs_3_.before_mine), channel_id=1, source_target_pairs={{0,2},{2,0},{4,6},{6,4},{8,10},{10,8},{12,14},{14,12},{1,3},{3,1},... | collective-permute-start | bytes 417800 | tf_op jit(solution)/shard_map/ppermute | solution.py:265
  20.9 5.8 %collective-permute-start.3 = (bf16[272,256]{1,0:T(8,128)(2,1)S(1)}, bf16[272,256]{1,0:T(8,128)(2,1)S(1)}, u32[]{:S(2)}, u32[]{:S(2)}) collective-permute-start(bf16[272,256]{1,0:T(8,128)(2,1)S(1)} %collective-permute-done.1.refs_1_), channel_id=1, source_target_pairs={{0,2},{2,0},{4,6},{6,4},{8,10},{10,8},{12,14},{14,12},{1,3},{3,1},... | collective-permute-start | bytes 417800 | tf_op jit(solution)/shard_map/ppermute | solution.py:265
  29.2 2.5 %collective-permute-start.7 = (bf16[27,128,128]{2,1,0:T(8,128)(2,1)S(1)}, bf16[27,128,128]{2,1,0:T(8,128)(2,1)S(1)}, u32[]{:S(2)}, u32[]{:S(2)}) collective-permute-start(bf16[27,128,128]{2,1,0:T(8,128)(2,1)S(1)} %get-tuple-element.50), channel_id=1, source_target_pairs={{0,1},{1,0},{2,3},{3,2},{4,5},{5,4},{6,7},{7,6},{8,9},{9,8},{10,11... | collective-permute-start | bytes 2654216 | tf_op jit(solution)/shard_map/ppermute | solution.py:342

commit v15 on v12

--- a/solution.py
+++ b/solution.py
@@ -75,9 +75,8 @@
         ground[pl.ds(at, STRIP), :] = ref[u * STRIP:(u + 1) * STRIP, :]
 
 
-def row_kernel(stage, strips, borders, *refs):
+def row_kernel(first_stage, final, groups, strips, borders, *refs):
     refs = list(refs)
-    first_stage, final = stage == 0, stage == ROW_STAGES - 1
     where_ref = refs.pop(0)
     pairs = [(refs.pop(0), refs.pop(0)) for _ in range(1 + max(pair for pair, _ in strips))]
     before = [refs.pop(0) for _ in range(0 if first_stage else 3)]
@@ -109,41 +108,40 @@
             near_act[k * width:(k + 1) * width, target * span:(target + 1) * span] = one[:width]
             near_cot[k * width:(k + 1) * width, target * span:(target + 1) * span] = one[width:]
 
-    for u in range(TILE):
-        gather(u, u, 9, HALF)
-    for target, source in borders:
-        gather(target, source, 0, 9)
-    low_from = span * targets[0]
-    low_to = span * (targets[-1] + 1)
-
-    def product(near, start, stop, first, last, side):
-        return jnp.dot(near[start * width:stop * width, first:last],
-                       ground[first:last, side * width:(side + 1) * width], preferred_element_type=jnp.float32)
-
-    pieces = []
-    for near, side in ((near_act, 1), (near_cot, 0)):
-        pieces.append(((0, 9), product(near, 0, 9, low_from, low_to, side)))
-        pieces.append(((9, HALF), product(near, 9, HALF, 0, TILE * span, side)))
-    centre = jnp.dot(turned[:width, :TILE * span], ground[:TILE * span, width:], preferred_element_type=jnp.float32)
-    if not first_stage:
-        centre = centre + before[2][...]
-    for i, ((start, stop), value) in enumerate(pieces):
-        turn = i // 2
+    if 1 in groups:
+        for u in range(TILE):
+            gather(u, u, 9, HALF)
+    if 0 in groups:
+        for target, source in borders:
+            gather(target, source, 0, 9)
+    extents = ((0, 9, span * targets[0], span * (targets[-1] + 1)), (9, HALF, 0, TILE * span))
+    for turn, near in ((0, near_act), (1, near_cot)):
+        for group in groups:
+            start, stop, first, last = extents[group]
+            other = ground[first:last, (1 - turn) * width:(2 - turn) * width]
+            value = jnp.dot(near[start * width:stop * width, first:last], other, preferred_element_type=jnp.float32)
+            if not first_stage:
+                value = value + before[turn][start * width:stop * width, :]
+            if not final:
+                outs[turn][start * width:stop * width, :] = value
+                continue
+            for k in range(start, stop):
+                one = value[(k - start) * width:(k - start + 1) * width, :]
+                to = 2 * HALF - k if turn else k
+                if turn:
+                    one = one.T
+                to = to - 9 if group == 1 else to - 9 * turn
+                outs[0][to] = one
+                outs[1][to] = one.astype(jnp.bfloat16)
+    if 1 in groups:
+        centre = jnp.dot(turned[:width, :TILE * span], ground[:TILE * span, width:], preferred_element_type=jnp.float32)
         if not first_stage:
-            value = value + before[turn][start * width:stop * width, :]
-        if not final:
-            outs[turn][start * width:stop * width, :] = value
-            continue
-        for k in range(start, stop):
-            one = value[(k - start) * width:(k - start + 1) * width, :]
-            one, to = (one.T, 2 * HALF - k) if turn else (one, k)
-            outs[0][to] = one
-            outs[1][to] = one.astype(jnp.bfloat16)
-    if final:
-        outs[0][HALF] = centre
-        outs[1][HALF] = centre.astype(jnp.bfloat16)
-    else:
-        outs[2][...] = centre
+            centre = centre + before[2][...]
+        if final:
+            outs[0][HALF - 9] = centre
+            outs[1][HALF - 9] = centre.astype(jnp.bfloat16)
+        else:
+            outs[2][...] = centre
 
 
 def turn_kernel(w_ref, forward_ref, back_ref):
@@ -218,11 +216,13 @@
     grad_ref[...] = (back * sig * (1.0 + z_val * (1.0 - sig))).astype(jnp.bfloat16)
 
 
-def finish_kernel(kept_ref, sent_ref, weight_hbm, weight, sems):
+def finish_kernel(sides_ref, sides_sent, middle_ref, middle_sent, weight_hbm, weight, sems):
     copies = []
     for i, first in enumerate(range(0, 27, FINISH_STEP)):
-        part = slice(first, first + FINISH_STEP)
-        weight[part] = kept_ref[part] + sent_ref[part].astype(jnp.float32)
+        kept, sent, at = (middle_ref, middle_sent, first - 9) if first // 9 == 1 else (
+            sides_ref, sides_sent, first if first < 9 else first - 9)
+        part, taken = pl.ds(first, FINISH_STEP), pl.ds(at, FINISH_STEP)
+        weight[part] = kept[taken] + sent[taken].astype(jnp.float32)
         copies.append(pltpu.make_async_copy(weight.at[part], weight_hbm.at[part], sems.at[i]))
         copies[-1].start()
     for copy in copies:
@@ -297,20 +297,12 @@
     before_pair = (before, across(before))
     after_pair = (after, across(after))
     far_pair = (far, across(far))
-    line = [(0, u) for u in range(TILE)]
-    stages = (
-        ((own_pair,), line, []),
-        ((before_pair, own_pair), line + [(1, 0)], [(TILE, TILE - 1)]),
-        ((after_pair, own_pair), line + [(1, TILE - 1)], [(0, TILE)]),
-        ((far_pair, before_pair, after_pair), line + [(1, 0), (2, TILE - 1)], [(TILE, TILE - 1), (0, TILE + 1)]),
-    )
-    sums = ()
-    for stage, (pairs, strips, borders) in enumerate(stages):
+    def row_sums(name, pairs, strips, borders, sums, groups=(0, 1), final=0):
         blocks = [block for pair in pairs for block in pair]
-        if stage == ROW_STAGES - 1:
+        if final:
             out_shape = (
-                jax.ShapeDtypeStruct((27, width, width), jnp.float32),
-                jax.ShapeDtypeStruct((27, width, width), jnp.bfloat16),
+                jax.ShapeDtypeStruct((final, width, width), jnp.float32),
+                jax.ShapeDtypeStruct((final, width, width), jnp.bfloat16),
             )
         else:
             out_shape = (
@@ -318,8 +310,8 @@
                 jax.ShapeDtypeStruct((HALF * width, width), jnp.float32),
                 jax.ShapeDtypeStruct((width, width), jnp.float32),
             )
-        sums = pl.pallas_call(
-            functools.partial(row_kernel, stage, strips, borders),
+        return pl.pallas_call(
+            functools.partial(row_kernel, not sums, bool(final), groups, strips, borders),
             out_shape=out_shape,
             in_specs=[smem] + [vmem] * (len(blocks) + len(sums)),
             out_specs=(vmem,) * len(out_shape),
@@ -332,10 +324,24 @@
             ],
             compiler_params=params,
             cost_estimate=pl.CostEstimate(flops=2 * 10**9, bytes_accessed=4 * 10**6, transcendentals=0),
-            name=f"weight_row_{stage}",
+            name=name,
         )(here, *blocks, *sums)
-    own, sent = sums
-    other = lax.ppermute(sent, "batch", [(0, 1), (1, 0)])
+
+    def swapped(block):
+        return lax.ppermute(block, "batch", [(0, 1), (1, 0)])
+
+    line = [(0, u) for u in range(TILE)]
+    sums = row_sums("weight_row_0", (own_pair,), line, [], ())
+    sums = row_sums("weight_row_1", (before_pair, own_pair), line + [(1, 0)], [(TILE, TILE - 1)], sums)
+    sums = row_sums("weight_row_2", (after_pair, own_pair), line + [(1, TILE - 1)], [(0, TILE)], sums)
+    sides, sides_sent = row_sums("weight_row_3", (far_pair, before_pair, after_pair),
+                                 line + [(1, 0), (2, TILE - 1)], [(TILE, TILE - 1), (0, TILE + 1)],
+                                 sums, groups=(0,), final=18)
+    sides_other = swapped(sides_sent)
+    centre, sides = lax.optimization_barrier((sums[2], sides))
+    middle, middle_sent = row_sums("weight_row_3_middle", (far_pair,), line, [], (sums[0], sums[1], centre),
+                                   groups=(1,), final=9)
+    middle_other = swapped(middle_sent)
     conv_out, feature_grad = pl.pallas_call(
         edge_kernel,
         out_shape=(jax.ShapeDtypeStruct((rows, width), jnp.bfloat16),) * 2,
@@ -350,11 +356,11 @@
         cost_estimate=pl.CostEstimate(flops=10**9, bytes_accessed=4 * 10**6, transcendentals=0),
         name="voxel_edges",
     )(here, *before_pair, *after_pair, code, w_forward, w_back, own_conv, own_grad, z_val)
-    other, conv_out = lax.optimization_barrier((other, conv_out))
+    middle_other, conv_out = lax.optimization_barrier((middle_other, conv_out))
     weight_grad = pl.pallas_call(
         finish_kernel,
         out_shape=jax.ShapeDtypeStruct((27, width, width), jnp.float32),
-        in_specs=[vmem] * 2,
+        in_specs=[vmem] * 4,
         out_specs=pl.BlockSpec(memory_space=pltpu.HBM),
         scratch_shapes=[
             pltpu.VMEM((27, width, width), jnp.float32),
@@ -362,7 +368,7 @@
         ],
         compiler_params=pltpu.CompilerParams(vmem_limit_bytes=PACK_VMEM),
         name="finish",
-    )(own, other)
+    )(sides, sides_other, middle, middle_other)
     return (conv_out[None], feature_grad[None], weight_grad)
 
 

time: 31.3 us -> 31.2 us (level)
  waiting for transfers between devices: 2.31 us -> 1.45 us
  starting transfers between devices: 11.6 us -> 12.2 us
    ppermute x1 -> x2, waiting for transfers between devices: 0.86 us -> 0.01 us  [swapped(): return lax.ppermute(block, 'batch', [(0, 1), (1, 0)])]
    ppermute x1 -> x2, starting transfers between devices: 0.07 us -> 0.63 us  [swapped(): return lax.ppermute(block, 'batch', [(0, 1), (1, 0)])]
    pallas_call x4 -> x5, Pallas kernels: 8.48 us -> 8.76 us  [row_sums(): pl.pallas_call(functools.partial(row_kernel, not sums, bool(final), group...]
  transfers between devices with their start and end apart: 8 -> 9, of which waited for: 3 -> 2; matrix products, arithmetic and copies ran while one was open for 0% -> 0% of each run, Pallas kernels for 31% -> 34%
where the time goes in v15:
time: 31.2 us; the launch traced here: 31 us
  Pallas kernels  14.8 us (47%)
  starting transfers between devices  12.2 us (39%)
  waiting for transfers between devices  1.45 us (5%)
  between operations  1.36 us (4%)
  local copies, waits for them, and re-layouts  1.17 us (4%)
    pallas_call x5, Pallas kernels, row_sums(): pl.pallas_call(functools.partial(row_kernel, not sums, bool(final), group...  8.76 us
    ppermute x4, starting transfers between devices, across(): return lax.ppermute(block, 'brick', [(i, i ^ 1) for i in range(peers)])  6.4 us
    ppermute x3, starting transfers between devices, along(): lax.ppermute(block, 'brick', [(i, (i + turn * tiles_y) % peers) for i in...  5.17 us
    pallas_call x1, Pallas kernels, whole_scene(): pl.pallas_call(own_kernel, out_shape=(jax.ShapeDtypeStruct((width, rows),...  1.86 us
    pallas_call x1, Pallas kernels, whole_scene(): pl.pallas_call(edge_kernel, out_shape=(jax.ShapeDtypeStruct((rows, width)...  1.55 us
    ppermute x3, waiting for transfers between devices, along(): lax.ppermute(block, 'brick', [(i, (i + turn * tiles_y) % peers) for i in...  1.43 us
    pallas_call x1, Pallas kernels, whole_scene(): pl.pallas_call(finish_kernel, out_shape=jax.ShapeDtypeStruct((27, width,...  1.29 us
    unnamed x2, local copies, waits for them, and re-layouts  1.17 us
  transfers between devices with their start and end apart: 9, of which 2 were waited for; matrix products, arithmetic and copies ran while one was open for 0% of the time, Pallas kernels for 34%

profile of v15, /device:TPU:0, one launch (start us, length us, event | category | flops | bytes accessed | tf_op | source)
XLA Modules:
  0.0 31.0 jit_solution(8204327716030607107)
XLA Ops:
  1.3 1.0 %pack_tile.1 = (bf16[272,256]{1,0:T(8,128)(2,1)S(1)}, f32[256,128]{1,0:T(8,128)S(1)}, f32[27,256]{1,0:T(8,128)S(1)}) custom-call(s32[1]{0:T(128)S(6)} %copy.10.time_ref, bf16[1,256,128]{2,1,0:T(8,128)(2,1)} %feat_hbm.1, bf16[1,256,128]{2,1,0:T(8,128)(2,1)} %cot_hbm.1, s32[27,256]{1,0:T(8,128)} %near_hbm.1, bf16[1,128]{1,0:T(2,128)(2,1)} %cond_hbm.1, ...), custom_call_target="tpu_custom_call" | custom-call | tf_op jit(solution)/shard_map/pack_tile/pallas_call | solution.py:239
  2.3 3.1 %collective-permute-start = (bf16[272,256]{1,0:T(8,128)(2,1)S(1)}, bf16[272,256]{1,0:T(8,128)(2,1)S(1)}, u32[]{:S(2)}, u32[]{:S(2)}) collective-permute-start(bf16[272,256]{1,0:T(8,128)(2,1)S(1)} %get-tuple-element.36.mine_ref.refs_1_.refs_3_), channel_id=1, source_target_pairs={{0,4},{2,6},{4,8},{6,10},{8,12},{10,14},{12,0},{14,2},{1,5},{3,7},... | collective-permute-start | bytes 417800 | tf_op jit(solution)/shard_map/ppermute | solution.py:264
  5.4 2.1 %collective-permute-start.4 = (bf16[272,256]{1,0:T(8,128)(2,1)S(1)}, bf16[272,256]{1,0:T(8,128)(2,1)S(1)}, u32[]{:S(2)}, u32[]{:S(2)}) collective-permute-start(bf16[272,256]{1,0:T(8,128)(2,1)S(1)} %get-tuple-element.36.mine_ref.refs_1_.refs_3_), channel_id=1, source_target_pairs={{0,12},{2,14},{4,0},{6,2},{8,4},{10,6},{12,8},{14,10},{1,13},{3,15... | collective-permute-start | bytes 417800 | tf_op jit(solution)/shard_map/ppermute | solution.py:264
  7.5 1.6 %collective-permute-start.2 = (bf16[272,256]{1,0:T(8,128)(2,1)S(1)}, bf16[272,256]{1,0:T(8,128)(2,1)S(1)}, u32[]{:S(2)}, u32[]{:S(2)}) collective-permute-start(bf16[272,256]{1,0:T(8,128)(2,1)S(1)} %get-tuple-element.36.mine_ref.refs_1_.refs_3_), channel_id=1, source_target_pairs={{0,2},{2,0},{4,6},{6,4},{8,10},{10,8},{12,14},{14,12},{1,3},{3,1},... | collective-permute-start | bytes 417800 | tf_op jit(solution)/shard_map/ppermute | solution.py:261
  9.1 0.0 copy-start
  9.1 1.2 %copy-done = bf16[27,128,128]{2,1,0:T(8,128)(2,1)S(1)} copy-done((bf16[27,128,128]{2,1,0:T(8,128)(2,1)S(1)}, bf16[27,128,128]{2,1,0:T(8,128)(2,1)}, u32[]{:S(2)}) %copy-start) | copy-done | bytes 884760
  10.3 0.4 %turn_weights.1 = (bf16[128,3456]{1,0:T(8,128)(2,1)S(1)}, bf16[128,3456]{1,0:T(8,128)(2,1)S(1)}) custom-call(bf16[27,128,128]{2,1,0:T(8,128)(2,1)S(1)} %copy-done), custom_call_target="tpu_custom_call" | custom-call | flops 200000000 | bytes 3000000 | tf_op jit(solution)/shard_map/turn_weights/pallas_call | solution.py:267
  10.7 1.3 %collective-permute-done.refs_1_.refs_3_.before_mine = bf16[272,256]{1,0:T(8,128)(2,1)S(1)} collective-permute-done((bf16[272,256]{1,0:T(8,128)(2,1)S(1)}, bf16[272,256]{1,0:T(8,128)(2,1)S(1)}, u32[]{:S(2)}, u32[]{:S(2)}) %collective-permute-start) | collective-permute-done | bytes 139296 | tf_op jit(solution)/shard_map/ppermute | solution.py:264
  11.9 0.0 collective-permute-start.1
  11.9 1.7 %collective-permute-start.6 = (bf16[272,256]{1,0:T(8,128)(2,1)S(1)}, bf16[272,256]{1,0:T(8,128)(2,1)S(1)}, u32[]{:S(2)}, u32[]{:S(2)}) collective-permute-start(bf16[272,256]{1,0:T(8,128)(2,1)S(1)} %collective-permute-done.refs_1_.refs_3_.before_mine), channel_id=1, source_target_pairs={{0,2},{2,0},{4,6},{6,4},{8,10},{10,8},{12,14},{14,12},{1,3},{3,1},... | collective-permute-start | bytes 417800 | tf_op jit(solution)/shard_map/ppermute | solution.py:261
  13.7 0.0 collective-permute-done.4.refs_1_.refs_5_.after_mine
  13.7 1.3 %collective-permute-start.5 = (bf16[272,256]{1,0:T(8,128)(2,1)S(1)}, bf16[272,256]{1,0:T(8,128)(2,1)S(1)}, u32[]{:S(2)}, u32[]{:S(2)}) collective-permute-start(bf16[272,256]{1,0:T(8,128)(2,1)S(1)} %collective-permute-done.4.refs_1_.refs_5_.after_mine), channel_id=1, source_target_pairs={{0,2},{2,0},{4,6},{6,4},{8,10},{10,8},{12,14},{14,12},{1,3},{3,1},... | collective-permute-start | bytes 417800 | tf_op jit(solution)/shard_map/ppermute | solution.py:261
  15.0 0.0 collective-permute-done.2.other_ref.refs_2_.refs_4_
  15.0 1.8 %weight_row_0.1 = (f32[1664,128]{1,0:T(8,128)S(1)}, f32[1664,128]{1,0:T(8,128)S(1)}, f32[128,128]{1,0:T(8,128)S(1)}) custom-call(s32[1]{0:T(128)} %bitcast.where_ref.refs_0_, bf16[272,256]{1,0:T(8,128)(2,1)S(1)} %get-tuple-element.36.mine_ref.refs_1_.refs_3_, bf16[272,256]{1,0:T(8,128)(2,1)S(1)} %collective-permute-done.2.other_ref.refs_2_.refs_4_), custom_call_target="tpu_custom_call" | custom-call | flops 2000000000 | bytes 4000000 | tf_op jit(solution)/shard_map/weight_row_0/pallas_call | solution.py:313
  16.8 1.9 %voxels_own_row.1 = (f32[128,256]{1,0:T(8,128)S(1)}, f32[128,256]{1,0:T(8,128)S(1)}) custom-call(s32[1]{0:T(128)} %bitcast.where_ref.refs_0_, bf16[272,256]{1,0:T(8,128)(2,1)S(1)} %get-tuple-element.36.mine_ref.refs_1_.refs_3_, bf16[272,256]{1,0:T(8,128)(2,1)S(1)} %collective-permute-done.2.other_ref.refs_2_.refs_4_, ...), custom_call_target="tpu_custom_call" | custom-call | flops 2000000000 | bytes 4000000 | tf_op jit(solution)/shard_map/voxels_own_row/pallas_call | solution.py:280
  18.6 0.2 collective-permute-done.1.refs_1_
  18.8 1.7 %collective-permute-start.3 = (bf16[272,256]{1,0:T(8,128)(2,1)S(1)}, bf16[272,256]{1,0:T(8,128)(2,1)S(1)}, u32[]{:S(2)}, u32[]{:S(2)}) collective-permute-start(bf16[272,256]{1,0:T(8,128)(2,1)S(1)} %collective-permute-done.1.refs_1_), channel_id=1, source_target_pairs={{0,2},{2,0},{4,6},{6,4},{8,10},{10,8},{12,14},{14,12},{1,3},{3,1},... | collective-permute-start | bytes 417800 | tf_op jit(solution)/shard_map/ppermute | solution.py:261
  20.5 0.0 collective-permute-done.6.refs_2_.refs_4_.before_other
  20.5 2.1 %weight_row_1.1 = (f32[1664,128]{1,0:T(8,128)S(1)}, f32[1664,128]{1,0:T(8,128)S(1)}, f32[128,128]{1,0:T(8,128)S(1)}) custom-call(s32[1]{0:T(128)} %bitcast.where_ref.refs_0_, bf16[272,256]{1,0:T(8,128)(2,1)S(1)} %collective-permute-done.refs_1_.refs_3_.before_mine, bf16[272,256]{1,0:T(8,128)(2,1)S(1)} %collective-permute-done.6.refs_2_.refs_4_.before_other, ...), custom_call_target="tpu_custom_call" | custom-call | flops 2000000000 | bytes 4000000 | tf_op jit(solution)/shard_map/weight_row_1/pallas_call | solution.py:313
  22.6 0.0 collective-permute-done.5.refs_2_.refs_6_.after_other
  22.6 2.1 %weight_row_2.1 = (f32[1664,128]{1,0:T(8,128)S(1)}, f32[1664,128]{1,0:T(8,128)S(1)}, f32[128,128]{1,0:T(8,128)S(1)}) custom-call(s32[1]{0:T(128)} %bitcast.where_ref.refs_0_, bf16[272,256]{1,0:T(8,128)(2,1)S(1)} %collective-permute-done.4.refs_1_.refs_5_.after_mine, bf16[272,256]{1,0:T(8,128)(2,1)S(1)} %collective-permute-done.5.refs_2_.refs_6_.after_other, ...), custom_call_target="tpu_custom_call" | custom-call | flops 2000000000 | bytes 4000000 | tf_op jit(solution)/shard_map/weight_row_2/pallas_call | solution.py:313
  24.7 0.0 collective-permute-done.3.refs_2_
  24.7 1.9 %weight_row_3.1 = (f32[18,128,128]{2,1,0:T(8,128)S(1)}, bf16[18,128,128]{2,1,0:T(8,128)(2,1)S(1)}) custom-call(s32[1]{0:T(128)} %bitcast.where_ref.refs_0_, bf16[272,256]{1,0:T(8,128)(2,1)S(1)} %collective-permute-done.1.refs_1_, bf16[272,256]{1,0:T(8,128)(2,1)S(1)} %collective-permute-done.3.refs_2_, ...), custom_call_target="tpu_custom_call" | custom-call | flops 2000000000 | bytes 4000000 | tf_op jit(solution)/shard_map/weight_row_3/pallas_call | solution.py:313
  26.7 0.1 collective-permute-start.8
  26.7 0.9 %weight_row_3_middle.1 = (f32[9,128,128]{2,1,0:T(8,128)S(1)}, bf16[9,128,128]{2,1,0:T(8,128)(2,1)S(1)}) custom-call(s32[1]{0:T(128)} %bitcast.where_ref.refs_0_, bf16[272,256]{1,0:T(8,128)(2,1)S(1)} %collective-permute-done.1.refs_1_, bf16[272,256]{1,0:T(8,128)(2,1)S(1)} %collective-permute-done.3.refs_2_, ...), custom_call_target="tpu_custom_call" | custom-call | flops 2000000000 | bytes 4000000 | tf_op jit(solution)/shard_map/weight_row_3_middle/pallas_call | solution.py:313
  27.6 0.6 %collective-permute-start.7 = (bf16[9,128,128]{2,1,0:T(8,128)(2,1)S(1)}, bf16[9,128,128]{2,1,0:T(8,128)(2,1)S(1)}, u32[]{:S(2)}, u32[]{:S(2)}) collective-permute-start(bf16[9,128,128]{2,1,0:T(8,128)(2,1)S(1)} %get-tuple-element.56), channel_id=1, source_target_pairs={{0,1},{1,0},{2,3},{3,2},{4,5},{5,4},{6,7},{7,6},{8,9},{9,8},{10,11... | collective-permute-start | bytes 884744 | tf_op jit(solution)/shard_map/ppermute | solution.py:331
  28.2 1.5 %voxel_edges.1 = (bf16[256,128]{1,0:T(8,128)(2,1)}, bf16[256,128]{1,0:T(8,128)(2,1)}) custom-call(s32[1]{0:T(128)} %bitcast.where_ref.refs_0_, bf16[272,256]{1,0:T(8,128)(2,1)S(1)} %collective-permute-done.refs_1_.refs_3_.before_mine, bf16[272,256]{1,0:T(8,128)(2,1)S(1)} %collective-permute-done.6.refs_2_.refs_4_.before_other, ...), custom_call_target="tpu_custom_call" | custom-call | flops 1000000000 | bytes 4000000 | tf_op jit(solution)/shard_map/voxel_edges/pallas_call | solution.py:345
  29.7 0.0 collective-permute-done.7.middle_sent
  29.7 0.0 collective-permute-done.8.sides_sent
  29.7 1.3 %finish.1 = f32[27,128,128]{2,1,0:T(8,128)} custom-call(f32[18,128,128]{2,1,0:T(8,128)S(1)} %get-tuple-element.63.sides_ref, bf16[18,128,128]{2,1,0:T(8,128)(2,1)S(1)} %collective-permute-done.8.sides_sent, f32[9,128,128]{2,1,0:T(8,128)S(1)} %get-tuple-element.65.middle_ref, bf16[9,128,128]{2,1,0:T(8,128)(2,1)S(1)} %collective-permute-done.7.middle_sent), custom_call_target="tpu_custom_call" | custom-call | tf_op jit(solution)/shard_map/finish/pallas_call | solution.py:360
Async XLA Ops:
  2.3 9.6 %collective-permute-start = (bf16[272,256]{1,0:T(8,128)(2,1)S(1)}, bf16[272,256]{1,0:T(8,128)(2,1)S(1)}, u32[]{:S(2)}, u32[]{:S(2)}) collective-permute-start(bf16[272,256]{1,0:T(8,128)(2,1)S(1)} %get-tuple-element.36.mine_ref.refs_1_.refs_3_), channel_id=1, source_target_pairs={{0,4},{2,6},{4,8},{6,10},{8,12},{10,14},{12,0},{14,2},{1,5},{3,7},... | collective-permute-start | bytes 417800 | tf_op jit(solution)/shard_map/ppermute | solution.py:264
  5.4 8.3 %collective-permute-start.4 = (bf16[272,256]{1,0:T(8,128)(2,1)S(1)}, bf16[272,256]{1,0:T(8,128)(2,1)S(1)}, u32[]{:S(2)}, u32[]{:S(2)}) collective-permute-start(bf16[272,256]{1,0:T(8,128)(2,1)S(1)} %get-tuple-element.36.mine_ref.refs_1_.refs_3_), channel_id=1, source_target_pairs={{0,12},{2,14},{4,0},{6,2},{8,4},{10,6},{12,8},{14,10},{1,13},{3,15... | collective-permute-start | bytes 417800 | tf_op jit(solution)/shard_map/ppermute | solution.py:264
  7.5 7.5 %collective-permute-start.2 = (bf16[272,256]{1,0:T(8,128)(2,1)S(1)}, bf16[272,256]{1,0:T(8,128)(2,1)S(1)}, u32[]{:S(2)}, u32[]{:S(2)}) collective-permute-start(bf16[272,256]{1,0:T(8,128)(2,1)S(1)} %get-tuple-element.36.mine_ref.refs_1_.refs_3_), channel_id=1, source_target_pairs={{0,2},{2,0},{4,6},{6,4},{8,10},{10,8},{12,14},{14,12},{1,3},{3,1},... | collective-permute-start | bytes 417800 | tf_op jit(solution)/shard_map/ppermute | solution.py:261
  9.1 1.2 %copy-start = (bf16[27,128,128]{2,1,0:T(8,128)(2,1)S(1)}, bf16[27,128,128]{2,1,0:T(8,128)(2,1)}, u32[]{:S(2)}) copy-start(bf16[27,128,128]{2,1,0:T(8,128)(2,1)} %w_ref) | copy-start | bytes 2654212
  11.9 6.9 %collective-permute-start.1 = (bf16[272,256]{1,0:T(8,128)(2,1)S(1)}, bf16[272,256]{1,0:T(8,128)(2,1)S(1)}, u32[]{:S(2)}, u32[]{:S(2)}) collective-permute-start(bf16[272,256]{1,0:T(8,128)(2,1)S(1)} %collective-permute-done.refs_1_.refs_3_.before_mine), channel_id=1, source_target_pairs={{0,4},{2,6},{4,8},{6,10},{8,12},{10,14},{12,0},{14,2},{1,5},{3,7},... | collective-permute-start | bytes 417800 | tf_op jit(solution)/shard_map/ppermute | solution.py:264
  11.9 8.6 %collective-permute-start.6 = (bf16[272,256]{1,0:T(8,128)(2,1)S(1)}, bf16[272,256]{1,0:T(8,128)(2,1)S(1)}, u32[]{:S(2)}, u32[]{:S(2)}) collective-permute-start(bf16[272,256]{1,0:T(8,128)(2,1)S(1)} %collective-permute-done.refs_1_.refs_3_.before_mine), channel_id=1, source_target_pairs={{0,2},{2,0},{4,6},{6,4},{8,10},{10,8},{12,14},{14,12},{1,3},{3,1},... | collective-permute-start | bytes 417800 | tf_op jit(solution)/shard_map/ppermute | solution.py:261
  13.7 9.0 %collective-permute-start.5 = (bf16[272,256]{1,0:T(8,128)(2,1)S(1)}, bf16[272,256]{1,0:T(8,128)(2,1)S(1)}, u32[]{:S(2)}, u32[]{:S(2)}) collective-permute-start(bf16[272,256]{1,0:T(8,128)(2,1)S(1)} %collective-permute-done.4.refs_1_.refs_5_.after_mine), channel_id=1, source_target_pairs={{0,2},{2,0},{4,6},{6,4},{8,10},{10,8},{12,14},{14,12},{1,3},{3,1},... | collective-permute-start | bytes 417800 | tf_op jit(solution)/shard_map/ppermute | solution.py:261
  18.8 5.9 %collective-permute-start.3 = (bf16[272,256]{1,0:T(8,128)(2,1)S(1)}, bf16[272,256]{1,0:T(8,128)(2,1)S(1)}, u32[]{:S(2)}, u32[]{:S(2)}) collective-permute-start(bf16[272,256]{1,0:T(8,128)(2,1)S(1)} %collective-permute-done.1.refs_1_), channel_id=1, source_target_pairs={{0,2},{2,0},{4,6},{6,4},{8,10},{10,8},{12,14},{14,12},{1,3},{3,1},... | collective-permute-start | bytes 417800 | tf_op jit(solution)/shard_map/ppermute | solution.py:261
  26.7 3.1 %collective-permute-start.8 = (bf16[18,128,128]{2,1,0:T(8,128)(2,1)S(1)}, bf16[18,128,128]{2,1,0:T(8,128)(2,1)S(1)}, u32[]{:S(2)}, u32[]{:S(2)}) collective-permute-start(bf16[18,128,128]{2,1,0:T(8,128)(2,1)S(1)} %get-tuple-element.64), channel_id=1, source_target_pairs={{0,1},{1,0},{2,3},{3,2},{4,5},{5,4},{6,7},{7,6},{8,9},{9,8},{10,11... | collective-permute-start | bytes 1769480 | tf_op jit(solution)/shard_map/ppermute | solution.py:331
  27.6 2.1 %collective-permute-start.7 = (bf16[9,128,128]{2,1,0:T(8,128)(2,1)S(1)}, bf16[9,128,128]{2,1,0:T(8,128)(2,1)S(1)}, u32[]{:S(2)}, u32[]{:S(2)}) collective-permute-start(bf16[9,128,128]{2,1,0:T(8,128)(2,1)S(1)} %get-tuple-element.56), channel_id=1, source_target_pairs={{0,1},{1,0},{2,3},{3,2},{4,5},{5,4},{6,7},{7,6},{8,9},{9,8},{10,11... | collective-permute-start | bytes 884744 | tf_op jit(solution)/shard_map/ppermute | solution.py:331

commit v16 on v15

--- a/solution.py
+++ b/solution.py
@@ -75,6 +75,20 @@
         ground[pl.ds(at, STRIP), :] = ref[u * STRIP:(u + 1) * STRIP, :]
 
 
+def look_up(window, picks, places):
+    ref, first, lanes = window
+    width = ref.shape[0] // 2
+    for i in range(0, len(picks), 2):
+        pair = picks[i:i + 2]
+        pick = jnp.concatenate(pair, axis=1) if len(pair) == 2 else pair[0]
+        span = pair[0].shape[1]
+        for side in range(2):
+            near = jnp.dot(ref[side * width:(side + 1) * width, first:first + lanes], pick,
+                           preferred_element_type=jnp.float32).astype(jnp.bfloat16)
+            for j, (to, row, lane) in enumerate(places[i:i + 2]):
+                to[side][row:row + width, lane:lane + span] = near[:, j * span:(j + 1) * span]
+
+
 def row_kernel(first_stage, final, groups, strips, borders, *refs):
     refs = list(refs)
     where_ref = refs.pop(0)
@@ -99,21 +113,14 @@
             turned[:, i * span:(i + 1) * span] = ground[i * span:(i + 1) * span, :].T
     place = lax.broadcasted_iota(jnp.int32, (span, span), 0).astype(jnp.float32)
 
-    def gather(target, source, start, stop):
-        picks = [(place == codes[target, k:k + 1, :]).astype(jnp.bfloat16) for k in range(start, stop)]
-        near = jnp.dot(turned[:, source * span:(source + 1) * span], jnp.concatenate(picks, axis=1),
-                       preferred_element_type=jnp.float32).astype(jnp.bfloat16)
-        for k in range(start, stop):
-            one = near[:, (k - start) * span:(k - start + 1) * span]
-            near_act[k * width:(k + 1) * width, target * span:(target + 1) * span] = one[:width]
-            near_cot[k * width:(k + 1) * width, target * span:(target + 1) * span] = one[width:]
-
-    if 1 in groups:
-        for u in range(TILE):
-            gather(u, u, 9, HALF)
-    if 0 in groups:
-        for target, source in borders:
-            gather(target, source, 0, 9)
+    to = (near_act, near_cot)
+    for source in range(TILE + 2):
+        found = [(source, k) for k in range(9, HALF)] if 1 in groups and source < TILE else []
+        if 0 in groups:
+            found += [(target, k) for target, origin in borders if origin == source for k in range(9)]
+        if found:
+            picks = [(place == codes[target, k:k + 1, :]).astype(jnp.bfloat16) for target, k in found]
+            look_up((turned, source * span, span), picks, [(to, k * width, target * span) for target, k in found])
     extents = ((0, 9, span * targets[0], span * (targets[-1] + 1)), (9, HALF, 0, TILE * span))
     for turn, near in ((0, near_act), (1, near_cot)):
         for group in groups:
@@ -171,12 +178,7 @@
             source = (2 * half + side) * span
             ks = range(9 * side, 9 * side + 9)
             picks = [(place == codes[k:k + 1, at:at + span]).astype(jnp.bfloat16) for k in ks]
-            near = jnp.dot(turned[:, source:source + 2 * span], jnp.concatenate(picks, axis=1),
-                           preferred_element_type=jnp.float32).astype(jnp.bfloat16)
-            for k in ks:
-                one = near[:, (k - 9 * side) * span:(k - 9 * side + 1) * span]
-                near_act[k * width:(k + 1) * width, at:at + span] = one[:width]
-                near_cot[k * width:(k + 1) * width, at:at + span] = one[width:]
+            look_up((turned, source, 2 * span), picks, [((near_act, near_cot), k * width, at) for k in ks])
     conv_ref[...] = jnp.dot(forward_ref[...], near_act[...], preferred_element_type=jnp.float32)
     grad_ref[...] = jnp.dot(back_ref[...], near_cot[...], preferred_element_type=jnp.float32)
 
@@ -196,10 +198,7 @@
     code = jnp.where(lane < STRIP, first, jnp.where(last >= 0, last + span, last))
     place = lax.broadcasted_iota(jnp.int32, (2 * span, span), 0).astype(jnp.float32)
     picks = [(place == code[k:k + 1, :]).astype(jnp.bfloat16) for k in range(9)]
-    found = jnp.dot(turned[...], jnp.concatenate(picks, axis=1), preferred_element_type=jnp.float32)
-    found = found.astype(jnp.bfloat16)
-    for k in range(9):
-        near[:, k * width:(k + 1) * width, :] = found[:, k * span:(k + 1) * span].reshape(2, width, span)
+    look_up((turned, 0, 2 * span), picks, [((near.at[0], near.at[1]), k * width, 0) for k in range(9)])
     lane = lax.broadcasted_iota(jnp.int32, (width, span), 1)
 
     def total(own_ref, weights, side):

time: 31.2 us -> 31.3 us (level)
  no operation moved by 1% of the time
where the time goes in v16:
time: 31.3 us; the launch traced here: 31.1 us
  Pallas kernels  14.8 us (47%)
  starting transfers between devices  12.2 us (39%)
  waiting for transfers between devices  1.54 us (5%)
  between operations  1.36 us (4%)
  local copies, waits for them, and re-layouts  1.17 us (4%)
    pallas_call x5, Pallas kernels, row_sums(): pl.pallas_call(functools.partial(row_kernel, not sums, bool(final), group...  8.84 us
    ppermute x4, starting transfers between devices, across(): return lax.ppermute(block, 'brick', [(i, i ^ 1) for i in range(peers)])  6.4 us
    ppermute x3, starting transfers between devices, along(): lax.ppermute(block, 'brick', [(i, (i + turn * tiles_y) % peers) for i in...  5.17 us
    pallas_call x1, Pallas kernels, whole_scene(): pl.pallas_call(own_kernel, out_shape=(jax.ShapeDtypeStruct((width, rows),...  1.77 us
    pallas_call x1, Pallas kernels, whole_scene(): pl.pallas_call(edge_kernel, out_shape=(jax.ShapeDtypeStruct((rows, width)...  1.55 us
    ppermute x3, waiting for transfers between devices, along(): lax.ppermute(block, 'brick', [(i, (i + turn * tiles_y) % peers) for i in...  1.52 us
    pallas_call x1, Pallas kernels, whole_scene(): pl.pallas_call(finish_kernel, out_shape=jax.ShapeDtypeStruct((27, width,...  1.29 us
    unnamed x2, local copies, waits for them, and re-layouts  1.17 us
  transfers between devices with their start and end apart: 9, of which 2 were waited for; matrix products, arithmetic and copies ran while one was open for 0% of the time, Pallas kernels for 34%

profile of v16, /device:TPU:0, one launch (start us, length us, event | category | flops | bytes accessed | tf_op | source)
XLA Modules:
  0.0 31.1 jit_solution(12274001446245695382)
XLA Ops:
  1.3 1.0 %pack_tile.1 = (bf16[272,256]{1,0:T(8,128)(2,1)S(1)}, f32[256,128]{1,0:T(8,128)S(1)}, f32[27,256]{1,0:T(8,128)S(1)}) custom-call(s32[1]{0:T(128)S(6)} %copy.10.time_ref, bf16[1,256,128]{2,1,0:T(8,128)(2,1)} %feat_hbm.1, bf16[1,256,128]{2,1,0:T(8,128)(2,1)} %cot_hbm.1, s32[27,256]{1,0:T(8,128)} %near_hbm.1, bf16[1,128]{1,0:T(2,128)(2,1)} %cond_hbm.1, ...), custom_call_target="tpu_custom_call" | custom-call | tf_op jit(solution)/shard_map/pack_tile/pallas_call | solution.py:238
  2.3 3.1 %collective-permute-start = (bf16[272,256]{1,0:T(8,128)(2,1)S(1)}, bf16[272,256]{1,0:T(8,128)(2,1)S(1)}, u32[]{:S(2)}, u32[]{:S(2)}) collective-permute-start(bf16[272,256]{1,0:T(8,128)(2,1)S(1)} %get-tuple-element.36.mine_ref.refs_1_.refs_3_), channel_id=1, source_target_pairs={{0,4},{2,6},{4,8},{6,10},{8,12},{10,14},{12,0},{14,2},{1,5},{3,7},... | collective-permute-start | bytes 417800 | tf_op jit(solution)/shard_map/ppermute | solution.py:263
  5.4 2.1 %collective-permute-start.4 = (bf16[272,256]{1,0:T(8,128)(2,1)S(1)}, bf16[272,256]{1,0:T(8,128)(2,1)S(1)}, u32[]{:S(2)}, u32[]{:S(2)}) collective-permute-start(bf16[272,256]{1,0:T(8,128)(2,1)S(1)} %get-tuple-element.36.mine_ref.refs_1_.refs_3_), channel_id=1, source_target_pairs={{0,12},{2,14},{4,0},{6,2},{8,4},{10,6},{12,8},{14,10},{1,13},{3,15... | collective-permute-start | bytes 417800 | tf_op jit(solution)/shard_map/ppermute | solution.py:263
  7.5 1.6 %collective-permute-start.2 = (bf16[272,256]{1,0:T(8,128)(2,1)S(1)}, bf16[272,256]{1,0:T(8,128)(2,1)S(1)}, u32[]{:S(2)}, u32[]{:S(2)}) collective-permute-start(bf16[272,256]{1,0:T(8,128)(2,1)S(1)} %get-tuple-element.36.mine_ref.refs_1_.refs_3_), channel_id=1, source_target_pairs={{0,2},{2,0},{4,6},{6,4},{8,10},{10,8},{12,14},{14,12},{1,3},{3,1},... | collective-permute-start | bytes 417800 | tf_op jit(solution)/shard_map/ppermute | solution.py:260
  9.1 0.0 copy-start
  9.1 1.2 %copy-done = bf16[27,128,128]{2,1,0:T(8,128)(2,1)S(1)} copy-done((bf16[27,128,128]{2,1,0:T(8,128)(2,1)S(1)}, bf16[27,128,128]{2,1,0:T(8,128)(2,1)}, u32[]{:S(2)}) %copy-start) | copy-done | bytes 884760
  10.3 0.4 %turn_weights.1 = (bf16[128,3456]{1,0:T(8,128)(2,1)S(1)}, bf16[128,3456]{1,0:T(8,128)(2,1)S(1)}) custom-call(bf16[27,128,128]{2,1,0:T(8,128)(2,1)S(1)} %copy-done), custom_call_target="tpu_custom_call" | custom-call | flops 200000000 | bytes 3000000 | tf_op jit(solution)/shard_map/turn_weights/pallas_call | solution.py:266
  10.7 1.3 %collective-permute-done.refs_1_.refs_3_.before_mine = bf16[272,256]{1,0:T(8,128)(2,1)S(1)} collective-permute-done((bf16[272,256]{1,0:T(8,128)(2,1)S(1)}, bf16[272,256]{1,0:T(8,128)(2,1)S(1)}, u32[]{:S(2)}, u32[]{:S(2)}) %collective-permute-start) | collective-permute-done | bytes 139296 | tf_op jit(solution)/shard_map/ppermute | solution.py:263
  11.9 0.0 collective-permute-start.1
  11.9 1.7 %collective-permute-start.6 = (bf16[272,256]{1,0:T(8,128)(2,1)S(1)}, bf16[272,256]{1,0:T(8,128)(2,1)S(1)}, u32[]{:S(2)}, u32[]{:S(2)}) collective-permute-start(bf16[272,256]{1,0:T(8,128)(2,1)S(1)} %collective-permute-done.refs_1_.refs_3_.before_mine), channel_id=1, source_target_pairs={{0,2},{2,0},{4,6},{6,4},{8,10},{10,8},{12,14},{14,12},{1,3},{3,1},... | collective-permute-start | bytes 417800 | tf_op jit(solution)/shard_map/ppermute | solution.py:260
  13.7 0.0 collective-permute-done.4.refs_1_.refs_5_.after_mine
  13.7 1.3 %collective-permute-start.5 = (bf16[272,256]{1,0:T(8,128)(2,1)S(1)}, bf16[272,256]{1,0:T(8,128)(2,1)S(1)}, u32[]{:S(2)}, u32[]{:S(2)}) collective-permute-start(bf16[272,256]{1,0:T(8,128)(2,1)S(1)} %collective-permute-done.4.refs_1_.refs_5_.after_mine), channel_id=1, source_target_pairs={{0,2},{2,0},{4,6},{6,4},{8,10},{10,8},{12,14},{14,12},{1,3},{3,1},... | collective-permute-start | bytes 417800 | tf_op jit(solution)/shard_map/ppermute | solution.py:260
  15.0 0.0 collective-permute-done.2.other_ref.refs_2_.refs_4_
  15.0 1.8 %weight_row_0.1 = (f32[1664,128]{1,0:T(8,128)S(1)}, f32[1664,128]{1,0:T(8,128)S(1)}, f32[128,128]{1,0:T(8,128)S(1)}) custom-call(s32[1]{0:T(128)} %bitcast.where_ref.refs_0_, bf16[272,256]{1,0:T(8,128)(2,1)S(1)} %get-tuple-element.36.mine_ref.refs_1_.refs_3_, bf16[272,256]{1,0:T(8,128)(2,1)S(1)} %collective-permute-done.2.other_ref.refs_2_.refs_4_), custom_call_target="tpu_custom_call" | custom-call | flops 2000000000 | bytes 4000000 | tf_op jit(solution)/shard_map/weight_row_0/pallas_call | solution.py:312
  16.8 1.8 %voxels_own_row.1 = (f32[128,256]{1,0:T(8,128)S(1)}, f32[128,256]{1,0:T(8,128)S(1)}) custom-call(s32[1]{0:T(128)} %bitcast.where_ref.refs_0_, bf16[272,256]{1,0:T(8,128)(2,1)S(1)} %get-tuple-element.36.mine_ref.refs_1_.refs_3_, bf16[272,256]{1,0:T(8,128)(2,1)S(1)} %collective-permute-done.2.other_ref.refs_2_.refs_4_, ...), custom_call_target="tpu_custom_call" | custom-call | flops 2000000000 | bytes 4000000 | tf_op jit(solution)/shard_map/voxels_own_row/pallas_call | solution.py:279
  18.5 0.3 collective-permute-done.1.refs_1_
  18.8 1.7 %collective-permute-start.3 = (bf16[272,256]{1,0:T(8,128)(2,1)S(1)}, bf16[272,256]{1,0:T(8,128)(2,1)S(1)}, u32[]{:S(2)}, u32[]{:S(2)}) collective-permute-start(bf16[272,256]{1,0:T(8,128)(2,1)S(1)} %collective-permute-done.1.refs_1_), channel_id=1, source_target_pairs={{0,2},{2,0},{4,6},{6,4},{8,10},{10,8},{12,14},{14,12},{1,3},{3,1},... | collective-permute-start | bytes 417800 | tf_op jit(solution)/shard_map/ppermute | solution.py:260
  20.5 0.0 collective-permute-done.6.refs_2_.refs_4_.before_other
  20.5 2.1 %weight_row_1.1 = (f32[1664,128]{1,0:T(8,128)S(1)}, f32[1664,128]{1,0:T(8,128)S(1)}, f32[128,128]{1,0:T(8,128)S(1)}) custom-call(s32[1]{0:T(128)} %bitcast.where_ref.refs_0_, bf16[272,256]{1,0:T(8,128)(2,1)S(1)} %collective-permute-done.refs_1_.refs_3_.before_mine, bf16[272,256]{1,0:T(8,128)(2,1)S(1)} %collective-permute-done.6.refs_2_.refs_4_.before_other, ...), custom_call_target="tpu_custom_call" | custom-call | flops 2000000000 | bytes 4000000 | tf_op jit(solution)/shard_map/weight_row_1/pallas_call | solution.py:312
  22.7 0.0 collective-permute-done.5.refs_2_.refs_6_.after_other
  22.7 2.1 %weight_row_2.1 = (f32[1664,128]{1,0:T(8,128)S(1)}, f32[1664,128]{1,0:T(8,128)S(1)}, f32[128,128]{1,0:T(8,128)S(1)}) custom-call(s32[1]{0:T(128)} %bitcast.where_ref.refs_0_, bf16[272,256]{1,0:T(8,128)(2,1)S(1)} %collective-permute-done.4.refs_1_.refs_5_.after_mine, bf16[272,256]{1,0:T(8,128)(2,1)S(1)} %collective-permute-done.5.refs_2_.refs_6_.after_other, ...), custom_call_target="tpu_custom_call" | custom-call | flops 2000000000 | bytes 4000000 | tf_op jit(solution)/shard_map/weight_row_2/pallas_call | solution.py:312
  24.8 0.0 collective-permute-done.3.refs_2_
  24.8 1.9 %weight_row_3.1 = (f32[18,128,128]{2,1,0:T(8,128)S(1)}, bf16[18,128,128]{2,1,0:T(8,128)(2,1)S(1)}) custom-call(s32[1]{0:T(128)} %bitcast.where_ref.refs_0_, bf16[272,256]{1,0:T(8,128)(2,1)S(1)} %collective-permute-done.1.refs_1_, bf16[272,256]{1,0:T(8,128)(2,1)S(1)} %collective-permute-done.3.refs_2_, ...), custom_call_target="tpu_custom_call" | custom-call | flops 2000000000 | bytes 4000000 | tf_op jit(solution)/shard_map/weight_row_3/pallas_call | solution.py:312
  26.7 0.1 collective-permute-start.8
  26.8 0.9 %weight_row_3_middle.1 = (f32[9,128,128]{2,1,0:T(8,128)S(1)}, bf16[9,128,128]{2,1,0:T(8,128)(2,1)S(1)}) custom-call(s32[1]{0:T(128)} %bitcast.where_ref.refs_0_, bf16[272,256]{1,0:T(8,128)(2,1)S(1)} %collective-permute-done.1.refs_1_, bf16[272,256]{1,0:T(8,128)(2,1)S(1)} %collective-permute-done.3.refs_2_, ...), custom_call_target="tpu_custom_call" | custom-call | flops 2000000000 | bytes 4000000 | tf_op jit(solution)/shard_map/weight_row_3_middle/pallas_call | solution.py:312
  27.7 0.6 %collective-permute-start.7 = (bf16[9,128,128]{2,1,0:T(8,128)(2,1)S(1)}, bf16[9,128,128]{2,1,0:T(8,128)(2,1)S(1)}, u32[]{:S(2)}, u32[]{:S(2)}) collective-permute-start(bf16[9,128,128]{2,1,0:T(8,128)(2,1)S(1)} %get-tuple-element.56), channel_id=1, source_target_pairs={{0,1},{1,0},{2,3},{3,2},{4,5},{5,4},{6,7},{7,6},{8,9},{9,8},{10,11... | collective-permute-start | bytes 884744 | tf_op jit(solution)/shard_map/ppermute | solution.py:330
  28.3 1.6 %voxel_edges.1 = (bf16[256,128]{1,0:T(8,128)(2,1)}, bf16[256,128]{1,0:T(8,128)(2,1)}) custom-call(s32[1]{0:T(128)} %bitcast.where_ref.refs_0_, bf16[272,256]{1,0:T(8,128)(2,1)S(1)} %collective-permute-done.refs_1_.refs_3_.before_mine, bf16[272,256]{1,0:T(8,128)(2,1)S(1)} %collective-permute-done.6.refs_2_.refs_4_.before_other, ...), custom_call_target="tpu_custom_call" | custom-call | flops 1000000000 | bytes 4000000 | tf_op jit(solution)/shard_map/voxel_edges/pallas_call | solution.py:344
  29.8 0.0 collective-permute-done.7.middle_sent
  29.8 0.0 collective-permute-done.8.sides_sent
  29.8 1.3 %finish.1 = f32[27,128,128]{2,1,0:T(8,128)} custom-call(f32[18,128,128]{2,1,0:T(8,128)S(1)} %get-tuple-element.63.sides_ref, bf16[18,128,128]{2,1,0:T(8,128)(2,1)S(1)} %collective-permute-done.8.sides_sent, f32[9,128,128]{2,1,0:T(8,128)S(1)} %get-tuple-element.65.middle_ref, bf16[9,128,128]{2,1,0:T(8,128)(2,1)S(1)} %collective-permute-done.7.middle_sent), custom_call_target="tpu_custom_call" | custom-call | tf_op jit(solution)/shard_map/finish/pallas_call | solution.py:359
Async XLA Ops:
  2.3 9.6 %collective-permute-start = (bf16[272,256]{1,0:T(8,128)(2,1)S(1)}, bf16[272,256]{1,0:T(8,128)(2,1)S(1)}, u32[]{:S(2)}, u32[]{:S(2)}) collective-permute-start(bf16[272,256]{1,0:T(8,128)(2,1)S(1)} %get-tuple-element.36.mine_ref.refs_1_.refs_3_), channel_id=1, source_target_pairs={{0,4},{2,6},{4,8},{6,10},{8,12},{10,14},{12,0},{14,2},{1,5},{3,7},... | collective-permute-start | bytes 417800 | tf_op jit(solution)/shard_map/ppermute | solution.py:263
  5.4 8.3 %collective-permute-start.4 = (bf16[272,256]{1,0:T(8,128)(2,1)S(1)}, bf16[272,256]{1,0:T(8,128)(2,1)S(1)}, u32[]{:S(2)}, u32[]{:S(2)}) collective-permute-start(bf16[272,256]{1,0:T(8,128)(2,1)S(1)} %get-tuple-element.36.mine_ref.refs_1_.refs_3_), channel_id=1, source_target_pairs={{0,12},{2,14},{4,0},{6,2},{8,4},{10,6},{12,8},{14,10},{1,13},{3,15... | collective-permute-start | bytes 417800 | tf_op jit(solution)/shard_map/ppermute | solution.py:263
  7.5 7.5 %collective-permute-start.2 = (bf16[272,256]{1,0:T(8,128)(2,1)S(1)}, bf16[272,256]{1,0:T(8,128)(2,1)S(1)}, u32[]{:S(2)}, u32[]{:S(2)}) collective-permute-start(bf16[272,256]{1,0:T(8,128)(2,1)S(1)} %get-tuple-element.36.mine_ref.refs_1_.refs_3_), channel_id=1, source_target_pairs={{0,2},{2,0},{4,6},{6,4},{8,10},{10,8},{12,14},{14,12},{1,3},{3,1},... | collective-permute-start | bytes 417800 | tf_op jit(solution)/shard_map/ppermute | solution.py:260
  9.1 1.2 %copy-start = (bf16[27,128,128]{2,1,0:T(8,128)(2,1)S(1)}, bf16[27,128,128]{2,1,0:T(8,128)(2,1)}, u32[]{:S(2)}) copy-start(bf16[27,128,128]{2,1,0:T(8,128)(2,1)} %w_ref) | copy-start | bytes 2654212
  11.9 6.9 %collective-permute-start.1 = (bf16[272,256]{1,0:T(8,128)(2,1)S(1)}, bf16[272,256]{1,0:T(8,128)(2,1)S(1)}, u32[]{:S(2)}, u32[]{:S(2)}) collective-permute-start(bf16[272,256]{1,0:T(8,128)(2,1)S(1)} %collective-permute-done.refs_1_.refs_3_.before_mine), channel_id=1, source_target_pairs={{0,4},{2,6},{4,8},{6,10},{8,12},{10,14},{12,0},{14,2},{1,5},{3,7},... | collective-permute-start | bytes 417800 | tf_op jit(solution)/shard_map/ppermute | solution.py:263
  11.9 8.6 %collective-permute-start.6 = (bf16[272,256]{1,0:T(8,128)(2,1)S(1)}, bf16[272,256]{1,0:T(8,128)(2,1)S(1)}, u32[]{:S(2)}, u32[]{:S(2)}) collective-permute-start(bf16[272,256]{1,0:T(8,128)(2,1)S(1)} %collective-permute-done.refs_1_.refs_3_.before_mine), channel_id=1, source_target_pairs={{0,2},{2,0},{4,6},{6,4},{8,10},{10,8},{12,14},{14,12},{1,3},{3,1},... | collective-permute-start | bytes 417800 | tf_op jit(solution)/shard_map/ppermute | solution.py:260
  13.7 9.0 %collective-permute-start.5 = (bf16[272,256]{1,0:T(8,128)(2,1)S(1)}, bf16[272,256]{1,0:T(8,128)(2,1)S(1)}, u32[]{:S(2)}, u32[]{:S(2)}) collective-permute-start(bf16[272,256]{1,0:T(8,128)(2,1)S(1)} %collective-permute-done.4.refs_1_.refs_5_.after_mine), channel_id=1, source_target_pairs={{0,2},{2,0},{4,6},{6,4},{8,10},{10,8},{12,14},{14,12},{1,3},{3,1},... | collective-permute-start | bytes 417800 | tf_op jit(solution)/shard_map/ppermute | solution.py:260
  18.8 6.0 %collective-permute-start.3 = (bf16[272,256]{1,0:T(8,128)(2,1)S(1)}, bf16[272,256]{1,0:T(8,128)(2,1)S(1)}, u32[]{:S(2)}, u32[]{:S(2)}) collective-permute-start(bf16[272,256]{1,0:T(8,128)(2,1)S(1)} %collective-permute-done.1.refs_1_), channel_id=1, source_target_pairs={{0,2},{2,0},{4,6},{6,4},{8,10},{10,8},{12,14},{14,12},{1,3},{3,1},... | collective-permute-start | bytes 417800 | tf_op jit(solution)/shard_map/ppermute | solution.py:260
  26.7 3.1 %collective-permute-start.8 = (bf16[18,128,128]{2,1,0:T(8,128)(2,1)S(1)}, bf16[18,128,128]{2,1,0:T(8,128)(2,1)S(1)}, u32[]{:S(2)}, u32[]{:S(2)}) collective-permute-start(bf16[18,128,128]{2,1,0:T(8,128)(2,1)S(1)} %get-tuple-element.64), channel_id=1, source_target_pairs={{0,1},{1,0},{2,3},{3,2},{4,5},{5,4},{6,7},{7,6},{8,9},{9,8},{10,11... | collective-permute-start | bytes 1769480 | tf_op jit(solution)/shard_map/ppermute | solution.py:330
  27.7 2.1 %collective-permute-start.7 = (bf16[9,128,128]{2,1,0:T(8,128)(2,1)S(1)}, bf16[9,128,128]{2,1,0:T(8,128)(2,1)S(1)}, u32[]{:S(2)}, u32[]{:S(2)}) collective-permute-start(bf16[9,128,128]{2,1,0:T(8,128)(2,1)S(1)} %get-tuple-element.56), channel_id=1, source_target_pairs={{0,1},{1,0},{2,3},{3,2},{4,5},{5,4},{6,7},{7,6},{8,9},{9,8},{10,11... | collective-permute-start | bytes 884744 | tf_op jit(solution)/shard_map/ppermute | solution.py:330

commit v17 on v16

--- a/solution.py
+++ b/solution.py
@@ -272,10 +272,11 @@
         cost_estimate=pl.CostEstimate(flops=2 * 10**8, bytes_accessed=3 * 10**6, transcendentals=0),
         name="turn_weights",
     )(w_conv)
-    before, after = along(packed, 1), along(packed, -1)
-    before, w_forward = lax.optimization_barrier((before, w_forward))
+    before, own_other = along(packed, 1), across(packed)
+    before, w_forward, packed = lax.optimization_barrier((before, w_forward, packed))
+    after = along(packed, -1)
     far = along(before, 1)
-    own_pair = (packed, across(packed))
+    own_pair = (packed, own_other)
     own_conv, own_grad = pl.pallas_call(
         own_kernel,
         out_shape=(jax.ShapeDtypeStruct((width, rows), jnp.float32),) * 2,
@@ -331,14 +332,14 @@
 
     line = [(0, u) for u in range(TILE)]
     sums = row_sums("weight_row_0", (own_pair,), line, [], ())
-    sums = row_sums("weight_row_1", (before_pair, own_pair), line + [(1, 0)], [(TILE, TILE - 1)], sums)
-    sums = row_sums("weight_row_2", (after_pair, own_pair), line + [(1, TILE - 1)], [(0, TILE)], sums)
-    sides, sides_sent = row_sums("weight_row_3", (far_pair, before_pair, after_pair),
-                                 line + [(1, 0), (2, TILE - 1)], [(TILE, TILE - 1), (0, TILE + 1)],
+    sums = row_sums("weight_row_before", (before_pair, own_pair), line + [(1, 0)], [(TILE, TILE - 1)], sums)
+    sums = row_sums("weight_row_far", (far_pair, before_pair), line + [(1, 0)], [(TILE, TILE - 1)], sums)
+    sides, sides_sent = row_sums("weight_row_after", (after_pair, own_pair, far_pair),
+                                 line + [(2, 0), (1, TILE - 1)], [(0, TILE + 1), (TILE, TILE - 1)],
                                  sums, groups=(0,), final=18)
     sides_other = swapped(sides_sent)
     centre, sides = lax.optimization_barrier((sums[2], sides))
-    middle, middle_sent = row_sums("weight_row_3_middle", (far_pair,), line, [], (sums[0], sums[1], centre),
+    middle, middle_sent = row_sums("weight_row_after_middle", (after_pair,), line, [], (sums[0], sums[1], centre),
                                    groups=(1,), final=9)
     middle_other = swapped(middle_sent)
     conv_out, feature_grad = pl.pallas_call(

time: 31.3 us -> 34 us (1.086)
  waiting for transfers between devices: 1.54 us -> 3.87 us
    ppermute x3, starting transfers between devices: 5.17 us -> 6.9 us  [along(): lax.ppermute(block, 'brick', [(i, (i + turn * tiles_y) % peers) for i in...]
    ppermute x3, waiting for transfers between devices: 1.52 us -> 2.99 us  [along(): lax.ppermute(block, 'brick', [(i, (i + turn * tiles_y) % peers) for i in...]
    ppermute x4, starting transfers between devices: 6.4 us -> 5.01 us  [across(): return lax.ppermute(block, 'brick', [(i, i ^ 1) for i in range(peers)])]
    ppermute x4, waiting for transfers between devices: 0.01 us -> 0.88 us  [across(): return lax.ppermute(block, 'brick', [(i, i ^ 1) for i in range(peers)])]
  transfers between devices with their start and end apart: 9 -> 9, of which waited for: 2 -> 3; matrix products, arithmetic and copies ran while one was open for 0% -> 0% of each run, Pallas kernels for 34% -> 31%
where the time goes in v17:
time: 34 us; the launch traced here: 33.8 us
  Pallas kernels  14.9 us (44%)
  starting transfers between devices  12.5 us (37%)
  waiting for transfers between devices  3.87 us (11%)
  between operations  1.35 us (4%)
  local copies, waits for them, and re-layouts  1.17 us (3%)
    pallas_call x5, Pallas kernels, row_sums(): pl.pallas_call(functools.partial(row_kernel, not sums, bool(final), group...  8.85 us
    ppermute x3, starting transfers between devices, along(): lax.ppermute(block, 'brick', [(i, (i + turn * tiles_y) % peers) for i in...  6.9 us
    ppermute x4, starting transfers between devices, across(): return lax.ppermute(block, 'brick', [(i, i ^ 1) for i in range(peers)])  5.01 us
    ppermute x3, waiting for transfers between devices, along(): lax.ppermute(block, 'brick', [(i, (i + turn * tiles_y) % peers) for i in...  2.99 us
    pallas_call x1, Pallas kernels, whole_scene(): pl.pallas_call(own_kernel, out_shape=(jax.ShapeDtypeStruct((width, rows),...  1.77 us
    pallas_call x1, Pallas kernels, whole_scene(): pl.pallas_call(edge_kernel, out_shape=(jax.ShapeDtypeStruct((rows, width)...  1.55 us
    pallas_call x1, Pallas kernels, whole_scene(): pl.pallas_call(finish_kernel, out_shape=jax.ShapeDtypeStruct((27, width,...  1.29 us
    unnamed x2, local copies, waits for them, and re-layouts  1.17 us
  transfers between devices with their start and end apart: 9, of which 3 were waited for; matrix products, arithmetic and copies ran while one was open for 0% of the time, Pallas kernels for 31%

profile of v17, /device:TPU:0, one launch (start us, length us, event | category | flops | bytes accessed | tf_op | source)
XLA Modules:
  0.0 33.8 jit_solution(11338131970237255357)
XLA Ops:
  1.3 1.0 %pack_tile.1 = (bf16[272,256]{1,0:T(8,128)(2,1)S(1)}, f32[256,128]{1,0:T(8,128)S(1)}, f32[27,256]{1,0:T(8,128)S(1)}) custom-call(s32[1]{0:T(128)S(6)} %copy.10.time_ref, bf16[1,256,128]{2,1,0:T(8,128)(2,1)} %feat_hbm.1, bf16[1,256,128]{2,1,0:T(8,128)(2,1)} %cot_hbm.1, s32[27,256]{1,0:T(8,128)} %near_hbm.1, bf16[1,128]{1,0:T(2,128)(2,1)} %cond_hbm.1, ...), custom_call_target="tpu_custom_call" | custom-call | tf_op jit(solution)/shard_map/pack_tile/pallas_call | solution.py:238
  2.3 3.1 %collective-permute-start = (bf16[272,256]{1,0:T(8,128)(2,1)S(1)}, bf16[272,256]{1,0:T(8,128)(2,1)S(1)}, u32[]{:S(2)}, u32[]{:S(2)}) collective-permute-start(bf16[272,256]{1,0:T(8,128)(2,1)S(1)} %get-tuple-element.40.mine_ref.refs_1_.refs_3_), channel_id=1, source_target_pairs={{0,4},{2,6},{4,8},{6,10},{8,12},{10,14},{12,0},{14,2},{1,5},{3,7},... | collective-permute-start | bytes 417800 | tf_op jit(solution)/shard_map/ppermute | solution.py:263
  5.4 1.5 %collective-permute-start.4 = (bf16[272,256]{1,0:T(8,128)(2,1)S(1)}, bf16[272,256]{1,0:T(8,128)(2,1)S(1)}, u32[]{:S(2)}, u32[]{:S(2)}) collective-permute-start(bf16[272,256]{1,0:T(8,128)(2,1)S(1)} %get-tuple-element.40.mine_ref.refs_1_.refs_3_), channel_id=1, source_target_pairs={{0,2},{2,0},{4,6},{6,4},{8,10},{10,8},{12,14},{14,12},{1,3},{3,1},... | collective-permute-start | bytes 417800 | tf_op jit(solution)/shard_map/ppermute | solution.py:260
  6.9 0.0 copy-start
  6.9 1.2 %copy-done = bf16[27,128,128]{2,1,0:T(8,128)(2,1)S(1)} copy-done((bf16[27,128,128]{2,1,0:T(8,128)(2,1)S(1)}, bf16[27,128,128]{2,1,0:T(8,128)(2,1)}, u32[]{:S(2)}) %copy-start) | copy-done | bytes 884760
  8.0 0.4 %turn_weights.1 = (bf16[128,3456]{1,0:T(8,128)(2,1)S(1)}, bf16[128,3456]{1,0:T(8,128)(2,1)S(1)}) custom-call(bf16[27,128,128]{2,1,0:T(8,128)(2,1)S(1)} %copy-done), custom_call_target="tpu_custom_call" | custom-call | flops 200000000 | bytes 3000000 | tf_op jit(solution)/shard_map/turn_weights/pallas_call | solution.py:266
  8.4 2.7 %collective-permute-done.refs_1_.refs_3_.before_mine = bf16[272,256]{1,0:T(8,128)(2,1)S(1)} collective-permute-done((bf16[272,256]{1,0:T(8,128)(2,1)S(1)}, bf16[272,256]{1,0:T(8,128)(2,1)S(1)}, u32[]{:S(2)}, u32[]{:S(2)}) %collective-permute-start) | collective-permute-done | bytes 139296 | tf_op jit(solution)/shard_map/ppermute | solution.py:263
  11.1 1.5 %collective-permute-start.6 = (bf16[272,256]{1,0:T(8,128)(2,1)S(1)}, bf16[272,256]{1,0:T(8,128)(2,1)S(1)}, u32[]{:S(2)}, u32[]{:S(2)}) collective-permute-start(bf16[272,256]{1,0:T(8,128)(2,1)S(1)} %collective-permute-done.refs_1_.refs_3_.before_mine), channel_id=1, source_target_pairs={{0,2},{2,0},{4,6},{6,4},{8,10},{10,8},{12,14},{14,12},{1,3},{3,1},... | collective-permute-start | bytes 417800 | tf_op jit(solution)/shard_map/ppermute | solution.py:260
  12.6 0.0 collective-permute-start.3
  12.6 3.8 %collective-permute-start.1 = (bf16[272,256]{1,0:T(8,128)(2,1)S(1)}, bf16[272,256]{1,0:T(8,128)(2,1)S(1)}, u32[]{:S(2)}, u32[]{:S(2)}) collective-permute-start(bf16[272,256]{1,0:T(8,128)(2,1)S(1)} %get-tuple-element.40.mine_ref.refs_1_.refs_3_), channel_id=1, source_target_pairs={{0,12},{2,14},{4,0},{6,2},{8,4},{10,6},{12,8},{14,10},{1,13},{3,15... | collective-permute-start | bytes 417800 | tf_op jit(solution)/shard_map/ppermute | solution.py:263
  16.4 0.0 collective-permute-done.4.other_ref.refs_2_.refs_4_
  16.4 1.8 %weight_row_0.1 = (f32[1664,128]{1,0:T(8,128)S(1)}, f32[1664,128]{1,0:T(8,128)S(1)}, f32[128,128]{1,0:T(8,128)S(1)}) custom-call(s32[1]{0:T(128)} %bitcast.where_ref.refs_0_, bf16[272,256]{1,0:T(8,128)(2,1)S(1)} %get-tuple-element.40.mine_ref.refs_1_.refs_3_, bf16[272,256]{1,0:T(8,128)(2,1)S(1)} %collective-permute-done.4.other_ref.refs_2_.refs_4_), custom_call_target="tpu_custom_call" | custom-call | flops 2000000000 | bytes 4000000 | tf_op jit(solution)/shard_map/weight_row_0/pallas_call | solution.py:313
  18.2 1.8 %voxels_own_row.1 = (f32[128,256]{1,0:T(8,128)S(1)}, f32[128,256]{1,0:T(8,128)S(1)}) custom-call(s32[1]{0:T(128)} %bitcast.where_ref.refs_0_, bf16[272,256]{1,0:T(8,128)(2,1)S(1)} %get-tuple-element.40.mine_ref.refs_1_.refs_3_, bf16[272,256]{1,0:T(8,128)(2,1)S(1)} %collective-permute-done.4.other_ref.refs_2_.refs_4_, ...), custom_call_target="tpu_custom_call" | custom-call | flops 2000000000 | bytes 4000000 | tf_op jit(solution)/shard_map/voxels_own_row/pallas_call | solution.py:280
  19.9 0.3 collective-permute-done.3.refs_1_.refs_5_
  20.3 0.7 %collective-permute-start.5 = (bf16[272,256]{1,0:T(8,128)(2,1)S(1)}, bf16[272,256]{1,0:T(8,128)(2,1)S(1)}, u32[]{:S(2)}, u32[]{:S(2)}) collective-permute-start(bf16[272,256]{1,0:T(8,128)(2,1)S(1)} %collective-permute-done.3.refs_1_.refs_5_), channel_id=1, source_target_pairs={{0,2},{2,0},{4,6},{6,4},{8,10},{10,8},{12,14},{14,12},{1,3},{3,1},... | collective-permute-start | bytes 417800 | tf_op jit(solution)/shard_map/ppermute | solution.py:260
  21.0 0.0 collective-permute-done.1.refs_1_.after_mine
  21.0 1.3 %collective-permute-start.2 = (bf16[272,256]{1,0:T(8,128)(2,1)S(1)}, bf16[272,256]{1,0:T(8,128)(2,1)S(1)}, u32[]{:S(2)}, u32[]{:S(2)}) collective-permute-start(bf16[272,256]{1,0:T(8,128)(2,1)S(1)} %collective-permute-done.1.refs_1_.after_mine), channel_id=1, source_target_pairs={{0,2},{2,0},{4,6},{6,4},{8,10},{10,8},{12,14},{14,12},{1,3},{3,1},... | collective-permute-start | bytes 417800 | tf_op jit(solution)/shard_map/ppermute | solution.py:260
  22.3 0.0 collective-permute-done.6.refs_2_.refs_4_.before_other
  22.3 2.1 %weight_row_before.1 = (f32[1664,128]{1,0:T(8,128)S(1)}, f32[1664,128]{1,0:T(8,128)S(1)}, f32[128,128]{1,0:T(8,128)S(1)}) custom-call(s32[1]{0:T(128)} %bitcast.where_ref.refs_0_, bf16[272,256]{1,0:T(8,128)(2,1)S(1)} %collective-permute-done.refs_1_.refs_3_.before_mine, bf16[272,256]{1,0:T(8,128)(2,1)S(1)} %collective-permute-done.6.refs_2_.refs_4_.before_other, ...), custom_call_target="tpu_custom_call" | custom-call | flops 2000000000 | bytes 4000000 | tf_op jit(solution)/shard_map/weight_row_before/pallas_call | solution.py:313
  24.5 0.9 %collective-permute-done.5.refs_2_.refs_6_ = bf16[272,256]{1,0:T(8,128)(2,1)S(1)} collective-permute-done((bf16[272,256]{1,0:T(8,128)(2,1)S(1)}, bf16[272,256]{1,0:T(8,128)(2,1)S(1)}, u32[]{:S(2)}, u32[]{:S(2)}) %collective-permute-start.5) | collective-permute-done | bytes 139296 | tf_op jit(solution)/shard_map/ppermute | solution.py:260
  25.3 2.1 %weight_row_far.1 = (f32[1664,128]{1,0:T(8,128)S(1)}, f32[1664,128]{1,0:T(8,128)S(1)}, f32[128,128]{1,0:T(8,128)S(1)}) custom-call(s32[1]{0:T(128)} %bitcast.where_ref.refs_0_, bf16[272,256]{1,0:T(8,128)(2,1)S(1)} %collective-permute-done.3.refs_1_.refs_5_, bf16[272,256]{1,0:T(8,128)(2,1)S(1)} %collective-permute-done.5.refs_2_.refs_6_, ...), custom_call_target="tpu_custom_call" | custom-call | flops 2000000000 | bytes 4000000 | tf_op jit(solution)/shard_map/weight_row_far/pallas_call | solution.py:313
  27.5 0.0 collective-permute-done.2.refs_2_.after_other
  27.5 1.9 %weight_row_after.1 = (f32[18,128,128]{2,1,0:T(8,128)S(1)}, bf16[18,128,128]{2,1,0:T(8,128)(2,1)S(1)}) custom-call(s32[1]{0:T(128)} %bitcast.where_ref.refs_0_, bf16[272,256]{1,0:T(8,128)(2,1)S(1)} %collective-permute-done.1.refs_1_.after_mine, bf16[272,256]{1,0:T(8,128)(2,1)S(1)} %collective-permute-done.2.refs_2_.after_other, ...), custom_call_target="tpu_custom_call" | custom-call | flops 2000000000 | bytes 4000000 | tf_op jit(solution)/shard_map/weight_row_after/pallas_call | solution.py:313
  29.4 0.1 collective-permute-start.8
  29.5 0.9 %weight_row_after_middle.1 = (f32[9,128,128]{2,1,0:T(8,128)S(1)}, bf16[9,128,128]{2,1,0:T(8,128)(2,1)S(1)}) custom-call(s32[1]{0:T(128)} %bitcast.where_ref.refs_0_, bf16[272,256]{1,0:T(8,128)(2,1)S(1)} %collective-permute-done.1.refs_1_.after_mine, bf16[272,256]{1,0:T(8,128)(2,1)S(1)} %collective-permute-done.2.refs_2_.after_other, ...), custom_call_target="tpu_custom_call" | custom-call | flops 2000000000 | bytes 4000000 | tf_op jit(solution)/shard_map/weight_row_after_middle/pallas_call | solution.py:313
  30.4 0.6 %collective-permute-start.7 = (bf16[9,128,128]{2,1,0:T(8,128)(2,1)S(1)}, bf16[9,128,128]{2,1,0:T(8,128)(2,1)S(1)}, u32[]{:S(2)}, u32[]{:S(2)}) collective-permute-start(bf16[9,128,128]{2,1,0:T(8,128)(2,1)S(1)} %get-tuple-element.58), channel_id=1, source_target_pairs={{0,1},{1,0},{2,3},{3,2},{4,5},{5,4},{6,7},{7,6},{8,9},{9,8},{10,11... | collective-permute-start | bytes 884744 | tf_op jit(solution)/shard_map/ppermute | solution.py:331
  30.9 1.6 %voxel_edges.1 = (bf16[256,128]{1,0:T(8,128)(2,1)}, bf16[256,128]{1,0:T(8,128)(2,1)}) custom-call(s32[1]{0:T(128)} %bitcast.where_ref.refs_0_, bf16[272,256]{1,0:T(8,128)(2,1)S(1)} %collective-permute-done.refs_1_.refs_3_.before_mine, bf16[272,256]{1,0:T(8,128)(2,1)S(1)} %collective-permute-done.6.refs_2_.refs_4_.before_other, ...), custom_call_target="tpu_custom_call" | custom-call | flops 1000000000 | bytes 4000000 | tf_op jit(solution)/shard_map/voxel_edges/pallas_call | solution.py:345
  32.5 0.0 collective-permute-done.7.middle_sent
  32.5 0.0 collective-permute-done.8.sides_sent
  32.5 1.3 %finish.1 = f32[27,128,128]{2,1,0:T(8,128)} custom-call(f32[18,128,128]{2,1,0:T(8,128)S(1)} %get-tuple-element.65.sides_ref, bf16[18,128,128]{2,1,0:T(8,128)(2,1)S(1)} %collective-permute-done.8.sides_sent, f32[9,128,128]{2,1,0:T(8,128)S(1)} %get-tuple-element.67.middle_ref, bf16[9,128,128]{2,1,0:T(8,128)(2,1)S(1)} %collective-permute-done.7.middle_sent), custom_call_target="tpu_custom_call" | custom-call | tf_op jit(solution)/shard_map/finish/pallas_call | solution.py:360
Async XLA Ops:
  2.3 8.8 %collective-permute-start = (bf16[272,256]{1,0:T(8,128)(2,1)S(1)}, bf16[272,256]{1,0:T(8,128)(2,1)S(1)}, u32[]{:S(2)}, u32[]{:S(2)}) collective-permute-start(bf16[272,256]{1,0:T(8,128)(2,1)S(1)} %get-tuple-element.40.mine_ref.refs_1_.refs_3_), channel_id=1, source_target_pairs={{0,4},{2,6},{4,8},{6,10},{8,12},{10,14},{12,0},{14,2},{1,5},{3,7},... | collective-permute-start | bytes 417800 | tf_op jit(solution)/shard_map/ppermute | solution.py:263
  5.4 11.0 %collective-permute-start.4 = (bf16[272,256]{1,0:T(8,128)(2,1)S(1)}, bf16[272,256]{1,0:T(8,128)(2,1)S(1)}, u32[]{:S(2)}, u32[]{:S(2)}) collective-permute-start(bf16[272,256]{1,0:T(8,128)(2,1)S(1)} %get-tuple-element.40.mine_ref.refs_1_.refs_3_), channel_id=1, source_target_pairs={{0,2},{2,0},{4,6},{6,4},{8,10},{10,8},{12,14},{14,12},{1,3},{3,1},... | collective-permute-start | bytes 417800 | tf_op jit(solution)/shard_map/ppermute | solution.py:260
  6.9 1.2 %copy-start = (bf16[27,128,128]{2,1,0:T(8,128)(2,1)S(1)}, bf16[27,128,128]{2,1,0:T(8,128)(2,1)}, u32[]{:S(2)}) copy-start(bf16[27,128,128]{2,1,0:T(8,128)(2,1)} %w_ref) | copy-start | bytes 2654212
  11.1 11.2 %collective-permute-start.6 = (bf16[272,256]{1,0:T(8,128)(2,1)S(1)}, bf16[272,256]{1,0:T(8,128)(2,1)S(1)}, u32[]{:S(2)}, u32[]{:S(2)}) collective-permute-start(bf16[272,256]{1,0:T(8,128)(2,1)S(1)} %collective-permute-done.refs_1_.refs_3_.before_mine), channel_id=1, source_target_pairs={{0,2},{2,0},{4,6},{6,4},{8,10},{10,8},{12,14},{14,12},{1,3},{3,1},... | collective-permute-start | bytes 417800 | tf_op jit(solution)/shard_map/ppermute | solution.py:260
  12.6 7.7 %collective-permute-start.3 = (bf16[272,256]{1,0:T(8,128)(2,1)S(1)}, bf16[272,256]{1,0:T(8,128)(2,1)S(1)}, u32[]{:S(2)}, u32[]{:S(2)}) collective-permute-start(bf16[272,256]{1,0:T(8,128)(2,1)S(1)} %collective-permute-done.refs_1_.refs_3_.before_mine), channel_id=1, source_target_pairs={{0,4},{2,6},{4,8},{6,10},{8,12},{10,14},{12,0},{14,2},{1,5},{3,7},... | collective-permute-start | bytes 417800 | tf_op jit(solution)/shard_map/ppermute | solution.py:263
  12.6 8.4 %collective-permute-start.1 = (bf16[272,256]{1,0:T(8,128)(2,1)S(1)}, bf16[272,256]{1,0:T(8,128)(2,1)S(1)}, u32[]{:S(2)}, u32[]{:S(2)}) collective-permute-start(bf16[272,256]{1,0:T(8,128)(2,1)S(1)} %get-tuple-element.40.mine_ref.refs_1_.refs_3_), channel_id=1, source_target_pairs={{0,12},{2,14},{4,0},{6,2},{8,4},{10,6},{12,8},{14,10},{1,13},{3,15... | collective-permute-start | bytes 417800 | tf_op jit(solution)/shard_map/ppermute | solution.py:263
  20.3 5.1 %collective-permute-start.5 = (bf16[272,256]{1,0:T(8,128)(2,1)S(1)}, bf16[272,256]{1,0:T(8,128)(2,1)S(1)}, u32[]{:S(2)}, u32[]{:S(2)}) collective-permute-start(bf16[272,256]{1,0:T(8,128)(2,1)S(1)} %collective-permute-done.3.refs_1_.refs_5_), channel_id=1, source_target_pairs={{0,2},{2,0},{4,6},{6,4},{8,10},{10,8},{12,14},{14,12},{1,3},{3,1},... | collective-permute-start | bytes 417800 | tf_op jit(solution)/shard_map/ppermute | solution.py:260
  21.0 6.5 %collective-permute-start.2 = (bf16[272,256]{1,0:T(8,128)(2,1)S(1)}, bf16[272,256]{1,0:T(8,128)(2,1)S(1)}, u32[]{:S(2)}, u32[]{:S(2)}) collective-permute-start(bf16[272,256]{1,0:T(8,128)(2,1)S(1)} %collective-permute-done.1.refs_1_.after_mine), channel_id=1, source_target_pairs={{0,2},{2,0},{4,6},{6,4},{8,10},{10,8},{12,14},{14,12},{1,3},{3,1},... | collective-permute-start | bytes 417800 | tf_op jit(solution)/shard_map/ppermute | solution.py:260
  29.4 3.1 %collective-permute-start.8 = (bf16[18,128,128]{2,1,0:T(8,128)(2,1)S(1)}, bf16[18,128,128]{2,1,0:T(8,128)(2,1)S(1)}, u32[]{:S(2)}, u32[]{:S(2)}) collective-permute-start(bf16[18,128,128]{2,1,0:T(8,128)(2,1)S(1)} %get-tuple-element.66), channel_id=1, source_target_pairs={{0,1},{1,0},{2,3},{3,2},{4,5},{5,4},{6,7},{7,6},{8,9},{9,8},{10,11... | collective-permute-start | bytes 1769480 | tf_op jit(solution)/shard_map/ppermute | solution.py:331
  30.4 2.1 %collective-permute-start.7 = (bf16[9,128,128]{2,1,0:T(8,128)(2,1)S(1)}, bf16[9,128,128]{2,1,0:T(8,128)(2,1)S(1)}, u32[]{:S(2)}, u32[]{:S(2)}) collective-permute-start(bf16[9,128,128]{2,1,0:T(8,128)(2,1)S(1)} %get-tuple-element.58), channel_id=1, source_target_pairs={{0,1},{1,0},{2,3},{3,2},{4,5},{5,4},{6,7},{7,6},{8,9},{9,8},{10,11... | collective-permute-start | bytes 884744 | tf_op jit(solution)/shard_map/ppermute | solution.py:331

commit v18 on v16

--- a/solution.py
+++ b/solution.py
@@ -89,20 +89,22 @@
                 to[side][row:row + width, lane:lane + span] = near[:, j * span:(j + 1) * span]
 
 
-def row_kernel(first_stage, final, groups, strips, borders, *refs):
+def row_kernel(first_stage, final, groups, laid, strips, borders, *refs):
     refs = list(refs)
     where_ref = refs.pop(0)
-    pairs = [(refs.pop(0), refs.pop(0)) for _ in range(1 + max(pair for pair, _ in strips))]
+    pairs = [] if laid else [(refs.pop(0), refs.pop(0)) for _ in range(1 + max(pair for pair, _ in strips))]
+    given = [refs.pop(0) for _ in range(3)] if laid else []
     before = [refs.pop(0) for _ in range(0 if first_stage else 3)]
     outs = [refs.pop(0) for _ in range(2 if final else 3)]
-    ground, turned, codes, near_act, near_cot = refs
+    ground, turned, codes = given or [refs.pop(0) for _ in range(3)]
+    near_act, near_cot = refs
     width = ground.shape[1] // 2
     rows = TILE * STRIP
     span = 2 * STRIP
     tile_y = where_ref[0] % 2
     borders = [(u, u - 1) for u in range(1, TILE)] + borders
     targets = sorted({target for target, _ in borders})
-    for i, (pair, u) in enumerate(strips):
+    for i, (pair, u) in enumerate([] if laid else strips):
         lay_strip(ground, i, tile_y, *pairs[pair], u)
         if i < TILE or i in targets:
             both = [ref[rows:, u * STRIP:(u + 1) * STRIP].astype(jnp.float32) for ref in pairs[pair]]
@@ -215,9 +217,17 @@
     grad_ref[...] = (back * sig * (1.0 + z_val * (1.0 - sig))).astype(jnp.bfloat16)
 
 
-def finish_kernel(sides_ref, sides_sent, middle_ref, middle_sent, weight_hbm, weight, sems):
-    copies = []
-    for i, first in enumerate(range(0, 27, FINISH_STEP)):
+def finish_kernel(sides_ref, sides_sent, middle_ref, middle_sent, conv_ref, grad_ref,
+                  weight_hbm, conv_hbm, grad_hbm, weight, sems):
+    steps = 27 // FINISH_STEP
+    copies = [
+        pltpu.make_async_copy(conv_ref, conv_hbm, sems.at[steps]),
+        pltpu.make_async_copy(grad_ref, grad_hbm, sems.at[steps + 1]),
+    ]
+    for copy in copies:
+        copy.start()
+    for i in range(steps):
+        first = i * FINISH_STEP
         kept, sent, at = (middle_ref, middle_sent, first - 9) if first // 9 == 1 else (
             sides_ref, sides_sent, first if first < 9 else first - 9)
         part, taken = pl.ds(first, FINISH_STEP), pl.ds(at, FINISH_STEP)
@@ -296,7 +306,7 @@
     before_pair = (before, across(before))
     after_pair = (after, across(after))
     far_pair = (far, across(far))
-    def row_sums(name, pairs, strips, borders, sums, groups=(0, 1), final=0):
+    def row_sums(name, pairs, strips, borders, sums, groups=(0, 1), final=0, keep=False, laid=()):
         blocks = [block for pair in pairs for block in pair]
         if final:
             out_shape = (
@@ -309,22 +319,28 @@
                 jax.ShapeDtypeStruct((HALF * width, width), jnp.float32),
                 jax.ShapeDtypeStruct((width, width), jnp.float32),
             )
+        layout = (
+            ((TILE + 2) * span, 2 * width, jnp.bfloat16),
+            (2 * width, (TILE + 2) * span, jnp.bfloat16),
+            (TILE + 1, CODE_ROWS, span, jnp.float32),
+        )
+        scratch = [] if laid or keep else [pltpu.VMEM(tuple(shape), kind) for *shape, kind in layout]
+        if keep:
+            out_shape += tuple(jax.ShapeDtypeStruct(tuple(shape), kind) for *shape, kind in layout)
+        operands = (*blocks, *laid, *sums)
         return pl.pallas_call(
-            functools.partial(row_kernel, not sums, bool(final), groups, strips, borders),
+            functools.partial(row_kernel, not sums, bool(final), groups, bool(laid), strips, borders),
             out_shape=out_shape,
-            in_specs=[smem] + [vmem] * (len(blocks) + len(sums)),
+            in_specs=[smem] + [vmem] * len(operands),
             out_specs=(vmem,) * len(out_shape),
-            scratch_shapes=[
-                pltpu.VMEM(((TILE + 2) * span, 2 * width), jnp.bfloat16),
-                pltpu.VMEM((2 * width, (TILE + 2) * span), jnp.bfloat16),
-                pltpu.VMEM((TILE + 1, CODE_ROWS, span), jnp.float32),
+            scratch_shapes=scratch + [
                 pltpu.VMEM((HALF * width, (TILE + 1) * span), jnp.bfloat16),
                 pltpu.VMEM((HALF * width, (TILE + 1) * span), jnp.bfloat16),
             ],
             compiler_params=params,
             cost_estimate=pl.CostEstimate(flops=2 * 10**9, bytes_accessed=4 * 10**6, transcendentals=0),
             name=name,
-        )(here, *blocks, *sums)
+        )(here, *operands)
 
     def swapped(block):
         return lax.ppermute(block, "batch", [(0, 1), (1, 0)])
@@ -333,13 +349,13 @@
     sums = row_sums("weight_row_0", (own_pair,), line, [], ())
     sums = row_sums("weight_row_1", (before_pair, own_pair), line + [(1, 0)], [(TILE, TILE - 1)], sums)
     sums = row_sums("weight_row_2", (after_pair, own_pair), line + [(1, TILE - 1)], [(0, TILE)], sums)
-    sides, sides_sent = row_sums("weight_row_3", (far_pair, before_pair, after_pair),
+    sides, sides_sent, *laid = row_sums("weight_row_3", (far_pair, before_pair, after_pair),
                                  line + [(1, 0), (2, TILE - 1)], [(TILE, TILE - 1), (0, TILE + 1)],
-                                 sums, groups=(0,), final=18)
+                                 sums, groups=(0,), final=18, keep=True)
     sides_other = swapped(sides_sent)
     centre, sides = lax.optimization_barrier((sums[2], sides))
-    middle, middle_sent = row_sums("weight_row_3_middle", (far_pair,), line, [], (sums[0], sums[1], centre),
-                                   groups=(1,), final=9)
+    middle, middle_sent = row_sums("weight_row_3_middle", (), line, [], (sums[0], sums[1], centre),
+                                   groups=(1,), final=9, laid=laid)
     middle_other = swapped(middle_sent)
     conv_out, feature_grad = pl.pallas_call(
         edge_kernel,
@@ -355,19 +371,23 @@
         cost_estimate=pl.CostEstimate(flops=10**9, bytes_accessed=4 * 10**6, transcendentals=0),
         name="voxel_edges",
     )(here, *before_pair, *after_pair, code, w_forward, w_back, own_conv, own_grad, z_val)
-    middle_other, conv_out = lax.optimization_barrier((middle_other, conv_out))
-    weight_grad = pl.pallas_call(
+    hbm = pl.BlockSpec(memory_space=pltpu.HBM)
+    weight_grad, conv_out, feature_grad = pl.pallas_call(
         finish_kernel,
-        out_shape=jax.ShapeDtypeStruct((27, width, width), jnp.float32),
-        in_specs=[vmem] * 4,
-        out_specs=pl.BlockSpec(memory_space=pltpu.HBM),
+        out_shape=(
+            jax.ShapeDtypeStruct((27, width, width), jnp.float32),
+            jax.ShapeDtypeStruct((rows, width), jnp.bfloat16),
+            jax.ShapeDtypeStruct((rows, width), jnp.bfloat16),
+        ),
+        in_specs=[vmem] * 6,
+        out_specs=(hbm, hbm, hbm),
         scratch_shapes=[
             pltpu.VMEM((27, width, width), jnp.float32),
-            pltpu.SemaphoreType.DMA((27 // FINISH_STEP,)),
+            pltpu.SemaphoreType.DMA((27 // FINISH_STEP + 2,)),
         ],
         compiler_params=pltpu.CompilerParams(vmem_limit_bytes=PACK_VMEM),
         name="finish",
-    )(sides, sides_other, middle, middle_other)
+    )(sides, sides_other, middle, middle_other, conv_out, feature_grad)
     return (conv_out[None], feature_grad[None], weight_grad)
 
 

time: 31.3 us -> 30.9 us (0.987)
  Pallas kernels: 14.8 us -> 14.1 us
    pallas_call x1, Pallas kernels: 1.55 us -> 0.91 us  [whole_scene(): pl.pallas_call(edge_kernel, out_shape=(jax.ShapeDtypeStruct((rows, width)...]
  transfers between devices with their start and end apart: 9 -> 9, of which waited for: 2 -> 3; matrix products, arithmetic and copies ran while one was open for 0% -> 0% of each run, Pallas kernels for 34% -> 32%
where the time goes in v18:
time: 30.9 us; the launch traced here: 30.7 us
  Pallas kernels  14.1 us (46%)
  starting transfers between devices  12.2 us (39%)
  waiting for transfers between devices  1.83 us (6%)
  between operations  1.36 us (4%)
  local copies, waits for them, and re-layouts  1.17 us (4%)
    pallas_call x5, Pallas kernels, row_sums(): pl.pallas_call(functools.partial(row_kernel, not sums, bool(final), group...  8.74 us
    ppermute x4, starting transfers between devices, across(): return lax.ppermute(block, 'brick', [(i, i ^ 1) for i in range(peers)])  6.4 us
    ppermute x3, starting transfers between devices, along(): lax.ppermute(block, 'brick', [(i, (i + turn * tiles_y) % peers) for i in...  5.17 us
    pallas_call x1, Pallas kernels, whole_scene(): pl.pallas_call(own_kernel, out_shape=(jax.ShapeDtypeStruct((width, rows),...  1.77 us
    ppermute x3, waiting for transfers between devices, along(): lax.ppermute(block, 'brick', [(i, (i + turn * tiles_y) % peers) for i in...  1.52 us
    pallas_call x1, Pallas kernels, whole_scene(): pl.pallas_call(finish_kernel, out_shape=(jax.ShapeDtypeStruct((27, width,...  1.33 us
    unnamed x2, local copies, waits for them, and re-layouts  1.17 us
    pallas_call x1, Pallas kernels, whole_scene(): pl.pallas_call(pack_kernel, out_shape=(jax.ShapeDtypeStruct((rows + CODE_...  1.03 us
  transfers between devices with their start and end apart: 9, of which 3 were waited for; matrix products, arithmetic and copies ran while one was open for 0% of the time, Pallas kernels for 32%

profile of v18, /device:TPU:0, one launch (start us, length us, event | category | flops | bytes accessed | tf_op | source)
XLA Modules:
  0.0 30.7 jit_solution(8030172612541381972)
XLA Ops:
  1.3 1.0 %pack_tile.1 = (bf16[272,256]{1,0:T(8,128)(2,1)S(1)}, f32[256,128]{1,0:T(8,128)S(1)}, f32[27,256]{1,0:T(8,128)S(1)}) custom-call(s32[1]{0:T(128)S(6)} %copy.10.time_ref, bf16[1,256,128]{2,1,0:T(8,128)(2,1)} %feat_hbm.1, bf16[1,256,128]{2,1,0:T(8,128)(2,1)} %cot_hbm.1, s32[27,256]{1,0:T(8,128)} %near_hbm.1, bf16[1,128]{1,0:T(2,128)(2,1)} %cond_hbm.1, ...), custom_call_target="tpu_custom_call" | custom-call | tf_op jit(solution)/shard_map/pack_tile/pallas_call | solution.py:248
  2.3 3.1 %collective-permute-start.3 = (bf16[272,256]{1,0:T(8,128)(2,1)S(1)}, bf16[272,256]{1,0:T(8,128)(2,1)S(1)}, u32[]{:S(2)}, u32[]{:S(2)}) collective-permute-start(bf16[272,256]{1,0:T(8,128)(2,1)S(1)} %get-tuple-element.40.refs_1_.refs_3_.mine_ref), channel_id=1, source_target_pairs={{0,4},{2,6},{4,8},{6,10},{8,12},{10,14},{12,0},{14,2},{1,5},{3,7},... | collective-permute-start | bytes 417800 | tf_op jit(solution)/shard_map/ppermute | solution.py:273
  5.4 2.1 %collective-permute-start = (bf16[272,256]{1,0:T(8,128)(2,1)S(1)}, bf16[272,256]{1,0:T(8,128)(2,1)S(1)}, u32[]{:S(2)}, u32[]{:S(2)}) collective-permute-start(bf16[272,256]{1,0:T(8,128)(2,1)S(1)} %get-tuple-element.40.refs_1_.refs_3_.mine_ref), channel_id=1, source_target_pairs={{0,12},{2,14},{4,0},{6,2},{8,4},{10,6},{12,8},{14,10},{1,13},{3,15... | collective-permute-start | bytes 417800 | tf_op jit(solution)/shard_map/ppermute | solution.py:273
  7.5 1.6 %collective-permute-start.2 = (bf16[272,256]{1,0:T(8,128)(2,1)S(1)}, bf16[272,256]{1,0:T(8,128)(2,1)S(1)}, u32[]{:S(2)}, u32[]{:S(2)}) collective-permute-start(bf16[272,256]{1,0:T(8,128)(2,1)S(1)} %get-tuple-element.40.refs_1_.refs_3_.mine_ref), channel_id=1, source_target_pairs={{0,2},{2,0},{4,6},{6,4},{8,10},{10,8},{12,14},{14,12},{1,3},{3,1},... | collective-permute-start | bytes 417800 | tf_op jit(solution)/shard_map/ppermute | solution.py:270
  9.1 0.0 copy-start
  9.1 1.2 %copy-done = bf16[27,128,128]{2,1,0:T(8,128)(2,1)S(1)} copy-done((bf16[27,128,128]{2,1,0:T(8,128)(2,1)S(1)}, bf16[27,128,128]{2,1,0:T(8,128)(2,1)}, u32[]{:S(2)}) %copy-start) | copy-done | bytes 884760
  10.3 0.4 %turn_weights.1 = (bf16[128,3456]{1,0:T(8,128)(2,1)S(1)}, bf16[128,3456]{1,0:T(8,128)(2,1)S(1)}) custom-call(bf16[27,128,128]{2,1,0:T(8,128)(2,1)S(1)} %copy-done), custom_call_target="tpu_custom_call" | custom-call | flops 200000000 | bytes 3000000 | tf_op jit(solution)/shard_map/turn_weights/pallas_call | solution.py:276
  10.7 1.3 %collective-permute-done.3.refs_1_.refs_3_.before_mine = bf16[272,256]{1,0:T(8,128)(2,1)S(1)} collective-permute-done((bf16[272,256]{1,0:T(8,128)(2,1)S(1)}, bf16[272,256]{1,0:T(8,128)(2,1)S(1)}, u32[]{:S(2)}, u32[]{:S(2)}) %collective-permute-start.3) | collective-permute-done | bytes 139296 | tf_op jit(solution)/shard_map/ppermute | solution.py:273
  11.9 0.0 collective-permute-start.5
  11.9 1.7 %collective-permute-start.4 = (bf16[272,256]{1,0:T(8,128)(2,1)S(1)}, bf16[272,256]{1,0:T(8,128)(2,1)S(1)}, u32[]{:S(2)}, u32[]{:S(2)}) collective-permute-start(bf16[272,256]{1,0:T(8,128)(2,1)S(1)} %collective-permute-done.3.refs_1_.refs_3_.before_mine), channel_id=1, source_target_pairs={{0,2},{2,0},{4,6},{6,4},{8,10},{10,8},{12,14},{14,12},{1,3},{3,1},... | collective-permute-start | bytes 417800 | tf_op jit(solution)/shard_map/ppermute | solution.py:270
  13.7 0.0 collective-permute-done.refs_1_.refs_5_.after_mine
  13.7 1.3 %collective-permute-start.1 = (bf16[272,256]{1,0:T(8,128)(2,1)S(1)}, bf16[272,256]{1,0:T(8,128)(2,1)S(1)}, u32[]{:S(2)}, u32[]{:S(2)}) collective-permute-start(bf16[272,256]{1,0:T(8,128)(2,1)S(1)} %collective-permute-done.refs_1_.refs_5_.after_mine), channel_id=1, source_target_pairs={{0,2},{2,0},{4,6},{6,4},{8,10},{10,8},{12,14},{14,12},{1,3},{3,1},... | collective-permute-start | bytes 417800 | tf_op jit(solution)/shard_map/ppermute | solution.py:270
  15.0 0.0 collective-permute-done.2.refs_2_.refs_4_.other_ref
  15.0 1.8 %weight_row_0.1 = (f32[1664,128]{1,0:T(8,128)S(1)}, f32[1664,128]{1,0:T(8,128)S(1)}, f32[128,128]{1,0:T(8,128)S(1)}) custom-call(s32[1]{0:T(128)} %bitcast.refs_0_.where_ref, bf16[272,256]{1,0:T(8,128)(2,1)S(1)} %get-tuple-element.40.refs_1_.refs_3_.mine_ref, bf16[272,256]{1,0:T(8,128)(2,1)S(1)} %collective-permute-done.2.refs_2_.refs_4_.other_ref), custom_call_target="tpu_custom_call" | custom-call | flops 2000000000 | bytes 4000000 | tf_op jit(solution)/shard_map/weight_row_0/pallas_call | solution.py:331
  16.8 1.8 %voxels_own_row.1 = (f32[128,256]{1,0:T(8,128)S(1)}, f32[128,256]{1,0:T(8,128)S(1)}) custom-call(s32[1]{0:T(128)} %bitcast.refs_0_.where_ref, bf16[272,256]{1,0:T(8,128)(2,1)S(1)} %get-tuple-element.40.refs_1_.refs_3_.mine_ref, bf16[272,256]{1,0:T(8,128)(2,1)S(1)} %collective-permute-done.2.refs_2_.refs_4_.other_ref, ...), custom_call_target="tpu_custom_call" | custom-call | flops 2000000000 | bytes 4000000 | tf_op jit(solution)/shard_map/voxels_own_row/pallas_call | solution.py:289
  18.5 0.2 collective-permute-done.5.refs_1_
  18.8 1.7 %collective-permute-start.6 = (bf16[272,256]{1,0:T(8,128)(2,1)S(1)}, bf16[272,256]{1,0:T(8,128)(2,1)S(1)}, u32[]{:S(2)}, u32[]{:S(2)}) collective-permute-start(bf16[272,256]{1,0:T(8,128)(2,1)S(1)} %collective-permute-done.5.refs_1_), channel_id=1, source_target_pairs={{0,2},{2,0},{4,6},{6,4},{8,10},{10,8},{12,14},{14,12},{1,3},{3,1},... | collective-permute-start | bytes 417800 | tf_op jit(solution)/shard_map/ppermute | solution.py:270
  20.5 0.0 collective-permute-done.4.refs_2_.refs_4_.before_other
  20.5 2.1 %weight_row_1.1 = (f32[1664,128]{1,0:T(8,128)S(1)}, f32[1664,128]{1,0:T(8,128)S(1)}, f32[128,128]{1,0:T(8,128)S(1)}) custom-call(s32[1]{0:T(128)} %bitcast.refs_0_.where_ref, bf16[272,256]{1,0:T(8,128)(2,1)S(1)} %collective-permute-done.3.refs_1_.refs_3_.before_mine, bf16[272,256]{1,0:T(8,128)(2,1)S(1)} %collective-permute-done.4.refs_2_.refs_4_.before_other, ...), custom_call_target="tpu_custom_call" | custom-call | flops 2000000000 | bytes 4000000 | tf_op jit(solution)/shard_map/weight_row_1/pallas_call | solution.py:331
  22.7 0.0 collective-permute-done.1.refs_2_.refs_6_.after_other
  22.7 2.1 %weight_row_2.1 = (f32[1664,128]{1,0:T(8,128)S(1)}, f32[1664,128]{1,0:T(8,128)S(1)}, f32[128,128]{1,0:T(8,128)S(1)}) custom-call(s32[1]{0:T(128)} %bitcast.refs_0_.where_ref, bf16[272,256]{1,0:T(8,128)(2,1)S(1)} %collective-permute-done.refs_1_.refs_5_.after_mine, bf16[272,256]{1,0:T(8,128)(2,1)S(1)} %collective-permute-done.1.refs_2_.refs_6_.after_other, ...), custom_call_target="tpu_custom_call" | custom-call | flops 2000000000 | bytes 4000000 | tf_op jit(solution)/shard_map/weight_row_2/pallas_call | solution.py:331
  24.8 0.0 collective-permute-done.6.refs_2_
  24.8 1.9 %weight_row_3.1 = (f32[18,128,128]{2,1,0:T(8,128)S(1)}, bf16[18,128,128]{2,1,0:T(8,128)(2,1)S(1)}, bf16[768,256]{1,0:T(8,128)(2,1)S(1)}, bf16[256,768]{1,0:T(8,128)(2,1)S(1)}, f32[5,16,128]{2,1,0:T(8,128)S(1)}) custom-call(s32[1]{0:T(128)} %bitcast.refs_0_.where_ref, bf16[272,256]{1,0:T(8,128)(2,1)S(1)} %collective-permute-done.5.refs_1_, ...), custom_call_target="tpu_custom_call" | custom-call | flops 2000000000 | bytes 4000000 | tf_op jit(solution)/shard_map/weight_row_3/pallas_call | solution.py:331
  26.7 0.1 collective-permute-start.7
  26.8 0.8 %weight_row_3_middle.1 = (f32[9,128,128]{2,1,0:T(8,128)S(1)}, bf16[9,128,128]{2,1,0:T(8,128)(2,1)S(1)}) custom-call(s32[1]{0:T(128)} %bitcast.refs_0_.where_ref, bf16[768,256]{1,0:T(8,128)(2,1)S(1)} %get-tuple-element.61.refs_1_, bf16[256,768]{1,0:T(8,128)(2,1)S(1)} %get-tuple-element.62.refs_2_, f32[5,16,128]{2,1,0:T(8,128)S(1)} %get-tuple-element.63.refs_3_, ...), custom_call_target="tpu_custom_call" | custom-call | flops 2000000000 | bytes 4000000 | tf_op jit(solution)/shard_map/weight_row_3_middle/pallas_call | solution.py:331
  27.6 0.6 %collective-permute-start.8 = (bf16[9,128,128]{2,1,0:T(8,128)(2,1)S(1)}, bf16[9,128,128]{2,1,0:T(8,128)(2,1)S(1)}, u32[]{:S(2)}, u32[]{:S(2)}) collective-permute-start(bf16[9,128,128]{2,1,0:T(8,128)(2,1)S(1)} %get-tuple-element.66), channel_id=1, source_target_pairs={{0,1},{1,0},{2,3},{3,2},{4,5},{5,4},{6,7},{7,6},{8,9},{9,8},{10,11... | collective-permute-start | bytes 884744 | tf_op jit(solution)/shard_map/ppermute | solution.py:346
  28.2 0.9 %voxel_edges.1 = (bf16[256,128]{1,0:T(8,128)(2,1)S(1)}, bf16[256,128]{1,0:T(8,128)(2,1)S(1)}) custom-call(s32[1]{0:T(128)} %bitcast.refs_0_.where_ref, bf16[272,256]{1,0:T(8,128)(2,1)S(1)} %collective-permute-done.3.refs_1_.refs_3_.before_mine, bf16[272,256]{1,0:T(8,128)(2,1)S(1)} %collective-permute-done.4.refs_2_.refs_4_.before_other, ...), custom_call_target="tpu_custom_call" | custom-call | flops 1000000000 | bytes 4000000 | tf_op jit(solution)/shard_map/voxel_edges/pallas_call | solution.py:360
  29.1 0.3 collective-permute-done.8.middle_sent
  29.4 0.0 collective-permute-done.7.sides_sent
  29.4 1.3 %finish.1 = (f32[27,128,128]{2,1,0:T(8,128)}, bf16[256,128]{1,0:T(8,128)(2,1)}, bf16[256,128]{1,0:T(8,128)(2,1)}) custom-call(f32[18,128,128]{2,1,0:T(8,128)S(1)} %get-tuple-element.59.sides_ref, bf16[18,128,128]{2,1,0:T(8,128)(2,1)S(1)} %collective-permute-done.7.sides_sent, f32[9,128,128]{2,1,0:T(8,128)S(1)} %get-tuple-element.65.middle_ref, ...), custom_call_target="tpu_custom_call" | custom-call | tf_op jit(solution)/shard_map/finish/pallas_call | solution.py:375
Async XLA Ops:
  2.3 9.6 %collective-permute-start.3 = (bf16[272,256]{1,0:T(8,128)(2,1)S(1)}, bf16[272,256]{1,0:T(8,128)(2,1)S(1)}, u32[]{:S(2)}, u32[]{:S(2)}) collective-permute-start(bf16[272,256]{1,0:T(8,128)(2,1)S(1)} %get-tuple-element.40.refs_1_.refs_3_.mine_ref), channel_id=1, source_target_pairs={{0,4},{2,6},{4,8},{6,10},{8,12},{10,14},{12,0},{14,2},{1,5},{3,7},... | collective-permute-start | bytes 417800 | tf_op jit(solution)/shard_map/ppermute | solution.py:273
  5.4 8.3 %collective-permute-start = (bf16[272,256]{1,0:T(8,128)(2,1)S(1)}, bf16[272,256]{1,0:T(8,128)(2,1)S(1)}, u32[]{:S(2)}, u32[]{:S(2)}) collective-permute-start(bf16[272,256]{1,0:T(8,128)(2,1)S(1)} %get-tuple-element.40.refs_1_.refs_3_.mine_ref), channel_id=1, source_target_pairs={{0,12},{2,14},{4,0},{6,2},{8,4},{10,6},{12,8},{14,10},{1,13},{3,15... | collective-permute-start | bytes 417800 | tf_op jit(solution)/shard_map/ppermute | solution.py:273
  7.5 7.5 %collective-permute-start.2 = (bf16[272,256]{1,0:T(8,128)(2,1)S(1)}, bf16[272,256]{1,0:T(8,128)(2,1)S(1)}, u32[]{:S(2)}, u32[]{:S(2)}) collective-permute-start(bf16[272,256]{1,0:T(8,128)(2,1)S(1)} %get-tuple-element.40.refs_1_.refs_3_.mine_ref), channel_id=1, source_target_pairs={{0,2},{2,0},{4,6},{6,4},{8,10},{10,8},{12,14},{14,12},{1,3},{3,1},... | collective-permute-start | bytes 417800 | tf_op jit(solution)/shard_map/ppermute | solution.py:270
  9.1 1.2 %copy-start = (bf16[27,128,128]{2,1,0:T(8,128)(2,1)S(1)}, bf16[27,128,128]{2,1,0:T(8,128)(2,1)}, u32[]{:S(2)}) copy-start(bf16[27,128,128]{2,1,0:T(8,128)(2,1)} %w_ref) | copy-start | bytes 2654212
  11.9 6.9 %collective-permute-start.5 = (bf16[272,256]{1,0:T(8,128)(2,1)S(1)}, bf16[272,256]{1,0:T(8,128)(2,1)S(1)}, u32[]{:S(2)}, u32[]{:S(2)}) collective-permute-start(bf16[272,256]{1,0:T(8,128)(2,1)S(1)} %collective-permute-done.3.refs_1_.refs_3_.before_mine), channel_id=1, source_target_pairs={{0,4},{2,6},{4,8},{6,10},{8,12},{10,14},{12,0},{14,2},{1,5},{3,7},... | collective-permute-start | bytes 417800 | tf_op jit(solution)/shard_map/ppermute | solution.py:273
  11.9 8.6 %collective-permute-start.4 = (bf16[272,256]{1,0:T(8,128)(2,1)S(1)}, bf16[272,256]{1,0:T(8,128)(2,1)S(1)}, u32[]{:S(2)}, u32[]{:S(2)}) collective-permute-start(bf16[272,256]{1,0:T(8,128)(2,1)S(1)} %collective-permute-done.3.refs_1_.refs_3_.before_mine), channel_id=1, source_target_pairs={{0,2},{2,0},{4,6},{6,4},{8,10},{10,8},{12,14},{14,12},{1,3},{3,1},... | collective-permute-start | bytes 417800 | tf_op jit(solution)/shard_map/ppermute | solution.py:270
  13.7 9.0 %collective-permute-start.1 = (bf16[272,256]{1,0:T(8,128)(2,1)S(1)}, bf16[272,256]{1,0:T(8,128)(2,1)S(1)}, u32[]{:S(2)}, u32[]{:S(2)}) collective-permute-start(bf16[272,256]{1,0:T(8,128)(2,1)S(1)} %collective-permute-done.refs_1_.refs_5_.after_mine), channel_id=1, source_target_pairs={{0,2},{2,0},{4,6},{6,4},{8,10},{10,8},{12,14},{14,12},{1,3},{3,1},... | collective-permute-start | bytes 417800 | tf_op jit(solution)/shard_map/ppermute | solution.py:270
  18.8 6.0 %collective-permute-start.6 = (bf16[272,256]{1,0:T(8,128)(2,1)S(1)}, bf16[272,256]{1,0:T(8,128)(2,1)S(1)}, u32[]{:S(2)}, u32[]{:S(2)}) collective-permute-start(bf16[272,256]{1,0:T(8,128)(2,1)S(1)} %collective-permute-done.5.refs_1_), channel_id=1, source_target_pairs={{0,2},{2,0},{4,6},{6,4},{8,10},{10,8},{12,14},{14,12},{1,3},{3,1},... | collective-permute-start | bytes 417800 | tf_op jit(solution)/shard_map/ppermute | solution.py:270
  26.7 2.6 %collective-permute-start.7 = (bf16[18,128,128]{2,1,0:T(8,128)(2,1)S(1)}, bf16[18,128,128]{2,1,0:T(8,128)(2,1)S(1)}, u32[]{:S(2)}, u32[]{:S(2)}) collective-permute-start(bf16[18,128,128]{2,1,0:T(8,128)(2,1)S(1)} %get-tuple-element.60), channel_id=1, source_target_pairs={{0,1},{1,0},{2,3},{3,2},{4,5},{5,4},{6,7},{7,6},{8,9},{9,8},{10,11... | collective-permute-start | bytes 1769480 | tf_op jit(solution)/shard_map/ppermute | solution.py:346
  27.6 1.8 %collective-permute-start.8 = (bf16[9,128,128]{2,1,0:T(8,128)(2,1)S(1)}, bf16[9,128,128]{2,1,0:T(8,128)(2,1)S(1)}, u32[]{:S(2)}, u32[]{:S(2)}) collective-permute-start(bf16[9,128,128]{2,1,0:T(8,128)(2,1)S(1)} %get-tuple-element.66), channel_id=1, source_target_pairs={{0,1},{1,0},{2,3},{3,2},{4,5},{5,4},{6,7},{7,6},{8,9},{9,8},{10,11... | collective-permute-start | bytes 884744 | tf_op jit(solution)/shard_map/ppermute | solution.py:346

commit v19 on v18

--- a/solution.py
+++ b/solution.py
@@ -1,4 +1,5 @@
 import functools
+import operator
 
 import jax
 import jax.numpy as jnp
@@ -89,7 +90,11 @@
                 to[side][row:row + width, lane:lane + span] = near[:, j * span:(j + 1) * span]
 
 
-def row_kernel(first_stage, final, groups, laid, strips, borders, *refs):
+def added(terms):
+    return functools.reduce(operator.add, terms)
+
+
+def row_kernel(first_stage, final, groups, laid, lines, strips, borders, *refs):
     refs = list(refs)
     where_ref = refs.pop(0)
     pairs = [] if laid else [(refs.pop(0), refs.pop(0)) for _ in range(1 + max(pair for pair, _ in strips))]
@@ -102,33 +107,36 @@
     rows = TILE * STRIP
     span = 2 * STRIP
     tile_y = where_ref[0] % 2
-    borders = [(u, u - 1) for u in range(1, TILE)] + borders
+    borders = [(at + u, at + u - 1) for at in lines for u in range(1, TILE)] + borders
     targets = sorted({target for target, _ in borders})
+    line_strips = [at + u for at in lines for u in range(TILE)]
+    spans = [(at * span, (at + TILE) * span) for at in lines]
     for i, (pair, u) in enumerate([] if laid else strips):
         lay_strip(ground, i, tile_y, *pairs[pair], u)
-        if i < TILE or i in targets:
+        if i in line_strips + targets:
             both = [ref[rows:, u * STRIP:(u + 1) * STRIP].astype(jnp.float32) for ref in pairs[pair]]
             first = jnp.where(tile_y == 0, both[0], both[1])
             second = jnp.where(tile_y == 0, both[1], both[0])
             codes[i] = jnp.concatenate([first, second], axis=1)
-        if i < TILE or i in [source for _, source in borders]:
+        if i in line_strips + [source for _, source in borders]:
             turned[:, i * span:(i + 1) * span] = ground[i * span:(i + 1) * span, :].T
     place = lax.broadcasted_iota(jnp.int32, (span, span), 0).astype(jnp.float32)
 
     to = (near_act, near_cot)
-    for source in range(TILE + 2):
-        found = [(source, k) for k in range(9, HALF)] if 1 in groups and source < TILE else []
+    for source in range(len(strips)):
+        found = [(source, k) for k in range(9, HALF)] if 1 in groups and source in line_strips else []
         if 0 in groups:
             found += [(target, k) for target, origin in borders if origin == source for k in range(9)]
         if found:
             picks = [(place == codes[target, k:k + 1, :]).astype(jnp.bfloat16) for target, k in found]
             look_up((turned, source * span, span), picks, [(to, k * width, target * span) for target, k in found])
-    extents = ((0, 9, span * targets[0], span * (targets[-1] + 1)), (9, HALF, 0, TILE * span))
+    extents = ((0, 9, [(span * targets[0], span * (targets[-1] + 1))] if targets else []), (9, HALF, spans))
     for turn, near in ((0, near_act), (1, near_cot)):
         for group in groups:
-            start, stop, first, last = extents[group]
-            other = ground[first:last, (1 - turn) * width:(2 - turn) * width]
-            value = jnp.dot(near[start * width:stop * width, first:last], other, preferred_element_type=jnp.float32)
+            start, stop, parts = extents[group]
+            value = added(jnp.dot(near[start * width:stop * width, first:last],
+                                ground[first:last, (1 - turn) * width:(2 - turn) * width],
+                                preferred_element_type=jnp.float32) for first, last in parts)
             if not first_stage:
                 value = value + before[turn][start * width:stop * width, :]
             if not final:
@@ -143,7 +151,8 @@
                 outs[0][to] = one
                 outs[1][to] = one.astype(jnp.bfloat16)
     if 1 in groups:
-        centre = jnp.dot(turned[:width, :TILE * span], ground[:TILE * span, width:], preferred_element_type=jnp.float32)
+        centre = added(jnp.dot(turned[:width, first:last], ground[first:last, width:], preferred_element_type=jnp.float32)
+                       for first, last in spans)
         if not first_stage:
             centre = centre + before[2][...]
         if final:
@@ -306,7 +315,7 @@
     before_pair = (before, across(before))
     after_pair = (after, across(after))
     far_pair = (far, across(far))
-    def row_sums(name, pairs, strips, borders, sums, groups=(0, 1), final=0, keep=False, laid=()):
+    def row_sums(name, pairs, strips, borders, sums, groups=(0, 1), final=0, keep=False, laid=(), lines=(0,)):
         blocks = [block for pair in pairs for block in pair]
         if final:
             out_shape = (
@@ -319,23 +328,24 @@
                 jax.ShapeDtypeStruct((HALF * width, width), jnp.float32),
                 jax.ShapeDtypeStruct((width, width), jnp.float32),
             )
+        room = max(len(strips), TILE + 2) if not laid else TILE + 2
         layout = (
-            ((TILE + 2) * span, 2 * width, jnp.bfloat16),
-            (2 * width, (TILE + 2) * span, jnp.bfloat16),
-            (TILE + 1, CODE_ROWS, span, jnp.float32),
+            (room * span, 2 * width, jnp.bfloat16),
+            (2 * width, room * span, jnp.bfloat16),
+            (room, CODE_ROWS, span, jnp.float32),
         )
         scratch = [] if laid or keep else [pltpu.VMEM(tuple(shape), kind) for *shape, kind in layout]
         if keep:
             out_shape += tuple(jax.ShapeDtypeStruct(tuple(shape), kind) for *shape, kind in layout)
         operands = (*blocks, *laid, *sums)
         return pl.pallas_call(
-            functools.partial(row_kernel, not sums, bool(final), groups, bool(laid), strips, borders),
+            functools.partial(row_kernel, not sums, bool(final), groups, bool(laid), lines, strips, borders),
             out_shape=out_shape,
             in_specs=[smem] + [vmem] * len(operands),
             out_specs=(vmem,) * len(out_shape),
             scratch_shapes=scratch + [
-                pltpu.VMEM((HALF * width, (TILE + 1) * span), jnp.bfloat16),
-                pltpu.VMEM((HALF * width, (TILE + 1) * span), jnp.bfloat16),
+                pltpu.VMEM((HALF * width, room * span), jnp.bfloat16),
+                pltpu.VMEM((HALF * width, room * span), jnp.bfloat16),
             ],
             compiler_params=params,
             cost_estimate=pl.CostEstimate(flops=2 * 10**9, bytes_accessed=4 * 10**6, transcendentals=0),
@@ -347,8 +357,9 @@
 
     line = [(0, u) for u in range(TILE)]
     sums = row_sums("weight_row_0", (own_pair,), line, [], ())
-    sums = row_sums("weight_row_1", (before_pair, own_pair), line + [(1, 0)], [(TILE, TILE - 1)], sums)
-    sums = row_sums("weight_row_2", (after_pair, own_pair), line + [(1, TILE - 1)], [(0, TILE)], sums)
+    around = line + [(1, 0)] + [(2, u) for u in range(TILE)] + [(1, TILE - 1)]
+    sums = row_sums("weight_rows_1_2", (before_pair, own_pair, after_pair), around,
+                    [(TILE, TILE - 1), (TILE + 1, 2 * TILE + 1)], sums, lines=(0, TILE + 1))
     sides, sides_sent, *laid = row_sums("weight_row_3", (far_pair, before_pair, after_pair),
                                  line + [(1, 0), (2, TILE - 1)], [(TILE, TILE - 1), (0, TILE + 1)],
                                  sums, groups=(0,), final=18, keep=True)

time: 30.9 us -> 30.9 us (level); the launches traced: 30.7 us -> 30.4 us
    pallas_call x5 -> x4, Pallas kernels: 8.74 us -> 8.44 us  [row_sums(): pl.pallas_call(functools.partial(row_kernel, not sums, bool(final), group...]
  transfers between devices with their start and end apart: 9 -> 9, of which waited for: 3 -> 3; matrix products, arithmetic and copies ran while one was open for 0% -> 0% of each run, Pallas kernels for 32% -> 31%
where the time goes in v19:
time: 30.9 us; the launch traced here: 30.4 us
  Pallas kernels  13.9 us (45%)
  starting transfers between devices  12.2 us (39%)
  waiting for transfers between devices  1.82 us (6%)
  between operations  1.35 us (4%)
  local copies, waits for them, and re-layouts  1.17 us (4%)
    pallas_call x4, Pallas kernels, row_sums(): pl.pallas_call(functools.partial(row_kernel, not sums, bool(final), group...  8.44 us
    ppermute x4, starting transfers between devices, across(): return lax.ppermute(block, 'brick', [(i, i ^ 1) for i in range(peers)])  6.4 us
    ppermute x3, starting transfers between devices, along(): lax.ppermute(block, 'brick', [(i, (i + turn * tiles_y) % peers) for i in...  5.17 us
    pallas_call x1, Pallas kernels, whole_scene(): pl.pallas_call(own_kernel, out_shape=(jax.ShapeDtypeStruct((width, rows),...  1.77 us
    ppermute x3, waiting for transfers between devices, along(): lax.ppermute(block, 'brick', [(i, (i + turn * tiles_y) % peers) for i in...  1.52 us
    pallas_call x1, Pallas kernels, whole_scene(): pl.pallas_call(finish_kernel, out_shape=(jax.ShapeDtypeStruct((27, width,...  1.33 us
    unnamed x2, local copies, waits for them, and re-layouts  1.17 us
    pallas_call x1, Pallas kernels, whole_scene(): pl.pallas_call(pack_kernel, out_shape=(jax.ShapeDtypeStruct((rows + CODE_...  1.03 us
  transfers between devices with their start and end apart: 9, of which 3 were waited for; matrix products, arithmetic and copies ran while one was open for 0% of the time, Pallas kernels for 31%

profile of v19, /device:TPU:0, one launch (start us, length us, event | category | flops | bytes accessed | tf_op | source)
XLA Modules:
  0.0 30.4 jit_solution(15603341451417473232)
XLA Ops:
  1.3 1.0 %pack_tile.1 = (bf16[272,256]{1,0:T(8,128)(2,1)S(1)}, f32[256,128]{1,0:T(8,128)S(1)}, f32[27,256]{1,0:T(8,128)S(1)}) custom-call(s32[1]{0:T(128)S(6)} %copy.10.time_ref, bf16[1,256,128]{2,1,0:T(8,128)(2,1)} %feat_hbm.1, bf16[1,256,128]{2,1,0:T(8,128)(2,1)} %cot_hbm.1, s32[27,256]{1,0:T(8,128)} %near_hbm.1, bf16[1,128]{1,0:T(2,128)(2,1)} %cond_hbm.1, ...), custom_call_target="tpu_custom_call" | custom-call | tf_op jit(solution)/shard_map/pack_tile/pallas_call | solution.py:257
  2.3 3.1 %collective-permute-start = (bf16[272,256]{1,0:T(8,128)(2,1)S(1)}, bf16[272,256]{1,0:T(8,128)(2,1)S(1)}, u32[]{:S(2)}, u32[]{:S(2)}) collective-permute-start(bf16[272,256]{1,0:T(8,128)(2,1)S(1)} %get-tuple-element.37.refs_1_.refs_3_.mine_ref), channel_id=1, source_target_pairs={{0,4},{2,6},{4,8},{6,10},{8,12},{10,14},{12,0},{14,2},{1,5},{3,7},... | collective-permute-start | bytes 417800 | tf_op jit(solution)/shard_map/ppermute | solution.py:282
  5.4 2.1 %collective-permute-start.3 = (bf16[272,256]{1,0:T(8,128)(2,1)S(1)}, bf16[272,256]{1,0:T(8,128)(2,1)S(1)}, u32[]{:S(2)}, u32[]{:S(2)}) collective-permute-start(bf16[272,256]{1,0:T(8,128)(2,1)S(1)} %get-tuple-element.37.refs_1_.refs_3_.mine_ref), channel_id=1, source_target_pairs={{0,12},{2,14},{4,0},{6,2},{8,4},{10,6},{12,8},{14,10},{1,13},{3,15... | collective-permute-start | bytes 417800 | tf_op jit(solution)/shard_map/ppermute | solution.py:282
  7.5 1.6 %collective-permute-start.2 = (bf16[272,256]{1,0:T(8,128)(2,1)S(1)}, bf16[272,256]{1,0:T(8,128)(2,1)S(1)}, u32[]{:S(2)}, u32[]{:S(2)}) collective-permute-start(bf16[272,256]{1,0:T(8,128)(2,1)S(1)} %get-tuple-element.37.refs_1_.refs_3_.mine_ref), channel_id=1, source_target_pairs={{0,2},{2,0},{4,6},{6,4},{8,10},{10,8},{12,14},{14,12},{1,3},{3,1},... | collective-permute-start | bytes 417800 | tf_op jit(solution)/shard_map/ppermute | solution.py:279
  9.1 0.0 copy-start
  9.1 1.2 %copy-done = bf16[27,128,128]{2,1,0:T(8,128)(2,1)S(1)} copy-done((bf16[27,128,128]{2,1,0:T(8,128)(2,1)S(1)}, bf16[27,128,128]{2,1,0:T(8,128)(2,1)}, u32[]{:S(2)}) %copy-start) | copy-done | bytes 884760
  10.3 0.4 %turn_weights.1 = (bf16[128,3456]{1,0:T(8,128)(2,1)S(1)}, bf16[128,3456]{1,0:T(8,128)(2,1)S(1)}) custom-call(bf16[27,128,128]{2,1,0:T(8,128)(2,1)S(1)} %copy-done), custom_call_target="tpu_custom_call" | custom-call | flops 200000000 | bytes 3000000 | tf_op jit(solution)/shard_map/turn_weights/pallas_call | solution.py:285
  10.7 1.3 %collective-permute-done.refs_1_.refs_3_.before_mine = bf16[272,256]{1,0:T(8,128)(2,1)S(1)} collective-permute-done((bf16[272,256]{1,0:T(8,128)(2,1)S(1)}, bf16[272,256]{1,0:T(8,128)(2,1)S(1)}, u32[]{:S(2)}, u32[]{:S(2)}) %collective-permute-start) | collective-permute-done | bytes 139296 | tf_op jit(solution)/shard_map/ppermute | solution.py:282
  11.9 0.0 collective-permute-start.5
  11.9 1.7 %collective-permute-start.1 = (bf16[272,256]{1,0:T(8,128)(2,1)S(1)}, bf16[272,256]{1,0:T(8,128)(2,1)S(1)}, u32[]{:S(2)}, u32[]{:S(2)}) collective-permute-start(bf16[272,256]{1,0:T(8,128)(2,1)S(1)} %collective-permute-done.refs_1_.refs_3_.before_mine), channel_id=1, source_target_pairs={{0,2},{2,0},{4,6},{6,4},{8,10},{10,8},{12,14},{14,12},{1,3},{3,1},... | collective-permute-start | bytes 417800 | tf_op jit(solution)/shard_map/ppermute | solution.py:279
  13.7 0.0 collective-permute-done.3.refs_5_.after_mine
  13.7 1.3 %collective-permute-start.4 = (bf16[272,256]{1,0:T(8,128)(2,1)S(1)}, bf16[272,256]{1,0:T(8,128)(2,1)S(1)}, u32[]{:S(2)}, u32[]{:S(2)}) collective-permute-start(bf16[272,256]{1,0:T(8,128)(2,1)S(1)} %collective-permute-done.3.refs_5_.after_mine), channel_id=1, source_target_pairs={{0,2},{2,0},{4,6},{6,4},{8,10},{10,8},{12,14},{14,12},{1,3},{3,1},... | collective-permute-start | bytes 417800 | tf_op jit(solution)/shard_map/ppermute | solution.py:279
  15.0 0.0 collective-permute-done.2.refs_2_.refs_4_.other_ref
  15.0 1.8 %weight_row_0.1 = (f32[1664,128]{1,0:T(8,128)S(1)}, f32[1664,128]{1,0:T(8,128)S(1)}, f32[128,128]{1,0:T(8,128)S(1)}) custom-call(s32[1]{0:T(128)} %bitcast.refs_0_.where_ref, bf16[272,256]{1,0:T(8,128)(2,1)S(1)} %get-tuple-element.37.refs_1_.refs_3_.mine_ref, bf16[272,256]{1,0:T(8,128)(2,1)S(1)} %collective-permute-done.2.refs_2_.refs_4_.other_ref), custom_call_target="tpu_custom_call" | custom-call | flops 2000000000 | bytes 4000000 | tf_op jit(solution)/shard_map/weight_row_0/pallas_call | solution.py:341
  16.8 1.8 %voxels_own_row.1 = (f32[128,256]{1,0:T(8,128)S(1)}, f32[128,256]{1,0:T(8,128)S(1)}) custom-call(s32[1]{0:T(128)} %bitcast.refs_0_.where_ref, bf16[272,256]{1,0:T(8,128)(2,1)S(1)} %get-tuple-element.37.refs_1_.refs_3_.mine_ref, bf16[272,256]{1,0:T(8,128)(2,1)S(1)} %collective-permute-done.2.refs_2_.refs_4_.other_ref, ...), custom_call_target="tpu_custom_call" | custom-call | flops 2000000000 | bytes 4000000 | tf_op jit(solution)/shard_map/voxels_own_row/pallas_call | solution.py:298
  18.5 0.3 collective-permute-done.5.refs_1_
  18.8 1.7 %collective-permute-start.6 = (bf16[272,256]{1,0:T(8,128)(2,1)S(1)}, bf16[272,256]{1,0:T(8,128)(2,1)S(1)}, u32[]{:S(2)}, u32[]{:S(2)}) collective-permute-start(bf16[272,256]{1,0:T(8,128)(2,1)S(1)} %collective-permute-done.5.refs_1_), channel_id=1, source_target_pairs={{0,2},{2,0},{4,6},{6,4},{8,10},{10,8},{12,14},{14,12},{1,3},{3,1},... | collective-permute-start | bytes 417800 | tf_op jit(solution)/shard_map/ppermute | solution.py:279
  20.5 0.0 collective-permute-done.1.refs_2_.refs_4_.before_other
  20.5 0.0 collective-permute-done.4.refs_6_.after_other
  20.5 4.0 %weight_rows_1_2.1 = (f32[1664,128]{1,0:T(8,128)S(1)}, f32[1664,128]{1,0:T(8,128)S(1)}, f32[128,128]{1,0:T(8,128)S(1)}) custom-call(s32[1]{0:T(128)} %bitcast.refs_0_.where_ref, bf16[272,256]{1,0:T(8,128)(2,1)S(1)} %collective-permute-done.refs_1_.refs_3_.before_mine, bf16[272,256]{1,0:T(8,128)(2,1)S(1)} %collective-permute-done.1.refs_2_.refs_4_.before_other, ...), custom_call_target="tpu_custom_call" | custom-call | flops 2000000000 | bytes 4000000 | tf_op jit(solution)/shard_map/weight_rows_1_2/pallas_call | solution.py:341
  24.5 0.0 collective-permute-done.6.refs_2_
  24.5 1.9 %weight_row_3.1 = (f32[18,128,128]{2,1,0:T(8,128)S(1)}, bf16[18,128,128]{2,1,0:T(8,128)(2,1)S(1)}, bf16[768,256]{1,0:T(8,128)(2,1)S(1)}, bf16[256,768]{1,0:T(8,128)(2,1)S(1)}, f32[6,16,128]{2,1,0:T(8,128)S(1)}) custom-call(s32[1]{0:T(128)} %bitcast.refs_0_.where_ref, bf16[272,256]{1,0:T(8,128)(2,1)S(1)} %collective-permute-done.5.refs_1_, ...), custom_call_target="tpu_custom_call" | custom-call | flops 2000000000 | bytes 4000000 | tf_op jit(solution)/shard_map/weight_row_3/pallas_call | solution.py:341
  26.4 0.1 collective-permute-start.7
  26.5 0.8 %weight_row_3_middle.1 = (f32[9,128,128]{2,1,0:T(8,128)S(1)}, bf16[9,128,128]{2,1,0:T(8,128)(2,1)S(1)}) custom-call(s32[1]{0:T(128)} %bitcast.refs_0_.where_ref, bf16[768,256]{1,0:T(8,128)(2,1)S(1)} %get-tuple-element.55.refs_1_, bf16[256,768]{1,0:T(8,128)(2,1)S(1)} %get-tuple-element.56.refs_2_, f32[6,16,128]{2,1,0:T(8,128)S(1)} %get-tuple-element.57.refs_3_, ...), custom_call_target="tpu_custom_call" | custom-call | flops 2000000000 | bytes 4000000 | tf_op jit(solution)/shard_map/weight_row_3_middle/pallas_call | solution.py:341
  27.3 0.6 %collective-permute-start.8 = (bf16[9,128,128]{2,1,0:T(8,128)(2,1)S(1)}, bf16[9,128,128]{2,1,0:T(8,128)(2,1)S(1)}, u32[]{:S(2)}, u32[]{:S(2)}) collective-permute-start(bf16[9,128,128]{2,1,0:T(8,128)(2,1)S(1)} %get-tuple-element.60), channel_id=1, source_target_pairs={{0,1},{1,0},{2,3},{3,2},{4,5},{5,4},{6,7},{7,6},{8,9},{9,8},{10,11... | collective-permute-start | bytes 884744 | tf_op jit(solution)/shard_map/ppermute | solution.py:356
  27.9 0.9 %voxel_edges.1 = (bf16[256,128]{1,0:T(8,128)(2,1)S(1)}, bf16[256,128]{1,0:T(8,128)(2,1)S(1)}) custom-call(s32[1]{0:T(128)} %bitcast.refs_0_.where_ref, bf16[272,256]{1,0:T(8,128)(2,1)S(1)} %collective-permute-done.refs_1_.refs_3_.before_mine, bf16[272,256]{1,0:T(8,128)(2,1)S(1)} %collective-permute-done.1.refs_2_.refs_4_.before_other, ...), custom_call_target="tpu_custom_call" | custom-call | flops 1000000000 | bytes 4000000 | tf_op jit(solution)/shard_map/voxel_edges/pallas_call | solution.py:371
  28.8 0.3 collective-permute-done.8.middle_sent
  29.1 0.0 collective-permute-done.7.sides_sent
  29.1 1.3 %finish.1 = (f32[27,128,128]{2,1,0:T(8,128)}, bf16[256,128]{1,0:T(8,128)(2,1)}, bf16[256,128]{1,0:T(8,128)(2,1)}) custom-call(f32[18,128,128]{2,1,0:T(8,128)S(1)} %get-tuple-element.53.sides_ref, bf16[18,128,128]{2,1,0:T(8,128)(2,1)S(1)} %collective-permute-done.7.sides_sent, f32[9,128,128]{2,1,0:T(8,128)S(1)} %get-tuple-element.59.middle_ref, ...), custom_call_target="tpu_custom_call" | custom-call | tf_op jit(solution)/shard_map/finish/pallas_call | solution.py:386
Async XLA Ops:
  2.3 9.6 %collective-permute-start = (bf16[272,256]{1,0:T(8,128)(2,1)S(1)}, bf16[272,256]{1,0:T(8,128)(2,1)S(1)}, u32[]{:S(2)}, u32[]{:S(2)}) collective-permute-start(bf16[272,256]{1,0:T(8,128)(2,1)S(1)} %get-tuple-element.37.refs_1_.refs_3_.mine_ref), channel_id=1, source_target_pairs={{0,4},{2,6},{4,8},{6,10},{8,12},{10,14},{12,0},{14,2},{1,5},{3,7},... | collective-permute-start | bytes 417800 | tf_op jit(solution)/shard_map/ppermute | solution.py:282
  5.4 8.3 %collective-permute-start.3 = (bf16[272,256]{1,0:T(8,128)(2,1)S(1)}, bf16[272,256]{1,0:T(8,128)(2,1)S(1)}, u32[]{:S(2)}, u32[]{:S(2)}) collective-permute-start(bf16[272,256]{1,0:T(8,128)(2,1)S(1)} %get-tuple-element.37.refs_1_.refs_3_.mine_ref), channel_id=1, source_target_pairs={{0,12},{2,14},{4,0},{6,2},{8,4},{10,6},{12,8},{14,10},{1,13},{3,15... | collective-permute-start | bytes 417800 | tf_op jit(solution)/shard_map/ppermute | solution.py:282
  7.5 7.5 %collective-permute-start.2 = (bf16[272,256]{1,0:T(8,128)(2,1)S(1)}, bf16[272,256]{1,0:T(8,128)(2,1)S(1)}, u32[]{:S(2)}, u32[]{:S(2)}) collective-permute-start(bf16[272,256]{1,0:T(8,128)(2,1)S(1)} %get-tuple-element.37.refs_1_.refs_3_.mine_ref), channel_id=1, source_target_pairs={{0,2},{2,0},{4,6},{6,4},{8,10},{10,8},{12,14},{14,12},{1,3},{3,1},... | collective-permute-start | bytes 417800 | tf_op jit(solution)/shard_map/ppermute | solution.py:279
  9.1 1.2 %copy-start = (bf16[27,128,128]{2,1,0:T(8,128)(2,1)S(1)}, bf16[27,128,128]{2,1,0:T(8,128)(2,1)}, u32[]{:S(2)}) copy-start(bf16[27,128,128]{2,1,0:T(8,128)(2,1)} %w_ref) | copy-start | bytes 2654212
  11.9 6.9 %collective-permute-start.5 = (bf16[272,256]{1,0:T(8,128)(2,1)S(1)}, bf16[272,256]{1,0:T(8,128)(2,1)S(1)}, u32[]{:S(2)}, u32[]{:S(2)}) collective-permute-start(bf16[272,256]{1,0:T(8,128)(2,1)S(1)} %collective-permute-done.refs_1_.refs_3_.before_mine), channel_id=1, source_target_pairs={{0,4},{2,6},{4,8},{6,10},{8,12},{10,14},{12,0},{14,2},{1,5},{3,7},... | collective-permute-start | bytes 417800 | tf_op jit(solution)/shard_map/ppermute | solution.py:282
  11.9 8.6 %collective-permute-start.1 = (bf16[272,256]{1,0:T(8,128)(2,1)S(1)}, bf16[272,256]{1,0:T(8,128)(2,1)S(1)}, u32[]{:S(2)}, u32[]{:S(2)}) collective-permute-start(bf16[272,256]{1,0:T(8,128)(2,1)S(1)} %collective-permute-done.refs_1_.refs_3_.before_mine), channel_id=1, source_target_pairs={{0,2},{2,0},{4,6},{6,4},{8,10},{10,8},{12,14},{14,12},{1,3},{3,1},... | collective-permute-start | bytes 417800 | tf_op jit(solution)/shard_map/ppermute | solution.py:279
  13.7 6.9 %collective-permute-start.4 = (bf16[272,256]{1,0:T(8,128)(2,1)S(1)}, bf16[272,256]{1,0:T(8,128)(2,1)S(1)}, u32[]{:S(2)}, u32[]{:S(2)}) collective-permute-start(bf16[272,256]{1,0:T(8,128)(2,1)S(1)} %collective-permute-done.3.refs_5_.after_mine), channel_id=1, source_target_pairs={{0,2},{2,0},{4,6},{6,4},{8,10},{10,8},{12,14},{14,12},{1,3},{3,1},... | collective-permute-start | bytes 417800 | tf_op jit(solution)/shard_map/ppermute | solution.py:279
  18.8 5.7 %collective-permute-start.6 = (bf16[272,256]{1,0:T(8,128)(2,1)S(1)}, bf16[272,256]{1,0:T(8,128)(2,1)S(1)}, u32[]{:S(2)}, u32[]{:S(2)}) collective-permute-start(bf16[272,256]{1,0:T(8,128)(2,1)S(1)} %collective-permute-done.5.refs_1_), channel_id=1, source_target_pairs={{0,2},{2,0},{4,6},{6,4},{8,10},{10,8},{12,14},{14,12},{1,3},{3,1},... | collective-permute-start | bytes 417800 | tf_op jit(solution)/shard_map/ppermute | solution.py:279
  26.4 2.6 %collective-permute-start.7 = (bf16[18,128,128]{2,1,0:T(8,128)(2,1)S(1)}, bf16[18,128,128]{2,1,0:T(8,128)(2,1)S(1)}, u32[]{:S(2)}, u32[]{:S(2)}) collective-permute-start(bf16[18,128,128]{2,1,0:T(8,128)(2,1)S(1)} %get-tuple-element.54), channel_id=1, source_target_pairs={{0,1},{1,0},{2,3},{3,2},{4,5},{5,4},{6,7},{7,6},{8,9},{9,8},{10,11... | collective-permute-start | bytes 1769480 | tf_op jit(solution)/shard_map/ppermute | solution.py:356
  27.3 1.8 %collective-permute-start.8 = (bf16[9,128,128]{2,1,0:T(8,128)(2,1)S(1)}, bf16[9,128,128]{2,1,0:T(8,128)(2,1)S(1)}, u32[]{:S(2)}, u32[]{:S(2)}) collective-permute-start(bf16[9,128,128]{2,1,0:T(8,128)(2,1)S(1)} %get-tuple-element.60), channel_id=1, source_target_pairs={{0,1},{1,0},{2,3},{3,2},{4,5},{5,4},{6,7},{7,6},{8,9},{9,8},{10,11... | collective-permute-start | bytes 884744 | tf_op jit(solution)/shard_map/ppermute | solution.py:356

commit v20 on v18

--- a/solution.py
+++ b/solution.py
@@ -304,7 +304,6 @@
     )(here, *own_pair, code, w_forward, w_back)
     far, own_conv = lax.optimization_barrier((far, own_conv))
     before_pair = (before, across(before))
-    after_pair = (after, across(after))
     far_pair = (far, across(far))
     def row_sums(name, pairs, strips, borders, sums, groups=(0, 1), final=0, keep=False, laid=()):
         blocks = [block for pair in pairs for block in pair]
@@ -347,6 +346,9 @@
 
     line = [(0, u) for u in range(TILE)]
     sums = row_sums("weight_row_0", (own_pair,), line, [], ())
+    after, centre = lax.optimization_barrier((after, sums[2]))
+    sums = (sums[0], sums[1], centre)
+    after_pair = (after, across(after))
     sums = row_sums("weight_row_1", (before_pair, own_pair), line + [(1, 0)], [(TILE, TILE - 1)], sums)
     sums = row_sums("weight_row_2", (after_pair, own_pair), line + [(1, TILE - 1)], [(0, TILE)], sums)
     sides, sides_sent, *laid = row_sums("weight_row_3", (far_pair, before_pair, after_pair),

time: 30.9 us -> 30.9 us (level)
  no operation moved by 1% of the time
where the time goes in v20:
time: 30.9 us; the launch traced here: 30.7 us
  Pallas kernels  14.2 us (46%)
  starting transfers between devices  12.2 us (39%)
  waiting for transfers between devices  1.83 us (6%)
  between operations  1.38 us (4%)
  local copies, waits for them, and re-layouts  1.17 us (4%)
    pallas_call x5, Pallas kernels, row_sums(): pl.pallas_call(functools.partial(row_kernel, not sums, bool(final), group...  8.74 us
    ppermute x4, starting transfers between devices, across(): return lax.ppermute(block, 'brick', [(i, i ^ 1) for i in range(peers)])  6.22 us
    ppermute x3, starting transfers between devices, along(): lax.ppermute(block, 'brick', [(i, (i + turn * tiles_y) % peers) for i in...  5.33 us
    pallas_call x1, Pallas kernels, whole_scene(): pl.pallas_call(own_kernel, out_shape=(jax.ShapeDtypeStruct((width, rows),...  1.77 us
    ppermute x3, waiting for transfers between devices, along(): lax.ppermute(block, 'brick', [(i, (i + turn * tiles_y) % peers) for i in...  1.53 us
    pallas_call x1, Pallas kernels, whole_scene(): pl.pallas_call(finish_kernel, out_shape=(jax.ShapeDtypeStruct((27, width,...  1.33 us
    unnamed x2, local copies, waits for them, and re-layouts  1.17 us
    pallas_call x1, Pallas kernels, whole_scene(): pl.pallas_call(pack_kernel, out_shape=(jax.ShapeDtypeStruct((rows + CODE_...  1.03 us
  transfers between devices with their start and end apart: 9, of which 3 were waited for; matrix products, arithmetic and copies ran while one was open for 0% of the time, Pallas kernels for 32%

profile of v20, /device:TPU:0, one launch (start us, length us, event | category | flops | bytes accessed | tf_op | source)
XLA Modules:
  0.0 30.7 jit_solution(11672041577207654584)
XLA Ops:
  1.3 1.0 %pack_tile.1 = (bf16[272,256]{1,0:T(8,128)(2,1)S(1)}, f32[256,128]{1,0:T(8,128)S(1)}, f32[27,256]{1,0:T(8,128)S(1)}) custom-call(s32[1]{0:T(128)S(6)} %copy.10.time_ref, bf16[1,256,128]{2,1,0:T(8,128)(2,1)} %feat_hbm.1, bf16[1,256,128]{2,1,0:T(8,128)(2,1)} %cot_hbm.1, s32[27,256]{1,0:T(8,128)} %near_hbm.1, bf16[1,128]{1,0:T(2,128)(2,1)} %cond_hbm.1, ...), custom_call_target="tpu_custom_call" | custom-call | tf_op jit(solution)/shard_map/pack_tile/pallas_call | solution.py:248
  2.3 3.1 %collective-permute-start.3 = (bf16[272,256]{1,0:T(8,128)(2,1)S(1)}, bf16[272,256]{1,0:T(8,128)(2,1)S(1)}, u32[]{:S(2)}, u32[]{:S(2)}) collective-permute-start(bf16[272,256]{1,0:T(8,128)(2,1)S(1)} %get-tuple-element.42.refs_1_.refs_3_.mine_ref), channel_id=1, source_target_pairs={{0,4},{2,6},{4,8},{6,10},{8,12},{10,14},{12,0},{14,2},{1,5},{3,7},... | collective-permute-start | bytes 417800 | tf_op jit(solution)/shard_map/ppermute | solution.py:273
  5.4 1.5 %collective-permute-start.1 = (bf16[272,256]{1,0:T(8,128)(2,1)S(1)}, bf16[272,256]{1,0:T(8,128)(2,1)S(1)}, u32[]{:S(2)}, u32[]{:S(2)}) collective-permute-start(bf16[272,256]{1,0:T(8,128)(2,1)S(1)} %get-tuple-element.42.refs_1_.refs_3_.mine_ref), channel_id=1, source_target_pairs={{0,2},{2,0},{4,6},{6,4},{8,10},{10,8},{12,14},{14,12},{1,3},{3,1},... | collective-permute-start | bytes 417800 | tf_op jit(solution)/shard_map/ppermute | solution.py:270
  6.9 2.2 %collective-permute-start = (bf16[272,256]{1,0:T(8,128)(2,1)S(1)}, bf16[272,256]{1,0:T(8,128)(2,1)S(1)}, u32[]{:S(2)}, u32[]{:S(2)}) collective-permute-start(bf16[272,256]{1,0:T(8,128)(2,1)S(1)} %get-tuple-element.42.refs_1_.refs_3_.mine_ref), channel_id=1, source_target_pairs={{0,12},{2,14},{4,0},{6,2},{8,4},{10,6},{12,8},{14,10},{1,13},{3,15... | collective-permute-start | bytes 417800 | tf_op jit(solution)/shard_map/ppermute | solution.py:273
  9.1 0.0 copy-start
  9.1 1.2 %copy-done = bf16[27,128,128]{2,1,0:T(8,128)(2,1)S(1)} copy-done((bf16[27,128,128]{2,1,0:T(8,128)(2,1)S(1)}, bf16[27,128,128]{2,1,0:T(8,128)(2,1)}, u32[]{:S(2)}) %copy-start) | copy-done | bytes 884760
  10.3 0.4 %turn_weights.1 = (bf16[128,3456]{1,0:T(8,128)(2,1)S(1)}, bf16[128,3456]{1,0:T(8,128)(2,1)S(1)}) custom-call(bf16[27,128,128]{2,1,0:T(8,128)(2,1)S(1)} %copy-done), custom_call_target="tpu_custom_call" | custom-call | flops 200000000 | bytes 3000000 | tf_op jit(solution)/shard_map/turn_weights/pallas_call | solution.py:276
  10.7 0.7 %collective-permute-done.3.refs_1_.refs_3_.before_mine = bf16[272,256]{1,0:T(8,128)(2,1)S(1)} collective-permute-done((bf16[272,256]{1,0:T(8,128)(2,1)S(1)}, bf16[272,256]{1,0:T(8,128)(2,1)S(1)}, u32[]{:S(2)}, u32[]{:S(2)}) %collective-permute-start.3) | collective-permute-done | bytes 139296 | tf_op jit(solution)/shard_map/ppermute | solution.py:273
  11.3 0.0 collective-permute-start.5
  11.3 2.3 %collective-permute-start.4 = (bf16[272,256]{1,0:T(8,128)(2,1)S(1)}, bf16[272,256]{1,0:T(8,128)(2,1)S(1)}, u32[]{:S(2)}, u32[]{:S(2)}) collective-permute-start(bf16[272,256]{1,0:T(8,128)(2,1)S(1)} %collective-permute-done.3.refs_1_.refs_3_.before_mine), channel_id=1, source_target_pairs={{0,2},{2,0},{4,6},{6,4},{8,10},{10,8},{12,14},{14,12},{1,3},{3,1},... | collective-permute-start | bytes 417800 | tf_op jit(solution)/shard_map/ppermute | solution.py:270
  13.7 0.0 collective-permute-done.1.refs_2_.refs_4_.other_ref
  13.7 1.8 %weight_row_0.1 = (f32[1664,128]{1,0:T(8,128)S(1)}, f32[1664,128]{1,0:T(8,128)S(1)}, f32[128,128]{1,0:T(8,128)S(1)}) custom-call(s32[1]{0:T(128)} %bitcast.refs_0_.where_ref, bf16[272,256]{1,0:T(8,128)(2,1)S(1)} %get-tuple-element.42.refs_1_.refs_3_.mine_ref, bf16[272,256]{1,0:T(8,128)(2,1)S(1)} %collective-permute-done.1.refs_2_.refs_4_.other_ref), custom_call_target="tpu_custom_call" | custom-call | flops 2000000000 | bytes 4000000 | tf_op jit(solution)/shard_map/weight_row_0/pallas_call | solution.py:330
  15.4 0.0 collective-permute-done.refs_1_.refs_5_.after_mine
  15.4 0.1 collective-permute-start.2
  15.5 1.8 %voxels_own_row.1 = (f32[128,256]{1,0:T(8,128)S(1)}, f32[128,256]{1,0:T(8,128)S(1)}) custom-call(s32[1]{0:T(128)} %bitcast.refs_0_.where_ref, bf16[272,256]{1,0:T(8,128)(2,1)S(1)} %get-tuple-element.42.refs_1_.refs_3_.mine_ref, bf16[272,256]{1,0:T(8,128)(2,1)S(1)} %collective-permute-done.1.refs_2_.refs_4_.other_ref, ...), custom_call_target="tpu_custom_call" | custom-call | flops 2000000000 | bytes 4000000 | tf_op jit(solution)/shard_map/voxels_own_row/pallas_call | solution.py:289
  17.3 0.9 %collective-permute-done.5.refs_1_ = bf16[272,256]{1,0:T(8,128)(2,1)S(1)} collective-permute-done((bf16[272,256]{1,0:T(8,128)(2,1)S(1)}, bf16[272,256]{1,0:T(8,128)(2,1)S(1)}, u32[]{:S(2)}, u32[]{:S(2)}) %collective-permute-start.5) | collective-permute-done | bytes 139296 | tf_op jit(solution)/shard_map/ppermute | solution.py:273
  18.2 2.3 %collective-permute-start.6 = (bf16[272,256]{1,0:T(8,128)(2,1)S(1)}, bf16[272,256]{1,0:T(8,128)(2,1)S(1)}, u32[]{:S(2)}, u32[]{:S(2)}) collective-permute-start(bf16[272,256]{1,0:T(8,128)(2,1)S(1)} %collective-permute-done.5.refs_1_), channel_id=1, source_target_pairs={{0,2},{2,0},{4,6},{6,4},{8,10},{10,8},{12,14},{14,12},{1,3},{3,1},... | collective-permute-start | bytes 417800 | tf_op jit(solution)/shard_map/ppermute | solution.py:270
  20.5 0.0 collective-permute-done.4.refs_2_.refs_4_.before_other
  20.5 2.1 %weight_row_1.1 = (f32[1664,128]{1,0:T(8,128)S(1)}, f32[1664,128]{1,0:T(8,128)S(1)}, f32[128,128]{1,0:T(8,128)S(1)}) custom-call(s32[1]{0:T(128)} %bitcast.refs_0_.where_ref, bf16[272,256]{1,0:T(8,128)(2,1)S(1)} %collective-permute-done.3.refs_1_.refs_3_.before_mine, bf16[272,256]{1,0:T(8,128)(2,1)S(1)} %collective-permute-done.4.refs_2_.refs_4_.before_other, ...), custom_call_target="tpu_custom_call" | custom-call | flops 2000000000 | bytes 4000000 | tf_op jit(solution)/shard_map/weight_row_1/pallas_call | solution.py:330
  22.7 0.0 collective-permute-done.2.refs_2_.refs_6_.after_other
  22.7 2.1 %weight_row_2.1 = (f32[1664,128]{1,0:T(8,128)S(1)}, f32[1664,128]{1,0:T(8,128)S(1)}, f32[128,128]{1,0:T(8,128)S(1)}) custom-call(s32[1]{0:T(128)} %bitcast.refs_0_.where_ref, bf16[272,256]{1,0:T(8,128)(2,1)S(1)} %collective-permute-done.refs_1_.refs_5_.after_mine, bf16[272,256]{1,0:T(8,128)(2,1)S(1)} %collective-permute-done.2.refs_2_.refs_6_.after_other, ...), custom_call_target="tpu_custom_call" | custom-call | flops 2000000000 | bytes 4000000 | tf_op jit(solution)/shard_map/weight_row_2/pallas_call | solution.py:330
  24.8 0.0 collective-permute-done.6.refs_2_
  24.8 1.9 %weight_row_3.1 = (f32[18,128,128]{2,1,0:T(8,128)S(1)}, bf16[18,128,128]{2,1,0:T(8,128)(2,1)S(1)}, bf16[768,256]{1,0:T(8,128)(2,1)S(1)}, bf16[256,768]{1,0:T(8,128)(2,1)S(1)}, f32[5,16,128]{2,1,0:T(8,128)S(1)}) custom-call(s32[1]{0:T(128)} %bitcast.refs_0_.where_ref, bf16[272,256]{1,0:T(8,128)(2,1)S(1)} %collective-permute-done.5.refs_1_, ...), custom_call_target="tpu_custom_call" | custom-call | flops 2000000000 | bytes 4000000 | tf_op jit(solution)/shard_map/weight_row_3/pallas_call | solution.py:330
  26.7 0.1 collective-permute-start.7
  26.8 0.8 %weight_row_3_middle.1 = (f32[9,128,128]{2,1,0:T(8,128)S(1)}, bf16[9,128,128]{2,1,0:T(8,128)(2,1)S(1)}) custom-call(s32[1]{0:T(128)} %bitcast.refs_0_.where_ref, bf16[768,256]{1,0:T(8,128)(2,1)S(1)} %get-tuple-element.65.refs_1_, bf16[256,768]{1,0:T(8,128)(2,1)S(1)} %get-tuple-element.66.refs_2_, f32[5,16,128]{2,1,0:T(8,128)S(1)} %get-tuple-element.67.refs_3_, ...), custom_call_target="tpu_custom_call" | custom-call | flops 2000000000 | bytes 4000000 | tf_op jit(solution)/shard_map/weight_row_3_middle/pallas_call | solution.py:330
  27.6 0.6 %collective-permute-start.8 = (bf16[9,128,128]{2,1,0:T(8,128)(2,1)S(1)}, bf16[9,128,128]{2,1,0:T(8,128)(2,1)S(1)}, u32[]{:S(2)}, u32[]{:S(2)}) collective-permute-start(bf16[9,128,128]{2,1,0:T(8,128)(2,1)S(1)} %get-tuple-element.70), channel_id=1, source_target_pairs={{0,1},{1,0},{2,3},{3,2},{4,5},{5,4},{6,7},{7,6},{8,9},{9,8},{10,11... | collective-permute-start | bytes 884744 | tf_op jit(solution)/shard_map/ppermute | solution.py:345
  28.2 0.9 %voxel_edges.1 = (bf16[256,128]{1,0:T(8,128)(2,1)S(1)}, bf16[256,128]{1,0:T(8,128)(2,1)S(1)}) custom-call(s32[1]{0:T(128)} %bitcast.refs_0_.where_ref, bf16[272,256]{1,0:T(8,128)(2,1)S(1)} %collective-permute-done.3.refs_1_.refs_3_.before_mine, bf16[272,256]{1,0:T(8,128)(2,1)S(1)} %collective-permute-done.4.refs_2_.refs_4_.before_other, ...), custom_call_target="tpu_custom_call" | custom-call | flops 1000000000 | bytes 4000000 | tf_op jit(solution)/shard_map/voxel_edges/pallas_call | solution.py:362
  29.1 0.3 collective-permute-done.8.middle_sent
  29.4 0.0 collective-permute-done.7.sides_sent
  29.4 1.3 %finish.1 = (f32[27,128,128]{2,1,0:T(8,128)}, bf16[256,128]{1,0:T(8,128)(2,1)}, bf16[256,128]{1,0:T(8,128)(2,1)}) custom-call(f32[18,128,128]{2,1,0:T(8,128)S(1)} %get-tuple-element.63.sides_ref, bf16[18,128,128]{2,1,0:T(8,128)(2,1)S(1)} %collective-permute-done.7.sides_sent, f32[9,128,128]{2,1,0:T(8,128)S(1)} %get-tuple-element.69.middle_ref, ...), custom_call_target="tpu_custom_call" | custom-call | tf_op jit(solution)/shard_map/finish/pallas_call | solution.py:377
Async XLA Ops:
  2.3 9.0 %collective-permute-start.3 = (bf16[272,256]{1,0:T(8,128)(2,1)S(1)}, bf16[272,256]{1,0:T(8,128)(2,1)S(1)}, u32[]{:S(2)}, u32[]{:S(2)}) collective-permute-start(bf16[272,256]{1,0:T(8,128)(2,1)S(1)} %get-tuple-element.42.refs_1_.refs_3_.mine_ref), channel_id=1, source_target_pairs={{0,4},{2,6},{4,8},{6,10},{8,12},{10,14},{12,0},{14,2},{1,5},{3,7},... | collective-permute-start | bytes 417800 | tf_op jit(solution)/shard_map/ppermute | solution.py:273
  5.4 8.3 %collective-permute-start.1 = (bf16[272,256]{1,0:T(8,128)(2,1)S(1)}, bf16[272,256]{1,0:T(8,128)(2,1)S(1)}, u32[]{:S(2)}, u32[]{:S(2)}) collective-permute-start(bf16[272,256]{1,0:T(8,128)(2,1)S(1)} %get-tuple-element.42.refs_1_.refs_3_.mine_ref), channel_id=1, source_target_pairs={{0,2},{2,0},{4,6},{6,4},{8,10},{10,8},{12,14},{14,12},{1,3},{3,1},... | collective-permute-start | bytes 417800 | tf_op jit(solution)/shard_map/ppermute | solution.py:270
  6.9 8.6 %collective-permute-start = (bf16[272,256]{1,0:T(8,128)(2,1)S(1)}, bf16[272,256]{1,0:T(8,128)(2,1)S(1)}, u32[]{:S(2)}, u32[]{:S(2)}) collective-permute-start(bf16[272,256]{1,0:T(8,128)(2,1)S(1)} %get-tuple-element.42.refs_1_.refs_3_.mine_ref), channel_id=1, source_target_pairs={{0,12},{2,14},{4,0},{6,2},{8,4},{10,6},{12,8},{14,10},{1,13},{3,15... | collective-permute-start | bytes 417800 | tf_op jit(solution)/shard_map/ppermute | solution.py:273
  9.1 1.2 %copy-start = (bf16[27,128,128]{2,1,0:T(8,128)(2,1)S(1)}, bf16[27,128,128]{2,1,0:T(8,128)(2,1)}, u32[]{:S(2)}) copy-start(bf16[27,128,128]{2,1,0:T(8,128)(2,1)} %w_ref) | copy-start | bytes 2654212
  11.3 6.9 %collective-permute-start.5 = (bf16[272,256]{1,0:T(8,128)(2,1)S(1)}, bf16[272,256]{1,0:T(8,128)(2,1)S(1)}, u32[]{:S(2)}, u32[]{:S(2)}) collective-permute-start(bf16[272,256]{1,0:T(8,128)(2,1)S(1)} %collective-permute-done.3.refs_1_.refs_3_.before_mine), channel_id=1, source_target_pairs={{0,4},{2,6},{4,8},{6,10},{8,12},{10,14},{12,0},{14,2},{1,5},{3,7},... | collective-permute-start | bytes 417800 | tf_op jit(solution)/shard_map/ppermute | solution.py:273
  11.3 9.2 %collective-permute-start.4 = (bf16[272,256]{1,0:T(8,128)(2,1)S(1)}, bf16[272,256]{1,0:T(8,128)(2,1)S(1)}, u32[]{:S(2)}, u32[]{:S(2)}) collective-permute-start(bf16[272,256]{1,0:T(8,128)(2,1)S(1)} %collective-permute-done.3.refs_1_.refs_3_.before_mine), channel_id=1, source_target_pairs={{0,2},{2,0},{4,6},{6,4},{8,10},{10,8},{12,14},{14,12},{1,3},{3,1},... | collective-permute-start | bytes 417800 | tf_op jit(solution)/shard_map/ppermute | solution.py:270
  15.4 7.2 %collective-permute-start.2 = (bf16[272,256]{1,0:T(8,128)(2,1)S(1)}, bf16[272,256]{1,0:T(8,128)(2,1)S(1)}, u32[]{:S(2)}, u32[]{:S(2)}) collective-permute-start(bf16[272,256]{1,0:T(8,128)(2,1)S(1)} %collective-permute-done.refs_1_.refs_5_.after_mine), channel_id=1, source_target_pairs={{0,2},{2,0},{4,6},{6,4},{8,10},{10,8},{12,14},{14,12},{1,3},{3,1},... | collective-permute-start | bytes 417800 | tf_op jit(solution)/shard_map/ppermute | solution.py:270
  18.2 6.6 %collective-permute-start.6 = (bf16[272,256]{1,0:T(8,128)(2,1)S(1)}, bf16[272,256]{1,0:T(8,128)(2,1)S(1)}, u32[]{:S(2)}, u32[]{:S(2)}) collective-permute-start(bf16[272,256]{1,0:T(8,128)(2,1)S(1)} %collective-permute-done.5.refs_1_), channel_id=1, source_target_pairs={{0,2},{2,0},{4,6},{6,4},{8,10},{10,8},{12,14},{14,12},{1,3},{3,1},... | collective-permute-start | bytes 417800 | tf_op jit(solution)/shard_map/ppermute | solution.py:270
  26.7 2.6 %collective-permute-start.7 = (bf16[18,128,128]{2,1,0:T(8,128)(2,1)S(1)}, bf16[18,128,128]{2,1,0:T(8,128)(2,1)S(1)}, u32[]{:S(2)}, u32[]{:S(2)}) collective-permute-start(bf16[18,128,128]{2,1,0:T(8,128)(2,1)S(1)} %get-tuple-element.64), channel_id=1, source_target_pairs={{0,1},{1,0},{2,3},{3,2},{4,5},{5,4},{6,7},{7,6},{8,9},{9,8},{10,11... | collective-permute-start | bytes 1769480 | tf_op jit(solution)/shard_map/ppermute | solution.py:345
  27.6 1.8 %collective-permute-start.8 = (bf16[9,128,128]{2,1,0:T(8,128)(2,1)S(1)}, bf16[9,128,128]{2,1,0:T(8,128)(2,1)S(1)}, u32[]{:S(2)}, u32[]{:S(2)}) collective-permute-start(bf16[9,128,128]{2,1,0:T(8,128)(2,1)S(1)} %get-tuple-element.70), channel_id=1, source_target_pairs={{0,1},{1,0},{2,3},{3,2},{4,5},{5,4},{6,7},{7,6},{8,9},{9,8},{10,11... | collective-permute-start | bytes 884744 | tf_op jit(solution)/shard_map/ppermute | solution.py:345

commit v21 on v20

--- a/solution.py
+++ b/solution.py
@@ -282,7 +282,9 @@
         cost_estimate=pl.CostEstimate(flops=2 * 10**8, bytes_accessed=3 * 10**6, transcendentals=0),
         name="turn_weights",
     )(w_conv)
-    before, after = along(packed, 1), along(packed, -1)
+    before = along(packed, 1)
+    w_back, later = lax.optimization_barrier((w_back, packed))
+    after = along(later, -1)
     before, w_forward = lax.optimization_barrier((before, w_forward))
     far = along(before, 1)
     own_pair = (packed, across(packed))

time: 30.9 us -> 30 us (0.971)
  starting transfers between devices: 12.2 us -> 10.8 us
  waiting for transfers between devices: 1.83 us -> 2.3 us
    ppermute x4, starting transfers between devices: 6.22 us -> 4.83 us  [across(): return lax.ppermute(block, 'brick', [(i, i ^ 1) for i in range(peers)])]
    ppermute x3, waiting for transfers between devices: 1.53 us -> 1.99 us  [along(): lax.ppermute(block, 'brick', [(i, (i + turn * tiles_y) % peers) for i in...]
  transfers between devices with their start and end apart: 9 -> 9, of which waited for: 3 -> 4; matrix products, arithmetic and copies ran while one was open for 0% -> 0% of each run, Pallas kernels for 32% -> 33%
where the time goes in v21:
time: 30 us; the launch traced here: 29.8 us
  Pallas kernels  14.1 us (47%)
  starting transfers between devices  10.8 us (36%)
  waiting for transfers between devices  2.3 us (8%)
  between operations  1.36 us (5%)
  local copies, waits for them, and re-layouts  1.17 us (4%)
    pallas_call x5, Pallas kernels, row_sums(): pl.pallas_call(functools.partial(row_kernel, not sums, bool(final), group...  8.76 us
    ppermute x3, starting transfers between devices, along(): lax.ppermute(block, 'brick', [(i, (i + turn * tiles_y) % peers) for i in...  5.38 us
    ppermute x4, starting transfers between devices, across(): return lax.ppermute(block, 'brick', [(i, i ^ 1) for i in range(peers)])  4.83 us
    ppermute x3, waiting for transfers between devices, along(): lax.ppermute(block, 'brick', [(i, (i + turn * tiles_y) % peers) for i in...  1.99 us
    pallas_call x1, Pallas kernels, whole_scene(): pl.pallas_call(own_kernel, out_shape=(jax.ShapeDtypeStruct((width, rows),...  1.72 us
    pallas_call x1, Pallas kernels, whole_scene(): pl.pallas_call(finish_kernel, out_shape=(jax.ShapeDtypeStruct((27, width,...  1.33 us
    unnamed x2, local copies, waits for them, and re-layouts  1.17 us
    pallas_call x1, Pallas kernels, whole_scene(): pl.pallas_call(pack_kernel, out_shape=(jax.ShapeDtypeStruct((rows + CODE_...  1.03 us
  transfers between devices with their start and end apart: 9, of which 4 were waited for; matrix products, arithmetic and copies ran while one was open for 0% of the time, Pallas kernels for 33%

profile of v21, /device:TPU:0, one launch (start us, length us, event | category | flops | bytes accessed | tf_op | source)
XLA Modules:
  0.0 29.8 jit_solution(9170580614665344977)
XLA Ops:
  1.3 1.0 %pack_tile.1 = (bf16[272,256]{1,0:T(8,128)(2,1)S(1)}, f32[256,128]{1,0:T(8,128)S(1)}, f32[27,256]{1,0:T(8,128)S(1)}) custom-call(s32[1]{0:T(128)S(6)} %copy.10.time_ref, bf16[1,256,128]{2,1,0:T(8,128)(2,1)} %feat_hbm.1, bf16[1,256,128]{2,1,0:T(8,128)(2,1)} %cot_hbm.1, s32[27,256]{1,0:T(8,128)} %near_hbm.1, bf16[1,128]{1,0:T(2,128)(2,1)} %cond_hbm.1, ...), custom_call_target="tpu_custom_call" | custom-call | tf_op jit(solution)/shard_map/pack_tile/pallas_call | solution.py:248
  2.3 3.1 %collective-permute-start.3 = (bf16[272,256]{1,0:T(8,128)(2,1)S(1)}, bf16[272,256]{1,0:T(8,128)(2,1)S(1)}, u32[]{:S(2)}, u32[]{:S(2)}) collective-permute-start(bf16[272,256]{1,0:T(8,128)(2,1)S(1)} %get-tuple-element.47.refs_1_.refs_3_.mine_ref), channel_id=1, source_target_pairs={{0,4},{2,6},{4,8},{6,10},{8,12},{10,14},{12,0},{14,2},{1,5},{3,7},... | collective-permute-start | bytes 417800 | tf_op jit(solution)/shard_map/ppermute | solution.py:273
  5.4 1.5 %collective-permute-start.1 = (bf16[272,256]{1,0:T(8,128)(2,1)S(1)}, bf16[272,256]{1,0:T(8,128)(2,1)S(1)}, u32[]{:S(2)}, u32[]{:S(2)}) collective-permute-start(bf16[272,256]{1,0:T(8,128)(2,1)S(1)} %get-tuple-element.47.refs_1_.refs_3_.mine_ref), channel_id=1, source_target_pairs={{0,2},{2,0},{4,6},{6,4},{8,10},{10,8},{12,14},{14,12},{1,3},{3,1},... | collective-permute-start | bytes 417800 | tf_op jit(solution)/shard_map/ppermute | solution.py:270
  6.9 0.0 copy-start
  6.9 1.2 %copy-done = bf16[27,128,128]{2,1,0:T(8,128)(2,1)S(1)} copy-done((bf16[27,128,128]{2,1,0:T(8,128)(2,1)S(1)}, bf16[27,128,128]{2,1,0:T(8,128)(2,1)}, u32[]{:S(2)}) %copy-start) | copy-done | bytes 884760
  8.0 0.4 %turn_weights.1 = (bf16[128,3456]{1,0:T(8,128)(2,1)S(1)}, bf16[128,3456]{1,0:T(8,128)(2,1)S(1)}) custom-call(bf16[27,128,128]{2,1,0:T(8,128)(2,1)S(1)} %copy-done), custom_call_target="tpu_custom_call" | custom-call | flops 200000000 | bytes 3000000 | tf_op jit(solution)/shard_map/turn_weights/pallas_call | solution.py:276
  8.4 2.3 %collective-permute-start = (bf16[272,256]{1,0:T(8,128)(2,1)S(1)}, bf16[272,256]{1,0:T(8,128)(2,1)S(1)}, u32[]{:S(2)}, u32[]{:S(2)}) collective-permute-start(bf16[272,256]{1,0:T(8,128)(2,1)S(1)} %get-tuple-element.47.refs_1_.refs_3_.mine_ref), channel_id=1, source_target_pairs={{0,12},{2,14},{4,0},{6,2},{8,4},{10,6},{12,8},{14,10},{1,13},{3,15... | collective-permute-start | bytes 417800 | tf_op jit(solution)/shard_map/ppermute | solution.py:273
  10.7 0.4 %collective-permute-done.3.refs_1_.refs_3_.before_mine = bf16[272,256]{1,0:T(8,128)(2,1)S(1)} collective-permute-done((bf16[272,256]{1,0:T(8,128)(2,1)S(1)}, bf16[272,256]{1,0:T(8,128)(2,1)S(1)}, u32[]{:S(2)}, u32[]{:S(2)}) %collective-permute-start.3) | collective-permute-done | bytes 139296 | tf_op jit(solution)/shard_map/ppermute | solution.py:273
  11.2 0.0 collective-permute-start.5
  11.2 1.5 %collective-permute-start.4 = (bf16[272,256]{1,0:T(8,128)(2,1)S(1)}, bf16[272,256]{1,0:T(8,128)(2,1)S(1)}, u32[]{:S(2)}, u32[]{:S(2)}) collective-permute-start(bf16[272,256]{1,0:T(8,128)(2,1)S(1)} %collective-permute-done.3.refs_1_.refs_3_.before_mine), channel_id=1, source_target_pairs={{0,2},{2,0},{4,6},{6,4},{8,10},{10,8},{12,14},{14,12},{1,3},{3,1},... | collective-permute-start | bytes 417800 | tf_op jit(solution)/shard_map/ppermute | solution.py:270
  12.7 0.0 collective-permute-done.1.refs_2_.refs_4_.other_ref
  12.7 1.8 %weight_row_0.1 = (f32[1664,128]{1,0:T(8,128)S(1)}, f32[1664,128]{1,0:T(8,128)S(1)}, f32[128,128]{1,0:T(8,128)S(1)}) custom-call(s32[1]{0:T(128)} %bitcast.refs_0_.where_ref, bf16[272,256]{1,0:T(8,128)(2,1)S(1)} %get-tuple-element.47.refs_1_.refs_3_.mine_ref, bf16[272,256]{1,0:T(8,128)(2,1)S(1)} %collective-permute-done.1.refs_2_.refs_4_.other_ref), custom_call_target="tpu_custom_call" | custom-call | flops 2000000000 | bytes 4000000 | tf_op jit(solution)/shard_map/weight_row_0/pallas_call | solution.py:332
  14.5 0.3 collective-permute-done.refs_1_.refs_5_.after_mine
  14.8 0.8 %collective-permute-start.2 = (bf16[272,256]{1,0:T(8,128)(2,1)S(1)}, bf16[272,256]{1,0:T(8,128)(2,1)S(1)}, u32[]{:S(2)}, u32[]{:S(2)}) collective-permute-start(bf16[272,256]{1,0:T(8,128)(2,1)S(1)} %collective-permute-done.refs_1_.refs_5_.after_mine), channel_id=1, source_target_pairs={{0,2},{2,0},{4,6},{6,4},{8,10},{10,8},{12,14},{14,12},{1,3},{3,1},... | collective-permute-start | bytes 417800 | tf_op jit(solution)/shard_map/ppermute | solution.py:270
  15.6 1.7 %voxels_own_row.1 = (f32[128,256]{1,0:T(8,128)S(1)}, f32[128,256]{1,0:T(8,128)S(1)}) custom-call(s32[1]{0:T(128)} %bitcast.refs_0_.where_ref, bf16[272,256]{1,0:T(8,128)(2,1)S(1)} %get-tuple-element.47.refs_1_.refs_3_.mine_ref, bf16[272,256]{1,0:T(8,128)(2,1)S(1)} %collective-permute-done.1.refs_2_.refs_4_.other_ref, ...), custom_call_target="tpu_custom_call" | custom-call | flops 2000000000 | bytes 4000000 | tf_op jit(solution)/shard_map/voxels_own_row/pallas_call | solution.py:291
  17.3 1.3 %collective-permute-done.5.refs_1_ = bf16[272,256]{1,0:T(8,128)(2,1)S(1)} collective-permute-done((bf16[272,256]{1,0:T(8,128)(2,1)S(1)}, bf16[272,256]{1,0:T(8,128)(2,1)S(1)}, u32[]{:S(2)}, u32[]{:S(2)}) %collective-permute-start.5) | collective-permute-done | bytes 139296 | tf_op jit(solution)/shard_map/ppermute | solution.py:273
  18.5 1.0 %collective-permute-start.6 = (bf16[272,256]{1,0:T(8,128)(2,1)S(1)}, bf16[272,256]{1,0:T(8,128)(2,1)S(1)}, u32[]{:S(2)}, u32[]{:S(2)}) collective-permute-start(bf16[272,256]{1,0:T(8,128)(2,1)S(1)} %collective-permute-done.5.refs_1_), channel_id=1, source_target_pairs={{0,2},{2,0},{4,6},{6,4},{8,10},{10,8},{12,14},{14,12},{1,3},{3,1},... | collective-permute-start | bytes 417800 | tf_op jit(solution)/shard_map/ppermute | solution.py:270
  19.6 0.0 collective-permute-done.4.refs_2_.refs_4_.before_other
  19.6 2.1 %weight_row_1.1 = (f32[1664,128]{1,0:T(8,128)S(1)}, f32[1664,128]{1,0:T(8,128)S(1)}, f32[128,128]{1,0:T(8,128)S(1)}) custom-call(s32[1]{0:T(128)} %bitcast.refs_0_.where_ref, bf16[272,256]{1,0:T(8,128)(2,1)S(1)} %collective-permute-done.3.refs_1_.refs_3_.before_mine, bf16[272,256]{1,0:T(8,128)(2,1)S(1)} %collective-permute-done.4.refs_2_.refs_4_.before_other, ...), custom_call_target="tpu_custom_call" | custom-call | flops 2000000000 | bytes 4000000 | tf_op jit(solution)/shard_map/weight_row_1/pallas_call | solution.py:332
  21.7 0.0 collective-permute-done.2.refs_2_.refs_6_.after_other
  21.7 2.1 %weight_row_2.1 = (f32[1664,128]{1,0:T(8,128)S(1)}, f32[1664,128]{1,0:T(8,128)S(1)}, f32[128,128]{1,0:T(8,128)S(1)}) custom-call(s32[1]{0:T(128)} %bitcast.refs_0_.where_ref, bf16[272,256]{1,0:T(8,128)(2,1)S(1)} %collective-permute-done.refs_1_.refs_5_.after_mine, bf16[272,256]{1,0:T(8,128)(2,1)S(1)} %collective-permute-done.2.refs_2_.refs_6_.after_other, ...), custom_call_target="tpu_custom_call" | custom-call | flops 2000000000 | bytes 4000000 | tf_op jit(solution)/shard_map/weight_row_2/pallas_call | solution.py:332
  23.9 0.0 collective-permute-done.6.refs_2_
  23.9 1.9 %weight_row_3.1 = (f32[18,128,128]{2,1,0:T(8,128)S(1)}, bf16[18,128,128]{2,1,0:T(8,128)(2,1)S(1)}, bf16[768,256]{1,0:T(8,128)(2,1)S(1)}, bf16[256,768]{1,0:T(8,128)(2,1)S(1)}, f32[5,16,128]{2,1,0:T(8,128)S(1)}) custom-call(s32[1]{0:T(128)} %bitcast.refs_0_.where_ref, bf16[272,256]{1,0:T(8,128)(2,1)S(1)} %collective-permute-done.5.refs_1_, ...), custom_call_target="tpu_custom_call" | custom-call | flops 2000000000 | bytes 4000000 | tf_op jit(solution)/shard_map/weight_row_3/pallas_call | solution.py:332
  25.8 0.1 collective-permute-start.7
  25.9 0.8 %weight_row_3_middle.1 = (f32[9,128,128]{2,1,0:T(8,128)S(1)}, bf16[9,128,128]{2,1,0:T(8,128)(2,1)S(1)}) custom-call(s32[1]{0:T(128)} %bitcast.refs_0_.where_ref, bf16[768,256]{1,0:T(8,128)(2,1)S(1)} %get-tuple-element.69.refs_1_, bf16[256,768]{1,0:T(8,128)(2,1)S(1)} %get-tuple-element.70.refs_2_, f32[5,16,128]{2,1,0:T(8,128)S(1)} %get-tuple-element.71.refs_3_, ...), custom_call_target="tpu_custom_call" | custom-call | flops 2000000000 | bytes 4000000 | tf_op jit(solution)/shard_map/weight_row_3_middle/pallas_call | solution.py:332
  26.7 0.6 %collective-permute-start.8 = (bf16[9,128,128]{2,1,0:T(8,128)(2,1)S(1)}, bf16[9,128,128]{2,1,0:T(8,128)(2,1)S(1)}, u32[]{:S(2)}, u32[]{:S(2)}) collective-permute-start(bf16[9,128,128]{2,1,0:T(8,128)(2,1)S(1)} %get-tuple-element.74), channel_id=1, source_target_pairs={{0,1},{1,0},{2,3},{3,2},{4,5},{5,4},{6,7},{7,6},{8,9},{9,8},{10,11... | collective-permute-start | bytes 884744 | tf_op jit(solution)/shard_map/ppermute | solution.py:347
  27.2 0.9 %voxel_edges.1 = (bf16[256,128]{1,0:T(8,128)(2,1)S(1)}, bf16[256,128]{1,0:T(8,128)(2,1)S(1)}) custom-call(s32[1]{0:T(128)} %bitcast.refs_0_.where_ref, bf16[272,256]{1,0:T(8,128)(2,1)S(1)} %collective-permute-done.3.refs_1_.refs_3_.before_mine, bf16[272,256]{1,0:T(8,128)(2,1)S(1)} %collective-permute-done.4.refs_2_.refs_4_.before_other, ...), custom_call_target="tpu_custom_call" | custom-call | flops 1000000000 | bytes 4000000 | tf_op jit(solution)/shard_map/voxel_edges/pallas_call | solution.py:364
  28.1 0.3 collective-permute-done.8.middle_sent
  28.4 0.0 collective-permute-done.7.sides_sent
  28.4 1.3 %finish.1 = (f32[27,128,128]{2,1,0:T(8,128)}, bf16[256,128]{1,0:T(8,128)(2,1)}, bf16[256,128]{1,0:T(8,128)(2,1)}) custom-call(f32[18,128,128]{2,1,0:T(8,128)S(1)} %get-tuple-element.67.sides_ref, bf16[18,128,128]{2,1,0:T(8,128)(2,1)S(1)} %collective-permute-done.7.sides_sent, f32[9,128,128]{2,1,0:T(8,128)S(1)} %get-tuple-element.73.middle_ref, ...), custom_call_target="tpu_custom_call" | custom-call | tf_op jit(solution)/shard_map/finish/pallas_call | solution.py:379
Async XLA Ops:
  2.3 8.9 %collective-permute-start.3 = (bf16[272,256]{1,0:T(8,128)(2,1)S(1)}, bf16[272,256]{1,0:T(8,128)(2,1)S(1)}, u32[]{:S(2)}, u32[]{:S(2)}) collective-permute-start(bf16[272,256]{1,0:T(8,128)(2,1)S(1)} %get-tuple-element.47.refs_1_.refs_3_.mine_ref), channel_id=1, source_target_pairs={{0,4},{2,6},{4,8},{6,10},{8,12},{10,14},{12,0},{14,2},{1,5},{3,7},... | collective-permute-start | bytes 417800 | tf_op jit(solution)/shard_map/ppermute | solution.py:273
  5.4 7.3 %collective-permute-start.1 = (bf16[272,256]{1,0:T(8,128)(2,1)S(1)}, bf16[272,256]{1,0:T(8,128)(2,1)S(1)}, u32[]{:S(2)}, u32[]{:S(2)}) collective-permute-start(bf16[272,256]{1,0:T(8,128)(2,1)S(1)} %get-tuple-element.47.refs_1_.refs_3_.mine_ref), channel_id=1, source_target_pairs={{0,2},{2,0},{4,6},{6,4},{8,10},{10,8},{12,14},{14,12},{1,3},{3,1},... | collective-permute-start | bytes 417800 | tf_op jit(solution)/shard_map/ppermute | solution.py:270
  6.9 1.2 %copy-start = (bf16[27,128,128]{2,1,0:T(8,128)(2,1)S(1)}, bf16[27,128,128]{2,1,0:T(8,128)(2,1)}, u32[]{:S(2)}) copy-start(bf16[27,128,128]{2,1,0:T(8,128)(2,1)} %w_ref) | copy-start | bytes 2654212
  8.4 6.3 %collective-permute-start = (bf16[272,256]{1,0:T(8,128)(2,1)S(1)}, bf16[272,256]{1,0:T(8,128)(2,1)S(1)}, u32[]{:S(2)}, u32[]{:S(2)}) collective-permute-start(bf16[272,256]{1,0:T(8,128)(2,1)S(1)} %get-tuple-element.47.refs_1_.refs_3_.mine_ref), channel_id=1, source_target_pairs={{0,12},{2,14},{4,0},{6,2},{8,4},{10,6},{12,8},{14,10},{1,13},{3,15... | collective-permute-start | bytes 417800 | tf_op jit(solution)/shard_map/ppermute | solution.py:273
  11.2 7.4 %collective-permute-start.5 = (bf16[272,256]{1,0:T(8,128)(2,1)S(1)}, bf16[272,256]{1,0:T(8,128)(2,1)S(1)}, u32[]{:S(2)}, u32[]{:S(2)}) collective-permute-start(bf16[272,256]{1,0:T(8,128)(2,1)S(1)} %collective-permute-done.3.refs_1_.refs_3_.before_mine), channel_id=1, source_target_pairs={{0,4},{2,6},{4,8},{6,10},{8,12},{10,14},{12,0},{14,2},{1,5},{3,7},... | collective-permute-start | bytes 417800 | tf_op jit(solution)/shard_map/ppermute | solution.py:273
  11.2 8.4 %collective-permute-start.4 = (bf16[272,256]{1,0:T(8,128)(2,1)S(1)}, bf16[272,256]{1,0:T(8,128)(2,1)S(1)}, u32[]{:S(2)}, u32[]{:S(2)}) collective-permute-start(bf16[272,256]{1,0:T(8,128)(2,1)S(1)} %collective-permute-done.3.refs_1_.refs_3_.before_mine), channel_id=1, source_target_pairs={{0,2},{2,0},{4,6},{6,4},{8,10},{10,8},{12,14},{14,12},{1,3},{3,1},... | collective-permute-start | bytes 417800 | tf_op jit(solution)/shard_map/ppermute | solution.py:270
  14.8 6.9 %collective-permute-start.2 = (bf16[272,256]{1,0:T(8,128)(2,1)S(1)}, bf16[272,256]{1,0:T(8,128)(2,1)S(1)}, u32[]{:S(2)}, u32[]{:S(2)}) collective-permute-start(bf16[272,256]{1,0:T(8,128)(2,1)S(1)} %collective-permute-done.refs_1_.refs_5_.after_mine), channel_id=1, source_target_pairs={{0,2},{2,0},{4,6},{6,4},{8,10},{10,8},{12,14},{14,12},{1,3},{3,1},... | collective-permute-start | bytes 417800 | tf_op jit(solution)/shard_map/ppermute | solution.py:270
  18.5 5.3 %collective-permute-start.6 = (bf16[272,256]{1,0:T(8,128)(2,1)S(1)}, bf16[272,256]{1,0:T(8,128)(2,1)S(1)}, u32[]{:S(2)}, u32[]{:S(2)}) collective-permute-start(bf16[272,256]{1,0:T(8,128)(2,1)S(1)} %collective-permute-done.5.refs_1_), channel_id=1, source_target_pairs={{0,2},{2,0},{4,6},{6,4},{8,10},{10,8},{12,14},{14,12},{1,3},{3,1},... | collective-permute-start | bytes 417800 | tf_op jit(solution)/shard_map/ppermute | solution.py:270
  25.8 2.6 %collective-permute-start.7 = (bf16[18,128,128]{2,1,0:T(8,128)(2,1)S(1)}, bf16[18,128,128]{2,1,0:T(8,128)(2,1)S(1)}, u32[]{:S(2)}, u32[]{:S(2)}) collective-permute-start(bf16[18,128,128]{2,1,0:T(8,128)(2,1)S(1)} %get-tuple-element.68), channel_id=1, source_target_pairs={{0,1},{1,0},{2,3},{3,2},{4,5},{5,4},{6,7},{7,6},{8,9},{9,8},{10,11... | collective-permute-start | bytes 1769480 | tf_op jit(solution)/shard_map/ppermute | solution.py:347
  26.7 1.8 %collective-permute-start.8 = (bf16[9,128,128]{2,1,0:T(8,128)(2,1)S(1)}, bf16[9,128,128]{2,1,0:T(8,128)(2,1)S(1)}, u32[]{:S(2)}, u32[]{:S(2)}) collective-permute-start(bf16[9,128,128]{2,1,0:T(8,128)(2,1)S(1)} %get-tuple-element.74), channel_id=1, source_target_pairs={{0,1},{1,0},{2,3},{3,2},{4,5},{5,4},{6,7},{7,6},{8,9},{9,8},{10,11... | collective-permute-start | bytes 884744 | tf_op jit(solution)/shard_map/ppermute | solution.py:347

commit v22 on v21

--- a/solution.py
+++ b/solution.py
@@ -89,7 +89,7 @@
                 to[side][row:row + width, lane:lane + span] = near[:, j * span:(j + 1) * span]
 
 
-def row_kernel(first_stage, final, groups, laid, strips, borders, *refs):
+def row_kernel(first_stage, final, groups, laid, skip_target, strips, borders, *refs):
     refs = list(refs)
     where_ref = refs.pop(0)
     pairs = [] if laid else [(refs.pop(0), refs.pop(0)) for _ in range(1 + max(pair for pair, _ in strips))]
@@ -120,9 +120,23 @@
         found = [(source, k) for k in range(9, HALF)] if 1 in groups and source < TILE else []
         if 0 in groups:
             found += [(target, k) for target, origin in borders if origin == source for k in range(9)]
+        outer = [(target, k) for target, k in found if target == skip_target]
+        found = [(target, k) for target, k in found if target != skip_target]
         if found:
             picks = [(place == codes[target, k:k + 1, :]).astype(jnp.bfloat16) for target, k in found]
             look_up((turned, source * span, span), picks, [(to, k * width, target * span) for target, k in found])
+        if outer:
+            first = skip_target * span
+
+            @pl.when(where_ref[0] < 2)
+            def _(first=first):
+                for near in to:
+                    near[:9 * width, first:first + span] = jnp.zeros((9 * width, span), jnp.bfloat16)
+
+            @pl.when(where_ref[0] >= 2)
+            def _(outer=outer, source=source):
+                picks = [(place == codes[target, k:k + 1, :]).astype(jnp.bfloat16) for target, k in outer]
+                look_up((turned, source * span, span), picks, [(to, k * width, target * span) for target, k in outer])
     extents = ((0, 9, span * targets[0], span * (targets[-1] + 1)), (9, HALF, 0, TILE * span))
     for turn, near in ((0, near_act), (1, near_cot)):
         for group in groups:
@@ -307,7 +321,7 @@
     far, own_conv = lax.optimization_barrier((far, own_conv))
     before_pair = (before, across(before))
     far_pair = (far, across(far))
-    def row_sums(name, pairs, strips, borders, sums, groups=(0, 1), final=0, keep=False, laid=()):
+    def row_sums(name, pairs, strips, borders, sums, groups=(0, 1), final=0, keep=False, laid=(), skip_target=-1):
         blocks = [block for pair in pairs for block in pair]
         if final:
             out_shape = (
@@ -330,7 +344,7 @@
             out_shape += tuple(jax.ShapeDtypeStruct(tuple(shape), kind) for *shape, kind in layout)
         operands = (*blocks, *laid, *sums)
         return pl.pallas_call(
-            functools.partial(row_kernel, not sums, bool(final), groups, bool(laid), strips, borders),
+            functools.partial(row_kernel, not sums, bool(final), groups, bool(laid), skip_target, strips, borders),
             out_shape=out_shape,
             in_specs=[smem] + [vmem] * len(operands),
             out_specs=(vmem,) * len(out_shape),
@@ -351,7 +365,8 @@
     after, centre = lax.optimization_barrier((after, sums[2]))
     sums = (sums[0], sums[1], centre)
     after_pair = (after, across(after))
-    sums = row_sums("weight_row_1", (before_pair, own_pair), line + [(1, 0)], [(TILE, TILE - 1)], sums)
+    sums = row_sums("weight_row_1", (before_pair, own_pair), line + [(1, 0)], [(TILE, TILE - 1)], sums,
+                    skip_target=TILE)
     sums = row_sums("weight_row_2", (after_pair, own_pair), line + [(1, TILE - 1)], [(0, TILE)], sums)
     sides, sides_sent, *laid = row_sums("weight_row_3", (far_pair, before_pair, after_pair),
                                  line + [(1, 0), (2, TILE - 1)], [(TILE, TILE - 1), (0, TILE + 1)],

time: 30 us -> 30.3 us (1.010)
  no operation moved by 1% of the time
where the time goes in v22:
time: 30.3 us; the launch traced here: 30.1 us
  Pallas kernels  14.3 us (47%)
  starting transfers between devices  10.8 us (36%)
  waiting for transfers between devices  2.3 us (8%)
  between operations  1.52 us (5%)
  local copies, waits for them, and re-layouts  1.17 us (4%)
    pallas_call x5, Pallas kernels, row_sums(): pl.pallas_call(functools.partial(row_kernel, not sums, bool(final), group...  8.95 us
    ppermute x3, starting transfers between devices, along(): lax.ppermute(block, 'brick', [(i, (i + turn * tiles_y) % peers) for i in...  5.38 us
    ppermute x4, starting transfers between devices, across(): return lax.ppermute(block, 'brick', [(i, i ^ 1) for i in range(peers)])  4.83 us
    ppermute x3, waiting for transfers between devices, along(): lax.ppermute(block, 'brick', [(i, (i + turn * tiles_y) % peers) for i in...  1.99 us
    pallas_call x1, Pallas kernels, whole_scene(): pl.pallas_call(own_kernel, out_shape=(jax.ShapeDtypeStruct((width, rows),...  1.72 us
    pallas_call x1, Pallas kernels, whole_scene(): pl.pallas_call(finish_kernel, out_shape=(jax.ShapeDtypeStruct((27, width,...  1.33 us
    unnamed x2, local copies, waits for them, and re-layouts  1.17 us
    pallas_call x1, Pallas kernels, whole_scene(): pl.pallas_call(pack_kernel, out_shape=(jax.ShapeDtypeStruct((rows + CODE_...  1.03 us
  transfers between devices with their start and end apart: 9, of which 4 were waited for; matrix products, arithmetic and copies ran while one was open for 0% of the time, Pallas kernels for 33%

profile of v22, /device:TPU:0, one launch (start us, length us, event | category | flops | bytes accessed | tf_op | source)
XLA Modules:
  0.0 30.1 jit_solution(12472895985434242402)
XLA Ops:
  1.3 1.0 %pack_tile.1 = (bf16[272,256]{1,0:T(8,128)(2,1)S(1)}, f32[256,128]{1,0:T(8,128)S(1)}, f32[27,256]{1,0:T(8,128)S(1)}) custom-call(s32[1]{0:T(128)S(6)} %copy.10.time_ref, bf16[1,256,128]{2,1,0:T(8,128)(2,1)} %feat_hbm.1, bf16[1,256,128]{2,1,0:T(8,128)(2,1)} %cot_hbm.1, s32[27,256]{1,0:T(8,128)} %near_hbm.1, bf16[1,128]{1,0:T(2,128)(2,1)} %cond_hbm.1, ...), custom_call_target="tpu_custom_call" | custom-call | tf_op jit(solution)/shard_map/pack_tile/pallas_call | solution.py:262
  2.3 3.1 %collective-permute-start.3 = (bf16[272,256]{1,0:T(8,128)(2,1)S(1)}, bf16[272,256]{1,0:T(8,128)(2,1)S(1)}, u32[]{:S(2)}, u32[]{:S(2)}) collective-permute-start(bf16[272,256]{1,0:T(8,128)(2,1)S(1)} %get-tuple-element.47.refs_1_.refs_3_.mine_ref), channel_id=1, source_target_pairs={{0,4},{2,6},{4,8},{6,10},{8,12},{10,14},{12,0},{14,2},{1,5},{3,7},... | collective-permute-start | bytes 417800 | tf_op jit(solution)/shard_map/ppermute | solution.py:287
  5.4 1.5 %collective-permute-start.1 = (bf16[272,256]{1,0:T(8,128)(2,1)S(1)}, bf16[272,256]{1,0:T(8,128)(2,1)S(1)}, u32[]{:S(2)}, u32[]{:S(2)}) collective-permute-start(bf16[272,256]{1,0:T(8,128)(2,1)S(1)} %get-tuple-element.47.refs_1_.refs_3_.mine_ref), channel_id=1, source_target_pairs={{0,2},{2,0},{4,6},{6,4},{8,10},{10,8},{12,14},{14,12},{1,3},{3,1},... | collective-permute-start | bytes 417800 | tf_op jit(solution)/shard_map/ppermute | solution.py:284
  6.9 0.0 copy-start
  6.9 1.2 %copy-done = bf16[27,128,128]{2,1,0:T(8,128)(2,1)S(1)} copy-done((bf16[27,128,128]{2,1,0:T(8,128)(2,1)S(1)}, bf16[27,128,128]{2,1,0:T(8,128)(2,1)}, u32[]{:S(2)}) %copy-start) | copy-done | bytes 884760
  8.0 0.4 %turn_weights.1 = (bf16[128,3456]{1,0:T(8,128)(2,1)S(1)}, bf16[128,3456]{1,0:T(8,128)(2,1)S(1)}) custom-call(bf16[27,128,128]{2,1,0:T(8,128)(2,1)S(1)} %copy-done), custom_call_target="tpu_custom_call" | custom-call | flops 200000000 | bytes 3000000 | tf_op jit(solution)/shard_map/turn_weights/pallas_call | solution.py:290
  8.4 2.3 %collective-permute-start = (bf16[272,256]{1,0:T(8,128)(2,1)S(1)}, bf16[272,256]{1,0:T(8,128)(2,1)S(1)}, u32[]{:S(2)}, u32[]{:S(2)}) collective-permute-start(bf16[272,256]{1,0:T(8,128)(2,1)S(1)} %get-tuple-element.47.refs_1_.refs_3_.mine_ref), channel_id=1, source_target_pairs={{0,12},{2,14},{4,0},{6,2},{8,4},{10,6},{12,8},{14,10},{1,13},{3,15... | collective-permute-start | bytes 417800 | tf_op jit(solution)/shard_map/ppermute | solution.py:287
  10.7 0.4 %collective-permute-done.3.refs_1_.refs_3_.before_mine = bf16[272,256]{1,0:T(8,128)(2,1)S(1)} collective-permute-done((bf16[272,256]{1,0:T(8,128)(2,1)S(1)}, bf16[272,256]{1,0:T(8,128)(2,1)S(1)}, u32[]{:S(2)}, u32[]{:S(2)}) %collective-permute-start.3) | collective-permute-done | bytes 139296 | tf_op jit(solution)/shard_map/ppermute | solution.py:287
  11.2 0.0 collective-permute-start.5
  11.2 1.5 %collective-permute-start.4 = (bf16[272,256]{1,0:T(8,128)(2,1)S(1)}, bf16[272,256]{1,0:T(8,128)(2,1)S(1)}, u32[]{:S(2)}, u32[]{:S(2)}) collective-permute-start(bf16[272,256]{1,0:T(8,128)(2,1)S(1)} %collective-permute-done.3.refs_1_.refs_3_.before_mine), channel_id=1, source_target_pairs={{0,2},{2,0},{4,6},{6,4},{8,10},{10,8},{12,14},{14,12},{1,3},{3,1},... | collective-permute-start | bytes 417800 | tf_op jit(solution)/shard_map/ppermute | solution.py:284
  12.7 0.0 collective-permute-done.1.refs_2_.refs_4_.other_ref
  12.7 1.8 %weight_row_0.1 = (f32[1664,128]{1,0:T(8,128)S(1)}, f32[1664,128]{1,0:T(8,128)S(1)}, f32[128,128]{1,0:T(8,128)S(1)}) custom-call(s32[1]{0:T(128)} %bitcast.refs_0_.where_ref, bf16[272,256]{1,0:T(8,128)(2,1)S(1)} %get-tuple-element.47.refs_1_.refs_3_.mine_ref, bf16[272,256]{1,0:T(8,128)(2,1)S(1)} %collective-permute-done.1.refs_2_.refs_4_.other_ref), custom_call_target="tpu_custom_call" | custom-call | flops 2000000000 | bytes 4000000 | tf_op jit(solution)/shard_map/weight_row_0/pallas_call | solution.py:346
  14.5 0.3 collective-permute-done.refs_1_.refs_5_.after_mine
  14.8 0.8 %collective-permute-start.2 = (bf16[272,256]{1,0:T(8,128)(2,1)S(1)}, bf16[272,256]{1,0:T(8,128)(2,1)S(1)}, u32[]{:S(2)}, u32[]{:S(2)}) collective-permute-start(bf16[272,256]{1,0:T(8,128)(2,1)S(1)} %collective-permute-done.refs_1_.refs_5_.after_mine), channel_id=1, source_target_pairs={{0,2},{2,0},{4,6},{6,4},{8,10},{10,8},{12,14},{14,12},{1,3},{3,1},... | collective-permute-start | bytes 417800 | tf_op jit(solution)/shard_map/ppermute | solution.py:284
  15.6 1.7 %voxels_own_row.1 = (f32[128,256]{1,0:T(8,128)S(1)}, f32[128,256]{1,0:T(8,128)S(1)}) custom-call(s32[1]{0:T(128)} %bitcast.refs_0_.where_ref, bf16[272,256]{1,0:T(8,128)(2,1)S(1)} %get-tuple-element.47.refs_1_.refs_3_.mine_ref, bf16[272,256]{1,0:T(8,128)(2,1)S(1)} %collective-permute-done.1.refs_2_.refs_4_.other_ref, ...), custom_call_target="tpu_custom_call" | custom-call | flops 2000000000 | bytes 4000000 | tf_op jit(solution)/shard_map/voxels_own_row/pallas_call | solution.py:305
  17.3 1.3 %collective-permute-done.5.refs_1_ = bf16[272,256]{1,0:T(8,128)(2,1)S(1)} collective-permute-done((bf16[272,256]{1,0:T(8,128)(2,1)S(1)}, bf16[272,256]{1,0:T(8,128)(2,1)S(1)}, u32[]{:S(2)}, u32[]{:S(2)}) %collective-permute-start.5) | collective-permute-done | bytes 139296 | tf_op jit(solution)/shard_map/ppermute | solution.py:287
  18.5 1.0 %collective-permute-start.6 = (bf16[272,256]{1,0:T(8,128)(2,1)S(1)}, bf16[272,256]{1,0:T(8,128)(2,1)S(1)}, u32[]{:S(2)}, u32[]{:S(2)}) collective-permute-start(bf16[272,256]{1,0:T(8,128)(2,1)S(1)} %collective-permute-done.5.refs_1_), channel_id=1, source_target_pairs={{0,2},{2,0},{4,6},{6,4},{8,10},{10,8},{12,14},{14,12},{1,3},{3,1},... | collective-permute-start | bytes 417800 | tf_op jit(solution)/shard_map/ppermute | solution.py:284
  19.6 0.0 collective-permute-done.4.refs_2_.refs_4_.before_other
  19.6 2.4 %weight_row_1.1 = (f32[1664,128]{1,0:T(8,128)S(1)}, f32[1664,128]{1,0:T(8,128)S(1)}, f32[128,128]{1,0:T(8,128)S(1)}) custom-call(s32[1]{0:T(128)} %bitcast.refs_0_.where_ref, bf16[272,256]{1,0:T(8,128)(2,1)S(1)} %collective-permute-done.3.refs_1_.refs_3_.before_mine, bf16[272,256]{1,0:T(8,128)(2,1)S(1)} %collective-permute-done.4.refs_2_.refs_4_.before_other, ...), custom_call_target="tpu_custom_call" | custom-call | flops 2000000000 | bytes 4000000 | tf_op jit(solution)/shard_map/weight_row_1/pallas_call | solution.py:346
  21.9 0.0 collective-permute-done.2.refs_2_.refs_6_.after_other
  21.9 2.1 %weight_row_2.1 = (f32[1664,128]{1,0:T(8,128)S(1)}, f32[1664,128]{1,0:T(8,128)S(1)}, f32[128,128]{1,0:T(8,128)S(1)}) custom-call(s32[1]{0:T(128)} %bitcast.refs_0_.where_ref, bf16[272,256]{1,0:T(8,128)(2,1)S(1)} %collective-permute-done.refs_1_.refs_5_.after_mine, bf16[272,256]{1,0:T(8,128)(2,1)S(1)} %collective-permute-done.2.refs_2_.refs_6_.after_other, ...), custom_call_target="tpu_custom_call" | custom-call | flops 2000000000 | bytes 4000000 | tf_op jit(solution)/shard_map/weight_row_2/pallas_call | solution.py:346
  24.1 0.0 collective-permute-done.6.refs_2_
  24.1 1.9 %weight_row_3.1 = (f32[18,128,128]{2,1,0:T(8,128)S(1)}, bf16[18,128,128]{2,1,0:T(8,128)(2,1)S(1)}, bf16[768,256]{1,0:T(8,128)(2,1)S(1)}, bf16[256,768]{1,0:T(8,128)(2,1)S(1)}, f32[5,16,128]{2,1,0:T(8,128)S(1)}) custom-call(s32[1]{0:T(128)} %bitcast.refs_0_.where_ref, bf16[272,256]{1,0:T(8,128)(2,1)S(1)} %collective-permute-done.5.refs_1_, ...), custom_call_target="tpu_custom_call" | custom-call | flops 2000000000 | bytes 4000000 | tf_op jit(solution)/shard_map/weight_row_3/pallas_call | solution.py:346
  26.0 0.1 collective-permute-start.7
  26.1 0.8 %weight_row_3_middle.1 = (f32[9,128,128]{2,1,0:T(8,128)S(1)}, bf16[9,128,128]{2,1,0:T(8,128)(2,1)S(1)}) custom-call(s32[1]{0:T(128)} %bitcast.refs_0_.where_ref, bf16[768,256]{1,0:T(8,128)(2,1)S(1)} %get-tuple-element.69.refs_1_, bf16[256,768]{1,0:T(8,128)(2,1)S(1)} %get-tuple-element.70.refs_2_, f32[5,16,128]{2,1,0:T(8,128)S(1)} %get-tuple-element.71.refs_3_, ...), custom_call_target="tpu_custom_call" | custom-call | flops 2000000000 | bytes 4000000 | tf_op jit(solution)/shard_map/weight_row_3_middle/pallas_call | solution.py:346
  26.9 0.6 %collective-permute-start.8 = (bf16[9,128,128]{2,1,0:T(8,128)(2,1)S(1)}, bf16[9,128,128]{2,1,0:T(8,128)(2,1)S(1)}, u32[]{:S(2)}, u32[]{:S(2)}) collective-permute-start(bf16[9,128,128]{2,1,0:T(8,128)(2,1)S(1)} %get-tuple-element.74), channel_id=1, source_target_pairs={{0,1},{1,0},{2,3},{3,2},{4,5},{5,4},{6,7},{7,6},{8,9},{9,8},{10,11... | collective-permute-start | bytes 884744 | tf_op jit(solution)/shard_map/ppermute | solution.py:361
  27.4 0.9 %voxel_edges.1 = (bf16[256,128]{1,0:T(8,128)(2,1)S(1)}, bf16[256,128]{1,0:T(8,128)(2,1)S(1)}) custom-call(s32[1]{0:T(128)} %bitcast.refs_0_.where_ref, bf16[272,256]{1,0:T(8,128)(2,1)S(1)} %collective-permute-done.3.refs_1_.refs_3_.before_mine, bf16[272,256]{1,0:T(8,128)(2,1)S(1)} %collective-permute-done.4.refs_2_.refs_4_.before_other, ...), custom_call_target="tpu_custom_call" | custom-call | flops 1000000000 | bytes 4000000 | tf_op jit(solution)/shard_map/voxel_edges/pallas_call | solution.py:379
  28.3 0.3 collective-permute-done.8.middle_sent
  28.6 0.0 collective-permute-done.7.sides_sent
  28.6 1.3 %finish.1 = (f32[27,128,128]{2,1,0:T(8,128)}, bf16[256,128]{1,0:T(8,128)(2,1)}, bf16[256,128]{1,0:T(8,128)(2,1)}) custom-call(f32[18,128,128]{2,1,0:T(8,128)S(1)} %get-tuple-element.67.sides_ref, bf16[18,128,128]{2,1,0:T(8,128)(2,1)S(1)} %collective-permute-done.7.sides_sent, f32[9,128,128]{2,1,0:T(8,128)S(1)} %get-tuple-element.73.middle_ref, ...), custom_call_target="tpu_custom_call" | custom-call | tf_op jit(solution)/shard_map/finish/pallas_call | solution.py:394
Async XLA Ops:
  2.3 8.9 %collective-permute-start.3 = (bf16[272,256]{1,0:T(8,128)(2,1)S(1)}, bf16[272,256]{1,0:T(8,128)(2,1)S(1)}, u32[]{:S(2)}, u32[]{:S(2)}) collective-permute-start(bf16[272,256]{1,0:T(8,128)(2,1)S(1)} %get-tuple-element.47.refs_1_.refs_3_.mine_ref), channel_id=1, source_target_pairs={{0,4},{2,6},{4,8},{6,10},{8,12},{10,14},{12,0},{14,2},{1,5},{3,7},... | collective-permute-start | bytes 417800 | tf_op jit(solution)/shard_map/ppermute | solution.py:287
  5.4 7.3 %collective-permute-start.1 = (bf16[272,256]{1,0:T(8,128)(2,1)S(1)}, bf16[272,256]{1,0:T(8,128)(2,1)S(1)}, u32[]{:S(2)}, u32[]{:S(2)}) collective-permute-start(bf16[272,256]{1,0:T(8,128)(2,1)S(1)} %get-tuple-element.47.refs_1_.refs_3_.mine_ref), channel_id=1, source_target_pairs={{0,2},{2,0},{4,6},{6,4},{8,10},{10,8},{12,14},{14,12},{1,3},{3,1},... | collective-permute-start | bytes 417800 | tf_op jit(solution)/shard_map/ppermute | solution.py:284
  6.9 1.2 %copy-start = (bf16[27,128,128]{2,1,0:T(8,128)(2,1)S(1)}, bf16[27,128,128]{2,1,0:T(8,128)(2,1)}, u32[]{:S(2)}) copy-start(bf16[27,128,128]{2,1,0:T(8,128)(2,1)} %w_ref) | copy-start | bytes 2654212
  8.4 6.3 %collective-permute-start = (bf16[272,256]{1,0:T(8,128)(2,1)S(1)}, bf16[272,256]{1,0:T(8,128)(2,1)S(1)}, u32[]{:S(2)}, u32[]{:S(2)}) collective-permute-start(bf16[272,256]{1,0:T(8,128)(2,1)S(1)} %get-tuple-element.47.refs_1_.refs_3_.mine_ref), channel_id=1, source_target_pairs={{0,12},{2,14},{4,0},{6,2},{8,4},{10,6},{12,8},{14,10},{1,13},{3,15... | collective-permute-start | bytes 417800 | tf_op jit(solution)/shard_map/ppermute | solution.py:287
  11.2 7.4 %collective-permute-start.5 = (bf16[272,256]{1,0:T(8,128)(2,1)S(1)}, bf16[272,256]{1,0:T(8,128)(2,1)S(1)}, u32[]{:S(2)}, u32[]{:S(2)}) collective-permute-start(bf16[272,256]{1,0:T(8,128)(2,1)S(1)} %collective-permute-done.3.refs_1_.refs_3_.before_mine), channel_id=1, source_target_pairs={{0,4},{2,6},{4,8},{6,10},{8,12},{10,14},{12,0},{14,2},{1,5},{3,7},... | collective-permute-start | bytes 417800 | tf_op jit(solution)/shard_map/ppermute | solution.py:287
  11.2 8.4 %collective-permute-start.4 = (bf16[272,256]{1,0:T(8,128)(2,1)S(1)}, bf16[272,256]{1,0:T(8,128)(2,1)S(1)}, u32[]{:S(2)}, u32[]{:S(2)}) collective-permute-start(bf16[272,256]{1,0:T(8,128)(2,1)S(1)} %collective-permute-done.3.refs_1_.refs_3_.before_mine), channel_id=1, source_target_pairs={{0,2},{2,0},{4,6},{6,4},{8,10},{10,8},{12,14},{14,12},{1,3},{3,1},... | collective-permute-start | bytes 417800 | tf_op jit(solution)/shard_map/ppermute | solution.py:284
  14.8 7.1 %collective-permute-start.2 = (bf16[272,256]{1,0:T(8,128)(2,1)S(1)}, bf16[272,256]{1,0:T(8,128)(2,1)S(1)}, u32[]{:S(2)}, u32[]{:S(2)}) collective-permute-start(bf16[272,256]{1,0:T(8,128)(2,1)S(1)} %collective-permute-done.refs_1_.refs_5_.after_mine), channel_id=1, source_target_pairs={{0,2},{2,0},{4,6},{6,4},{8,10},{10,8},{12,14},{14,12},{1,3},{3,1},... | collective-permute-start | bytes 417800 | tf_op jit(solution)/shard_map/ppermute | solution.py:284
  18.5 5.5 %collective-permute-start.6 = (bf16[272,256]{1,0:T(8,128)(2,1)S(1)}, bf16[272,256]{1,0:T(8,128)(2,1)S(1)}, u32[]{:S(2)}, u32[]{:S(2)}) collective-permute-start(bf16[272,256]{1,0:T(8,128)(2,1)S(1)} %collective-permute-done.5.refs_1_), channel_id=1, source_target_pairs={{0,2},{2,0},{4,6},{6,4},{8,10},{10,8},{12,14},{14,12},{1,3},{3,1},... | collective-permute-start | bytes 417800 | tf_op jit(solution)/shard_map/ppermute | solution.py:284
  26.0 2.6 %collective-permute-start.7 = (bf16[18,128,128]{2,1,0:T(8,128)(2,1)S(1)}, bf16[18,128,128]{2,1,0:T(8,128)(2,1)S(1)}, u32[]{:S(2)}, u32[]{:S(2)}) collective-permute-start(bf16[18,128,128]{2,1,0:T(8,128)(2,1)S(1)} %get-tuple-element.68), channel_id=1, source_target_pairs={{0,1},{1,0},{2,3},{3,2},{4,5},{5,4},{6,7},{7,6},{8,9},{9,8},{10,11... | collective-permute-start | bytes 1769480 | tf_op jit(solution)/shard_map/ppermute | solution.py:361
  26.9 1.8 %collective-permute-start.8 = (bf16[9,128,128]{2,1,0:T(8,128)(2,1)S(1)}, bf16[9,128,128]{2,1,0:T(8,128)(2,1)S(1)}, u32[]{:S(2)}, u32[]{:S(2)}) collective-permute-start(bf16[9,128,128]{2,1,0:T(8,128)(2,1)S(1)} %get-tuple-element.74), channel_id=1, source_target_pairs={{0,1},{1,0},{2,3},{3,2},{4,5},{5,4},{6,7},{7,6},{8,9},{9,8},{10,11... | collective-permute-start | bytes 884744 | tf_op jit(solution)/shard_map/ppermute | solution.py:361

commit v23 on v21

--- a/solution.py
+++ b/solution.py
@@ -94,8 +94,9 @@
     where_ref = refs.pop(0)
     pairs = [] if laid else [(refs.pop(0), refs.pop(0)) for _ in range(1 + max(pair for pair, _ in strips))]
     given = [refs.pop(0) for _ in range(3)] if laid else []
-    before = [refs.pop(0) for _ in range(0 if first_stage else 3)]
-    outs = [refs.pop(0) for _ in range(2 if final else 3)]
+    before = {} if first_stage else {group: [refs.pop(0) for _ in range(2 + group)] for group in groups}
+    outs = [refs.pop(0) for _ in range(2)] if final else {
+        group: [refs.pop(0) for _ in range(2 + group)] for group in groups}
     ground, turned, codes = given or [refs.pop(0) for _ in range(3)]
     near_act, near_cot = refs
     width = ground.shape[1] // 2
@@ -130,9 +131,9 @@
             other = ground[first:last, (1 - turn) * width:(2 - turn) * width]
             value = jnp.dot(near[start * width:stop * width, first:last], other, preferred_element_type=jnp.float32)
             if not first_stage:
-                value = value + before[turn][start * width:stop * width, :]
+                value = value + before[group][turn][...]
             if not final:
-                outs[turn][start * width:stop * width, :] = value
+                outs[group][turn][...] = value
                 continue
             for k in range(start, stop):
                 one = value[(k - start) * width:(k - start + 1) * width, :]
@@ -145,12 +146,12 @@
     if 1 in groups:
         centre = jnp.dot(turned[:width, :TILE * span], ground[:TILE * span, width:], preferred_element_type=jnp.float32)
         if not first_stage:
-            centre = centre + before[2][...]
+            centre = centre + before[1][2][...]
         if final:
             outs[0][HALF - 9] = centre
             outs[1][HALF - 9] = centre.astype(jnp.bfloat16)
         else:
-            outs[2][...] = centre
+            outs[1][2][...] = centre
 
 
 def turn_kernel(w_ref, forward_ref, back_ref):
@@ -304,36 +305,34 @@
         cost_estimate=pl.CostEstimate(flops=2 * 10**9, bytes_accessed=4 * 10**6, transcendentals=0),
         name="voxels_own_row",
     )(here, *own_pair, code, w_forward, w_back)
-    far, own_conv = lax.optimization_barrier((far, own_conv))
     before_pair = (before, across(before))
-    far_pair = (far, across(far))
     def row_sums(name, pairs, strips, borders, sums, groups=(0, 1), final=0, keep=False, laid=()):
         blocks = [block for pair in pairs for block in pair]
         if final:
-            out_shape = (
+            out_shape = [
                 jax.ShapeDtypeStruct((final, width, width), jnp.float32),
                 jax.ShapeDtypeStruct((final, width, width), jnp.bfloat16),
-            )
+            ]
         else:
-            out_shape = (
-                jax.ShapeDtypeStruct((HALF * width, width), jnp.float32),
-                jax.ShapeDtypeStruct((HALF * width, width), jnp.float32),
-                jax.ShapeDtypeStruct((width, width), jnp.float32),
-            )
+            lengths = {0: (9, 9), 1: (HALF - 9, HALF - 9, 1)}
+            out_shape = [jax.ShapeDtypeStruct((length * width, width), jnp.float32)
+                         for group in groups for length in lengths[group]]
         layout = (
             ((TILE + 2) * span, 2 * width, jnp.bfloat16),
             (2 * width, (TILE + 2) * span, jnp.bfloat16),
             (TILE + 1, CODE_ROWS, span, jnp.float32),
         )
         scratch = [] if laid or keep else [pltpu.VMEM(tuple(shape), kind) for *shape, kind in layout]
+        results = len(out_shape)
         if keep:
-            out_shape += tuple(jax.ShapeDtypeStruct(tuple(shape), kind) for *shape, kind in layout)
-        operands = (*blocks, *laid, *sums)
-        return pl.pallas_call(
+            out_shape += [jax.ShapeDtypeStruct(tuple(shape), kind) for *shape, kind in layout]
+        earlier = [part for group in groups for part in sums[group]] if sums else []
+        operands = (*blocks, *laid, *earlier)
+        out = pl.pallas_call(
             functools.partial(row_kernel, not sums, bool(final), groups, bool(laid), strips, borders),
             out_shape=out_shape,
             in_specs=[smem] + [vmem] * len(operands),
-            out_specs=(vmem,) * len(out_shape),
+            out_specs=[vmem] * len(out_shape),
             scratch_shapes=scratch + [
                 pltpu.VMEM((HALF * width, (TILE + 1) * span), jnp.bfloat16),
                 pltpu.VMEM((HALF * width, (TILE + 1) * span), jnp.bfloat16),
@@ -342,24 +341,39 @@
             cost_estimate=pl.CostEstimate(flops=2 * 10**9, bytes_accessed=4 * 10**6, transcendentals=0),
             name=name,
         )(here, *operands)
+        if final:
+            return out
+        totals, parts = dict(sums), list(out[:results])
+        for group in groups:
+            totals[group] = tuple(parts.pop(0) for _ in range(2 + group))
+        return totals, out[results:]
 
     def swapped(block):
         return lax.ppermute(block, "batch", [(0, 1), (1, 0)])
 
     line = [(0, u) for u in range(TILE)]
-    sums = row_sums("weight_row_0", (own_pair,), line, [], ())
-    after, centre = lax.optimization_barrier((after, sums[2]))
-    sums = (sums[0], sums[1], centre)
+    sums, _ = row_sums("weight_row_0", (own_pair,), line, [], {})
+    low, high, centre = sums[1]
+    after, centre = lax.optimization_barrier((after, centre))
+    sums[1] = (low, high, centre)
     after_pair = (after, across(after))
-    sums = row_sums("weight_row_1", (before_pair, own_pair), line + [(1, 0)], [(TILE, TILE - 1)], sums)
-    sums = row_sums("weight_row_2", (after_pair, own_pair), line + [(1, TILE - 1)], [(0, TILE)], sums)
+    border = [(TILE, TILE - 1)]
+    sums, laid = row_sums("weight_row_1_middle", (before_pair, own_pair), line + [(1, 0)], border, sums,
+                          groups=(1,), keep=True)
+    low, high, centre = sums[1]
+    far, own_conv, centre = lax.optimization_barrier((far, own_conv, centre))
+    sums[1] = (low, high, centre)
+    far_pair = (far, across(far))
+    sums, _ = row_sums("weight_row_1", (), line + [(1, 0)], border, sums, groups=(0,), laid=laid)
+    sums, _ = row_sums("weight_row_2", (after_pair, own_pair), line + [(1, TILE - 1)], [(0, TILE)], sums)
     sides, sides_sent, *laid = row_sums("weight_row_3", (far_pair, before_pair, after_pair),
-                                 line + [(1, 0), (2, TILE - 1)], [(TILE, TILE - 1), (0, TILE + 1)],
-                                 sums, groups=(0,), final=18, keep=True)
+                                        line + [(1, 0), (2, TILE - 1)], [(TILE, TILE - 1), (0, TILE + 1)],
+                                        sums, groups=(0,), final=18, keep=True)
     sides_other = swapped(sides_sent)
-    centre, sides = lax.optimization_barrier((sums[2], sides))
-    middle, middle_sent = row_sums("weight_row_3_middle", (), line, [], (sums[0], sums[1], centre),
-                                   groups=(1,), final=9, laid=laid)
+    low, high, centre = sums[1]
+    centre, sides = lax.optimization_barrier((centre, sides))
+    sums[1] = (low, high, centre)
+    middle, middle_sent = row_sums("weight_row_3_middle", (), line, [], sums, groups=(1,), final=9, laid=laid)
     middle_other = swapped(middle_sent)
     conv_out, feature_grad = pl.pallas_call(
         edge_kernel,

time: 30 us -> 30.7 us (1.023)
  waiting for transfers between devices: 2.3 us -> 3.36 us
  starting transfers between devices: 10.8 us -> 10.4 us
    ppermute x4, waiting for transfers between devices: 0.01 us -> 0.97 us  [across(): return lax.ppermute(block, 'brick', [(i, i ^ 1) for i in range(peers)])]
    ppermute x4, starting transfers between devices: 4.83 us -> 4.35 us  [across(): return lax.ppermute(block, 'brick', [(i, i ^ 1) for i in range(peers)])]
    pallas_call x5 -> x6, Pallas kernels: 8.76 us -> 8.9 us  [row_sums(): pl.pallas_call(functools.partial(row_kernel, not sums, bool(final), group...]
  transfers between devices with their start and end apart: 9 -> 9, of which waited for: 4 -> 5; matrix products, arithmetic and copies ran while one was open for 0% -> 0% of each run, Pallas kernels for 33% -> 33%
where the time goes in v23:
time: 30.7 us; the launch traced here: 30.5 us
  Pallas kernels  14.2 us (46%)
  starting transfers between devices  10.4 us (34%)
  waiting for transfers between devices  3.36 us (11%)
  between operations  1.37 us (4%)
  local copies, waits for them, and re-layouts  1.17 us (4%)
    pallas_call x6, Pallas kernels, row_sums(): pl.pallas_call(functools.partial(row_kernel, not sums, bool(final), group...  8.9 us
    ppermute x3, starting transfers between devices, along(): lax.ppermute(block, 'brick', [(i, (i + turn * tiles_y) % peers) for i in...  5.38 us
    ppermute x4, starting transfers between devices, across(): return lax.ppermute(block, 'brick', [(i, i ^ 1) for i in range(peers)])  4.35 us
    ppermute x3, waiting for transfers between devices, along(): lax.ppermute(block, 'brick', [(i, (i + turn * tiles_y) % peers) for i in...  2.09 us
    pallas_call x1, Pallas kernels, whole_scene(): pl.pallas_call(own_kernel, out_shape=(jax.ShapeDtypeStruct((width, rows),...  1.72 us
    pallas_call x1, Pallas kernels, whole_scene(): pl.pallas_call(finish_kernel, out_shape=(jax.ShapeDtypeStruct((27, width,...  1.33 us
    unnamed x2, local copies, waits for them, and re-layouts  1.17 us
    pallas_call x1, Pallas kernels, whole_scene(): pl.pallas_call(pack_kernel, out_shape=(jax.ShapeDtypeStruct((rows + CODE_...  1.03 us
  transfers between devices with their start and end apart: 9, of which 5 were waited for; matrix products, arithmetic and copies ran while one was open for 0% of the time, Pallas kernels for 33%

profile of v23, /device:TPU:0, one launch (start us, length us, event | category | flops | bytes accessed | tf_op | source)
XLA Modules:
  0.0 30.5 jit_solution(18089974917029665294)
XLA Ops:
  1.3 1.0 %pack_tile.1 = (bf16[272,256]{1,0:T(8,128)(2,1)S(1)}, f32[256,128]{1,0:T(8,128)S(1)}, f32[27,256]{1,0:T(8,128)S(1)}) custom-call(s32[1]{0:T(128)S(6)} %copy.10.time_ref, bf16[1,256,128]{2,1,0:T(8,128)(2,1)} %feat_hbm.1, bf16[1,256,128]{2,1,0:T(8,128)(2,1)} %cot_hbm.1, s32[27,256]{1,0:T(8,128)} %near_hbm.1, bf16[1,128]{1,0:T(2,128)(2,1)} %cond_hbm.1, ...), custom_call_target="tpu_custom_call" | custom-call | tf_op jit(solution)/shard_map/pack_tile/pallas_call | solution.py:249
  2.3 3.1 %collective-permute-start.3 = (bf16[272,256]{1,0:T(8,128)(2,1)S(1)}, bf16[272,256]{1,0:T(8,128)(2,1)S(1)}, u32[]{:S(2)}, u32[]{:S(2)}) collective-permute-start(bf16[272,256]{1,0:T(8,128)(2,1)S(1)} %get-tuple-element.57.refs_1_.refs_3_.mine_ref), channel_id=1, source_target_pairs={{0,4},{2,6},{4,8},{6,10},{8,12},{10,14},{12,0},{14,2},{1,5},{3,7},... | collective-permute-start | bytes 417800 | tf_op jit(solution)/shard_map/ppermute | solution.py:274
  5.4 1.5 %collective-permute-start.1 = (bf16[272,256]{1,0:T(8,128)(2,1)S(1)}, bf16[272,256]{1,0:T(8,128)(2,1)S(1)}, u32[]{:S(2)}, u32[]{:S(2)}) collective-permute-start(bf16[272,256]{1,0:T(8,128)(2,1)S(1)} %get-tuple-element.57.refs_1_.refs_3_.mine_ref), channel_id=1, source_target_pairs={{0,2},{2,0},{4,6},{6,4},{8,10},{10,8},{12,14},{14,12},{1,3},{3,1},... | collective-permute-start | bytes 417800 | tf_op jit(solution)/shard_map/ppermute | solution.py:271
  6.9 0.0 copy-start
  6.9 1.2 %copy-done = bf16[27,128,128]{2,1,0:T(8,128)(2,1)S(1)} copy-done((bf16[27,128,128]{2,1,0:T(8,128)(2,1)S(1)}, bf16[27,128,128]{2,1,0:T(8,128)(2,1)}, u32[]{:S(2)}) %copy-start) | copy-done | bytes 884760
  8.0 0.4 %turn_weights.1 = (bf16[128,3456]{1,0:T(8,128)(2,1)S(1)}, bf16[128,3456]{1,0:T(8,128)(2,1)S(1)}) custom-call(bf16[27,128,128]{2,1,0:T(8,128)(2,1)S(1)} %copy-done), custom_call_target="tpu_custom_call" | custom-call | flops 200000000 | bytes 3000000 | tf_op jit(solution)/shard_map/turn_weights/pallas_call | solution.py:277
  8.4 2.3 %collective-permute-start = (bf16[272,256]{1,0:T(8,128)(2,1)S(1)}, bf16[272,256]{1,0:T(8,128)(2,1)S(1)}, u32[]{:S(2)}, u32[]{:S(2)}) collective-permute-start(bf16[272,256]{1,0:T(8,128)(2,1)S(1)} %get-tuple-element.57.refs_1_.refs_3_.mine_ref), channel_id=1, source_target_pairs={{0,12},{2,14},{4,0},{6,2},{8,4},{10,6},{12,8},{14,10},{1,13},{3,15... | collective-permute-start | bytes 417800 | tf_op jit(solution)/shard_map/ppermute | solution.py:274
  10.7 0.4 %collective-permute-done.3.refs_1_.refs_3_.before_mine = bf16[272,256]{1,0:T(8,128)(2,1)S(1)} collective-permute-done((bf16[272,256]{1,0:T(8,128)(2,1)S(1)}, bf16[272,256]{1,0:T(8,128)(2,1)S(1)}, u32[]{:S(2)}, u32[]{:S(2)}) %collective-permute-start.3) | collective-permute-done | bytes 139296 | tf_op jit(solution)/shard_map/ppermute | solution.py:274
  11.2 1.5 %collective-permute-start.4 = (bf16[272,256]{1,0:T(8,128)(2,1)S(1)}, bf16[272,256]{1,0:T(8,128)(2,1)S(1)}, u32[]{:S(2)}, u32[]{:S(2)}) collective-permute-start(bf16[272,256]{1,0:T(8,128)(2,1)S(1)} %collective-permute-done.3.refs_1_.refs_3_.before_mine), channel_id=1, source_target_pairs={{0,2},{2,0},{4,6},{6,4},{8,10},{10,8},{12,14},{14,12},{1,3},{3,1},... | collective-permute-start | bytes 417800 | tf_op jit(solution)/shard_map/ppermute | solution.py:271
  12.7 0.0 collective-permute-start.5
  12.7 0.0 collective-permute-done.1.refs_2_.refs_4_.other_ref
  12.7 1.8 %weight_row_0.1 = (f32[1152,128]{1,0:T(8,128)S(1)}, f32[1152,128]{1,0:T(8,128)S(1)}, f32[512,128]{1,0:T(8,128)S(1)}, f32[512,128]{1,0:T(8,128)S(1)}, f32[128,128]{1,0:T(8,128)S(1)}) custom-call(s32[1]{0:T(128)} %bitcast.refs_0_.where_ref, bf16[272,256]{1,0:T(8,128)(2,1)S(1)} %get-tuple-element.57.refs_1_.refs_3_.mine_ref, ...), custom_call_target="tpu_custom_call" | custom-call | flops 2000000000 | bytes 4000000 | tf_op jit(solution)/shard_map/weight_row_0/pallas_call | solution.py:331
  14.5 0.2 collective-permute-done.refs_1_.refs_5_.after_mine
  14.7 0.8 %collective-permute-start.2 = (bf16[272,256]{1,0:T(8,128)(2,1)S(1)}, bf16[272,256]{1,0:T(8,128)(2,1)S(1)}, u32[]{:S(2)}, u32[]{:S(2)}) collective-permute-start(bf16[272,256]{1,0:T(8,128)(2,1)S(1)} %collective-permute-done.refs_1_.refs_5_.after_mine), channel_id=1, source_target_pairs={{0,2},{2,0},{4,6},{6,4},{8,10},{10,8},{12,14},{14,12},{1,3},{3,1},... | collective-permute-start | bytes 417800 | tf_op jit(solution)/shard_map/ppermute | solution.py:271
  15.6 1.7 %voxels_own_row.1 = (f32[128,256]{1,0:T(8,128)S(1)}, f32[128,256]{1,0:T(8,128)S(1)}) custom-call(s32[1]{0:T(128)} %bitcast.refs_0_.where_ref, bf16[272,256]{1,0:T(8,128)(2,1)S(1)} %get-tuple-element.57.refs_1_.refs_3_.mine_ref, bf16[272,256]{1,0:T(8,128)(2,1)S(1)} %collective-permute-done.1.refs_2_.refs_4_.other_ref, ...), custom_call_target="tpu_custom_call" | custom-call | flops 2000000000 | bytes 4000000 | tf_op jit(solution)/shard_map/voxels_own_row/pallas_call | solution.py:292
  17.3 0.0 collective-permute-done.4.refs_2_.refs_4_.before_other
  17.3 0.8 %weight_row_1_middle.1 = (f32[512,128]{1,0:T(8,128)S(1)}, f32[512,128]{1,0:T(8,128)S(1)}, f32[128,128]{1,0:T(8,128)S(1)}, bf16[768,256]{1,0:T(8,128)(2,1)S(1)}, ...) custom-call(s32[1]{0:T(128)} %bitcast.refs_0_.where_ref, ...), custom_call_target="tpu_custom_call" | custom-call | flops 2000000000 | bytes 4000000 | tf_op jit(solution)/shard_map/weight_row_1_middle/pallas_call | solution.py:331
  18.2 1.4 %collective-permute-done.5.refs_1_ = bf16[272,256]{1,0:T(8,128)(2,1)S(1)} collective-permute-done((bf16[272,256]{1,0:T(8,128)(2,1)S(1)}, bf16[272,256]{1,0:T(8,128)(2,1)S(1)}, u32[]{:S(2)}, u32[]{:S(2)}) %collective-permute-start.5) | collective-permute-done | bytes 139296 | tf_op jit(solution)/shard_map/ppermute | solution.py:274
  19.6 0.5 %collective-permute-start.6 = (bf16[272,256]{1,0:T(8,128)(2,1)S(1)}, bf16[272,256]{1,0:T(8,128)(2,1)S(1)}, u32[]{:S(2)}, u32[]{:S(2)}) collective-permute-start(bf16[272,256]{1,0:T(8,128)(2,1)S(1)} %collective-permute-done.5.refs_1_), channel_id=1, source_target_pairs={{0,2},{2,0},{4,6},{6,4},{8,10},{10,8},{12,14},{14,12},{1,3},{3,1},... | collective-permute-start | bytes 417800 | tf_op jit(solution)/shard_map/ppermute | solution.py:271
  20.0 1.5 %weight_row_1.1 = (f32[1152,128]{1,0:T(8,128)S(1)}, f32[1152,128]{1,0:T(8,128)S(1)}) custom-call(s32[1]{0:T(128)} %bitcast.refs_0_.where_ref, bf16[768,256]{1,0:T(8,128)(2,1)S(1)} %get-tuple-element.65.refs_1_, bf16[256,768]{1,0:T(8,128)(2,1)S(1)} %get-tuple-element.66.refs_2_, f32[5,16,128]{2,1,0:T(8,128)S(1)} %get-tuple-element.67.refs_3_, ...), custom_call_target="tpu_custom_call" | custom-call | flops 2000000000 | bytes 4000000 | tf_op jit(solution)/shard_map/weight_row_1/pallas_call | solution.py:331
  21.5 0.0 collective-permute-done.2.refs_2_.refs_6_.after_other
  21.5 2.1 %weight_row_2.1 = (f32[1152,128]{1,0:T(8,128)S(1)}, f32[1152,128]{1,0:T(8,128)S(1)}, f32[512,128]{1,0:T(8,128)S(1)}, f32[512,128]{1,0:T(8,128)S(1)}, f32[128,128]{1,0:T(8,128)S(1)}) custom-call(s32[1]{0:T(128)} %bitcast.refs_0_.where_ref, bf16[272,256]{1,0:T(8,128)(2,1)S(1)} %collective-permute-done.refs_1_.refs_5_.after_mine, ...), custom_call_target="tpu_custom_call" | custom-call | flops 2000000000 | bytes 4000000 | tf_op jit(solution)/shard_map/weight_row_2/pallas_call | solution.py:331
  23.7 1.0 %collective-permute-done.6.refs_2_ = bf16[272,256]{1,0:T(8,128)(2,1)S(1)} collective-permute-done((bf16[272,256]{1,0:T(8,128)(2,1)S(1)}, bf16[272,256]{1,0:T(8,128)(2,1)S(1)}, u32[]{:S(2)}, u32[]{:S(2)}) %collective-permute-start.6) | collective-permute-done | bytes 139296 | tf_op jit(solution)/shard_map/ppermute | solution.py:271
  24.6 1.9 %weight_row_3.1 = (f32[18,128,128]{2,1,0:T(8,128)S(1)}, bf16[18,128,128]{2,1,0:T(8,128)(2,1)S(1)}, bf16[768,256]{1,0:T(8,128)(2,1)S(1)}, bf16[256,768]{1,0:T(8,128)(2,1)S(1)}, f32[5,16,128]{2,1,0:T(8,128)S(1)}) custom-call(s32[1]{0:T(128)} %bitcast.refs_0_.where_ref, bf16[272,256]{1,0:T(8,128)(2,1)S(1)} %collective-permute-done.5.refs_1_, ...), custom_call_target="tpu_custom_call" | custom-call | flops 2000000000 | bytes 4000000 | tf_op jit(solution)/shard_map/weight_row_3/pallas_call | solution.py:331
  26.5 0.1 collective-permute-start.7
  26.6 0.8 %weight_row_3_middle.1 = (f32[9,128,128]{2,1,0:T(8,128)S(1)}, bf16[9,128,128]{2,1,0:T(8,128)(2,1)S(1)}) custom-call(s32[1]{0:T(128)} %bitcast.refs_0_.where_ref, bf16[768,256]{1,0:T(8,128)(2,1)S(1)} %get-tuple-element.87.refs_1_, bf16[256,768]{1,0:T(8,128)(2,1)S(1)} %get-tuple-element.88.refs_2_, f32[5,16,128]{2,1,0:T(8,128)S(1)} %get-tuple-element.89.refs_3_, ...), custom_call_target="tpu_custom_call" | custom-call | flops 2000000000 | bytes 4000000 | tf_op jit(solution)/shard_map/weight_row_3_middle/pallas_call | solution.py:331
  27.4 0.6 %collective-permute-start.8 = (bf16[9,128,128]{2,1,0:T(8,128)(2,1)S(1)}, bf16[9,128,128]{2,1,0:T(8,128)(2,1)S(1)}, u32[]{:S(2)}, u32[]{:S(2)}) collective-permute-start(bf16[9,128,128]{2,1,0:T(8,128)(2,1)S(1)} %get-tuple-element.94), channel_id=1, source_target_pairs={{0,1},{1,0},{2,3},{3,2},{4,5},{5,4},{6,7},{7,6},{8,9},{9,8},{10,11... | collective-permute-start | bytes 884744 | tf_op jit(solution)/shard_map/ppermute | solution.py:352
  28.0 0.9 %voxel_edges.1 = (bf16[256,128]{1,0:T(8,128)(2,1)S(1)}, bf16[256,128]{1,0:T(8,128)(2,1)S(1)}) custom-call(s32[1]{0:T(128)} %bitcast.refs_0_.where_ref, bf16[272,256]{1,0:T(8,128)(2,1)S(1)} %collective-permute-done.3.refs_1_.refs_3_.before_mine, bf16[272,256]{1,0:T(8,128)(2,1)S(1)} %collective-permute-done.4.refs_2_.refs_4_.before_other, ...), custom_call_target="tpu_custom_call" | custom-call | flops 1000000000 | bytes 4000000 | tf_op jit(solution)/shard_map/voxel_edges/pallas_call | solution.py:378
  28.9 0.3 collective-permute-done.8.middle_sent
  29.2 0.0 collective-permute-done.7.sides_sent
  29.2 1.3 %finish.1 = (f32[27,128,128]{2,1,0:T(8,128)}, bf16[256,128]{1,0:T(8,128)(2,1)}, bf16[256,128]{1,0:T(8,128)(2,1)}) custom-call(f32[18,128,128]{2,1,0:T(8,128)S(1)} %get-tuple-element.85.sides_ref, bf16[18,128,128]{2,1,0:T(8,128)(2,1)S(1)} %collective-permute-done.7.sides_sent, f32[9,128,128]{2,1,0:T(8,128)S(1)} %get-tuple-element.93.middle_ref, ...), custom_call_target="tpu_custom_call" | custom-call | tf_op jit(solution)/shard_map/finish/pallas_call | solution.py:393
Async XLA Ops:
  2.3 8.9 %collective-permute-start.3 = (bf16[272,256]{1,0:T(8,128)(2,1)S(1)}, bf16[272,256]{1,0:T(8,128)(2,1)S(1)}, u32[]{:S(2)}, u32[]{:S(2)}) collective-permute-start(bf16[272,256]{1,0:T(8,128)(2,1)S(1)} %get-tuple-element.57.refs_1_.refs_3_.mine_ref), channel_id=1, source_target_pairs={{0,4},{2,6},{4,8},{6,10},{8,12},{10,14},{12,0},{14,2},{1,5},{3,7},... | collective-permute-start | bytes 417800 | tf_op jit(solution)/shard_map/ppermute | solution.py:274
  5.4 7.3 %collective-permute-start.1 = (bf16[272,256]{1,0:T(8,128)(2,1)S(1)}, bf16[272,256]{1,0:T(8,128)(2,1)S(1)}, u32[]{:S(2)}, u32[]{:S(2)}) collective-permute-start(bf16[272,256]{1,0:T(8,128)(2,1)S(1)} %get-tuple-element.57.refs_1_.refs_3_.mine_ref), channel_id=1, source_target_pairs={{0,2},{2,0},{4,6},{6,4},{8,10},{10,8},{12,14},{14,12},{1,3},{3,1},... | collective-permute-start | bytes 417800 | tf_op jit(solution)/shard_map/ppermute | solution.py:271
  6.9 1.2 %copy-start = (bf16[27,128,128]{2,1,0:T(8,128)(2,1)S(1)}, bf16[27,128,128]{2,1,0:T(8,128)(2,1)}, u32[]{:S(2)}) copy-start(bf16[27,128,128]{2,1,0:T(8,128)(2,1)} %w_ref) | copy-start | bytes 2654212
  8.4 6.3 %collective-permute-start = (bf16[272,256]{1,0:T(8,128)(2,1)S(1)}, bf16[272,256]{1,0:T(8,128)(2,1)S(1)}, u32[]{:S(2)}, u32[]{:S(2)}) collective-permute-start(bf16[272,256]{1,0:T(8,128)(2,1)S(1)} %get-tuple-element.57.refs_1_.refs_3_.mine_ref), channel_id=1, source_target_pairs={{0,12},{2,14},{4,0},{6,2},{8,4},{10,6},{12,8},{14,10},{1,13},{3,15... | collective-permute-start | bytes 417800 | tf_op jit(solution)/shard_map/ppermute | solution.py:274
  11.2 6.1 %collective-permute-start.4 = (bf16[272,256]{1,0:T(8,128)(2,1)S(1)}, bf16[272,256]{1,0:T(8,128)(2,1)S(1)}, u32[]{:S(2)}, u32[]{:S(2)}) collective-permute-start(bf16[272,256]{1,0:T(8,128)(2,1)S(1)} %collective-permute-done.3.refs_1_.refs_3_.before_mine), channel_id=1, source_target_pairs={{0,2},{2,0},{4,6},{6,4},{8,10},{10,8},{12,14},{14,12},{1,3},{3,1},... | collective-permute-start | bytes 417800 | tf_op jit(solution)/shard_map/ppermute | solution.py:271
  12.7 6.9 %collective-permute-start.5 = (bf16[272,256]{1,0:T(8,128)(2,1)S(1)}, bf16[272,256]{1,0:T(8,128)(2,1)S(1)}, u32[]{:S(2)}, u32[]{:S(2)}) collective-permute-start(bf16[272,256]{1,0:T(8,128)(2,1)S(1)} %collective-permute-done.3.refs_1_.refs_3_.before_mine), channel_id=1, source_target_pairs={{0,4},{2,6},{4,8},{6,10},{8,12},{10,14},{12,0},{14,2},{1,5},{3,7},... | collective-permute-start | bytes 417800 | tf_op jit(solution)/shard_map/ppermute | solution.py:274
  14.7 6.8 %collective-permute-start.2 = (bf16[272,256]{1,0:T(8,128)(2,1)S(1)}, bf16[272,256]{1,0:T(8,128)(2,1)S(1)}, u32[]{:S(2)}, u32[]{:S(2)}) collective-permute-start(bf16[272,256]{1,0:T(8,128)(2,1)S(1)} %collective-permute-done.refs_1_.refs_5_.after_mine), channel_id=1, source_target_pairs={{0,2},{2,0},{4,6},{6,4},{8,10},{10,8},{12,14},{14,12},{1,3},{3,1},... | collective-permute-start | bytes 417800 | tf_op jit(solution)/shard_map/ppermute | solution.py:271
  19.6 5.1 %collective-permute-start.6 = (bf16[272,256]{1,0:T(8,128)(2,1)S(1)}, bf16[272,256]{1,0:T(8,128)(2,1)S(1)}, u32[]{:S(2)}, u32[]{:S(2)}) collective-permute-start(bf16[272,256]{1,0:T(8,128)(2,1)S(1)} %collective-permute-done.5.refs_1_), channel_id=1, source_target_pairs={{0,2},{2,0},{4,6},{6,4},{8,10},{10,8},{12,14},{14,12},{1,3},{3,1},... | collective-permute-start | bytes 417800 | tf_op jit(solution)/shard_map/ppermute | solution.py:271
  26.5 2.6 %collective-permute-start.7 = (bf16[18,128,128]{2,1,0:T(8,128)(2,1)S(1)}, bf16[18,128,128]{2,1,0:T(8,128)(2,1)S(1)}, u32[]{:S(2)}, u32[]{:S(2)}) collective-permute-start(bf16[18,128,128]{2,1,0:T(8,128)(2,1)S(1)} %get-tuple-element.86), channel_id=1, source_target_pairs={{0,1},{1,0},{2,3},{3,2},{4,5},{5,4},{6,7},{7,6},{8,9},{9,8},{10,11... | collective-permute-start | bytes 1769480 | tf_op jit(solution)/shard_map/ppermute | solution.py:352
  27.4 1.8 %collective-permute-start.8 = (bf16[9,128,128]{2,1,0:T(8,128)(2,1)S(1)}, bf16[9,128,128]{2,1,0:T(8,128)(2,1)S(1)}, u32[]{:S(2)}, u32[]{:S(2)}) collective-permute-start(bf16[9,128,128]{2,1,0:T(8,128)(2,1)S(1)} %get-tuple-element.94), channel_id=1, source_target_pairs={{0,1},{1,0},{2,3},{3,2},{4,5},{5,4},{6,7},{7,6},{8,9},{9,8},{10,11... | collective-permute-start | bytes 884744 | tf_op jit(solution)/shard_map/ppermute | solution.py:352

commit v24 on v21

--- a/solution.py
+++ b/solution.py
@@ -13,7 +13,7 @@
 HALF = 13
 CODE_ROWS = 16
 ROW_STAGES = 4
-FINISH_STEP = 3
+FINISH_STEP = 9
 PACK_VMEM = 8 * 1024 * 1024
 KERNEL_VMEM = 24 * 1024 * 1024
 

time: 30 us -> 30 us (level)
  no operation moved by 1% of the time
where the time goes in v24:
time: 30 us; the launch traced here: 29.7 us
  Pallas kernels  14.1 us (47%)
  starting transfers between devices  10.8 us (36%)
  waiting for transfers between devices  2.3 us (8%)
  between operations  1.36 us (5%)
  local copies, waits for them, and re-layouts  1.17 us (4%)
    pallas_call x5, Pallas kernels, row_sums(): pl.pallas_call(functools.partial(row_kernel, not sums, bool(final), group...  8.76 us
    ppermute x3, starting transfers between devices, along(): lax.ppermute(block, 'brick', [(i, (i + turn * tiles_y) % peers) for i in...  5.38 us
    ppermute x4, starting transfers between devices, across(): return lax.ppermute(block, 'brick', [(i, i ^ 1) for i in range(peers)])  4.83 us
    ppermute x3, waiting for transfers between devices, along(): lax.ppermute(block, 'brick', [(i, (i + turn * tiles_y) % peers) for i in...  1.99 us
    pallas_call x1, Pallas kernels, whole_scene(): pl.pallas_call(own_kernel, out_shape=(jax.ShapeDtypeStruct((width, rows),...  1.72 us
    pallas_call x1, Pallas kernels, whole_scene(): pl.pallas_call(finish_kernel, out_shape=(jax.ShapeDtypeStruct((27, width,...  1.3 us
    unnamed x2, local copies, waits for them, and re-layouts  1.17 us
    pallas_call x1, Pallas kernels, whole_scene(): pl.pallas_call(pack_kernel, out_shape=(jax.ShapeDtypeStruct((rows + CODE_...  1.03 us
  transfers between devices with their start and end apart: 9, of which 4 were waited for; matrix products, arithmetic and copies ran while one was open for 0% of the time, Pallas kernels for 33%

profile of v24, /device:TPU:0, one launch (start us, length us, event | category | flops | bytes accessed | tf_op | source)
XLA Modules:
  0.0 29.7 jit_solution(15741949033120820488)
XLA Ops:
  1.3 1.0 %pack_tile.1 = (bf16[272,256]{1,0:T(8,128)(2,1)S(1)}, f32[256,128]{1,0:T(8,128)S(1)}, f32[27,256]{1,0:T(8,128)S(1)}) custom-call(s32[1]{0:T(128)S(6)} %copy.10.time_ref, bf16[1,256,128]{2,1,0:T(8,128)(2,1)} %feat_hbm.1, bf16[1,256,128]{2,1,0:T(8,128)(2,1)} %cot_hbm.1, s32[27,256]{1,0:T(8,128)} %near_hbm.1, bf16[1,128]{1,0:T(2,128)(2,1)} %cond_hbm.1, ...), custom_call_target="tpu_custom_call" | custom-call | tf_op jit(solution)/shard_map/pack_tile/pallas_call | solution.py:248
  2.3 3.1 %collective-permute-start.3 = (bf16[272,256]{1,0:T(8,128)(2,1)S(1)}, bf16[272,256]{1,0:T(8,128)(2,1)S(1)}, u32[]{:S(2)}, u32[]{:S(2)}) collective-permute-start(bf16[272,256]{1,0:T(8,128)(2,1)S(1)} %get-tuple-element.47.refs_1_.refs_3_.mine_ref), channel_id=1, source_target_pairs={{0,4},{2,6},{4,8},{6,10},{8,12},{10,14},{12,0},{14,2},{1,5},{3,7},... | collective-permute-start | bytes 417800 | tf_op jit(solution)/shard_map/ppermute | solution.py:273
  5.4 1.5 %collective-permute-start.1 = (bf16[272,256]{1,0:T(8,128)(2,1)S(1)}, bf16[272,256]{1,0:T(8,128)(2,1)S(1)}, u32[]{:S(2)}, u32[]{:S(2)}) collective-permute-start(bf16[272,256]{1,0:T(8,128)(2,1)S(1)} %get-tuple-element.47.refs_1_.refs_3_.mine_ref), channel_id=1, source_target_pairs={{0,2},{2,0},{4,6},{6,4},{8,10},{10,8},{12,14},{14,12},{1,3},{3,1},... | collective-permute-start | bytes 417800 | tf_op jit(solution)/shard_map/ppermute | solution.py:270
  6.9 0.0 copy-start
  6.9 1.2 %copy-done = bf16[27,128,128]{2,1,0:T(8,128)(2,1)S(1)} copy-done((bf16[27,128,128]{2,1,0:T(8,128)(2,1)S(1)}, bf16[27,128,128]{2,1,0:T(8,128)(2,1)}, u32[]{:S(2)}) %copy-start) | copy-done | bytes 884760
  8.0 0.4 %turn_weights.1 = (bf16[128,3456]{1,0:T(8,128)(2,1)S(1)}, bf16[128,3456]{1,0:T(8,128)(2,1)S(1)}) custom-call(bf16[27,128,128]{2,1,0:T(8,128)(2,1)S(1)} %copy-done), custom_call_target="tpu_custom_call" | custom-call | flops 200000000 | bytes 3000000 | tf_op jit(solution)/shard_map/turn_weights/pallas_call | solution.py:276
  8.4 2.3 %collective-permute-start = (bf16[272,256]{1,0:T(8,128)(2,1)S(1)}, bf16[272,256]{1,0:T(8,128)(2,1)S(1)}, u32[]{:S(2)}, u32[]{:S(2)}) collective-permute-start(bf16[272,256]{1,0:T(8,128)(2,1)S(1)} %get-tuple-element.47.refs_1_.refs_3_.mine_ref), channel_id=1, source_target_pairs={{0,12},{2,14},{4,0},{6,2},{8,4},{10,6},{12,8},{14,10},{1,13},{3,15... | collective-permute-start | bytes 417800 | tf_op jit(solution)/shard_map/ppermute | solution.py:273
  10.7 0.4 %collective-permute-done.3.refs_1_.refs_3_.before_mine = bf16[272,256]{1,0:T(8,128)(2,1)S(1)} collective-permute-done((bf16[272,256]{1,0:T(8,128)(2,1)S(1)}, bf16[272,256]{1,0:T(8,128)(2,1)S(1)}, u32[]{:S(2)}, u32[]{:S(2)}) %collective-permute-start.3) | collective-permute-done | bytes 139296 | tf_op jit(solution)/shard_map/ppermute | solution.py:273
  11.2 0.0 collective-permute-start.5
  11.2 1.5 %collective-permute-start.4 = (bf16[272,256]{1,0:T(8,128)(2,1)S(1)}, bf16[272,256]{1,0:T(8,128)(2,1)S(1)}, u32[]{:S(2)}, u32[]{:S(2)}) collective-permute-start(bf16[272,256]{1,0:T(8,128)(2,1)S(1)} %collective-permute-done.3.refs_1_.refs_3_.before_mine), channel_id=1, source_target_pairs={{0,2},{2,0},{4,6},{6,4},{8,10},{10,8},{12,14},{14,12},{1,3},{3,1},... | collective-permute-start | bytes 417800 | tf_op jit(solution)/shard_map/ppermute | solution.py:270
  12.7 0.0 collective-permute-done.1.refs_2_.refs_4_.other_ref
  12.7 1.8 %weight_row_0.1 = (f32[1664,128]{1,0:T(8,128)S(1)}, f32[1664,128]{1,0:T(8,128)S(1)}, f32[128,128]{1,0:T(8,128)S(1)}) custom-call(s32[1]{0:T(128)} %bitcast.refs_0_.where_ref, bf16[272,256]{1,0:T(8,128)(2,1)S(1)} %get-tuple-element.47.refs_1_.refs_3_.mine_ref, bf16[272,256]{1,0:T(8,128)(2,1)S(1)} %collective-permute-done.1.refs_2_.refs_4_.other_ref), custom_call_target="tpu_custom_call" | custom-call | flops 2000000000 | bytes 4000000 | tf_op jit(solution)/shard_map/weight_row_0/pallas_call | solution.py:332
  14.5 0.3 collective-permute-done.refs_1_.refs_5_.after_mine
  14.8 0.8 %collective-permute-start.2 = (bf16[272,256]{1,0:T(8,128)(2,1)S(1)}, bf16[272,256]{1,0:T(8,128)(2,1)S(1)}, u32[]{:S(2)}, u32[]{:S(2)}) collective-permute-start(bf16[272,256]{1,0:T(8,128)(2,1)S(1)} %collective-permute-done.refs_1_.refs_5_.after_mine), channel_id=1, source_target_pairs={{0,2},{2,0},{4,6},{6,4},{8,10},{10,8},{12,14},{14,12},{1,3},{3,1},... | collective-permute-start | bytes 417800 | tf_op jit(solution)/shard_map/ppermute | solution.py:270
  15.6 1.7 %voxels_own_row.1 = (f32[128,256]{1,0:T(8,128)S(1)}, f32[128,256]{1,0:T(8,128)S(1)}) custom-call(s32[1]{0:T(128)} %bitcast.refs_0_.where_ref, bf16[272,256]{1,0:T(8,128)(2,1)S(1)} %get-tuple-element.47.refs_1_.refs_3_.mine_ref, bf16[272,256]{1,0:T(8,128)(2,1)S(1)} %collective-permute-done.1.refs_2_.refs_4_.other_ref, ...), custom_call_target="tpu_custom_call" | custom-call | flops 2000000000 | bytes 4000000 | tf_op jit(solution)/shard_map/voxels_own_row/pallas_call | solution.py:291
  17.3 1.3 %collective-permute-done.5.refs_1_ = bf16[272,256]{1,0:T(8,128)(2,1)S(1)} collective-permute-done((bf16[272,256]{1,0:T(8,128)(2,1)S(1)}, bf16[272,256]{1,0:T(8,128)(2,1)S(1)}, u32[]{:S(2)}, u32[]{:S(2)}) %collective-permute-start.5) | collective-permute-done | bytes 139296 | tf_op jit(solution)/shard_map/ppermute | solution.py:273
  18.5 1.0 %collective-permute-start.6 = (bf16[272,256]{1,0:T(8,128)(2,1)S(1)}, bf16[272,256]{1,0:T(8,128)(2,1)S(1)}, u32[]{:S(2)}, u32[]{:S(2)}) collective-permute-start(bf16[272,256]{1,0:T(8,128)(2,1)S(1)} %collective-permute-done.5.refs_1_), channel_id=1, source_target_pairs={{0,2},{2,0},{4,6},{6,4},{8,10},{10,8},{12,14},{14,12},{1,3},{3,1},... | collective-permute-start | bytes 417800 | tf_op jit(solution)/shard_map/ppermute | solution.py:270
  19.6 0.0 collective-permute-done.4.refs_2_.refs_4_.before_other
  19.6 2.1 %weight_row_1.1 = (f32[1664,128]{1,0:T(8,128)S(1)}, f32[1664,128]{1,0:T(8,128)S(1)}, f32[128,128]{1,0:T(8,128)S(1)}) custom-call(s32[1]{0:T(128)} %bitcast.refs_0_.where_ref, bf16[272,256]{1,0:T(8,128)(2,1)S(1)} %collective-permute-done.3.refs_1_.refs_3_.before_mine, bf16[272,256]{1,0:T(8,128)(2,1)S(1)} %collective-permute-done.4.refs_2_.refs_4_.before_other, ...), custom_call_target="tpu_custom_call" | custom-call | flops 2000000000 | bytes 4000000 | tf_op jit(solution)/shard_map/weight_row_1/pallas_call | solution.py:332
  21.7 0.0 collective-permute-done.2.refs_2_.refs_6_.after_other
  21.7 2.1 %weight_row_2.1 = (f32[1664,128]{1,0:T(8,128)S(1)}, f32[1664,128]{1,0:T(8,128)S(1)}, f32[128,128]{1,0:T(8,128)S(1)}) custom-call(s32[1]{0:T(128)} %bitcast.refs_0_.where_ref, bf16[272,256]{1,0:T(8,128)(2,1)S(1)} %collective-permute-done.refs_1_.refs_5_.after_mine, bf16[272,256]{1,0:T(8,128)(2,1)S(1)} %collective-permute-done.2.refs_2_.refs_6_.after_other, ...), custom_call_target="tpu_custom_call" | custom-call | flops 2000000000 | bytes 4000000 | tf_op jit(solution)/shard_map/weight_row_2/pallas_call | solution.py:332
  23.9 0.0 collective-permute-done.6.refs_2_
  23.9 1.9 %weight_row_3.1 = (f32[18,128,128]{2,1,0:T(8,128)S(1)}, bf16[18,128,128]{2,1,0:T(8,128)(2,1)S(1)}, bf16[768,256]{1,0:T(8,128)(2,1)S(1)}, bf16[256,768]{1,0:T(8,128)(2,1)S(1)}, f32[5,16,128]{2,1,0:T(8,128)S(1)}) custom-call(s32[1]{0:T(128)} %bitcast.refs_0_.where_ref, bf16[272,256]{1,0:T(8,128)(2,1)S(1)} %collective-permute-done.5.refs_1_, ...), custom_call_target="tpu_custom_call" | custom-call | flops 2000000000 | bytes 4000000 | tf_op jit(solution)/shard_map/weight_row_3/pallas_call | solution.py:332
  25.8 0.1 collective-permute-start.7
  25.9 0.8 %weight_row_3_middle.1 = (f32[9,128,128]{2,1,0:T(8,128)S(1)}, bf16[9,128,128]{2,1,0:T(8,128)(2,1)S(1)}) custom-call(s32[1]{0:T(128)} %bitcast.refs_0_.where_ref, bf16[768,256]{1,0:T(8,128)(2,1)S(1)} %get-tuple-element.69.refs_1_, bf16[256,768]{1,0:T(8,128)(2,1)S(1)} %get-tuple-element.70.refs_2_, f32[5,16,128]{2,1,0:T(8,128)S(1)} %get-tuple-element.71.refs_3_, ...), custom_call_target="tpu_custom_call" | custom-call | flops 2000000000 | bytes 4000000 | tf_op jit(solution)/shard_map/weight_row_3_middle/pallas_call | solution.py:332
  26.7 0.6 %collective-permute-start.8 = (bf16[9,128,128]{2,1,0:T(8,128)(2,1)S(1)}, bf16[9,128,128]{2,1,0:T(8,128)(2,1)S(1)}, u32[]{:S(2)}, u32[]{:S(2)}) collective-permute-start(bf16[9,128,128]{2,1,0:T(8,128)(2,1)S(1)} %get-tuple-element.74), channel_id=1, source_target_pairs={{0,1},{1,0},{2,3},{3,2},{4,5},{5,4},{6,7},{7,6},{8,9},{9,8},{10,11... | collective-permute-start | bytes 884744 | tf_op jit(solution)/shard_map/ppermute | solution.py:347
  27.2 0.9 %voxel_edges.1 = (bf16[256,128]{1,0:T(8,128)(2,1)S(1)}, bf16[256,128]{1,0:T(8,128)(2,1)S(1)}) custom-call(s32[1]{0:T(128)} %bitcast.refs_0_.where_ref, bf16[272,256]{1,0:T(8,128)(2,1)S(1)} %collective-permute-done.3.refs_1_.refs_3_.before_mine, bf16[272,256]{1,0:T(8,128)(2,1)S(1)} %collective-permute-done.4.refs_2_.refs_4_.before_other, ...), custom_call_target="tpu_custom_call" | custom-call | flops 1000000000 | bytes 4000000 | tf_op jit(solution)/shard_map/voxel_edges/pallas_call | solution.py:364
  28.1 0.3 collective-permute-done.8.middle_sent
  28.4 0.0 collective-permute-done.7.sides_sent
  28.4 1.3 %finish.1 = (f32[27,128,128]{2,1,0:T(8,128)}, bf16[256,128]{1,0:T(8,128)(2,1)}, bf16[256,128]{1,0:T(8,128)(2,1)}) custom-call(f32[18,128,128]{2,1,0:T(8,128)S(1)} %get-tuple-element.67.sides_ref, bf16[18,128,128]{2,1,0:T(8,128)(2,1)S(1)} %collective-permute-done.7.sides_sent, f32[9,128,128]{2,1,0:T(8,128)S(1)} %get-tuple-element.73.middle_ref, ...), custom_call_target="tpu_custom_call" | custom-call | tf_op jit(solution)/shard_map/finish/pallas_call | solution.py:379
Async XLA Ops:
  2.3 8.9 %collective-permute-start.3 = (bf16[272,256]{1,0:T(8,128)(2,1)S(1)}, bf16[272,256]{1,0:T(8,128)(2,1)S(1)}, u32[]{:S(2)}, u32[]{:S(2)}) collective-permute-start(bf16[272,256]{1,0:T(8,128)(2,1)S(1)} %get-tuple-element.47.refs_1_.refs_3_.mine_ref), channel_id=1, source_target_pairs={{0,4},{2,6},{4,8},{6,10},{8,12},{10,14},{12,0},{14,2},{1,5},{3,7},... | collective-permute-start | bytes 417800 | tf_op jit(solution)/shard_map/ppermute | solution.py:273
  5.4 7.3 %collective-permute-start.1 = (bf16[272,256]{1,0:T(8,128)(2,1)S(1)}, bf16[272,256]{1,0:T(8,128)(2,1)S(1)}, u32[]{:S(2)}, u32[]{:S(2)}) collective-permute-start(bf16[272,256]{1,0:T(8,128)(2,1)S(1)} %get-tuple-element.47.refs_1_.refs_3_.mine_ref), channel_id=1, source_target_pairs={{0,2},{2,0},{4,6},{6,4},{8,10},{10,8},{12,14},{14,12},{1,3},{3,1},... | collective-permute-start | bytes 417800 | tf_op jit(solution)/shard_map/ppermute | solution.py:270
  6.9 1.2 %copy-start = (bf16[27,128,128]{2,1,0:T(8,128)(2,1)S(1)}, bf16[27,128,128]{2,1,0:T(8,128)(2,1)}, u32[]{:S(2)}) copy-start(bf16[27,128,128]{2,1,0:T(8,128)(2,1)} %w_ref) | copy-start | bytes 2654212
  8.4 6.3 %collective-permute-start = (bf16[272,256]{1,0:T(8,128)(2,1)S(1)}, bf16[272,256]{1,0:T(8,128)(2,1)S(1)}, u32[]{:S(2)}, u32[]{:S(2)}) collective-permute-start(bf16[272,256]{1,0:T(8,128)(2,1)S(1)} %get-tuple-element.47.refs_1_.refs_3_.mine_ref), channel_id=1, source_target_pairs={{0,12},{2,14},{4,0},{6,2},{8,4},{10,6},{12,8},{14,10},{1,13},{3,15... | collective-permute-start | bytes 417800 | tf_op jit(solution)/shard_map/ppermute | solution.py:273
  11.2 7.4 %collective-permute-start.5 = (bf16[272,256]{1,0:T(8,128)(2,1)S(1)}, bf16[272,256]{1,0:T(8,128)(2,1)S(1)}, u32[]{:S(2)}, u32[]{:S(2)}) collective-permute-start(bf16[272,256]{1,0:T(8,128)(2,1)S(1)} %collective-permute-done.3.refs_1_.refs_3_.before_mine), channel_id=1, source_target_pairs={{0,4},{2,6},{4,8},{6,10},{8,12},{10,14},{12,0},{14,2},{1,5},{3,7},... | collective-permute-start | bytes 417800 | tf_op jit(solution)/shard_map/ppermute | solution.py:273
  11.2 8.4 %collective-permute-start.4 = (bf16[272,256]{1,0:T(8,128)(2,1)S(1)}, bf16[272,256]{1,0:T(8,128)(2,1)S(1)}, u32[]{:S(2)}, u32[]{:S(2)}) collective-permute-start(bf16[272,256]{1,0:T(8,128)(2,1)S(1)} %collective-permute-done.3.refs_1_.refs_3_.before_mine), channel_id=1, source_target_pairs={{0,2},{2,0},{4,6},{6,4},{8,10},{10,8},{12,14},{14,12},{1,3},{3,1},... | collective-permute-start | bytes 417800 | tf_op jit(solution)/shard_map/ppermute | solution.py:270
  14.8 6.9 %collective-permute-start.2 = (bf16[272,256]{1,0:T(8,128)(2,1)S(1)}, bf16[272,256]{1,0:T(8,128)(2,1)S(1)}, u32[]{:S(2)}, u32[]{:S(2)}) collective-permute-start(bf16[272,256]{1,0:T(8,128)(2,1)S(1)} %collective-permute-done.refs_1_.refs_5_.after_mine), channel_id=1, source_target_pairs={{0,2},{2,0},{4,6},{6,4},{8,10},{10,8},{12,14},{14,12},{1,3},{3,1},... | collective-permute-start | bytes 417800 | tf_op jit(solution)/shard_map/ppermute | solution.py:270
  18.5 5.3 %collective-permute-start.6 = (bf16[272,256]{1,0:T(8,128)(2,1)S(1)}, bf16[272,256]{1,0:T(8,128)(2,1)S(1)}, u32[]{:S(2)}, u32[]{:S(2)}) collective-permute-start(bf16[272,256]{1,0:T(8,128)(2,1)S(1)} %collective-permute-done.5.refs_1_), channel_id=1, source_target_pairs={{0,2},{2,0},{4,6},{6,4},{8,10},{10,8},{12,14},{14,12},{1,3},{3,1},... | collective-permute-start | bytes 417800 | tf_op jit(solution)/shard_map/ppermute | solution.py:270
  25.8 2.6 %collective-permute-start.7 = (bf16[18,128,128]{2,1,0:T(8,128)(2,1)S(1)}, bf16[18,128,128]{2,1,0:T(8,128)(2,1)S(1)}, u32[]{:S(2)}, u32[]{:S(2)}) collective-permute-start(bf16[18,128,128]{2,1,0:T(8,128)(2,1)S(1)} %get-tuple-element.68), channel_id=1, source_target_pairs={{0,1},{1,0},{2,3},{3,2},{4,5},{5,4},{6,7},{7,6},{8,9},{9,8},{10,11... | collective-permute-start | bytes 1769480 | tf_op jit(solution)/shard_map/ppermute | solution.py:347
  26.7 1.8 %collective-permute-start.8 = (bf16[9,128,128]{2,1,0:T(8,128)(2,1)S(1)}, bf16[9,128,128]{2,1,0:T(8,128)(2,1)S(1)}, u32[]{:S(2)}, u32[]{:S(2)}) collective-permute-start(bf16[9,128,128]{2,1,0:T(8,128)(2,1)S(1)} %get-tuple-element.74), channel_id=1, source_target_pairs={{0,1},{1,0},{2,3},{3,2},{4,5},{5,4},{6,7},{7,6},{8,9},{9,8},{10,11... | collective-permute-start | bytes 884744 | tf_op jit(solution)/shard_map/ppermute | solution.py:347

commit v25 on v24

--- a/solution.py
+++ b/solution.py
@@ -95,7 +95,7 @@
     pairs = [] if laid else [(refs.pop(0), refs.pop(0)) for _ in range(1 + max(pair for pair, _ in strips))]
     given = [refs.pop(0) for _ in range(3)] if laid else []
     before = [refs.pop(0) for _ in range(0 if first_stage else 3)]
-    outs = [refs.pop(0) for _ in range(2 if final else 3)]
+    outs = [refs.pop(0) for _ in range(1 if final else 3)]
     ground, turned, codes = given or [refs.pop(0) for _ in range(3)]
     near_act, near_cot = refs
     width = ground.shape[1] // 2
@@ -140,15 +140,13 @@
                 if turn:
                     one = one.T
                 to = to - 9 if group == 1 else to - 9 * turn
-                outs[0][to] = one
-                outs[1][to] = one.astype(jnp.bfloat16)
+                outs[0][to] = one.astype(jnp.bfloat16)
     if 1 in groups:
         centre = jnp.dot(turned[:width, :TILE * span], ground[:TILE * span, width:], preferred_element_type=jnp.float32)
         if not first_stage:
             centre = centre + before[2][...]
         if final:
-            outs[0][HALF - 9] = centre
-            outs[1][HALF - 9] = centre.astype(jnp.bfloat16)
+            outs[0][HALF - 9] = centre.astype(jnp.bfloat16)
         else:
             outs[2][...] = centre
 
@@ -231,7 +229,7 @@
         kept, sent, at = (middle_ref, middle_sent, first - 9) if first // 9 == 1 else (
             sides_ref, sides_sent, first if first < 9 else first - 9)
         part, taken = pl.ds(first, FINISH_STEP), pl.ds(at, FINISH_STEP)
-        weight[part] = kept[taken] + sent[taken].astype(jnp.float32)
+        weight[part] = kept[taken].astype(jnp.float32) + sent[taken].astype(jnp.float32)
         copies.append(pltpu.make_async_copy(weight.at[part], weight_hbm.at[part], sems.at[i]))
         copies[-1].start()
     for copy in copies:
@@ -310,10 +308,7 @@
     def row_sums(name, pairs, strips, borders, sums, groups=(0, 1), final=0, keep=False, laid=()):
         blocks = [block for pair in pairs for block in pair]
         if final:
-            out_shape = (
-                jax.ShapeDtypeStruct((final, width, width), jnp.float32),
-                jax.ShapeDtypeStruct((final, width, width), jnp.bfloat16),
-            )
+            out_shape = (jax.ShapeDtypeStruct((final, width, width), jnp.bfloat16),)
         else:
             out_shape = (
                 jax.ShapeDtypeStruct((HALF * width, width), jnp.float32),
@@ -353,14 +348,14 @@
     after_pair = (after, across(after))
     sums = row_sums("weight_row_1", (before_pair, own_pair), line + [(1, 0)], [(TILE, TILE - 1)], sums)
     sums = row_sums("weight_row_2", (after_pair, own_pair), line + [(1, TILE - 1)], [(0, TILE)], sums)
-    sides, sides_sent, *laid = row_sums("weight_row_3", (far_pair, before_pair, after_pair),
+    sides, *laid = row_sums("weight_row_3", (far_pair, before_pair, after_pair),
                                  line + [(1, 0), (2, TILE - 1)], [(TILE, TILE - 1), (0, TILE + 1)],
                                  sums, groups=(0,), final=18, keep=True)
-    sides_other = swapped(sides_sent)
+    sides_other = swapped(sides)
     centre, sides = lax.optimization_barrier((sums[2], sides))
-    middle, middle_sent = row_sums("weight_row_3_middle", (), line, [], (sums[0], sums[1], centre),
+    middle, = row_sums("weight_row_3_middle", (), line, [], (sums[0], sums[1], centre),
                                    groups=(1,), final=9, laid=laid)
-    middle_other = swapped(middle_sent)
+    middle_other = swapped(middle)
     conv_out, feature_grad = pl.pallas_call(
         edge_kernel,
         out_shape=(jax.ShapeDtypeStruct((rows, width), jnp.bfloat16),) * 2,

time: 30 us -> 29.9 us (level)
  no operation moved by 1% of the time
where the time goes in v25:
time: 29.9 us; the launch traced here: 29.7 us
  Pallas kernels  14.1 us (47%)
  starting transfers between devices  10.8 us (36%)
  waiting for transfers between devices  2.3 us (8%)
  between operations  1.36 us (5%)
  local copies, waits for them, and re-layouts  1.17 us (4%)
    pallas_call x5, Pallas kernels, row_sums(): pl.pallas_call(functools.partial(row_kernel, not sums, bool(final), group...  8.73 us
    ppermute x3, starting transfers between devices, along(): lax.ppermute(block, 'brick', [(i, (i + turn * tiles_y) % peers) for i in...  5.38 us
    ppermute x4, starting transfers between devices, across(): return lax.ppermute(block, 'brick', [(i, i ^ 1) for i in range(peers)])  4.83 us
    ppermute x3, waiting for transfers between devices, along(): lax.ppermute(block, 'brick', [(i, (i + turn * tiles_y) % peers) for i in...  1.99 us
    pallas_call x1, Pallas kernels, whole_scene(): pl.pallas_call(own_kernel, out_shape=(jax.ShapeDtypeStruct((width, rows),...  1.72 us
    pallas_call x1, Pallas kernels, whole_scene(): pl.pallas_call(finish_kernel, out_shape=(jax.ShapeDtypeStruct((27, width,...  1.31 us
    unnamed x2, local copies, waits for them, and re-layouts  1.17 us
    pallas_call x1, Pallas kernels, whole_scene(): pl.pallas_call(pack_kernel, out_shape=(jax.ShapeDtypeStruct((rows + CODE_...  1.03 us
  transfers between devices with their start and end apart: 9, of which 4 were waited for; matrix products, arithmetic and copies ran while one was open for 0% of the time, Pallas kernels for 33%

profile of v25, /device:TPU:0, one launch (start us, length us, event | category | flops | bytes accessed | tf_op | source)
XLA Modules:
  0.0 29.7 jit_solution(2726712445914457505)
XLA Ops:
  1.3 1.0 %pack_tile.1 = (bf16[272,256]{1,0:T(8,128)(2,1)S(1)}, f32[256,128]{1,0:T(8,128)S(1)}, f32[27,256]{1,0:T(8,128)S(1)}) custom-call(s32[1]{0:T(128)S(6)} %copy.10.time_ref, bf16[1,256,128]{2,1,0:T(8,128)(2,1)} %feat_hbm.1, bf16[1,256,128]{2,1,0:T(8,128)(2,1)} %cot_hbm.1, s32[27,256]{1,0:T(8,128)} %near_hbm.1, bf16[1,128]{1,0:T(2,128)(2,1)} %cond_hbm.1, ...), custom_call_target="tpu_custom_call" | custom-call | tf_op jit(solution)/shard_map/pack_tile/pallas_call | solution.py:246
  2.3 3.1 %collective-permute-start.3 = (bf16[272,256]{1,0:T(8,128)(2,1)S(1)}, bf16[272,256]{1,0:T(8,128)(2,1)S(1)}, u32[]{:S(2)}, u32[]{:S(2)}) collective-permute-start(bf16[272,256]{1,0:T(8,128)(2,1)S(1)} %get-tuple-element.44.refs_1_.refs_3_.mine_ref), channel_id=1, source_target_pairs={{0,4},{2,6},{4,8},{6,10},{8,12},{10,14},{12,0},{14,2},{1,5},{3,7},... | collective-permute-start | bytes 417800 | tf_op jit(solution)/shard_map/ppermute | solution.py:271
  5.4 1.5 %collective-permute-start.1 = (bf16[272,256]{1,0:T(8,128)(2,1)S(1)}, bf16[272,256]{1,0:T(8,128)(2,1)S(1)}, u32[]{:S(2)}, u32[]{:S(2)}) collective-permute-start(bf16[272,256]{1,0:T(8,128)(2,1)S(1)} %get-tuple-element.44.refs_1_.refs_3_.mine_ref), channel_id=1, source_target_pairs={{0,2},{2,0},{4,6},{6,4},{8,10},{10,8},{12,14},{14,12},{1,3},{3,1},... | collective-permute-start | bytes 417800 | tf_op jit(solution)/shard_map/ppermute | solution.py:268
  6.9 0.0 copy-start
  6.9 1.2 %copy-done = bf16[27,128,128]{2,1,0:T(8,128)(2,1)S(1)} copy-done((bf16[27,128,128]{2,1,0:T(8,128)(2,1)S(1)}, bf16[27,128,128]{2,1,0:T(8,128)(2,1)}, u32[]{:S(2)}) %copy-start) | copy-done | bytes 884760
  8.0 0.4 %turn_weights.1 = (bf16[128,3456]{1,0:T(8,128)(2,1)S(1)}, bf16[128,3456]{1,0:T(8,128)(2,1)S(1)}) custom-call(bf16[27,128,128]{2,1,0:T(8,128)(2,1)S(1)} %copy-done), custom_call_target="tpu_custom_call" | custom-call | flops 200000000 | bytes 3000000 | tf_op jit(solution)/shard_map/turn_weights/pallas_call | solution.py:274
  8.4 2.3 %collective-permute-start = (bf16[272,256]{1,0:T(8,128)(2,1)S(1)}, bf16[272,256]{1,0:T(8,128)(2,1)S(1)}, u32[]{:S(2)}, u32[]{:S(2)}) collective-permute-start(bf16[272,256]{1,0:T(8,128)(2,1)S(1)} %get-tuple-element.44.refs_1_.refs_3_.mine_ref), channel_id=1, source_target_pairs={{0,12},{2,14},{4,0},{6,2},{8,4},{10,6},{12,8},{14,10},{1,13},{3,15... | collective-permute-start | bytes 417800 | tf_op jit(solution)/shard_map/ppermute | solution.py:271
  10.7 0.4 %collective-permute-done.3.refs_1_.refs_3_.before_mine = bf16[272,256]{1,0:T(8,128)(2,1)S(1)} collective-permute-done((bf16[272,256]{1,0:T(8,128)(2,1)S(1)}, bf16[272,256]{1,0:T(8,128)(2,1)S(1)}, u32[]{:S(2)}, u32[]{:S(2)}) %collective-permute-start.3) | collective-permute-done | bytes 139296 | tf_op jit(solution)/shard_map/ppermute | solution.py:271
  11.2 0.0 collective-permute-start.5
  11.2 1.5 %collective-permute-start.4 = (bf16[272,256]{1,0:T(8,128)(2,1)S(1)}, bf16[272,256]{1,0:T(8,128)(2,1)S(1)}, u32[]{:S(2)}, u32[]{:S(2)}) collective-permute-start(bf16[272,256]{1,0:T(8,128)(2,1)S(1)} %collective-permute-done.3.refs_1_.refs_3_.before_mine), channel_id=1, source_target_pairs={{0,2},{2,0},{4,6},{6,4},{8,10},{10,8},{12,14},{14,12},{1,3},{3,1},... | collective-permute-start | bytes 417800 | tf_op jit(solution)/shard_map/ppermute | solution.py:268
  12.7 0.0 collective-permute-done.1.refs_2_.refs_4_.other_ref
  12.7 1.8 %weight_row_0.1 = (f32[1664,128]{1,0:T(8,128)S(1)}, f32[1664,128]{1,0:T(8,128)S(1)}, f32[128,128]{1,0:T(8,128)S(1)}) custom-call(s32[1]{0:T(128)} %bitcast.refs_0_.where_ref, bf16[272,256]{1,0:T(8,128)(2,1)S(1)} %get-tuple-element.44.refs_1_.refs_3_.mine_ref, bf16[272,256]{1,0:T(8,128)(2,1)S(1)} %collective-permute-done.1.refs_2_.refs_4_.other_ref), custom_call_target="tpu_custom_call" | custom-call | flops 2000000000 | bytes 4000000 | tf_op jit(solution)/shard_map/weight_row_0/pallas_call | solution.py:327
  14.5 0.3 collective-permute-done.refs_1_.refs_5_.after_mine
  14.8 0.8 %collective-permute-start.2 = (bf16[272,256]{1,0:T(8,128)(2,1)S(1)}, bf16[272,256]{1,0:T(8,128)(2,1)S(1)}, u32[]{:S(2)}, u32[]{:S(2)}) collective-permute-start(bf16[272,256]{1,0:T(8,128)(2,1)S(1)} %collective-permute-done.refs_1_.refs_5_.after_mine), channel_id=1, source_target_pairs={{0,2},{2,0},{4,6},{6,4},{8,10},{10,8},{12,14},{14,12},{1,3},{3,1},... | collective-permute-start | bytes 417800 | tf_op jit(solution)/shard_map/ppermute | solution.py:268
  15.6 1.7 %voxels_own_row.1 = (f32[128,256]{1,0:T(8,128)S(1)}, f32[128,256]{1,0:T(8,128)S(1)}) custom-call(s32[1]{0:T(128)} %bitcast.refs_0_.where_ref, bf16[272,256]{1,0:T(8,128)(2,1)S(1)} %get-tuple-element.44.refs_1_.refs_3_.mine_ref, bf16[272,256]{1,0:T(8,128)(2,1)S(1)} %collective-permute-done.1.refs_2_.refs_4_.other_ref, ...), custom_call_target="tpu_custom_call" | custom-call | flops 2000000000 | bytes 4000000 | tf_op jit(solution)/shard_map/voxels_own_row/pallas_call | solution.py:289
  17.3 1.3 %collective-permute-done.5.refs_1_ = bf16[272,256]{1,0:T(8,128)(2,1)S(1)} collective-permute-done((bf16[272,256]{1,0:T(8,128)(2,1)S(1)}, bf16[272,256]{1,0:T(8,128)(2,1)S(1)}, u32[]{:S(2)}, u32[]{:S(2)}) %collective-permute-start.5) | collective-permute-done | bytes 139296 | tf_op jit(solution)/shard_map/ppermute | solution.py:271
  18.5 1.0 %collective-permute-start.6 = (bf16[272,256]{1,0:T(8,128)(2,1)S(1)}, bf16[272,256]{1,0:T(8,128)(2,1)S(1)}, u32[]{:S(2)}, u32[]{:S(2)}) collective-permute-start(bf16[272,256]{1,0:T(8,128)(2,1)S(1)} %collective-permute-done.5.refs_1_), channel_id=1, source_target_pairs={{0,2},{2,0},{4,6},{6,4},{8,10},{10,8},{12,14},{14,12},{1,3},{3,1},... | collective-permute-start | bytes 417800 | tf_op jit(solution)/shard_map/ppermute | solution.py:268
  19.6 0.0 collective-permute-done.4.refs_2_.refs_4_.before_other
  19.6 2.1 %weight_row_1.1 = (f32[1664,128]{1,0:T(8,128)S(1)}, f32[1664,128]{1,0:T(8,128)S(1)}, f32[128,128]{1,0:T(8,128)S(1)}) custom-call(s32[1]{0:T(128)} %bitcast.refs_0_.where_ref, bf16[272,256]{1,0:T(8,128)(2,1)S(1)} %collective-permute-done.3.refs_1_.refs_3_.before_mine, bf16[272,256]{1,0:T(8,128)(2,1)S(1)} %collective-permute-done.4.refs_2_.refs_4_.before_other, ...), custom_call_target="tpu_custom_call" | custom-call | flops 2000000000 | bytes 4000000 | tf_op jit(solution)/shard_map/weight_row_1/pallas_call | solution.py:327
  21.7 0.0 collective-permute-done.2.refs_2_.refs_6_.after_other
  21.7 2.1 %weight_row_2.1 = (f32[1664,128]{1,0:T(8,128)S(1)}, f32[1664,128]{1,0:T(8,128)S(1)}, f32[128,128]{1,0:T(8,128)S(1)}) custom-call(s32[1]{0:T(128)} %bitcast.refs_0_.where_ref, bf16[272,256]{1,0:T(8,128)(2,1)S(1)} %collective-permute-done.refs_1_.refs_5_.after_mine, bf16[272,256]{1,0:T(8,128)(2,1)S(1)} %collective-permute-done.2.refs_2_.refs_6_.after_other, ...), custom_call_target="tpu_custom_call" | custom-call | flops 2000000000 | bytes 4000000 | tf_op jit(solution)/shard_map/weight_row_2/pallas_call | solution.py:327
  23.9 0.0 collective-permute-done.6.refs_2_
  23.9 1.9 %weight_row_3.1 = (bf16[18,128,128]{2,1,0:T(8,128)(2,1)S(1)}, bf16[768,256]{1,0:T(8,128)(2,1)S(1)}, bf16[256,768]{1,0:T(8,128)(2,1)S(1)}, f32[5,16,128]{2,1,0:T(8,128)S(1)}) custom-call(s32[1]{0:T(128)} %bitcast.refs_0_.where_ref, bf16[272,256]{1,0:T(8,128)(2,1)S(1)} %collective-permute-done.5.refs_1_, bf16[272,256]{1,0:T(8,128)(2,1)S(1)} %collective-permute-done.6.refs_2_, ...), custom_call_target="tpu_custom_call" | custom-call | flops 2000000000 | bytes 4000000 | tf_op jit(solution)/shard_map/weight_row_3/pallas_call | solution.py:327
  25.8 0.1 collective-permute-start.7
  25.9 0.8 %weight_row_3_middle.1.middle_ref = bf16[9,128,128]{2,1,0:T(8,128)(2,1)S(1)} custom-call(s32[1]{0:T(128)} %bitcast.refs_0_.where_ref, bf16[768,256]{1,0:T(8,128)(2,1)S(1)} %get-tuple-element.65.refs_1_, bf16[256,768]{1,0:T(8,128)(2,1)S(1)} %get-tuple-element.66.refs_2_, f32[5,16,128]{2,1,0:T(8,128)S(1)} %get-tuple-element.67.refs_3_, ...), custom_call_target="tpu_custom_call" | custom-call | flops 2000000000 | bytes 4000000 | tf_op jit(solution)/shard_map/weight_row_3_middle/pallas_call | solution.py:327
  26.6 0.6 %collective-permute-start.8 = (bf16[9,128,128]{2,1,0:T(8,128)(2,1)S(1)}, bf16[9,128,128]{2,1,0:T(8,128)(2,1)S(1)}, u32[]{:S(2)}, u32[]{:S(2)}) collective-permute-start(bf16[9,128,128]{2,1,0:T(8,128)(2,1)S(1)} %weight_row_3_middle.1.middle_ref), channel_id=1, source_target_pairs={{0,1},{1,0},{2,3},{3,2},{4,5},{5,4},{6,7},{7,6},{8,9},{9,8},{10,11... | collective-permute-start | bytes 884744 | tf_op jit(solution)/shard_map/ppermute | solution.py:342
  27.2 0.9 %voxel_edges.1 = (bf16[256,128]{1,0:T(8,128)(2,1)S(1)}, bf16[256,128]{1,0:T(8,128)(2,1)S(1)}) custom-call(s32[1]{0:T(128)} %bitcast.refs_0_.where_ref, bf16[272,256]{1,0:T(8,128)(2,1)S(1)} %collective-permute-done.3.refs_1_.refs_3_.before_mine, bf16[272,256]{1,0:T(8,128)(2,1)S(1)} %collective-permute-done.4.refs_2_.refs_4_.before_other, ...), custom_call_target="tpu_custom_call" | custom-call | flops 1000000000 | bytes 4000000 | tf_op jit(solution)/shard_map/voxel_edges/pallas_call | solution.py:359
  28.1 0.3 collective-permute-done.8.middle_sent
  28.4 0.0 collective-permute-done.7.sides_sent
  28.4 1.3 %finish.1 = (f32[27,128,128]{2,1,0:T(8,128)}, bf16[256,128]{1,0:T(8,128)(2,1)}, bf16[256,128]{1,0:T(8,128)(2,1)}) custom-call(bf16[18,128,128]{2,1,0:T(8,128)(2,1)S(1)} %get-tuple-element.64.sides_ref, bf16[18,128,128]{2,1,0:T(8,128)(2,1)S(1)} %collective-permute-done.7.sides_sent, bf16[9,128,128]{2,1,0:T(8,128)(2,1)S(1)} %weight_row_3_middle.1.middle_ref, ...), custom_call_target="tpu_custom_call" | custom-call | tf_op jit(solution)/shard_map/finish/pallas_call | solution.py:374
Async XLA Ops:
  2.3 8.9 %collective-permute-start.3 = (bf16[272,256]{1,0:T(8,128)(2,1)S(1)}, bf16[272,256]{1,0:T(8,128)(2,1)S(1)}, u32[]{:S(2)}, u32[]{:S(2)}) collective-permute-start(bf16[272,256]{1,0:T(8,128)(2,1)S(1)} %get-tuple-element.44.refs_1_.refs_3_.mine_ref), channel_id=1, source_target_pairs={{0,4},{2,6},{4,8},{6,10},{8,12},{10,14},{12,0},{14,2},{1,5},{3,7},... | collective-permute-start | bytes 417800 | tf_op jit(solution)/shard_map/ppermute | solution.py:271
  5.4 7.3 %collective-permute-start.1 = (bf16[272,256]{1,0:T(8,128)(2,1)S(1)}, bf16[272,256]{1,0:T(8,128)(2,1)S(1)}, u32[]{:S(2)}, u32[]{:S(2)}) collective-permute-start(bf16[272,256]{1,0:T(8,128)(2,1)S(1)} %get-tuple-element.44.refs_1_.refs_3_.mine_ref), channel_id=1, source_target_pairs={{0,2},{2,0},{4,6},{6,4},{8,10},{10,8},{12,14},{14,12},{1,3},{3,1},... | collective-permute-start | bytes 417800 | tf_op jit(solution)/shard_map/ppermute | solution.py:268
  6.9 1.2 %copy-start = (bf16[27,128,128]{2,1,0:T(8,128)(2,1)S(1)}, bf16[27,128,128]{2,1,0:T(8,128)(2,1)}, u32[]{:S(2)}) copy-start(bf16[27,128,128]{2,1,0:T(8,128)(2,1)} %w_ref) | copy-start | bytes 2654212
  8.4 6.3 %collective-permute-start = (bf16[272,256]{1,0:T(8,128)(2,1)S(1)}, bf16[272,256]{1,0:T(8,128)(2,1)S(1)}, u32[]{:S(2)}, u32[]{:S(2)}) collective-permute-start(bf16[272,256]{1,0:T(8,128)(2,1)S(1)} %get-tuple-element.44.refs_1_.refs_3_.mine_ref), channel_id=1, source_target_pairs={{0,12},{2,14},{4,0},{6,2},{8,4},{10,6},{12,8},{14,10},{1,13},{3,15... | collective-permute-start | bytes 417800 | tf_op jit(solution)/shard_map/ppermute | solution.py:271
  11.2 7.4 %collective-permute-start.5 = (bf16[272,256]{1,0:T(8,128)(2,1)S(1)}, bf16[272,256]{1,0:T(8,128)(2,1)S(1)}, u32[]{:S(2)}, u32[]{:S(2)}) collective-permute-start(bf16[272,256]{1,0:T(8,128)(2,1)S(1)} %collective-permute-done.3.refs_1_.refs_3_.before_mine), channel_id=1, source_target_pairs={{0,4},{2,6},{4,8},{6,10},{8,12},{10,14},{12,0},{14,2},{1,5},{3,7},... | collective-permute-start | bytes 417800 | tf_op jit(solution)/shard_map/ppermute | solution.py:271
  11.2 8.4 %collective-permute-start.4 = (bf16[272,256]{1,0:T(8,128)(2,1)S(1)}, bf16[272,256]{1,0:T(8,128)(2,1)S(1)}, u32[]{:S(2)}, u32[]{:S(2)}) collective-permute-start(bf16[272,256]{1,0:T(8,128)(2,1)S(1)} %collective-permute-done.3.refs_1_.refs_3_.before_mine), channel_id=1, source_target_pairs={{0,2},{2,0},{4,6},{6,4},{8,10},{10,8},{12,14},{14,12},{1,3},{3,1},... | collective-permute-start | bytes 417800 | tf_op jit(solution)/shard_map/ppermute | solution.py:268
  14.8 6.9 %collective-permute-start.2 = (bf16[272,256]{1,0:T(8,128)(2,1)S(1)}, bf16[272,256]{1,0:T(8,128)(2,1)S(1)}, u32[]{:S(2)}, u32[]{:S(2)}) collective-permute-start(bf16[272,256]{1,0:T(8,128)(2,1)S(1)} %collective-permute-done.refs_1_.refs_5_.after_mine), channel_id=1, source_target_pairs={{0,2},{2,0},{4,6},{6,4},{8,10},{10,8},{12,14},{14,12},{1,3},{3,1},... | collective-permute-start | bytes 417800 | tf_op jit(solution)/shard_map/ppermute | solution.py:268
  18.5 5.3 %collective-permute-start.6 = (bf16[272,256]{1,0:T(8,128)(2,1)S(1)}, bf16[272,256]{1,0:T(8,128)(2,1)S(1)}, u32[]{:S(2)}, u32[]{:S(2)}) collective-permute-start(bf16[272,256]{1,0:T(8,128)(2,1)S(1)} %collective-permute-done.5.refs_1_), channel_id=1, source_target_pairs={{0,2},{2,0},{4,6},{6,4},{8,10},{10,8},{12,14},{14,12},{1,3},{3,1},... | collective-permute-start | bytes 417800 | tf_op jit(solution)/shard_map/ppermute | solution.py:268
  25.8 2.6 %collective-permute-start.7 = (bf16[18,128,128]{2,1,0:T(8,128)(2,1)S(1)}, bf16[18,128,128]{2,1,0:T(8,128)(2,1)S(1)}, u32[]{:S(2)}, u32[]{:S(2)}) collective-permute-start(bf16[18,128,128]{2,1,0:T(8,128)(2,1)S(1)} %get-tuple-element.64.sides_ref), channel_id=1, source_target_pairs={{0,1},{1,0},{2,3},{3,2},{4,5},{5,4},{6,7},{7,6},{8,9},{9,8},{10,11... | collective-permute-start | bytes 1769480 | tf_op jit(solution)/shard_map/ppermute | solution.py:342
  26.6 1.8 %collective-permute-start.8 = (bf16[9,128,128]{2,1,0:T(8,128)(2,1)S(1)}, bf16[9,128,128]{2,1,0:T(8,128)(2,1)S(1)}, u32[]{:S(2)}, u32[]{:S(2)}) collective-permute-start(bf16[9,128,128]{2,1,0:T(8,128)(2,1)S(1)} %weight_row_3_middle.1.middle_ref), channel_id=1, source_target_pairs={{0,1},{1,0},{2,3},{3,2},{4,5},{5,4},{6,7},{7,6},{8,9},{9,8},{10,11... | collective-permute-start | bytes 884744 | tf_op jit(solution)/shard_map/ppermute | solution.py:342
